TPU v7x, 32 devices: a whole 2x2x4 slice. The times are simulated.
32 devices in a mesh: shard: 8 (over z, x), rep: 4 (over y, core).
Axes of the slice: x: 2, y: 2, z: 4, core: 2. Of those that a mesh axis runs over, the one named last changes fastest.
Arguments:
- embeddings: bfloat16 [51200, 1024], P('shard'), may hold values from -6 to 6
- send_index: int32 [51200], P('shard'), may hold values from 0 to 6399, as said below
- place_index: int32 [51200], P('shard'), may hold values from 0 to 6654, as said below
- slot_cluster: int32 [53248], P('shard'), may hold values from -1 to 207, as said below
- pair_list: int32 [2816, 2], P(('shard', 'rep')), may hold values from 0 to 25, as said below
Outputs:
- best_cosine: float32 [51200], P('shard')
Inputs may be any that keep to these rules, and one draw needn't show every extreme that they name: `send_index`: on each device, the entries o * 800 to (o + 1) * 800 - 1 of its block are the local documents sent to owner o; the device's 8 * 800 entries are a permutation of its 6400 documents, so each device sends exactly 800 documents to each owner. `place_index`: on each owner, the 6400 entries are distinct slots, exactly the slots whose slot_cluster is not -1. `slot_cluster`: an owner's 26 * 256 slots form 26 blocks of 256; it holds two or more clusters, each filling one or more consecutive whole blocks with its members first and 1 to 255 padding slots (-1) at the end of its last block, 256 padding slots in all. Ids of owner o lie in o * 26 to o * 26 + 25. `pair_list`: row (o * 4 + r) * 88 + p holds a pair (i, j), i <= j, of blocks of owner o that belong to one cluster; over its 352 rows, owner o lists every such pair at least once, some of them more than once.
All inputs are finite; a program needn't handle non-finite values.
Results may differ from a plain program's by a relative error of at most 0.0014.
Values may be sent and summed in bfloat16 or wider, within the bound.
No kernel may reach another device: no remote copies, remote signals or barrier semaphores. Data moves between devices by JAX's collectives and lax.ppermute only.
A program may use at most 128 MiB of HBM per device.

v0:
```python
import jax
import jax.numpy as jnp
from jax import lax
from jax.sharding import PartitionSpec as P

D = 1024
BLK = 256


def shards(embeddings, send_index, place_index, slot_cluster, pair_list):
    owners = lax.axis_size("shard")
    share = send_index.shape[0] // owners
    blocks_held = slot_cluster.shape[0] // BLK
    wide = embeddings.astype(jnp.float32)
    normed = (wide * lax.rsqrt(jnp.sum(wide * wide, axis=1, keepdims=True) + 1e-06)).astype(
        jnp.bfloat16
    )
    outgoing = normed[send_index].reshape(owners, share, D)
    arrived = lax.all_to_all(outgoing, "shard", split_axis=0, concat_axis=0, tiled=True)
    slots = (
        jnp.zeros((blocks_held * BLK, D), jnp.bfloat16).at[place_index].set(arrived.reshape(-1, D))
    )
    blocks = slots.reshape(blocks_held, BLK, D)
    cluster_blocks = slot_cluster.reshape(blocks_held, BLK)
    groups = pair_list.reshape(-1, 8, 2)
    diagonal = jnp.eye(BLK, dtype=bool)

    def visit(best, group):
        first = group[:, 0]
        second = group[:, 1]
        gram = jnp.einsum(
            "pad,pbd->pab", blocks[first], blocks[second], preferred_element_type=jnp.float32
        )
        left = cluster_blocks[first]
        right = cluster_blocks[second]
        counts = (left[:, :, None] == right[:, None, :]) & (left[:, :, None] >= 0)
        counts = counts & ~((first == second)[:, None, None] & diagonal[None, :, :])
        values = jnp.where(counts, gram, jnp.float32(-1.0))
        best = best.at[first].max(jnp.max(values, axis=2))
        best = best.at[second].max(jnp.max(values, axis=1))
        return (best, None)

    start = jnp.full((blocks_held, BLK), -1.0, jnp.float32)
    best_flat = lax.scan(visit, start, groups)[0].reshape(-1)
    merged = lax.pmax(best_flat, "rep")
    outbound = merged[place_index].reshape(owners, share)
    returned = lax.all_to_all(outbound, "shard", split_axis=0, concat_axis=0, tiled=True)
    result = jnp.zeros((embeddings.shape[0],), jnp.float32).at[send_index].set(returned.reshape(-1))
    return result


def solution(mesh):
    return jax.shard_map(
        shards,
        mesh=mesh,
        in_specs=(P("shard", None), P("shard"), P("shard"), P("shard"), P(("shard", "rep"), None)),
        out_specs=P("shard"),
        check_vma=False,
    )
```

profile of v0, /device:TPU:0, one launch (start us, length us, event | category | flops | bytes accessed | tf_op | source)
XLA Modules:
  0.0 733.4 jit_solution(12762785982610513077)
XLA Ops:
  0.0 0.8 compare_select_fusion.3
  0.8 7.4 %fusion.4 = f32[6400]{0:T(1024)S(1)} fusion(bf16[6400,1024]{1,0:T(8,128)(2,1)} %param.7), kind=kLoop, calls=%fused_computation.24 | loop fusion | flops 19654400 | bytes 13132800 | tf_op jit(solution)/shard_map/reduce_sum | solution.py:15
  8.1 11.7 %fusion.5 = bf16[6400,1024]{1,0:T(8,128)(2,1)} fusion(bf16[6400,1024]{1,0:T(8,128)(2,1)} %param.7, f32[6400]{0:T(1024)S(1)} %add_rsqrt_fusion), kind=kLoop, calls=%fused_computation.25 | loop fusion | flops 19660800 | bytes 26240000 | tf_op jit(solution)/shard_map/convert_element_type | solution.py:15
  19.9 34.7 %gather_fusion.4 = bf16[6400,1024]{1,0:T(8,128)(2,1)} fusion(bf16[6400,1024]{1,0:T(8,128)(2,1)} %fusion.5, s32[7168]{0:T(1024)S(1)} %pad_clamp_fusion.3), kind=kCustom, calls=%fused_computation.4 | custom fusion | bytes 26240000 | tf_op jit(solution)/shard_map/gather | solution.py:18
  54.5 7.4 %all-to-all-start = ((bf16[8,800,1024]{2,1,0:T(8,128)(2,1)}), bf16[8,800,1024]{2,1,0:T(8,128)(2,1)}, u32[]{:S(2)}, u32[]{:S(2)}) async-start(bf16[8,800,1024]{2,1,0:T(8,128)(2,1)} %bitcast.27), calls=%async_computation | async-start | bytes 26214400 | tf_op jit(solution)/shard_map/all_to_all | solution.py:19
  62.1 284.1 %all-to-all-done = bf16[8,800,1024]{2,1,0:T(8,128)(2,1)} async-done(((bf16[8,800,1024]{2,1,0:T(8,128)(2,1)}), bf16[8,800,1024]{2,1,0:T(8,128)(2,1)}, u32[]{:S(2)}, u32[]{:S(2)}) %all-to-all-start) | async-done | bytes 13107232 | tf_op jit(solution)/shard_map/all_to_all | solution.py:19
  346.2 41.2 %scatter_custom_fusion.2 = bf16[6656,1024]{1,0:T(8,128)(2,1)} fusion(s32[6400]{0:T(1024)S(1)} %compare_select_fusion.2, bf16[6400,1024]{1,0:T(8,128)(2,1)} %bitcast.1, bf16[]{:T(256)} %constant.23.clone.1), kind=kCustom, calls=%fused_computation.26 | custom fusion | bytes 13632000 | tf_op jit(solution)/shard_map/scatter | solution.py:21
  387.4 266.5 %while.11 = (s32[]{:T(128)}, f32[26,256]{1,0:T(8,128)S(1)}, s32[11,8,2]{1,0,2:T(8,128)S(1)}, s32[26,256]{1,0:T(8,128)S(1)}, bf16[26,256,1024]{2,1,0:T(8,128)(2,1)}, /*index=5*/s32[]{:T(128)}) while((s32[]{:T(128)}, f32[26,256]{1,0:T(8,128)S(1)}, s32[11,8,2]{1,0,2:T(8,128)S(1)}, s32[26,256]{1,0:T(8,128)S(1)}, ...), condition=%wide.region_7.8_spmd.clone, body=%wide.region_2.7_spmd.clone.sunk | while | flops 1078005760 | bytes 25432728 | solution.py:44
  388.0 7.6 %gather_fusion = bf16[8,256,1024]{2,1,0:T(8,128)(2,1)} fusion(bf16[26,256,1024]{2,1,0:T(8,128)(2,1)} %get-tuple-element.130, s32[1024]{0:T(1024)S(1)} %get-tuple-element.110), kind=kCustom, calls=%fused_computation.2.clone.clone.1 | custom fusion | bytes 8388640 | tf_op jit(solution)/shard_map/while/body/eval_jaxpr/gather | solution.py:32
  395.7 7.7 %gather_fusion.1 = bf16[8,256,1024]{2,1,0:T(8,128)(2,1)} fusion(bf16[26,256,1024]{2,1,0:T(8,128)(2,1)} %get-tuple-element.130, s32[1024]{0:T(1024)S(1)} %get-tuple-element.111), kind=kCustom, calls=%fused_computation.3.clone.clone.1 | custom fusion | bytes 8388640 | tf_op jit(solution)/shard_map/while/body/eval_jaxpr/gather | solution.py:32
  404.0 6.3 fusion.20
  412.3 7.6 %gather_fusion = bf16[8,256,1024]{2,1,0:T(8,128)(2,1)} fusion(bf16[26,256,1024]{2,1,0:T(8,128)(2,1)} %get-tuple-element.130, s32[1024]{0:T(1024)S(1)} %get-tuple-element.110), kind=kCustom, calls=%fused_computation.2.clone.clone.1 | custom fusion | bytes 8388640 | tf_op jit(solution)/shard_map/while/body/eval_jaxpr/gather | solution.py:32
  419.9 7.7 %gather_fusion.1 = bf16[8,256,1024]{2,1,0:T(8,128)(2,1)} fusion(bf16[26,256,1024]{2,1,0:T(8,128)(2,1)} %get-tuple-element.130, s32[1024]{0:T(1024)S(1)} %get-tuple-element.111), kind=kCustom, calls=%fused_computation.3.clone.clone.1 | custom fusion | bytes 8388640 | tf_op jit(solution)/shard_map/while/body/eval_jaxpr/gather | solution.py:32
  428.2 6.3 fusion.20
  436.5 7.6 %gather_fusion = bf16[8,256,1024]{2,1,0:T(8,128)(2,1)} fusion(bf16[26,256,1024]{2,1,0:T(8,128)(2,1)} %get-tuple-element.130, s32[1024]{0:T(1024)S(1)} %get-tuple-element.110), kind=kCustom, calls=%fused_computation.2.clone.clone.1 | custom fusion | bytes 8388640 | tf_op jit(solution)/shard_map/while/body/eval_jaxpr/gather | solution.py:32
  444.1 7.7 %gather_fusion.1 = bf16[8,256,1024]{2,1,0:T(8,128)(2,1)} fusion(bf16[26,256,1024]{2,1,0:T(8,128)(2,1)} %get-tuple-element.130, s32[1024]{0:T(1024)S(1)} %get-tuple-element.111), kind=kCustom, calls=%fused_computation.3.clone.clone.1 | custom fusion | bytes 8388640 | tf_op jit(solution)/shard_map/while/body/eval_jaxpr/gather | solution.py:32
  452.4 6.3 fusion.20
  460.7 7.6 %gather_fusion = bf16[8,256,1024]{2,1,0:T(8,128)(2,1)} fusion(bf16[26,256,1024]{2,1,0:T(8,128)(2,1)} %get-tuple-element.130, s32[1024]{0:T(1024)S(1)} %get-tuple-element.110), kind=kCustom, calls=%fused_computation.2.clone.clone.1 | custom fusion | bytes 8388640 | tf_op jit(solution)/shard_map/while/body/eval_jaxpr/gather | solution.py:32
  468.4 7.7 %gather_fusion.1 = bf16[8,256,1024]{2,1,0:T(8,128)(2,1)} fusion(bf16[26,256,1024]{2,1,0:T(8,128)(2,1)} %get-tuple-element.130, s32[1024]{0:T(1024)S(1)} %get-tuple-element.111), kind=kCustom, calls=%fused_computation.3.clone.clone.1 | custom fusion | bytes 8388640 | tf_op jit(solution)/shard_map/while/body/eval_jaxpr/gather | solution.py:32
  476.7 6.3 fusion.20
  485.0 7.6 %gather_fusion = bf16[8,256,1024]{2,1,0:T(8,128)(2,1)} fusion(bf16[26,256,1024]{2,1,0:T(8,128)(2,1)} %get-tuple-element.130, s32[1024]{0:T(1024)S(1)} %get-tuple-element.110), kind=kCustom, calls=%fused_computation.2.clone.clone.1 | custom fusion | bytes 8388640 | tf_op jit(solution)/shard_map/while/body/eval_jaxpr/gather | solution.py:32
  492.6 7.7 %gather_fusion.1 = bf16[8,256,1024]{2,1,0:T(8,128)(2,1)} fusion(bf16[26,256,1024]{2,1,0:T(8,128)(2,1)} %get-tuple-element.130, s32[1024]{0:T(1024)S(1)} %get-tuple-element.111), kind=kCustom, calls=%fused_computation.3.clone.clone.1 | custom fusion | bytes 8388640 | tf_op jit(solution)/shard_map/while/body/eval_jaxpr/gather | solution.py:32
  500.9 6.3 fusion.20
  507.1 0.7 scatter_fusion
  507.8 0.7 scatter_fusion.1
  509.2 7.6 %gather_fusion = bf16[8,256,1024]{2,1,0:T(8,128)(2,1)} fusion(bf16[26,256,1024]{2,1,0:T(8,128)(2,1)} %get-tuple-element.130, s32[1024]{0:T(1024)S(1)} %get-tuple-element.110), kind=kCustom, calls=%fused_computation.2.clone.clone.1 | custom fusion | bytes 8388640 | tf_op jit(solution)/shard_map/while/body/eval_jaxpr/gather | solution.py:32
  516.8 7.7 %gather_fusion.1 = bf16[8,256,1024]{2,1,0:T(8,128)(2,1)} fusion(bf16[26,256,1024]{2,1,0:T(8,128)(2,1)} %get-tuple-element.130, s32[1024]{0:T(1024)S(1)} %get-tuple-element.111), kind=kCustom, calls=%fused_computation.3.clone.clone.1 | custom fusion | bytes 8388640 | tf_op jit(solution)/shard_map/while/body/eval_jaxpr/gather | solution.py:32
  525.1 6.3 fusion.20
  533.4 7.6 %gather_fusion = bf16[8,256,1024]{2,1,0:T(8,128)(2,1)} fusion(bf16[26,256,1024]{2,1,0:T(8,128)(2,1)} %get-tuple-element.130, s32[1024]{0:T(1024)S(1)} %get-tuple-element.110), kind=kCustom, calls=%fused_computation.2.clone.clone.1 | custom fusion | bytes 8388640 | tf_op jit(solution)/shard_map/while/body/eval_jaxpr/gather | solution.py:32
  541.0 7.7 %gather_fusion.1 = bf16[8,256,1024]{2,1,0:T(8,128)(2,1)} fusion(bf16[26,256,1024]{2,1,0:T(8,128)(2,1)} %get-tuple-element.130, s32[1024]{0:T(1024)S(1)} %get-tuple-element.111), kind=kCustom, calls=%fused_computation.3.clone.clone.1 | custom fusion | bytes 8388640 | tf_op jit(solution)/shard_map/while/body/eval_jaxpr/gather | solution.py:32
  549.3 6.3 fusion.20
  557.6 7.6 %gather_fusion = bf16[8,256,1024]{2,1,0:T(8,128)(2,1)} fusion(bf16[26,256,1024]{2,1,0:T(8,128)(2,1)} %get-tuple-element.130, s32[1024]{0:T(1024)S(1)} %get-tuple-element.110), kind=kCustom, calls=%fused_computation.2.clone.clone.1 | custom fusion | bytes 8388640 | tf_op jit(solution)/shard_map/while/body/eval_jaxpr/gather | solution.py:32
  565.3 7.7 %gather_fusion.1 = bf16[8,256,1024]{2,1,0:T(8,128)(2,1)} fusion(bf16[26,256,1024]{2,1,0:T(8,128)(2,1)} %get-tuple-element.130, s32[1024]{0:T(1024)S(1)} %get-tuple-element.111), kind=kCustom, calls=%fused_computation.3.clone.clone.1 | custom fusion | bytes 8388640 | tf_op jit(solution)/shard_map/while/body/eval_jaxpr/gather | solution.py:32
  573.6 6.3 fusion.20
  581.9 7.6 %gather_fusion = bf16[8,256,1024]{2,1,0:T(8,128)(2,1)} fusion(bf16[26,256,1024]{2,1,0:T(8,128)(2,1)} %get-tuple-element.130, s32[1024]{0:T(1024)S(1)} %get-tuple-element.110), kind=kCustom, calls=%fused_computation.2.clone.clone.1 | custom fusion | bytes 8388640 | tf_op jit(solution)/shard_map/while/body/eval_jaxpr/gather | solution.py:32
  589.5 7.7 %gather_fusion.1 = bf16[8,256,1024]{2,1,0:T(8,128)(2,1)} fusion(bf16[26,256,1024]{2,1,0:T(8,128)(2,1)} %get-tuple-element.130, s32[1024]{0:T(1024)S(1)} %get-tuple-element.111), kind=kCustom, calls=%fused_computation.3.clone.clone.1 | custom fusion | bytes 8388640 | tf_op jit(solution)/shard_map/while/body/eval_jaxpr/gather | solution.py:32
  597.8 6.3 fusion.20
  606.1 7.6 %gather_fusion = bf16[8,256,1024]{2,1,0:T(8,128)(2,1)} fusion(bf16[26,256,1024]{2,1,0:T(8,128)(2,1)} %get-tuple-element.130, s32[1024]{0:T(1024)S(1)} %get-tuple-element.110), kind=kCustom, calls=%fused_computation.2.clone.clone.1 | custom fusion | bytes 8388640 | tf_op jit(solution)/shard_map/while/body/eval_jaxpr/gather | solution.py:32
  613.7 7.7 %gather_fusion.1 = bf16[8,256,1024]{2,1,0:T(8,128)(2,1)} fusion(bf16[26,256,1024]{2,1,0:T(8,128)(2,1)} %get-tuple-element.130, s32[1024]{0:T(1024)S(1)} %get-tuple-element.111), kind=kCustom, calls=%fused_computation.3.clone.clone.1 | custom fusion | bytes 8388640 | tf_op jit(solution)/shard_map/while/body/eval_jaxpr/gather | solution.py:32
  622.0 6.3 fusion.20
  629.0 0.7 scatter_fusion.1
  630.3 7.6 %gather_fusion = bf16[8,256,1024]{2,1,0:T(8,128)(2,1)} fusion(bf16[26,256,1024]{2,1,0:T(8,128)(2,1)} %get-tuple-element.130, s32[1024]{0:T(1024)S(1)} %get-tuple-element.110), kind=kCustom, calls=%fused_computation.2.clone.clone.1 | custom fusion | bytes 8388640 | tf_op jit(solution)/shard_map/while/body/eval_jaxpr/gather | solution.py:32
  637.9 7.7 %gather_fusion.1 = bf16[8,256,1024]{2,1,0:T(8,128)(2,1)} fusion(bf16[26,256,1024]{2,1,0:T(8,128)(2,1)} %get-tuple-element.130, s32[1024]{0:T(1024)S(1)} %get-tuple-element.111), kind=kCustom, calls=%fused_computation.3.clone.clone.1 | custom fusion | bytes 8388640 | tf_op jit(solution)/shard_map/while/body/eval_jaxpr/gather | solution.py:32
  646.2 6.3 fusion.20
  653.9 10.3 %pmax.7 = f32[6656]{0:T(1024)S(1)} all-reduce(f32[6656]{0:T(1024)S(1)} %reshape.54), channel_id=1, replica_groups=mesh['shard'=8,'rep'=4] {'rep'}, use_global_device_ids=true, to_apply=%region_8.9 | all-reduce | flops 6656 | bytes 53248 | tf_op jit(solution)/shard_map/pmax | solution.py:45
  664.2 33.2 %gather_fusion.5 = f32[6400]{0:T(1024)S(1)} fusion(f32[6656]{0:T(1024)S(1)} %pmax.7, s32[7168]{0:T(1024)S(1)} %pad_clamp_fusion.2), kind=kCustom, calls=%fused_computation.5 | custom fusion | bytes 76800 | tf_op jit(solution)/shard_map/gather | solution.py:46
  697.6 11.2 %all_to_all.14 = f32[8,1,800]{2,1,0:T(1,128)S(1)} all-to-all(f32[8,1,800]{2,1,0:T(1,128)S(1)} %all_to_all.10), channel_id=1, replica_groups=mesh['shard'=8,'rep'=4] {'shard'}, dimensions={0} | all-to-all | bytes 51200 | tf_op jit(solution)/shard_map/all_to_all | solution.py:47
  708.9 24.5 %scatter_custom_fusion.3 = f32[6400]{0:T(1024)} fusion(s32[6400]{0:T(1024)S(1)} %compare_select_fusion.3, f32[6400]{0:T(1024)S(1)} %reshape.132, f32[]{:T(128)} %constant.3.clone.1), kind=kCustom, calls=%fused_computation.33 | custom fusion | bytes 25604 | tf_op jit(solution)/shard_map/scatter | solution.py:48
  (124 shorter events, 26.6 us)
Async XLA Ops:
  54.5 7.4 %copy-start.1 = (s32[6656]{0:T(1024)S(1)}, s32[6656]{0:T(1024)}, u32[]{:S(2)}) copy-start(s32[6656]{0:T(1024)} %param.10) | copy-start | bytes 79876
  54.5 7.4 %copy-start.2 = (s32[88,2]{0,1:T(2,128)S(1)}, s32[88,2]{0,1:T(2,128)}, u32[]{:S(2)}) copy-start(s32[88,2]{0,1:T(2,128)} %param.11) | copy-start | bytes 2116
  54.5 7.5 %copy-start = (s32[6400]{0:T(1024)S(1)}, s32[6400]{0:T(1024)}, u32[]{:S(2)}) copy-start(s32[6400]{0:T(1024)} %param.9) | copy-start | bytes 76804
  54.5 291.7 %all-to-all-start = ((bf16[8,800,1024]{2,1,0:T(8,128)(2,1)}), bf16[8,800,1024]{2,1,0:T(8,128)(2,1)}, u32[]{:S(2)}, u32[]{:S(2)}) async-start(bf16[8,800,1024]{2,1,0:T(8,128)(2,1)} %bitcast.27), calls=%async_computation | async-start | bytes 26214400 | tf_op jit(solution)/shard_map/all_to_all | solution.py:19
where the time goes:
time: 735 us; the launch traced here: 733 us
  local copies, waits for them, and re-layouts  315 us (43%)
  waiting for transfers between devices  284 us (39%)
  matrix products  68.8 us (9%)
  other arithmetic  35.8 us (5%)
  blocking collectives  21.5 us (3%)
  starting transfers between devices  7.39 us (1%)
    all_to_all x1, waiting for transfers between devices, shards(): lax.all_to_all(outgoing, 'shard', split_axis=0, concat_axis=0, tiled=True)  284 us
    gather x11, local copies, waits for them, and re-layouts, visit(): blocks[second]  84.6 us
    gather x11, local copies, waits for them, and re-layouts, visit(): blocks[first]  83.9 us
    dot_general x11, matrix products, visit(): jnp.einsum('pad,pbd->pab', blocks[first], blocks[second], preferred_eleme...  68.8 us
    scatter x1, local copies, waits for them, and re-layouts, shards(): jnp.zeros((blocks_held * BLK, D), jnp.bfloat16).at[place_index]  41.2 us
    gather x1, local copies, waits for them, and re-layouts, shards(): outgoing = normed[send_index].reshape(owners, share, D)  34.7 us
    gather x1, local copies, waits for them, and re-layouts, shards(): outbound = merged[place_index].reshape(owners, share)  33.2 us
    scatter x1, local copies, waits for them, and re-layouts, shards(): jnp.zeros((embeddings.shape[0],), jnp.float32).at[send_index]  24.5 us
  transfers between devices with their start and end apart: 1, of which 1 were waited for; matrix products, arithmetic and copies ran while one was open for 0% of the time, Pallas kernels for 0%

commit v1 on v0

v1 whole, which is shorter than its diff:
```python
import functools

import jax
import jax.numpy as jnp
import numpy as np
from jax import lax
from jax.experimental import pallas as pl
from jax.experimental.pallas import tpu as pltpu
from jax.sharding import PartitionSpec as P

BLK = 256
LANES = 128
NT = (((1,), (1,)), ((), ()))
VMEM_LIMIT = 56 * 1024 * 1024

HOSTS = (2, 3, 4, 5)
ROUNDS = ((4, 6, 5, 7, 2, 1, 3), (2, 1, 3, 6, 4, 7, 5))


def host_of(owner):
    z, x = owner // 2, owner % 2
    return (1 if z < 2 else 2) * 2 + x, z % 2


def plan():
    owner_at = {host_of(owner): owner for owner in range(8)}
    sends = np.zeros((8, 4, 4), np.int32)
    order = np.zeros((8, 4, 16), np.int32)
    for s in range(8):
        for rep in range(4):
            y, core = divmod(rep, 2)
            steps = [(step, k) for step, k in enumerate(ROUNDS[core]) if s ^ k in HOSTS]
            assert [step // 2 for step, _ in steps] == list(range(len(steps)))
            targets = [s ^ k for _, k in steps]
            if s in HOSTS:
                targets.append(s)
            sends[s, rep] = [owner_at[target, y] for target in targets]
            for side in range(2):
                half = core ^ side
                for step, k in enumerate((0,) + ROUNDS[half]):
                    order[s, rep, 2 * step + side] = (s ^ k) * 2 + half
    return sends, order


def round_pairs(step):
    pairs = []
    for rep in range(4):
        for host in HOSTS:
            pairs.append(((host ^ ROUNDS[rep % 2][step]) * 4 + rep, host * 4 + rep))
    return pairs


SIBLINGS = [(host * 4 + rep, host * 4 + (rep ^ 1)) for host in HOSTS for rep in range(4)]


def metadata_pairs():
    pairs = []
    for owner in range(8):
        host, y = host_of(owner)
        for core in range(2):
            pairs.append((owner * 4 + y * 2 + core, host * 4 + y * 2 + core))
    return pairs


def normalize(rows):
    wide = rows.astype(jnp.float32)
    return (wide * lax.rsqrt(jnp.sum(wide * wide, axis=1, keepdims=True) + 1e-06)).astype(
        jnp.bfloat16
    )


def arrival_clusters(place_index, slot_cluster):
    heads = slot_cluster.reshape(-1, BLK)[:, 0]
    block = place_index // BLK
    hit = block[None, :] == jnp.arange(heads.shape[0], dtype=jnp.int32)[:, None]
    return jnp.sum(jnp.where(hit, heads[:, None], 0), axis=0)


def row_layout(column, size):
    return jnp.max(jnp.transpose(column), axis=0, keepdims=True)[:, :size]


def gram_kernel(news, count, size, first, *refs):
    chunks = refs[:count]
    cluster_row, cluster_column, best_ref, held, acc, sems = refs[count:]
    for i in range(count):
        pltpu.make_async_copy(chunks[i], held.at[i], sems.at[i]).start()
    best_ref[...] = jnp.full_like(best_ref, -1.0)
    ids = lax.broadcasted_iota(jnp.int32, (size, size), 0)
    diagonal = ids == lax.broadcasted_iota(jnp.int32, (size, size), 1)
    for a in range(news):
        pltpu.make_async_copy(chunks[a], held.at[a], sems.at[a]).wait()
    for a in range(news):
        acc[...] = jnp.full_like(acc, -1.0)

        def visit(i, _, a=a):
            @pl.when((a == 0) & (i >= news))
            def _():
                pltpu.make_async_copy(held.at[i], held.at[i], sems.at[i]).wait()

            gram = lax.dot_general(held[a], held[i], NT, preferred_element_type=jnp.float32)
            left = jnp.tile(cluster_column[a], (1, -(-size // LANES)))[:, :size]
            counts = (left == cluster_row[i]) & ~((i == a) & diagonal)
            values = jnp.where(counts, gram, jnp.float32(-1.0))
            best_ref[i] = jnp.maximum(best_ref[i], jnp.max(values, axis=0, keepdims=True))
            acc[0:size, :] = jnp.maximum(
                acc[0:size, :], jnp.broadcast_to(jnp.max(values, axis=1, keepdims=True), (size, LANES))
            )
            return 0

        lax.fori_loop(first, count, visit, 0)
        best_ref[a] = jnp.maximum(best_ref[a], row_layout(acc[...], size))


def gram_best(chunks, news, cluster_row, first=0):
    count = len(chunks)
    size, width = chunks[0].shape
    padded = -(-size // LANES) * LANES
    cluster_column = jnp.broadcast_to(cluster_row[:news, 0, :, None], (news, size, LANES))
    return pl.pallas_call(
        functools.partial(gram_kernel, news, count, size, first),
        out_shape=jax.ShapeDtypeStruct((count, 1, size), jnp.float32),
        in_specs=[pl.BlockSpec(memory_space=pl.ANY)] * count
        + [pl.BlockSpec(memory_space=pltpu.VMEM)] * 2,
        out_specs=pl.BlockSpec(memory_space=pltpu.VMEM),
        scratch_shapes=[
            pltpu.VMEM((count, size, width), jnp.bfloat16),
            pltpu.VMEM((padded, LANES), jnp.float32),
            pltpu.SemaphoreType.DMA((count,)),
        ],
        compiler_params=pltpu.CompilerParams(vmem_limit_bytes=VMEM_LIMIT),
        cost_estimate=pl.CostEstimate(
            flops=2 * news * count * size * size * width,
            bytes_accessed=2 * count * size * width,
            transcendentals=0,
        ),
    )(*chunks, cluster_row, cluster_column)


def settle_kernel(groups, size, high, index_ref, values_ref, out_ref):
    total = jnp.zeros((high, LANES), jnp.float32)
    for g in range(groups):
        index = index_ref[g : g + 1, :]
        rows = lax.broadcasted_iota(jnp.int32, (high, size), 0)
        lanes = lax.broadcasted_iota(jnp.int32, (LANES, size), 0)
        left = jnp.where(rows == index // LANES, values_ref[g : g + 1, :], 0.0)
        right = jnp.where(lanes == index % LANES, jnp.float32(1.0), jnp.float32(0.0))
        total += lax.dot_general(
            left, right, NT, precision=lax.Precision.HIGHEST, preferred_element_type=jnp.float32
        )
    out_ref[...] = total


def settle(index, values, documents):
    groups, size = index.shape
    high = -(-documents // (8 * LANES)) * 8
    out = pl.pallas_call(
        functools.partial(settle_kernel, groups, size, high),
        out_shape=jax.ShapeDtypeStruct((high, LANES), jnp.float32),
        compiler_params=pltpu.CompilerParams(vmem_limit_bytes=VMEM_LIMIT),
    )(index, values)
    return out.reshape(-1)[:documents]


def hosted(embeddings, send_index, place_index, slot_cluster):
    documents = embeddings.shape[0]
    share = send_index.shape[0] // 8
    size = share // 2
    s, rep = lax.axis_index("shard"), lax.axis_index("rep")
    core = rep % 2
    axes = ("shard", "rep")
    sends, order = plan()
    sends = jnp.asarray(sends)[s, rep]
    order = jnp.asarray(order)[s, rep]
    outgoing = []
    for slot in range(4):
        index = lax.dynamic_slice(send_index, (sends[slot] * share + core * size,), (size,))
        outgoing.append(normalize(embeddings.at[index].get(mode="promise_in_bounds")))
    clusters = lax.ppermute(arrival_clusters(place_index, slot_cluster), axes, metadata_pairs())
    clusters = clusters.reshape(16, 1, size)[order]
    own = [outgoing[3]] + [lax.ppermute(outgoing[r // 2], axes, round_pairs(r)) for r in range(7)]
    other = [lax.ppermute(chunk, axes, SIBLINGS) for chunk in own]

    best = jnp.full((16, 1, size), -1.0, jnp.float32)
    for steps in ((0, 1, 2, 3), (4, 5), (6,), (7,)):
        news = [2 * step for step in steps]
        rest = [i for i in range(2 * steps[-1] + 2) if i not in news]
        picks = news + rest
        chunks = [(own, other)[i % 2][i // 2] for i in picks]
        found = gram_best(chunks, len(news), clusters[jnp.asarray(picks)])
        best = best.at[jnp.asarray(picks)].max(found)
    home = jnp.zeros((16, size), jnp.float32).at[order].set(best[:, 0])
    outbound = jnp.broadcast_to(home.reshape(8, 1, 2, size), (8, 4, 2, size)).reshape(32, 2, size)
    returned = lax.all_to_all(outbound, axes, split_axis=0, concat_axis=0, tiled=True)
    returned = jnp.max(returned.reshape(8, 2, 2, 2, size), axis=2)
    values = jnp.concatenate([returned[host_of(owner)] for owner in range(8)])
    return settle(send_index.reshape(16, size), values, documents)


def gathered(embeddings, send_index, place_index, slot_cluster):
    documents, width = embeddings.shape
    owners = lax.axis_size("shard")
    reps = lax.axis_size("rep")
    rep = lax.axis_index("rep")
    share = send_index.shape[0] // owners
    outgoing = normalize(embeddings.at[send_index].get(mode="promise_in_bounds"))
    arrived = lax.all_to_all(
        outgoing.reshape(owners, share, width), "shard", split_axis=0, concat_axis=0, tiled=True
    )
    parts = 16
    size = documents // parts
    news = parts // reps
    turn = rep * news
    arrived = jnp.roll(arrived.reshape(parts, size, width), -turn, axis=0)
    clusters = arrival_clusters(place_index, slot_cluster).reshape(parts, 1, size)
    clusters = jnp.roll(clusters, -turn, axis=0)
    best = gram_best([arrived[i] for i in range(parts)], news, clusters)[:news]
    best = lax.all_gather(best.reshape(-1), "rep", axis=0, tiled=True)
    returned = lax.all_to_all(
        best.reshape(owners, share), "shard", split_axis=0, concat_axis=0, tiled=True
    )
    return settle(send_index.reshape(parts, size), returned.reshape(parts, size), documents)


def solution(mesh):
    planned = mesh.shape["shard"] == 8 and mesh.shape["rep"] == 4

    def shards(embeddings, send_index, place_index, slot_cluster, pair_list):
        del pair_list
        run = hosted if planned else gathered
        return run(embeddings, send_index, place_index, slot_cluster)

    return jax.shard_map(
        shards,
        mesh=mesh,
        in_specs=(P("shard", None), P("shard"), P("shard"), P("shard"), P(("shard", "rep"), None)),
        out_specs=P("shard"),
        check_vma=False,
    )
```

time: 735 us -> 232 us (0.32)
  waiting for transfers between devices: 284 us -> 18.6 us
  local copies, waits for them, and re-layouts: 315 us -> 52.2 us
  Pallas kernels: 0 us -> 80 us
  matrix products: 68.8 us -> 0 us
  starting transfers between devices: 7.39 us -> 68.7 us
  other arithmetic: 35.8 us -> 8.33 us
  blocking collectives: 21.5 us -> 0 us
    all_to_all x1, waiting for transfers between devices: 284 us -> 7.3 us  [hosted(): lax.all_to_all(outbound, axes, split_axis=0, concat_axis=0, tiled=True)]
    gather x46 -> x13, local copies, waits for them, and re-layouts: 249 us -> 42.1 us  [the longest x4 36.7 us: hosted(): embeddings.at[index].get(mode='promise_in_bounds')]
    pallas_call x0 -> x5, Pallas kernels: none -> 80 us  [the longest x4 73.8 us: gram_best(): pl.pallas_call(functools.partial(gram_kernel, news, count, size, first),...]
    dot_general x11 -> x0, matrix products: 68.8 us -> none  [visit(): jnp.einsum('pad,pbd->pab', blocks[first], blocks[second], preferred_eleme...]
    scatter x2 -> x1, local copies, waits for them, and re-layouts: 65.7 us -> 0.67 us  [hosted(): home = jnp.zeros((16, size), jnp.float32).at[order].set(best[:, 0])]
    ppermute x0 -> x16, starting transfers between devices: none -> 60.3 us  [the longest x7 48.2 us: hosted(): lax.ppermute(outgoing[r // 2], axes, round_pairs(r))]
    another operation x22 -> x4, other arithmetic: 15.3 us -> 3.7 us  [hosted(): best = best.at[jnp.asarray(picks)].max(found)]
    ppermute x0 -> x16, waiting for transfers between devices: none -> 11.3 us  [the longest x7 6.21 us: hosted(): lax.ppermute(outgoing[r // 2], axes, round_pairs(r))]
  transfers between devices with their start and end apart: 1 -> 17, of which waited for: 1 -> 3; matrix products, arithmetic and copies ran while one was open for 0% -> 19% of each run, Pallas kernels for 0% -> 26%
where the time goes in v1:
time: 232 us; the launch traced here: 231 us
  Pallas kernels  80 us (34%)
  starting transfers between devices  68.7 us (30%)
  local copies, waits for them, and re-layouts  52.2 us (22%)
  waiting for transfers between devices  18.6 us (8%)
  other arithmetic  8.33 us (4%)
  between operations  3.05 us (1%)
    pallas_call x4, Pallas kernels, gram_best(): pl.pallas_call(functools.partial(gram_kernel, news, count, size, first),...  73.8 us
    ppermute x7, starting transfers between devices, hosted(): lax.ppermute(outgoing[r // 2], axes, round_pairs(r))  48.2 us
    gather x4, local copies, waits for them, and re-layouts, hosted(): embeddings.at[index].get(mode='promise_in_bounds')  36.7 us
    ppermute x8, starting transfers between devices, hosted(): other = [lax.ppermute(chunk, axes, SIBLINGS) for chunk in own]  10.8 us
    all_to_all x1, starting transfers between devices, hosted(): lax.all_to_all(outbound, axes, split_axis=0, concat_axis=0, tiled=True)  8.48 us
    all_to_all x1, waiting for transfers between devices, hosted(): lax.all_to_all(outbound, axes, split_axis=0, concat_axis=0, tiled=True)  7.3 us
    ppermute x7, waiting for transfers between devices, hosted(): lax.ppermute(outgoing[r // 2], axes, round_pairs(r))  6.21 us
    pallas_call x1, Pallas kernels, settle(): pl.pallas_call(functools.partial(settle_kernel, groups, size, high), out_...  6.15 us
  transfers between devices with their start and end apart: 17, of which 3 were waited for; matrix products, arithmetic and copies ran while one was open for 19% of the time, Pallas kernels for 26%

profile of v1, /device:TPU:0, one launch (start us, length us, event | category | flops | bytes accessed | tf_op | source)
XLA Modules:
  0.0 230.9 jit_solution(6313243215275763725)
XLA Ops:
  0.0 0.7 constant_dynamic-slice_fusion
  0.7 0.7 fusion.26
  3.9 0.9 compare_select_fusion
  4.8 9.2 %gather_fusion.5 = bf16[400,1024]{1,0:T(8,128)(2,1)S(1)} fusion(bf16[6400,1024]{1,0:T(8,128)(2,1)} %param.15, s32[1024]{0:T(1024)S(1)} %get-tuple-element.21), kind=kCustom, calls=%fused_computation.5 | custom fusion | bytes 1640000 | tf_op jit(solution)/shard_map/gather | solution.py:178
  14.4 5.8 %collective-permute-start.9 = (bf16[400,1024]{1,0:T(8,128)(2,1)S(1)}, bf16[400,1024]{1,0:T(8,128)(2,1)}, u32[]{:S(2)}, u32[]{:S(2)}) collective-permute-start(bf16[400,1024]{1,0:T(8,128)(2,1)S(1)} %fusion.7), channel_id=1, source_target_pairs={{0,8},{4,12},{24,16},{28,20},{25,9},{29,13},{1,17},{5,21},{2,10},{... | collective-permute-start | bytes 2457608 | tf_op jit(solution)/shard_map/ppermute | solution.py:181
  20.2 1.6 collective-permute-start.12
  21.8 9.2 %gather_fusion.2 = bf16[400,1024]{1,0:T(8,128)(2,1)S(1)} fusion(bf16[6400,1024]{1,0:T(8,128)(2,1)} %param.15, s32[1024]{0:T(1024)S(1)} %get-tuple-element.22), kind=kCustom, calls=%fused_computation.2 | custom fusion | bytes 1640000 | tf_op jit(solution)/shard_map/gather | solution.py:178
  31.5 1.6 collective-permute-start.8
  33.1 5.9 %collective-permute-start.2 = (bf16[400,1024]{1,0:T(8,128)(2,1)S(1)}, bf16[400,1024]{1,0:T(8,128)(2,1)}, u32[]{:S(2)}, u32[]{:S(2)}) collective-permute-start(bf16[400,1024]{1,0:T(8,128)(2,1)S(1)} %fusion.5), channel_id=1, source_target_pairs={{28,8},{24,12},{4,16},{0,20},{5,9},{1,13},{29,17},{25,21},{30,10},... | collective-permute-start | bytes 2457608 | tf_op jit(solution)/shard_map/ppermute | solution.py:181
  39.3 1.3 collective-permute-start.7
  40.6 9.2 %gather_fusion.1 = bf16[400,1024]{1,0:T(8,128)(2,1)S(1)} fusion(bf16[6400,1024]{1,0:T(8,128)(2,1)} %param.15, s32[1024]{0:T(1024)S(1)} %get-tuple-element.23), kind=kCustom, calls=%fused_computation.1 | custom fusion | bytes 1640000 | tf_op jit(solution)/shard_map/gather | solution.py:178
  50.1 1.1 fusion.3
  51.2 5.1 %collective-permute-done.7 = s32[6400]{0:T(1024)S(1)} collective-permute-done((s32[6400]{0:T(1024)S(1)}, s32[6400]{0:T(1024)S(1)}, u32[]{:S(2)}, u32[]{:S(2)}) %collective-permute-start.7) | collective-permute-done | bytes 25632 | tf_op jit(solution)/shard_map/ppermute | solution.py:179
  56.3 2.2 collective-permute-start
  58.5 1.6 collective-permute-start.1
  60.1 9.2 %gather_fusion = bf16[400,1024]{1,0:T(8,128)(2,1)S(1)} fusion(bf16[6400,1024]{1,0:T(8,128)(2,1)} %param.15, s32[1024]{0:T(1024)S(1)} %get-tuple-element.24), kind=kCustom, calls=%fused_computation | custom fusion | bytes 1640000 | tf_op jit(solution)/shard_map/gather | solution.py:178
  69.8 29.6 %collective-permute-start.14 = (bf16[400,1024]{1,0:T(8,128)(2,1)S(1)}, bf16[400,1024]{1,0:T(8,128)(2,1)}, u32[]{:S(2)}, u32[]{:S(2)}) collective-permute-start(bf16[400,1024]{1,0:T(8,128)(2,1)S(1)} %fusion.1.refs_0_.refs_2_.refs_1_), channel_id=1, source_target_pairs={{4,8},{0,12},{28,16},{24,20},{29,9},{25,13},{5,17},{1,21},{6,10},{... | collective-permute-start | bytes 2457608 | tf_op jit(solution)/shard_map/ppermute | solution.py:181
  99.4 0.7 collective-permute-start.3
  100.1 0.7 collective-permute-start.6
  100.8 1.6 collective-permute-start.4
  102.4 1.6 collective-permute-start.5
  104.0 0.7 fusion.25
  106.0 0.6 reshape.174.refs_16_
  110.3 6.2 %collective-permute-done.14.refs_0_ = bf16[400,1024]{1,0:T(8,128)(2,1)} collective-permute-done((bf16[400,1024]{1,0:T(8,128)(2,1)S(1)}, bf16[400,1024]{1,0:T(8,128)(2,1)}, u32[]{:S(2)}, u32[]{:S(2)}) %collective-permute-start.14) | collective-permute-done | bytes 819232 | tf_op jit(solution)/shard_map/ppermute | solution.py:181
  116.5 1.5 collective-permute-start.10
  118.0 1.6 collective-permute-start.11
  119.6 1.6 collective-permute-start.13
  121.1 1.6 collective-permute-start.15
  122.7 1.2 broadcast_in_dim.110.refs_9_
  123.9 26.6 %shard_map.136 = f32[8,1,400]{2,1,0:T(1,128)} custom-call(bf16[400,1024]{1,0:T(8,128)(2,1)} %copy-done, bf16[400,1024]{1,0:T(8,128)(2,1)} %collective-permute-done.refs_1_.refs_4_.refs_3_, bf16[400,1024]{1,0:T(8,128)(2,1)} %collective-permute-done.1.refs_2_.refs_6_.refs_5_, bf16[400,1024]{1,0:T(8,128)(2,1)} %collective-permute-done.2.refs_3_.refs_8_.refs_7_, ...), custom_call_target="tpu_custom_call" | custom-call | flops 10485760000 | bytes 6553600 | tf_op jit(solution)/shard_map/pallas_call | solution.py:120
  150.6 0.8 scatter_custom_fusion
  151.4 1.0 broadcast_in_dim.115.refs_13_
  152.4 20.2 %shard_map.137 = f32[12,1,400]{2,1,0:T(1,128)} custom-call(bf16[400,1024]{1,0:T(8,128)(2,1)} %collective-permute-done.8.refs_0_.refs_9_, bf16[400,1024]{1,0:T(8,128)(2,1)} %collective-permute-done.9.refs_1_.refs_11_, bf16[400,1024]{1,0:T(8,128)(2,1)} %copy-done, bf16[400,1024]{1,0:T(8,128)(2,1)} %copy-done.10, ...), custom_call_target="tpu_custom_call" | custom-call | flops 7864320000 | bytes 9830400 | tf_op jit(solution)/shard_map/pallas_call | solution.py:120
  172.6 0.9 scatter_custom_fusion.1
  173.5 0.8 broadcast_in_dim.119.refs_15_
  174.4 12.8 %shard_map.138 = f32[14,1,400]{2,1,0:T(1,128)} custom-call(bf16[400,1024]{1,0:T(8,128)(2,1)} %collective-permute-done.12.refs_0_.refs_13_, bf16[400,1024]{1,0:T(8,128)(2,1)} %copy-done, bf16[400,1024]{1,0:T(8,128)(2,1)} %copy-done.10, bf16[400,1024]{1,0:T(8,128)(2,1)} %collective-permute-done.refs_1_.refs_4_.refs_3_, ...), custom_call_target="tpu_custom_call" | custom-call | flops 4587520000 | bytes 11468800 | tf_op jit(solution)/shard_map/pallas_call | solution.py:120
  187.2 1.0 scatter_custom_fusion.2
  188.2 0.8 broadcast_in_dim.123.refs_17_
  189.0 14.2 %shard_map.139 = f32[16,1,400]{2,1,0:T(1,128)} custom-call(bf16[400,1024]{1,0:T(8,128)(2,1)} %collective-permute-done.14.refs_0_, bf16[400,1024]{1,0:T(8,128)(2,1)} %copy-done, bf16[400,1024]{1,0:T(8,128)(2,1)} %copy-done.10, bf16[400,1024]{1,0:T(8,128)(2,1)} %collective-permute-done.refs_1_.refs_4_.refs_3_, ...), custom_call_target="tpu_custom_call" | custom-call | flops 5242880000 | bytes 13107200 | tf_op jit(solution)/shard_map/pallas_call | solution.py:120
  203.2 1.0 scatter_custom_fusion.3
  204.2 0.7 scatter_custom_fusion.4
  204.9 0.7 broadcast_in_dim.125
  205.6 8.5 %all-to-all-start = ((f32[32,2,400]{2,1,0:T(2,128)}), f32[32,2,400]{2,1,0:T(2,128)S(1)}, u32[]{:S(2)}, u32[]{:S(2)}) async-start(f32[32,2,400]{2,1,0:T(2,128)} %bitcast.8), calls=%async_computation | async-start | bytes 262144 | tf_op jit(solution)/shard_map/all_to_all | solution.py:194
  214.1 0.7 reshape.96.index_ref
  214.8 7.3 %all-to-all-done = f32[32,2,400]{2,1,0:T(2,128)S(1)} async-done(((f32[32,2,400]{2,1,0:T(2,128)}), f32[32,2,400]{2,1,0:T(2,128)S(1)}, u32[]{:S(2)}, u32[]{:S(2)}) %all-to-all-start) | async-done | bytes 102432 | tf_op jit(solution)/shard_map/all_to_all | solution.py:194
  222.2 1.2 concatenate.3.values_ref
  223.4 6.1 %shard_map.140 = f32[56,128]{1,0:T(8,128)} custom-call(s32[16,400]{1,0:T(8,128)} %reshape.96.index_ref, f32[16,400]{1,0:T(8,128)} %concatenate.3.values_ref), custom_call_target="tpu_custom_call" | custom-call | tf_op jit(solution)/shard_map/pallas_call | solution.py:157
  229.6 1.4 slice_bitcast_fusion
  (78 shorter events, 7.0 us)
Async XLA Ops:
  14.4 55.4 %collective-permute-start.9 = (bf16[400,1024]{1,0:T(8,128)(2,1)S(1)}, bf16[400,1024]{1,0:T(8,128)(2,1)}, u32[]{:S(2)}, u32[]{:S(2)}) collective-permute-start(bf16[400,1024]{1,0:T(8,128)(2,1)S(1)} %fusion.7), channel_id=1, source_target_pairs={{0,8},{4,12},{24,16},{28,20},{25,9},{29,13},{1,17},{5,21},{2,10},{... | collective-permute-start | bytes 2457608 | tf_op jit(solution)/shard_map/ppermute | solution.py:181
  20.2 79.1 %collective-permute-start.12 = (bf16[400,1024]{1,0:T(8,128)(2,1)S(1)}, bf16[400,1024]{1,0:T(8,128)(2,1)}, u32[]{:S(2)}, u32[]{:S(2)}) collective-permute-start(bf16[400,1024]{1,0:T(8,128)(2,1)S(1)} %fusion.7), channel_id=1, source_target_pairs={{12,8},{8,12},{20,16},{16,20},{21,9},{17,13},{13,17},{9,21},{14,10... | collective-permute-start | bytes 2457608 | tf_op jit(solution)/shard_map/ppermute | solution.py:181
  31.0 7.9 %copy-start.5 = (s32[6656]{0:T(1024)S(1)}, s32[6656]{0:T(1024)}, u32[]{:S(2)}) copy-start(s32[6656]{0:T(1024)} %param.18) | copy-start | bytes 79876
  31.0 8.1 %copy-start.4 = (s32[6400]{0:T(1024)S(1)}, s32[6400]{0:T(1024)}, u32[]{:S(2)}) copy-start(s32[6400]{0:T(1024)} %param.17) | copy-start | bytes 76804
  31.5 27.0 %collective-permute-start.8 = (bf16[400,1024]{1,0:T(8,128)(2,1)S(1)}, bf16[400,1024]{1,0:T(8,128)(2,1)}, u32[]{:S(2)}, u32[]{:S(2)}) collective-permute-start(bf16[400,1024]{1,0:T(8,128)(2,1)S(1)} %fusion.5), channel_id=1, source_target_pairs={{20,8},{16,12},{12,16},{8,20},{17,9},{21,13},{9,17},{13,21},{22,10... | collective-permute-start | bytes 2457608 | tf_op jit(solution)/shard_map/ppermute | solution.py:181
  33.1 67.0 %collective-permute-start.2 = (bf16[400,1024]{1,0:T(8,128)(2,1)S(1)}, bf16[400,1024]{1,0:T(8,128)(2,1)}, u32[]{:S(2)}, u32[]{:S(2)}) collective-permute-start(bf16[400,1024]{1,0:T(8,128)(2,1)S(1)} %fusion.5), channel_id=1, source_target_pairs={{28,8},{24,12},{4,16},{0,20},{5,9},{1,13},{29,17},{25,21},{30,10},... | collective-permute-start | bytes 2457608 | tf_op jit(solution)/shard_map/ppermute | solution.py:181
  39.3 17.0 %collective-permute-start.7 = (s32[6400]{0:T(1024)S(1)}, s32[6400]{0:T(1024)S(1)}, u32[]{:S(2)}, u32[]{:S(2)}) collective-permute-start(s32[6400]{0:T(1024)S(1)} %select_reduce_fusion), channel_id=1, source_target_pairs={{0,8},{1,9},{4,12},{5,13},{10,10},{11,11},{14,14},{15,15},{16,16},... | collective-permute-start | bytes 76808 | tf_op jit(solution)/shard_map/ppermute | solution.py:179
  56.3 44.5 %collective-permute-start = (bf16[400,1024]{1,0:T(8,128)(2,1)}, bf16[400,1024]{1,0:T(8,128)(2,1)}, u32[]{:S(2)}, u32[]{:S(2)}) collective-permute-start(bf16[400,1024]{1,0:T(8,128)(2,1)} %fusion.3), channel_id=1, source_target_pairs={{24,8},{28,12},{0,16},{4,20},{1,9},{5,13},{25,17},{29,21},{26,10},... | collective-permute-start | bytes 2457608 | tf_op jit(solution)/shard_map/ppermute | solution.py:181
  58.5 43.9 %collective-permute-start.1 = (bf16[400,1024]{1,0:T(8,128)(2,1)}, bf16[400,1024]{1,0:T(8,128)(2,1)}, u32[]{:S(2)}, u32[]{:S(2)}) collective-permute-start(bf16[400,1024]{1,0:T(8,128)(2,1)} %fusion.3), channel_id=1, source_target_pairs={{16,8},{20,12},{8,16},{12,20},{13,9},{9,13},{21,17},{17,21},{18,10... | collective-permute-start | bytes 2457608 | tf_op jit(solution)/shard_map/ppermute | solution.py:181
  69.3 35.4 %copy-start.6 = (s32[16]{0:T(128)S(1)}, s32[16]{0:T(128)}, u32[]{:S(2)}) copy-start(s32[16]{0:T(128)} %constant.110) | copy-start | bytes 196
  69.3 35.4 %copy-start.7 = (s32[14]{0:T(128)S(1)}, s32[14]{0:T(128)}, u32[]{:S(2)}) copy-start(s32[14]{0:T(128)} %constant.108) | copy-start | bytes 172
  69.3 35.4 %copy-start.8 = (s32[12]{0:T(128)S(1)}, s32[12]{0:T(128)}, u32[]{:S(2)}) copy-start(s32[12]{0:T(128)} %constant.106) | copy-start | bytes 148
  69.3 35.4 %copy-start.9 = (s32[8]{0:T(128)S(1)}, s32[8]{0:T(128)}, u32[]{:S(2)}) copy-start(s32[8]{0:T(128)} %constant.104) | copy-start | bytes 100
  69.8 54.2 %copy-start = (bf16[400,1024]{1,0:T(8,128)(2,1)}, bf16[400,1024]{1,0:T(8,128)(2,1)S(1)}, u32[]{:S(2)}) copy-start(bf16[400,1024]{1,0:T(8,128)(2,1)S(1)} %fusion.1.refs_0_.refs_2_.refs_1_) | copy-start | bytes 2457604
  69.8 46.7 %collective-permute-start.14 = (bf16[400,1024]{1,0:T(8,128)(2,1)S(1)}, bf16[400,1024]{1,0:T(8,128)(2,1)}, u32[]{:S(2)}, u32[]{:S(2)}) collective-permute-start(bf16[400,1024]{1,0:T(8,128)(2,1)S(1)} %fusion.1.refs_0_.refs_2_.refs_1_), channel_id=1, source_target_pairs={{4,8},{0,12},{28,16},{24,20},{29,9},{25,13},{5,17},{1,21},{6,10},{... | collective-permute-start | bytes 2457608 | tf_op jit(solution)/shard_map/ppermute | solution.py:181
  99.4 18.6 %collective-permute-start.3 = (bf16[400,1024]{1,0:T(8,128)(2,1)S(1)}, bf16[400,1024]{1,0:T(8,128)(2,1)S(1)}, u32[]{:S(2)}, u32[]{:S(2)}) collective-permute-start(bf16[400,1024]{1,0:T(8,128)(2,1)S(1)} %fusion.1.refs_0_.refs_2_.refs_1_), channel_id=1, source_target_pairs={{8,9},{9,8},{10,11},{11,10},{12,13},{13,12},{14,15},{15,14},{16,17... | collective-permute-start | bytes 2457608 | tf_op jit(solution)/shard_map/ppermute | solution.py:182
  100.1 19.5 %collective-permute-start.6 = (bf16[400,1024]{1,0:T(8,128)(2,1)}, bf16[400,1024]{1,0:T(8,128)(2,1)S(1)}, u32[]{:S(2)}, u32[]{:S(2)}) collective-permute-start(bf16[400,1024]{1,0:T(8,128)(2,1)} %collective-permute-done.2.refs_3_.refs_8_.refs_7_), channel_id=1, source_target_pairs={{8,9},{9,8},{10,11},{11,10},{12,13},{13,12},{14,15},{15,14},{16,17... | collective-permute-start | bytes 2457608 | tf_op jit(solution)/shard_map/ppermute | solution.py:182
  100.8 20.3 %collective-permute-start.4 = (bf16[400,1024]{1,0:T(8,128)(2,1)}, bf16[400,1024]{1,0:T(8,128)(2,1)}, u32[]{:S(2)}, u32[]{:S(2)}) collective-permute-start(bf16[400,1024]{1,0:T(8,128)(2,1)} %collective-permute-done.refs_1_.refs_4_.refs_3_), channel_id=1, source_target_pairs={{8,9},{9,8},{10,11},{11,10},{12,13},{13,12},{14,15},{15,14},{16,17... | collective-permute-start | bytes 2457608 | tf_op jit(solution)/shard_map/ppermute | solution.py:182
  102.4 20.3 %collective-permute-start.5 = (bf16[400,1024]{1,0:T(8,128)(2,1)}, bf16[400,1024]{1,0:T(8,128)(2,1)}, u32[]{:S(2)}, u32[]{:S(2)}) collective-permute-start(bf16[400,1024]{1,0:T(8,128)(2,1)} %collective-permute-done.1.refs_2_.refs_6_.refs_5_), channel_id=1, source_target_pairs={{8,9},{9,8},{10,11},{11,10},{12,13},{13,12},{14,15},{15,14},{16,17... | collective-permute-start | bytes 2457608 | tf_op jit(solution)/shard_map/ppermute | solution.py:182
  106.0 44.5 %copy-start.1 = (s32[16,400]{1,0:T(8,128)}, s32[16,400]{1,0:T(8,128)S(1)}, u32[]{:S(2)}) copy-start(s32[16,400]{1,0:T(8,128)S(1)} %gather_fusion.8) | copy-start | bytes 76804
  107.2 43.3 %copy-start.2 = (s32[14,400]{1,0:T(8,128)}, s32[14,400]{1,0:T(8,128)S(1)}, u32[]{:S(2)}) copy-start(s32[14,400]{1,0:T(8,128)S(1)} %gather_fusion.7) | copy-start | bytes 67204
  116.5 35.0 %collective-permute-start.10 = (bf16[400,1024]{1,0:T(8,128)(2,1)}, bf16[400,1024]{1,0:T(8,128)(2,1)}, u32[]{:S(2)}, u32[]{:S(2)}) collective-permute-start(bf16[400,1024]{1,0:T(8,128)(2,1)} %collective-permute-done.8.refs_0_.refs_9_), channel_id=1, source_target_pairs={{8,9},{9,8},{10,11},{11,10},{12,13},{13,12},{14,15},{15,14},{16,17... | collective-permute-start | bytes 2457608 | tf_op jit(solution)/shard_map/ppermute | solution.py:182
  118.0 5.9 %copy-start.10 = (bf16[400,1024]{1,0:T(8,128)(2,1)}, bf16[400,1024]{1,0:T(8,128)(2,1)S(1)}, u32[]{:S(2)}) copy-start(bf16[400,1024]{1,0:T(8,128)(2,1)S(1)} %collective-permute-done.3.refs_4_.refs_3_.refs_2_) | copy-start | bytes 2457604
  118.0 33.4 %collective-permute-start.11 = (bf16[400,1024]{1,0:T(8,128)(2,1)}, bf16[400,1024]{1,0:T(8,128)(2,1)}, u32[]{:S(2)}, u32[]{:S(2)}) collective-permute-start(bf16[400,1024]{1,0:T(8,128)(2,1)} %collective-permute-done.9.refs_1_.refs_11_), channel_id=1, source_target_pairs={{8,9},{9,8},{10,11},{11,10},{12,13},{13,12},{14,15},{15,14},{16,17... | collective-permute-start | bytes 2457608 | tf_op jit(solution)/shard_map/ppermute | solution.py:182
  119.6 4.4 %copy-start.11 = (bf16[400,1024]{1,0:T(8,128)(2,1)}, bf16[400,1024]{1,0:T(8,128)(2,1)S(1)}, u32[]{:S(2)}) copy-start(bf16[400,1024]{1,0:T(8,128)(2,1)S(1)} %collective-permute-done.6.refs_7_.refs_9_.refs_8_) | copy-start | bytes 2457604
  119.6 54.0 %collective-permute-start.13 = (bf16[400,1024]{1,0:T(8,128)(2,1)}, bf16[400,1024]{1,0:T(8,128)(2,1)}, u32[]{:S(2)}, u32[]{:S(2)}) collective-permute-start(bf16[400,1024]{1,0:T(8,128)(2,1)} %collective-permute-done.12.refs_0_.refs_13_), channel_id=1, source_target_pairs={{8,9},{9,8},{10,11},{11,10},{12,13},{13,12},{14,15},{15,14},{16,17... | collective-permute-start | bytes 2457608 | tf_op jit(solution)/shard_map/ppermute | solution.py:182
  121.1 67.0 %collective-permute-start.15 = (bf16[400,1024]{1,0:T(8,128)(2,1)}, bf16[400,1024]{1,0:T(8,128)(2,1)}, u32[]{:S(2)}, u32[]{:S(2)}) collective-permute-start(bf16[400,1024]{1,0:T(8,128)(2,1)} %collective-permute-done.14.refs_0_), channel_id=1, source_target_pairs={{8,9},{9,8},{10,11},{11,10},{12,13},{13,12},{14,15},{15,14},{16,17... | collective-permute-start | bytes 2457608 | tf_op jit(solution)/shard_map/ppermute | solution.py:182
  152.4 21.1 %slice-start.1 = ((s32[14,400]{1,0:T(8,128)}), s32[1,400]{1,0:T(1,128)S(1)}, s32[]{:S(2)}) async-start(s32[14,400]{1,0:T(8,128)} %copy-done.2), calls=%async_computation.2 | async-start | bytes 4096 | tf_op jit(solution)/shard_map/slice | solution.py:119
  174.4 13.8 %slice-start = ((s32[16,400]{1,0:T(8,128)}), s32[1,400]{1,0:T(1,128)S(1)}, s32[]{:S(2)}) async-start(s32[16,400]{1,0:T(8,128)} %copy-done.1), calls=%async_computation.1 | async-start | bytes 4096 | tf_op jit(solution)/shard_map/slice | solution.py:119
  189.0 25.1 %copy-start.3 = (s32[6400]{0:T(1024)S(1)}, s32[6400]{0:T(1024)}, u32[]{:S(2)}) copy-start(s32[6400]{0:T(1024)} %param.16) | copy-start | bytes 76804
  205.6 16.5 %all-to-all-start = ((f32[32,2,400]{2,1,0:T(2,128)}), f32[32,2,400]{2,1,0:T(2,128)S(1)}, u32[]{:S(2)}, u32[]{:S(2)}) async-start(f32[32,2,400]{2,1,0:T(2,128)} %bitcast.8), calls=%async_computation | async-start | bytes 262144 | tf_op jit(solution)/shard_map/all_to_all | solution.py:194

commit v2 on v1

v2 whole, which is shorter than its diff:
```python
import functools

import jax
import jax.numpy as jnp
import numpy as np
from jax import lax
from jax.experimental import pallas as pl
from jax.experimental.pallas import tpu as pltpu
from jax.sharding import PartitionSpec as P

BLK = 256
LANES = 128
NT = (((1,), (1,)), ((), ()))
VMEM_LIMIT = 56 * 1024 * 1024

HOSTS = (2, 3, 4, 5)
ROUNDS = ((4, 6, 5, 7, 2, 1, 3), (2, 1, 3, 6, 4, 7, 5))


def host_of(owner):
    z, x = owner // 2, owner % 2
    return (1 if z < 2 else 2) * 2 + x, z % 2


def plan():
    owner_at = {host_of(owner): owner for owner in range(8)}
    sends = np.zeros((8, 4, 4), np.int32)
    order = np.zeros((8, 4, 16), np.int32)
    for s in range(8):
        for rep in range(4):
            y, core = divmod(rep, 2)
            steps = [(step, k) for step, k in enumerate(ROUNDS[core]) if s ^ k in HOSTS]
            assert [step // 2 for step, _ in steps] == list(range(len(steps)))
            targets = [s ^ k for _, k in steps]
            if s in HOSTS:
                targets.append(s)
            sends[s, rep] = [owner_at[target, y] for target in targets]
            for side in range(2):
                half = core ^ side
                for step, k in enumerate((0,) + ROUNDS[half]):
                    order[s, rep, 2 * step + side] = (s ^ k) * 2 + half
    return sends, order


def round_pairs(step):
    pairs = []
    for rep in range(4):
        for host in HOSTS:
            pairs.append(((host ^ ROUNDS[rep % 2][step]) * 4 + rep, host * 4 + rep))
    return pairs


SIBLINGS = [(host * 4 + rep, host * 4 + (rep ^ 1)) for host in HOSTS for rep in range(4)]


def metadata_pairs():
    pairs = []
    for owner in range(8):
        host, y = host_of(owner)
        for core in range(2):
            pairs.append((owner * 4 + y * 2 + core, host * 4 + y * 2 + core))
    return pairs


def normalize(rows):
    wide = rows.astype(jnp.float32)
    return (wide * lax.rsqrt(jnp.sum(wide * wide, axis=1, keepdims=True) + 1e-06)).astype(
        jnp.bfloat16
    )


def arrival_clusters(place_index, slot_cluster):
    heads = slot_cluster.reshape(-1, BLK)[:, 0]
    block = place_index // BLK
    hit = block[None, :] == jnp.arange(heads.shape[0], dtype=jnp.int32)[:, None]
    return jnp.sum(jnp.where(hit, heads[:, None], 0), axis=0)


def gather_kernel(count, size, sections, *refs):
    table_ref, index_ref, rows_ref = refs[:3]
    out_ref, raw, wide, picked, sems = refs[-5:]
    part = raw.shape[0] // sections
    copies = []
    for i in range(sections):
        rows = pl.ds(i * part, part)
        copies.append(pltpu.make_async_copy(rows_ref.at[rows], raw.at[rows], sems.at[i]))
        copies[-1].start()
    step = 80
    for i in range(sections):
        copies[i].wait()

        def widen(j, _, i=i):
            rows = pl.ds(pl.multiple_of(i * part + j * step, step), step)
            wide[rows, :] = raw[rows, :].astype(jnp.float32)
            return 0

        lax.fori_loop(0, part // step, widen, 0)
    group = 16
    for c in range(count):
        base = table_ref[c]

        def pick(j, _, c=c, base=base):
            for t in range(group):
                source = index_ref[base + j * group + t]
                picked[pl.ds(t, 1), :] = wide[pl.ds(source, 1), :]
            rows = picked[...]
            scale = lax.rsqrt(jnp.sum(rows * rows, axis=1, keepdims=True) + 1e-06)
            out_ref[c, pl.ds(pl.multiple_of(j * group, group), group), :] = (rows * scale).astype(
                jnp.bfloat16
            )
            return 0

        lax.fori_loop(0, size // group, pick, 0)


def gather_rows(embeddings, index, starts, size, after=()):
    documents, width = embeddings.shape
    count = starts.shape[0]
    sections = 8
    return pl.pallas_call(
        functools.partial(gather_kernel, count, size, sections),
        out_shape=jax.ShapeDtypeStruct((count, size, width), jnp.bfloat16),
        in_specs=[
            pl.BlockSpec(memory_space=pltpu.SMEM),
            pl.BlockSpec(memory_space=pltpu.SMEM),
            pl.BlockSpec(memory_space=pl.ANY),
        ]
        + [pl.BlockSpec(memory_space=pl.ANY)] * len(after),
        out_specs=pl.BlockSpec(memory_space=pltpu.VMEM),
        scratch_shapes=[
            pltpu.VMEM((documents, width), jnp.bfloat16),
            pltpu.VMEM((documents, width), jnp.float32),
            pltpu.VMEM((16, width), jnp.float32),
            pltpu.SemaphoreType.DMA((sections,)),
        ],
        compiler_params=pltpu.CompilerParams(vmem_limit_bytes=VMEM_LIMIT),
        cost_estimate=pl.CostEstimate(
            flops=3 * count * size * width, bytes_accessed=2 * documents * width, transcendentals=0
        ),
    )(starts, index, embeddings, *after)


def best_of_rows(acc, size):
    return jnp.max(jnp.transpose(acc), axis=0, keepdims=True)[:, :size]


def gram_kernel(passes, count, size, first, *refs):
    chunks = refs[:count]
    cluster_row, cluster_column, before_ref, best_ref, held, acc, sems = refs[count:]
    limit = count * size

    def copy(i):
        return pltpu.make_async_copy(chunks[i], held.at[pl.ds(i * size, size)], sems.at[i])

    def arrive(i):
        rows = held.at[pl.ds(0, size)]
        pltpu.make_async_copy(rows, rows, sems.at[i]).wait()

    copy(first).start()
    for i in range(count):
        if i != first:
            copy(i).start()
    best_ref[...] = before_ref[...]
    copy(first).wait()
    for n, (chunk, place, groups, group, meets, last) in enumerate(passes):
        acc[...] = jnp.full_like(acc, -1.0)
        rows = held[chunk * size : (chunk + 1) * size, :]
        left = cluster_column[place]
        left = jnp.concatenate([left, left], axis=1)

        def tile(start, special, chunk=chunk, rows=rows, left=left):
            gram = lax.dot_general(
                rows, held[pl.ds(start, BLK), :], NT, preferred_element_type=jnp.float32
            )
            counts = left == cluster_row[:, pl.ds(start, BLK)]
            if special:
                column = start + lax.broadcasted_iota(jnp.int32, (size, BLK), 1)
                row = chunk * size + lax.broadcasted_iota(jnp.int32, (size, BLK), 0)
                counts = counts & (column != row) & (column < limit)
            values = jnp.where(counts, gram, jnp.float32(-1.0))
            top = jnp.max(values, axis=0, keepdims=True)
            best_ref[:, pl.ds(start, BLK)] = jnp.maximum(best_ref[:, pl.ds(start, BLK)], top)
            acc[0:size, :] = jnp.maximum(
                acc[0:size, :], jnp.maximum(values[:, :LANES], values[:, LANES:])
            )

        def visit(u, _, n=n, group=group, meets=meets, tile=tile):
            if n == 0:
                for i in (2 * u, 2 * u + 1):

                    @pl.when(i < count)
                    def _(i=i):
                        @pl.when(i != first)
                        def _():
                            arrive(i)

            for t in range(group):
                tile(pl.multiple_of((u * group + t) * BLK, BLK), meets)
            return 0

        lax.fori_loop(0, groups, visit, 0)
        if n == 0:
            for i in range(2 * groups, count):
                if i != first:
                    arrive(i)
        for t in last:
            tile(t * BLK, True)
        span = slice(chunk * size, (chunk + 1) * size)
        best_ref[:, span] = jnp.maximum(best_ref[:, span], best_of_rows(acc[...], size))


def gram_best(chunks, cluster_row, cluster_column, before, passes, first):
    count = len(chunks)
    size, width = chunks[0].shape
    total = before.shape[1]
    held = -(-count * size // BLK) * BLK
    padded = -(-size // LANES) * LANES
    work = sum((groups * group + len(last)) * BLK for _, _, groups, group, _, last in passes)
    return pl.pallas_call(
        functools.partial(gram_kernel, passes, count, size, first),
        out_shape=jax.ShapeDtypeStruct((1, total), jnp.float32),
        in_specs=[pl.BlockSpec(memory_space=pl.ANY)] * count
        + [pl.BlockSpec(memory_space=pltpu.VMEM)] * 3,
        out_specs=pl.BlockSpec(memory_space=pltpu.VMEM),
        scratch_shapes=[
            pltpu.VMEM((held, width), jnp.bfloat16),
            pltpu.VMEM((padded, LANES), jnp.float32),
            pltpu.SemaphoreType.DMA((count,)),
        ],
        compiler_params=pltpu.CompilerParams(vmem_limit_bytes=VMEM_LIMIT),
        cost_estimate=pl.CostEstimate(
            flops=2 * size * work * width,
            bytes_accessed=2 * count * size * width,
            transcendentals=0,
        ),
    )(*chunks, cluster_row, cluster_column, before)


def step_passes(step, size):
    groups = 2 * step * size // (3 * BLK)
    tiles = -(-(2 * step + 1) * size // BLK)
    passes = [(2 * step, step, groups, 3, False, tuple(range(3 * groups, tiles)))]
    low = (2 * step - 1) * size // BLK if step > 1 else 0
    passes.append((2 * step - 2, step - 1, 0, 1, True, tuple(range(low, -(-2 * step * size // BLK)))))
    return tuple(passes)


def finish_kernel(size, order_ref, own_ref, other_ref, clusters_ref, column_ref, best_ref, out_ref, acc):
    gram = lax.dot_general(own_ref[...], other_ref[...], NT, preferred_element_type=jnp.float32)
    left = jnp.tile(column_ref[...], (1, -(-size // LANES)))[:, :size]
    last = 15 * size
    values = jnp.where(left == clusters_ref[:, last : last + size], gram, jnp.float32(-1.0))
    acc[...] = jnp.full_like(acc, -1.0)
    acc[0:size, :] = jnp.broadcast_to(jnp.max(values, axis=1, keepdims=True), (size, LANES))
    for i in range(16):
        found = best_ref[:, i * size : (i + 1) * size]
        if i == 14:
            found = jnp.maximum(found, best_of_rows(acc[...], size))
        if i == 15:
            found = jnp.maximum(found, jnp.max(values, axis=0, keepdims=True))
        place = order_ref[i]
        source, half = place // 2, place % 2
        for rep in range(4):
            out_ref[source * 4 + rep, pl.ds(half, 1), :] = found


def finish(order, own, other, clusters, column, best):
    size = own.shape[0]
    padded = -(-size // LANES) * LANES
    return pl.pallas_call(
        functools.partial(finish_kernel, size),
        out_shape=jax.ShapeDtypeStruct((32, 2, size), jnp.float32),
        in_specs=[pl.BlockSpec(memory_space=pltpu.SMEM)]
        + [pl.BlockSpec(memory_space=pltpu.VMEM)] * 5,
        out_specs=pl.BlockSpec(memory_space=pltpu.VMEM),
        scratch_shapes=[pltpu.VMEM((padded, LANES), jnp.float32)],
        compiler_params=pltpu.CompilerParams(vmem_limit_bytes=VMEM_LIMIT),
    )(order, own, other, clusters, column, best)


def settle_kernel(sources, size, high, index_ref, values_ref, out_ref, left_ref, right_ref):
    wide = left_ref.shape[1] // len(sources)
    left_ref[...] = jnp.zeros_like(left_ref)
    right_ref[...] = jnp.zeros_like(right_ref)
    rows = lax.broadcasted_iota(jnp.int32, (high, size), 0)
    lanes = lax.broadcasted_iota(jnp.int32, (LANES, size), 0)
    for g, places in enumerate(sources):
        index = index_ref[g // 2, g % 2 : g % 2 + 1, :] if index_ref.ndim == 3 else index_ref[g : g + 1, :]
        value = values_ref[places[0][0], places[0][1] : places[0][1] + 1, :]
        for a, b in places[1:]:
            value = jnp.maximum(value, values_ref[a, b : b + 1, :])
        span = slice(g * wide, g * wide + size)
        here = rows == index // LANES
        for piece in range(3):
            head = value.astype(jnp.bfloat16).astype(jnp.float32)
            value = value - head
            left_ref[piece * high : (piece + 1) * high, span] = jnp.where(here, head, 0.0).astype(
                jnp.bfloat16
            )
        right_ref[:, span] = jnp.where(lanes == index % LANES, 1.0, 0.0).astype(jnp.bfloat16)
    total = lax.dot_general(left_ref[...], right_ref[...], NT, preferred_element_type=jnp.float32)
    total = total[2 * high : 3 * high] + total[high : 2 * high] + total[:high]
    out_ref[...] = total[: out_ref.shape[0]]


def settle(index, values, sources, documents):
    size = index.shape[-1]
    high = -(-documents // (16 * LANES)) * 16
    wide = -(-size // LANES) * LANES * len(sources)
    out = pl.pallas_call(
        functools.partial(settle_kernel, sources, size, high),
        out_shape=jax.ShapeDtypeStruct((documents // LANES, LANES), jnp.float32),
        scratch_shapes=[
            pltpu.VMEM((3 * high, wide), jnp.bfloat16),
            pltpu.VMEM((LANES, wide), jnp.bfloat16),
        ],
        compiler_params=pltpu.CompilerParams(vmem_limit_bytes=VMEM_LIMIT),
    )(index, values)
    return out.reshape(-1)


def hosted(embeddings, send_index, place_index, slot_cluster):
    documents = embeddings.shape[0]
    share = send_index.shape[0] // 8
    size = share // 2
    s, rep = lax.axis_index("shard"), lax.axis_index("rep")
    axes = ("shard", "rep")
    sends, order = plan()
    starts = sends * share + (np.arange(4) % 2 * size)[None, :, None].astype(np.int32)
    starts = jnp.asarray(starts)[s, rep]
    order = jnp.asarray(order)[s, rep]
    early = gather_rows(embeddings, send_index, starts[:1], size)
    late = gather_rows(embeddings, send_index, starts[1:], size, (early,))
    outgoing = [early[0], late[0], late[1], late[2]]
    own = [outgoing[3]] + [lax.ppermute(outgoing[r // 2], axes, round_pairs(r)) for r in range(7)]
    other = [lax.ppermute(chunk, axes, SIBLINGS) for chunk in own]
    clusters = lax.ppermute(arrival_clusters(place_index, slot_cluster), axes, metadata_pairs())
    clusters = clusters.reshape(16, size)[order]
    column = jnp.broadcast_to(clusters[0::2, :, None], (8, size, LANES))
    clusters = clusters.reshape(1, 16 * size)

    best = jnp.full((1, 16 * size), -1.0, jnp.float32)
    chunks = [(own, other)[i % 2][i // 2] for i in range(16)]
    for step in range(1, 8):
        best = gram_best(
            chunks[: 2 * step + 1], clusters, column, best, step_passes(step, size), 2 * step
        )
    outbound = finish(order, own[7], other[7], clusters, column[7], best)
    returned = lax.all_to_all(outbound, axes, split_axis=0, concat_axis=0, tiled=True)
    sources = []
    for owner in range(8):
        host, y = host_of(owner)
        for half in range(2):
            sources.append(tuple((host * 4 + y * 2 + core, half) for core in range(2)))
    return settle(send_index.reshape(8, 2, size), returned, tuple(sources), documents)


def gathered(embeddings, send_index, place_index, slot_cluster):
    documents, width = embeddings.shape
    owners = lax.axis_size("shard")
    reps = lax.axis_size("rep")
    share = send_index.shape[0] // owners
    outgoing = normalize(embeddings.at[send_index].get(mode="promise_in_bounds"))
    arrived = lax.all_to_all(
        outgoing.reshape(owners, share, width), "shard", split_axis=0, concat_axis=0, tiled=True
    )
    parts = 16
    size = documents // parts
    news = parts // reps
    turn = lax.axis_index("rep") * news
    arrived = jnp.roll(arrived.reshape(parts, size, width), -turn, axis=0)
    clusters = arrival_clusters(place_index, slot_cluster).reshape(parts, size)
    clusters = jnp.roll(clusters, -turn, axis=0)
    column = jnp.broadcast_to(clusters[:news, :, None], (news, size, LANES))
    best = jnp.full((1, documents), -1.0, jnp.float32)
    tiles = tuple(range(documents // BLK))
    passes = tuple((chunk, chunk, 0, 1, True, tiles) for chunk in range(news))
    best = gram_best(
        [arrived[i] for i in range(parts)], clusters.reshape(1, -1), column, best, passes, 0
    )
    best = lax.all_gather(best[0, : news * size], "rep", axis=0, tiled=True)
    returned = lax.all_to_all(
        best.reshape(owners, share), "shard", split_axis=0, concat_axis=0, tiled=True
    )
    sources = tuple(((0, g),) for g in range(parts))
    return settle(send_index.reshape(parts, size), returned.reshape(1, parts, size), sources, documents)


def solution(mesh):
    planned = mesh.shape["shard"] == 8 and mesh.shape["rep"] == 4

    def shards(embeddings, send_index, place_index, slot_cluster, pair_list):
        del pair_list
        run = hosted if planned else gathered
        return run(embeddings, send_index, place_index, slot_cluster)

    return jax.shard_map(
        shards,
        mesh=mesh,
        in_specs=(P("shard", None), P("shard"), P("shard"), P("shard"), P(("shard", "rep"), None)),
        out_specs=P("shard"),
        check_vma=False,
    )
```

time: 232 us -> 222 us (0.957)
  local copies, waits for them, and re-layouts: 52.2 us -> 14.1 us
  waiting for transfers between devices: 18.6 us -> 37.4 us
  Pallas kernels: 80 us -> 96 us
  other arithmetic: 8.33 us -> 0.93 us
  starting transfers between devices: 68.7 us -> 71.6 us
  between operations: 3.05 us -> 0.41 us
    gather x13 -> x1, local copies, waits for them, and re-layouts: 42.1 us -> 0.58 us  [hosted(): clusters = clusters.reshape(16, size)[order]]
    all_to_all x1, starting transfers between devices: 8.48 us -> 36.4 us  [hosted(): lax.all_to_all(outbound, axes, split_axis=0, concat_axis=0, tiled=True)]
    ppermute x7, starting transfers between devices: 48.2 us -> 24.3 us  [hosted(): lax.ppermute(outgoing[r // 2], axes, round_pairs(r))]
    pallas_call x5 -> x11, Pallas kernels: 80 us -> 96 us  [the longest x7 61.1 us: gram_best(): pl.pallas_call(functools.partial(gram_kernel, passes, count, size, first)...]
    ppermute x7, waiting for transfers between devices: 6.21 us -> 17.8 us  [hosted(): lax.ppermute(outgoing[r // 2], axes, round_pairs(r))]
    ppermute x1, waiting for transfers between devices: 5.1 us -> 12.1 us  [hosted(): lax.ppermute(arrival_clusters(place_index, slot_cluster), axes, metadata_...]
    unnamed x24 -> x32, local copies, waits for them, and re-layouts: 0.06 us -> 4.37 us
    another operation x4 -> x0, other arithmetic: 3.7 us -> none  [hosted(): best = best.at[jnp.asarray(picks)].max(found)]
  transfers between devices with their start and end apart: 17 -> 17, of which waited for: 3 -> 4; matrix products, arithmetic and copies ran while one was open for 19% -> 3% of each run, Pallas kernels for 26% -> 28%
where the time goes in v2:
time: 222 us; the launch traced here: 220 us
  Pallas kernels  96 us (43%)
  starting transfers between devices  71.6 us (32%)
  waiting for transfers between devices  37.4 us (17%)
  local copies, waits for them, and re-layouts  14.1 us (6%)
    pallas_call x7, Pallas kernels, gram_best(): pl.pallas_call(functools.partial(gram_kernel, passes, count, size, first)...  61.1 us
    all_to_all x1, starting transfers between devices, hosted(): lax.all_to_all(outbound, axes, split_axis=0, concat_axis=0, tiled=True)  36.4 us
    pallas_call x2, Pallas kernels, gather_rows(): pl.pallas_call(functools.partial(gather_kernel, count, size, sections), o...  28.6 us
    ppermute x7, starting transfers between devices, hosted(): lax.ppermute(outgoing[r // 2], axes, round_pairs(r))  24.3 us
    ppermute x7, waiting for transfers between devices, hosted(): lax.ppermute(outgoing[r // 2], axes, round_pairs(r))  17.8 us
    ppermute x1, waiting for transfers between devices, hosted(): lax.ppermute(arrival_clusters(place_index, slot_cluster), axes, metadata_...  12.1 us
    ppermute x8, starting transfers between devices, hosted(): other = [lax.ppermute(chunk, axes, SIBLINGS) for chunk in own]  9.59 us
    all_to_all x1, waiting for transfers between devices, hosted(): lax.all_to_all(outbound, axes, split_axis=0, concat_axis=0, tiled=True)  7.51 us
  transfers between devices with their start and end apart: 17, of which 4 were waited for; matrix products, arithmetic and copies ran while one was open for 3% of the time, Pallas kernels for 28%

profile of v2, /device:TPU:0, one launch (start us, length us, event | category | flops | bytes accessed | tf_op | source)
XLA Modules:
  0.0 220.4 jit_solution(16543491638799476009)
XLA Ops:
  0.0 0.7 constant_dynamic-slice_fusion
  0.7 0.6 slice_bitcast_fusion.3.refs_0_
  1.3 11.0 %shard_map.64.refs_3_ = bf16[1,400,1024]{2,1,0:T(8,128)(2,1)} custom-call(s32[1]{0:T(128)} %bitcast.22, s32[6400]{0:T(1024)} %refs_1_.3, bf16[6400,1024]{1,0:T(8,128)(2,1)} %refs_2_.3), custom_call_target="tpu_custom_call" | custom-call | flops 1228800 | bytes 13107200 | tf_op jit(solution)/shard_map/pallas_call | solution.py:120
  12.3 17.6 %shard_map.65 = bf16[3,400,1024]{2,1,0:T(8,128)(2,1)} custom-call(s32[3]{0:T(128)} %slice_bitcast_fusion.3.refs_0_, s32[6400]{0:T(1024)} %refs_1_.3, bf16[6400,1024]{1,0:T(8,128)(2,1)} %refs_2_.3, bf16[1,400,1024]{2,1,0:T(8,128)(2,1)} %shard_map.64.refs_3_), custom_call_target="tpu_custom_call" | custom-call | flops 3686400 | bytes 13107200 | tf_op jit(solution)/shard_map/pallas_call | solution.py:120
  29.9 1.9 slice_bitcast_fusion
  31.8 1.6 collective-permute-start.3
  33.4 7.2 %collective-permute-start.4 = (bf16[400,1024]{1,0:T(8,128)(2,1)S(1)}, bf16[400,1024]{1,0:T(8,128)(2,1)}, u32[]{:S(2)}, u32[]{:S(2)}) collective-permute-start(bf16[400,1024]{1,0:T(8,128)(2,1)S(1)} %bitcast.19), channel_id=1, source_target_pairs={{24,8},{28,12},{0,16},{4,20},{1,9},{5,13},{25,17},{29,21},{26,10},... | collective-permute-start | bytes 2457608 | tf_op jit(solution)/shard_map/ppermute | solution.py:335
  41.0 1.3 collective-permute-start.2
  42.3 1.6 collective-permute-start.6
  43.9 3.0 %collective-permute-start.8 = (bf16[400,1024]{1,0:T(8,128)(2,1)S(1)}, bf16[400,1024]{1,0:T(8,128)(2,1)}, u32[]{:S(2)}, u32[]{:S(2)}) collective-permute-start(bf16[400,1024]{1,0:T(8,128)(2,1)S(1)} %get-tuple-element.6), channel_id=1, source_target_pairs={{28,8},{24,12},{4,16},{0,20},{5,9},{1,13},{29,17},{25,21},{30,10},... | collective-permute-start | bytes 2457608 | tf_op jit(solution)/shard_map/ppermute | solution.py:335
  46.9 12.1 %collective-permute-done.2 = s32[6400]{0:T(1024)S(1)} collective-permute-done((s32[6400]{0:T(1024)S(1)}, s32[6400]{0:T(1024)S(1)}, u32[]{:S(2)}, u32[]{:S(2)}) %collective-permute-start.2) | collective-permute-done | bytes 25632 | tf_op jit(solution)/shard_map/ppermute | solution.py:337
  59.0 0.7 collective-permute-start.10
  59.7 5.6 %collective-permute-start.12 = (bf16[400,1024]{1,0:T(8,128)(2,1)S(1)}, bf16[400,1024]{1,0:T(8,128)(2,1)S(1)}, u32[]{:S(2)}, u32[]{:S(2)}) collective-permute-start(bf16[400,1024]{1,0:T(8,128)(2,1)S(1)} %get-tuple-element.5), channel_id=1, source_target_pairs={{0,8},{4,12},{24,16},{28,20},{25,9},{29,13},{1,17},{5,21},{2,10},{... | collective-permute-start | bytes 2457608 | tf_op jit(solution)/shard_map/ppermute | solution.py:335
  65.4 1.6 collective-permute-start.5
  67.0 0.7 collective-permute-start.14
  67.7 8.9 %collective-permute-done.8.refs_6_ = bf16[400,1024]{1,0:T(8,128)(2,1)} collective-permute-done((bf16[400,1024]{1,0:T(8,128)(2,1)S(1)}, bf16[400,1024]{1,0:T(8,128)(2,1)}, u32[]{:S(2)}, u32[]{:S(2)}) %collective-permute-start.8) | collective-permute-done | bytes 819232 | tf_op jit(solution)/shard_map/ppermute | solution.py:335
  76.6 5.5 %collective-permute-start = (bf16[400,1024]{1,0:T(8,128)(2,1)S(1)}, bf16[400,1024]{1,0:T(8,128)(2,1)}, u32[]{:S(2)}, u32[]{:S(2)}) collective-permute-start(bf16[400,1024]{1,0:T(8,128)(2,1)S(1)} %get-tuple-element.7.refs_0_), channel_id=1, source_target_pairs={{4,8},{0,12},{28,16},{24,20},{29,9},{25,13},{5,17},{1,21},{6,10},{... | collective-permute-start | bytes 2457608 | tf_op jit(solution)/shard_map/ppermute | solution.py:335
  82.1 0.9 copy-done.8
  82.9 1.6 collective-permute-start.7
  84.6 0.7 fusion.2
  85.3 8.9 %collective-permute-done.12.refs_10_ = bf16[400,1024]{1,0:T(8,128)(2,1)S(1)} collective-permute-done((bf16[400,1024]{1,0:T(8,128)(2,1)S(1)}, bf16[400,1024]{1,0:T(8,128)(2,1)S(1)}, u32[]{:S(2)}, u32[]{:S(2)}) %collective-permute-start.12) | collective-permute-done | bytes 819232 | tf_op jit(solution)/shard_map/ppermute | solution.py:335
  94.2 1.6 collective-permute-start.9
  95.8 1.3 fusion.3.order_ref
  97.1 0.6 gather_fusion
  97.7 0.7 reshape.53.refs_3_.refs_5_.refs_7_.refs_9_.refs_11_.refs_13_.refs_15_.clusters_ref
  98.5 1.5 broadcast_in_dim.35.refs_4_.refs_6_.refs_8_.refs_10_.refs_12_.refs_14_.refs_16_
  99.9 0.6 broadcast_in_dim.36.refs_5_
  100.6 6.1 %shard_map.66.refs_7_ = f32[1,6400]{1,0:T(1,128)} custom-call(bf16[400,1024]{1,0:T(8,128)(2,1)} %copy-done.1, bf16[400,1024]{1,0:T(8,128)(2,1)} %collective-permute-done.3.refs_1_, bf16[400,1024]{1,0:T(8,128)(2,1)} %collective-permute-done.4.refs_2_, s32[1,6400]{1,0:T(1,128)} %reshape.53.refs_3_.refs_5_.refs_7_.refs_9_.refs_11_.refs_13_.refs_15_.clusters_ref, ...), custom_call_target="tpu_custom_call" | custom-call | flops 1887436800 | bytes 2457600 | tf_op jit(solution)/shard_map/pallas_call | solution.py:219
  106.7 0.8 collective-permute-start.11
  107.5 6.9 %shard_map.67.refs_9_ = f32[1,6400]{1,0:T(1,128)} custom-call(bf16[400,1024]{1,0:T(8,128)(2,1)} %copy-done.1, bf16[400,1024]{1,0:T(8,128)(2,1)} %collective-permute-done.3.refs_1_, bf16[400,1024]{1,0:T(8,128)(2,1)} %collective-permute-done.4.refs_2_, bf16[400,1024]{1,0:T(8,128)(2,1)} %collective-permute-done.5.refs_3_, ...), custom_call_target="tpu_custom_call" | custom-call | flops 2306867200 | bytes 4096000 | tf_op jit(solution)/shard_map/pallas_call | solution.py:219
  114.5 0.7 collective-permute-start.13
  115.2 0.7 collective-permute-start.15
  116.0 0.9 collective-permute-start.1
  116.9 7.8 %shard_map.68.refs_11_ = f32[1,6400]{1,0:T(1,128)} custom-call(bf16[400,1024]{1,0:T(8,128)(2,1)} %copy-done.1, bf16[400,1024]{1,0:T(8,128)(2,1)} %collective-permute-done.3.refs_1_, bf16[400,1024]{1,0:T(8,128)(2,1)} %collective-permute-done.4.refs_2_, bf16[400,1024]{1,0:T(8,128)(2,1)} %collective-permute-done.5.refs_3_, ...), custom_call_target="tpu_custom_call" | custom-call | flops 2936012800 | bytes 5734400 | tf_op jit(solution)/shard_map/pallas_call | solution.py:219
  124.7 8.9 %shard_map.69.refs_13_ = f32[1,6400]{1,0:T(1,128)} custom-call(bf16[400,1024]{1,0:T(8,128)(2,1)} %copy-done.1, bf16[400,1024]{1,0:T(8,128)(2,1)} %collective-permute-done.3.refs_1_, bf16[400,1024]{1,0:T(8,128)(2,1)} %collective-permute-done.4.refs_2_, bf16[400,1024]{1,0:T(8,128)(2,1)} %collective-permute-done.5.refs_3_, ...), custom_call_target="tpu_custom_call" | custom-call | flops 3774873600 | bytes 7372800 | tf_op jit(solution)/shard_map/pallas_call | solution.py:219
  133.6 0.9 copy-done.13
  134.5 9.5 %shard_map.70.refs_15_ = f32[1,6400]{1,0:T(1,128)} custom-call(bf16[400,1024]{1,0:T(8,128)(2,1)} %copy-done.1, bf16[400,1024]{1,0:T(8,128)(2,1)} %collective-permute-done.3.refs_1_, bf16[400,1024]{1,0:T(8,128)(2,1)} %collective-permute-done.4.refs_2_, bf16[400,1024]{1,0:T(8,128)(2,1)} %collective-permute-done.5.refs_3_, ...), custom_call_target="tpu_custom_call" | custom-call | flops 4194304000 | bytes 9011200 | tf_op jit(solution)/shard_map/pallas_call | solution.py:219
  144.1 0.9 copy-done.14
  145.0 10.5 %shard_map.71.refs_17_ = f32[1,6400]{1,0:T(1,128)} custom-call(bf16[400,1024]{1,0:T(8,128)(2,1)} %copy-done.1, bf16[400,1024]{1,0:T(8,128)(2,1)} %collective-permute-done.3.refs_1_, bf16[400,1024]{1,0:T(8,128)(2,1)} %collective-permute-done.4.refs_2_, bf16[400,1024]{1,0:T(8,128)(2,1)} %collective-permute-done.5.refs_3_, ...), custom_call_target="tpu_custom_call" | custom-call | flops 4823449600 | bytes 10649600 | tf_op jit(solution)/shard_map/pallas_call | solution.py:219
  155.5 0.9 copy-done.15
  156.4 11.3 %shard_map.72.best_ref = f32[1,6400]{1,0:T(1,128)} custom-call(bf16[400,1024]{1,0:T(8,128)(2,1)} %copy-done.1, bf16[400,1024]{1,0:T(8,128)(2,1)} %collective-permute-done.3.refs_1_, bf16[400,1024]{1,0:T(8,128)(2,1)} %collective-permute-done.4.refs_2_, bf16[400,1024]{1,0:T(8,128)(2,1)} %collective-permute-done.5.refs_3_, ...), custom_call_target="tpu_custom_call" | custom-call | flops 5452595200 | bytes 12288000 | tf_op jit(solution)/shard_map/pallas_call | solution.py:219
  167.8 0.9 broadcast_in_dim.34.column_ref
  168.8 3.0 %shard_map.73 = f32[32,2,400]{2,1,0:T(2,128)} custom-call(s32[16]{0:T(128)} %fusion.3.order_ref, bf16[400,1024]{1,0:T(8,128)(2,1)} %collective-permute-done.refs_14_.own_ref, bf16[400,1024]{1,0:T(8,128)(2,1)} %copy-done.2, s32[1,6400]{1,0:T(1,128)} %reshape.53.refs_3_.refs_5_.refs_7_.refs_9_.refs_11_.refs_13_.refs_15_.clusters_ref, ...), custom_call_target="tpu_custom_call" | custom-call | tf_op jit(solution)/shard_map/pallas_call | solution.py:270
  171.8 36.4 %all-to-all-start = ((f32[32,2,400]{2,1,0:T(2,128)}), f32[32,2,400]{2,1,0:T(2,128)S(1)}, u32[]{:S(2)}, u32[]{:S(2)}) async-start(f32[32,2,400]{2,1,0:T(2,128)} %shard_map.73), calls=%async_computation | async-start | bytes 262144 | tf_op jit(solution)/shard_map/all_to_all | solution.py:349
  208.2 0.7 reshape.50.index_ref
  209.0 7.5 %all-to-all-done.values_ref = f32[32,2,400]{2,1,0:T(2,128)S(1)} async-done(((f32[32,2,400]{2,1,0:T(2,128)}), f32[32,2,400]{2,1,0:T(2,128)S(1)}, u32[]{:S(2)}, u32[]{:S(2)}) %all-to-all-start) | async-done | bytes 102432 | tf_op jit(solution)/shard_map/all_to_all | solution.py:349
  216.5 0.6 copy-done.3
  217.1 3.3 %shard_map.74 = f32[50,128]{1,0:T(8,128)} custom-call(s32[8,2,400]{2,1,0:T(2,128)} %reshape.50.index_ref, f32[32,2,400]{2,1,0:T(2,128)} %copy-done.3), custom_call_target="tpu_custom_call" | custom-call | tf_op jit(solution)/shard_map/pallas_call | solution.py:310
  (48 shorter events, 0.6 us)
Async XLA Ops:
  0.7 0.6 copy-start.7
  29.9 3.5 %copy-start = (bf16[1,400,1024]{2,1,0:T(8,128)(2,1)S(1)}, bf16[1,400,1024]{2,1,0:T(8,128)(2,1)}, u32[]{:S(2)}) copy-start(bf16[1,400,1024]{2,1,0:T(8,128)(2,1)} %shard_map.64.refs_3_) | copy-start | bytes 2457604
  29.9 10.7 %copy-start.6 = (s32[6656]{0:T(1024)S(1)}, s32[6656]{0:T(1024)}, u32[]{:S(2)}) copy-start(s32[6656]{0:T(1024)} %param.10) | copy-start | bytes 79876
  29.9 10.8 %copy-start.5 = (s32[6400]{0:T(1024)S(1)}, s32[6400]{0:T(1024)}, u32[]{:S(2)}) copy-start(s32[6400]{0:T(1024)} %param.9) | copy-start | bytes 76804
  31.8 68.7 %copy-start.1 = (bf16[400,1024]{1,0:T(8,128)(2,1)}, bf16[400,1024]{1,0:T(8,128)(2,1)S(1)}, u32[]{:S(2)}) copy-start(bf16[400,1024]{1,0:T(8,128)(2,1)S(1)} %get-tuple-element.7.refs_0_) | copy-start | bytes 2457604
  31.8 27.9 %collective-permute-start.3 = (bf16[400,1024]{1,0:T(8,128)(2,1)S(1)}, bf16[400,1024]{1,0:T(8,128)(2,1)}, u32[]{:S(2)}, u32[]{:S(2)}) collective-permute-start(bf16[400,1024]{1,0:T(8,128)(2,1)S(1)} %get-tuple-element.7.refs_0_), channel_id=1, source_target_pairs={{8,9},{9,8},{10,11},{11,10},{12,13},{13,12},{14,15},{15,14},{16,17... | collective-permute-start | bytes 2457608 | tf_op jit(solution)/shard_map/ppermute | solution.py:336
  33.4 32.0 %collective-permute-start.4 = (bf16[400,1024]{1,0:T(8,128)(2,1)S(1)}, bf16[400,1024]{1,0:T(8,128)(2,1)}, u32[]{:S(2)}, u32[]{:S(2)}) collective-permute-start(bf16[400,1024]{1,0:T(8,128)(2,1)S(1)} %bitcast.19), channel_id=1, source_target_pairs={{24,8},{28,12},{0,16},{4,20},{1,9},{5,13},{25,17},{29,21},{26,10},... | collective-permute-start | bytes 2457608 | tf_op jit(solution)/shard_map/ppermute | solution.py:335
  41.0 18.0 %collective-permute-start.2 = (s32[6400]{0:T(1024)S(1)}, s32[6400]{0:T(1024)S(1)}, u32[]{:S(2)}, u32[]{:S(2)}) collective-permute-start(s32[6400]{0:T(1024)S(1)} %select_reduce_fusion), channel_id=1, source_target_pairs={{0,8},{1,9},{4,12},{5,13},{10,10},{11,11},{14,14},{15,15},{16,16},... | collective-permute-start | bytes 76808 | tf_op jit(solution)/shard_map/ppermute | solution.py:337
  42.3 24.7 %collective-permute-start.6 = (bf16[400,1024]{1,0:T(8,128)(2,1)S(1)}, bf16[400,1024]{1,0:T(8,128)(2,1)}, u32[]{:S(2)}, u32[]{:S(2)}) collective-permute-start(bf16[400,1024]{1,0:T(8,128)(2,1)S(1)} %bitcast.20), channel_id=1, source_target_pairs={{16,8},{20,12},{8,16},{12,20},{13,9},{9,13},{21,17},{17,21},{18,10... | collective-permute-start | bytes 2457608 | tf_op jit(solution)/shard_map/ppermute | solution.py:335
  43.9 32.7 %collective-permute-start.8 = (bf16[400,1024]{1,0:T(8,128)(2,1)S(1)}, bf16[400,1024]{1,0:T(8,128)(2,1)}, u32[]{:S(2)}, u32[]{:S(2)}) collective-permute-start(bf16[400,1024]{1,0:T(8,128)(2,1)S(1)} %get-tuple-element.6), channel_id=1, source_target_pairs={{28,8},{24,12},{4,16},{0,20},{5,9},{1,13},{29,17},{25,21},{30,10},... | collective-permute-start | bytes 2457608 | tf_op jit(solution)/shard_map/ppermute | solution.py:335
  59.0 23.0 %collective-permute-start.10 = (bf16[400,1024]{1,0:T(8,128)(2,1)S(1)}, bf16[400,1024]{1,0:T(8,128)(2,1)S(1)}, u32[]{:S(2)}, u32[]{:S(2)}) collective-permute-start(bf16[400,1024]{1,0:T(8,128)(2,1)S(1)} %get-tuple-element.6), channel_id=1, source_target_pairs={{20,8},{16,12},{12,16},{8,20},{17,9},{21,13},{9,17},{13,21},{22,10... | collective-permute-start | bytes 2457608 | tf_op jit(solution)/shard_map/ppermute | solution.py:335
  59.7 34.4 %collective-permute-start.12 = (bf16[400,1024]{1,0:T(8,128)(2,1)S(1)}, bf16[400,1024]{1,0:T(8,128)(2,1)S(1)}, u32[]{:S(2)}, u32[]{:S(2)}) collective-permute-start(bf16[400,1024]{1,0:T(8,128)(2,1)S(1)} %get-tuple-element.5), channel_id=1, source_target_pairs={{0,8},{4,12},{24,16},{28,20},{25,9},{29,13},{1,17},{5,21},{2,10},{... | collective-permute-start | bytes 2457608 | tf_op jit(solution)/shard_map/ppermute | solution.py:335
  65.4 41.3 %collective-permute-start.5 = (bf16[400,1024]{1,0:T(8,128)(2,1)}, bf16[400,1024]{1,0:T(8,128)(2,1)}, u32[]{:S(2)}, u32[]{:S(2)}) collective-permute-start(bf16[400,1024]{1,0:T(8,128)(2,1)} %collective-permute-done.4.refs_2_), channel_id=1, source_target_pairs={{8,9},{9,8},{10,11},{11,10},{12,13},{13,12},{14,15},{15,14},{16,17... | collective-permute-start | bytes 2457608 | tf_op jit(solution)/shard_map/ppermute | solution.py:336
  67.0 47.5 %collective-permute-start.14 = (bf16[400,1024]{1,0:T(8,128)(2,1)S(1)}, bf16[400,1024]{1,0:T(8,128)(2,1)S(1)}, u32[]{:S(2)}, u32[]{:S(2)}) collective-permute-start(bf16[400,1024]{1,0:T(8,128)(2,1)S(1)} %get-tuple-element.5), channel_id=1, source_target_pairs={{12,8},{8,12},{20,16},{16,20},{21,9},{17,13},{13,17},{9,21},{14,10... | collective-permute-start | bytes 2457608 | tf_op jit(solution)/shard_map/ppermute | solution.py:335
  76.6 38.6 %collective-permute-start = (bf16[400,1024]{1,0:T(8,128)(2,1)S(1)}, bf16[400,1024]{1,0:T(8,128)(2,1)}, u32[]{:S(2)}, u32[]{:S(2)}) collective-permute-start(bf16[400,1024]{1,0:T(8,128)(2,1)S(1)} %get-tuple-element.7.refs_0_), channel_id=1, source_target_pairs={{4,8},{0,12},{28,16},{24,20},{29,9},{25,13},{5,17},{1,21},{6,10},{... | collective-permute-start | bytes 2457608 | tf_op jit(solution)/shard_map/ppermute | solution.py:335
  82.1 0.9 copy-start.8
  82.9 33.0 %collective-permute-start.7 = (bf16[400,1024]{1,0:T(8,128)(2,1)}, bf16[400,1024]{1,0:T(8,128)(2,1)}, u32[]{:S(2)}, u32[]{:S(2)}) collective-permute-start(bf16[400,1024]{1,0:T(8,128)(2,1)} %collective-permute-done.6.refs_4_), channel_id=1, source_target_pairs={{8,9},{9,8},{10,11},{11,10},{12,13},{13,12},{14,15},{15,14},{16,17... | collective-permute-start | bytes 2457608 | tf_op jit(solution)/shard_map/ppermute | solution.py:336
  94.2 2.9 %copy-start.10 = (bf16[400,1024]{1,0:T(8,128)(2,1)}, bf16[400,1024]{1,0:T(8,128)(2,1)S(1)}, u32[]{:S(2)}) copy-start(bf16[400,1024]{1,0:T(8,128)(2,1)S(1)} %collective-permute-done.12.refs_10_) | copy-start | bytes 2457604
  94.2 30.5 %collective-permute-start.9 = (bf16[400,1024]{1,0:T(8,128)(2,1)}, bf16[400,1024]{1,0:T(8,128)(2,1)}, u32[]{:S(2)}, u32[]{:S(2)}) collective-permute-start(bf16[400,1024]{1,0:T(8,128)(2,1)} %collective-permute-done.8.refs_6_), channel_id=1, source_target_pairs={{8,9},{9,8},{10,11},{11,10},{12,13},{13,12},{14,15},{15,14},{16,17... | collective-permute-start | bytes 2457608 | tf_op jit(solution)/shard_map/ppermute | solution.py:336
  100.6 6.1 %copy-start.9 = (bf16[400,1024]{1,0:T(8,128)(2,1)S(1)}, bf16[400,1024]{1,0:T(8,128)(2,1)}, u32[]{:S(2)}) copy-start(bf16[400,1024]{1,0:T(8,128)(2,1)} %copy-done.8) | copy-start | bytes 2457604
  106.7 7.8 %copy-start.11 = (bf16[400,1024]{1,0:T(8,128)(2,1)S(1)}, bf16[400,1024]{1,0:T(8,128)(2,1)}, u32[]{:S(2)}) copy-start(bf16[400,1024]{1,0:T(8,128)(2,1)} %copy-done.10) | copy-start | bytes 2457604
  106.7 26.9 %collective-permute-start.11 = (bf16[400,1024]{1,0:T(8,128)(2,1)S(1)}, bf16[400,1024]{1,0:T(8,128)(2,1)S(1)}, u32[]{:S(2)}, u32[]{:S(2)}) collective-permute-start(bf16[400,1024]{1,0:T(8,128)(2,1)S(1)} %copy-done.9), channel_id=1, source_target_pairs={{8,9},{9,8},{10,11},{11,10},{12,13},{13,12},{14,15},{15,14},{16,17... | collective-permute-start | bytes 2457608 | tf_op jit(solution)/shard_map/ppermute | solution.py:336
  114.5 10.2 %copy-start.12 = (bf16[400,1024]{1,0:T(8,128)(2,1)}, bf16[400,1024]{1,0:T(8,128)(2,1)S(1)}, u32[]{:S(2)}) copy-start(bf16[400,1024]{1,0:T(8,128)(2,1)S(1)} %collective-permute-done.14.refs_12_) | copy-start | bytes 2457604
  114.5 29.6 %collective-permute-start.13 = (bf16[400,1024]{1,0:T(8,128)(2,1)S(1)}, bf16[400,1024]{1,0:T(8,128)(2,1)S(1)}, u32[]{:S(2)}, u32[]{:S(2)}) collective-permute-start(bf16[400,1024]{1,0:T(8,128)(2,1)S(1)} %copy-done.11), channel_id=1, source_target_pairs={{8,9},{9,8},{10,11},{11,10},{12,13},{13,12},{14,15},{15,14},{16,17... | collective-permute-start | bytes 2457608 | tf_op jit(solution)/shard_map/ppermute | solution.py:336
  115.2 40.3 %collective-permute-start.15 = (bf16[400,1024]{1,0:T(8,128)(2,1)S(1)}, bf16[400,1024]{1,0:T(8,128)(2,1)S(1)}, u32[]{:S(2)}, u32[]{:S(2)}) collective-permute-start(bf16[400,1024]{1,0:T(8,128)(2,1)S(1)} %collective-permute-done.14.refs_12_), channel_id=1, source_target_pairs={{8,9},{9,8},{10,11},{11,10},{12,13},{13,12},{14,15},{15,14},{16,17... | collective-permute-start | bytes 2457608 | tf_op jit(solution)/shard_map/ppermute | solution.py:336
  116.0 51.8 %collective-permute-start.1 = (bf16[400,1024]{1,0:T(8,128)(2,1)}, bf16[400,1024]{1,0:T(8,128)(2,1)S(1)}, u32[]{:S(2)}, u32[]{:S(2)}) collective-permute-start(bf16[400,1024]{1,0:T(8,128)(2,1)} %collective-permute-done.refs_14_.own_ref), channel_id=1, source_target_pairs={{8,9},{9,8},{10,11},{11,10},{12,13},{13,12},{14,15},{15,14},{16,17... | collective-permute-start | bytes 2457608 | tf_op jit(solution)/shard_map/ppermute | solution.py:336
  133.6 0.9 copy-start.13
  144.1 1.0 copy-start.14
  155.5 0.9 copy-start.15
  167.8 40.5 %copy-start.4 = (s32[6400]{0:T(1024)S(1)}, s32[6400]{0:T(1024)}, u32[]{:S(2)}) copy-start(s32[6400]{0:T(1024)} %refs_1_.3) | copy-start | bytes 76804
  167.8 1.0 copy-start.2
  171.8 44.6 %all-to-all-start = ((f32[32,2,400]{2,1,0:T(2,128)}), f32[32,2,400]{2,1,0:T(2,128)S(1)}, u32[]{:S(2)}, u32[]{:S(2)}) async-start(f32[32,2,400]{2,1,0:T(2,128)} %shard_map.73), calls=%async_computation | async-start | bytes 262144 | tf_op jit(solution)/shard_map/all_to_all | solution.py:349
  216.5 0.7 copy-start.3

commit v3 on v2

--- a/solution.py
+++ b/solution.py
@@ -15,6 +15,14 @@
 
 HOSTS = (2, 3, 4, 5)
 ROUNDS = ((4, 6, 5, 7, 2, 1, 3), (2, 1, 3, 6, 4, 7, 5))
+
+
+CHUNKS = (
+    (0, 0), (1, 0), (0, 1), (1, 1),
+    (2, 0), (3, 0), (2, 1), (3, 1),
+    (4, 0), (5, 0), (4, 1), (5, 1),
+    (6, 0), (6, 1), (7, 0), (7, 1),
+)
 
 
 def host_of(owner):
@@ -38,7 +46,7 @@
             for side in range(2):
                 half = core ^ side
                 for step, k in enumerate((0,) + ROUNDS[half]):
-                    order[s, rep, 2 * step + side] = (s ^ k) * 2 + half
+                    order[s, rep, CHUNKS.index((step, side))] = (s ^ k) * 2 + half
     return sends, order
 
 
@@ -60,6 +68,10 @@
         for core in range(2):
             pairs.append((owner * 4 + y * 2 + core, host * 4 + y * 2 + core))
     return pairs
+
+
+def tie(value, *after):
+    return lax.optimization_barrier((value, *after))[0]
 
 
 def normalize(rows):
@@ -134,9 +146,7 @@
             pltpu.SemaphoreType.DMA((sections,)),
         ],
         compiler_params=pltpu.CompilerParams(vmem_limit_bytes=VMEM_LIMIT),
-        cost_estimate=pl.CostEstimate(
-            flops=3 * count * size * width, bytes_accessed=2 * documents * width, transcendentals=0
-        ),
+        cost_estimate=pl.CostEstimate(flops=0, bytes_accessed=0, transcendentals=0),
     )(starts, index, embeddings, *after)
 
 
@@ -156,43 +166,44 @@
         rows = held.at[pl.ds(0, size)]
         pltpu.make_async_copy(rows, rows, sems.at[i]).wait()
 
-    copy(first).start()
+    for i in first:
+        copy(i).start()
     for i in range(count):
-        if i != first:
+        if i not in first:
             copy(i).start()
     best_ref[...] = before_ref[...]
-    copy(first).wait()
-    for n, (chunk, place, groups, group, meets, last) in enumerate(passes):
+    for i in first:
+        copy(i).wait()
+    for n, (chunk, news, groups, group, meets, last) in enumerate(passes):
+        height = news * size
         acc[...] = jnp.full_like(acc, -1.0)
-        rows = held[chunk * size : (chunk + 1) * size, :]
-        left = cluster_column[place]
+        rows = held[chunk * size : chunk * size + height, :]
+        left = cluster_column[n]
         left = jnp.concatenate([left, left], axis=1)
 
-        def tile(start, special, chunk=chunk, rows=rows, left=left):
+        def tile(start, special, chunk=chunk, height=height, rows=rows, left=left):
             gram = lax.dot_general(
                 rows, held[pl.ds(start, BLK), :], NT, preferred_element_type=jnp.float32
             )
             counts = left == cluster_row[:, pl.ds(start, BLK)]
             if special:
-                column = start + lax.broadcasted_iota(jnp.int32, (size, BLK), 1)
-                row = chunk * size + lax.broadcasted_iota(jnp.int32, (size, BLK), 0)
+                column = start + lax.broadcasted_iota(jnp.int32, (height, BLK), 1)
+                row = chunk * size + lax.broadcasted_iota(jnp.int32, (height, BLK), 0)
                 counts = counts & (column != row) & (column < limit)
             values = jnp.where(counts, gram, jnp.float32(-1.0))
             top = jnp.max(values, axis=0, keepdims=True)
             best_ref[:, pl.ds(start, BLK)] = jnp.maximum(best_ref[:, pl.ds(start, BLK)], top)
-            acc[0:size, :] = jnp.maximum(
-                acc[0:size, :], jnp.maximum(values[:, :LANES], values[:, LANES:])
+            acc[0:height, :] = jnp.maximum(
+                acc[0:height, :], jnp.maximum(values[:, :LANES], values[:, LANES:])
             )
 
         def visit(u, _, n=n, group=group, meets=meets, tile=tile):
             if n == 0:
                 for i in (2 * u, 2 * u + 1):
 
-                    @pl.when(i < count)
+                    @pl.when(i < first[0])
                     def _(i=i):
-                        @pl.when(i != first)
-                        def _():
-                            arrive(i)
+                        arrive(i)
 
             for t in range(group):
                 tile(pl.multiple_of((u * group + t) * BLK, BLK), meets)
@@ -200,13 +211,13 @@
 
         lax.fori_loop(0, groups, visit, 0)
         if n == 0:
-            for i in range(2 * groups, count):
-                if i != first:
+            for i in range(count):
+                if i not in first and not i < min(2 * groups, first[0]):
                     arrive(i)
         for t in last:
             tile(t * BLK, True)
-        span = slice(chunk * size, (chunk + 1) * size)
-        best_ref[:, span] = jnp.maximum(best_ref[:, span], best_of_rows(acc[...], size))
+        span = slice(chunk * size, chunk * size + height)
+        best_ref[:, span] = jnp.maximum(best_ref[:, span], best_of_rows(acc[...], height))
 
 
 def gram_best(chunks, cluster_row, cluster_column, before, passes, first):
@@ -214,8 +225,9 @@
     size, width = chunks[0].shape
     total = before.shape[1]
     held = -(-count * size // BLK) * BLK
-    padded = -(-size // LANES) * LANES
-    work = sum((groups * group + len(last)) * BLK for _, _, groups, group, _, last in passes)
+    tall = max(news for _, news, *_ in passes) * size
+    padded = -(-tall // LANES) * LANES
+    work = sum(news * (groups * group + len(last)) * BLK for _, news, groups, group, _, last in passes)
     return pl.pallas_call(
         functools.partial(gram_kernel, passes, count, size, first),
         out_shape=jax.ShapeDtypeStruct((1, total), jnp.float32),
@@ -228,21 +240,15 @@
             pltpu.SemaphoreType.DMA((count,)),
         ],
         compiler_params=pltpu.CompilerParams(vmem_limit_bytes=VMEM_LIMIT),
-        cost_estimate=pl.CostEstimate(
-            flops=2 * size * work * width,
-            bytes_accessed=2 * count * size * width,
-            transcendentals=0,
-        ),
+        cost_estimate=pl.CostEstimate(flops=0, bytes_accessed=0, transcendentals=0),
     )(*chunks, cluster_row, cluster_column, before)
 
 
-def step_passes(step, size):
-    groups = 2 * step * size // (3 * BLK)
-    tiles = -(-(2 * step + 1) * size // BLK)
-    passes = [(2 * step, step, groups, 3, False, tuple(range(3 * groups, tiles)))]
-    low = (2 * step - 1) * size // BLK if step > 1 else 0
-    passes.append((2 * step - 2, step - 1, 0, 1, True, tuple(range(low, -(-2 * step * size // BLK)))))
-    return tuple(passes)
+def one_pass(chunk, news, count, size):
+    group = 3
+    groups = chunk * size // (group * BLK)
+    tiles = -(-count * size // BLK)
+    return ((chunk, news, groups, group, False, tuple(range(groups * group, tiles))),)
 
 
 def finish_kernel(size, order_ref, own_ref, other_ref, clusters_ref, column_ref, best_ref, out_ref, acc):
@@ -326,26 +332,64 @@
     s, rep = lax.axis_index("shard"), lax.axis_index("rep")
     axes = ("shard", "rep")
     sends, order = plan()
-    starts = sends * share + (np.arange(4) % 2 * size)[None, :, None].astype(np.int32)
+    halves = np.arange(4)[:, None] % 2 ^ np.array([0, 0, 0, 0, 1])
+    starts = sends[:, :, [0, 1, 2, 3, 3]] * share + (halves * size).astype(np.int32)
     starts = jnp.asarray(starts)[s, rep]
     order = jnp.asarray(order)[s, rep]
-    early = gather_rows(embeddings, send_index, starts[:1], size)
-    late = gather_rows(embeddings, send_index, starts[1:], size, (early,))
-    outgoing = [early[0], late[0], late[1], late[2]]
-    own = [outgoing[3]] + [lax.ppermute(outgoing[r // 2], axes, round_pairs(r)) for r in range(7)]
-    other = [lax.ppermute(chunk, axes, SIBLINGS) for chunk in own]
     clusters = lax.ppermute(arrival_clusters(place_index, slot_cluster), axes, metadata_pairs())
     clusters = clusters.reshape(16, size)[order]
-    column = jnp.broadcast_to(clusters[0::2, :, None], (8, size, LANES))
-    clusters = clusters.reshape(1, 16 * size)
-
+    early = gather_rows(embeddings, send_index, starts[:2], size)
+
+    def go(step, chunk):
+        return lax.ppermute(chunk, axes, round_pairs(step - 1))
+
+    def swap(chunk):
+        return lax.ppermute(chunk, axes, SIBLINGS)
+
+    own, other = [None] * 8, [None] * 8
+    for step in (1, 2, 3):
+        own[step] = go(step, early[(step - 1) // 2])
+    own[4] = go(4, tie(early[1], own[1]))
+    late = gather_rows(embeddings, send_index, starts[2:], size, (own[1],))
+    own[0], other[0] = late[1], late[2]
+    other[1] = swap(own[1])
+    other[2] = swap(own[2])
+    own[5] = go(5, tie(late[0], own[2]))
+    def columns(chunk, news):
+        part = clusters[chunk : chunk + news].reshape(1, news * size, 1)
+        return jnp.broadcast_to(part, (1, news * size, LANES))
+
+    flat = clusters.reshape(1, 16 * size)
     best = jnp.full((1, 16 * size), -1.0, jnp.float32)
-    chunks = [(own, other)[i % 2][i // 2] for i in range(16)]
-    for step in range(1, 8):
-        best = gram_best(
-            chunks[: 2 * step + 1], clusters, column, best, step_passes(step, size), 2 * step
+
+    def score(best, chunk, news, count):
+        return gram_best(
+            [(own, other)[side][r] for r, side in CHUNKS[:count]],
+            flat,
+            columns(chunk, news),
+            best,
+            one_pass(chunk, news, count, size),
+            tuple(range(chunk, chunk + news)),
         )
-    outbound = finish(order, own[7], other[7], clusters, column[7], best)
+
+    best = score(best, 0, 2, 4)
+    own[3] = tie(own[3], best)
+    other[3] = swap(own[3])
+    own[6] = go(6, tie(late[0], own[3]))
+    own[4] = tie(own[4], best)
+    other[4] = swap(own[4])
+    own[7] = go(7, tie(late[1], own[4]))
+    best = score(best, 4, 2, 8)
+    own[5] = tie(own[5], best)
+    other[5] = swap(own[5])
+    own[6] = tie(own[6], best)
+    other[6] = swap(own[6])
+    best = score(best, 8, 2, 12)
+    own[7] = tie(own[7], best)
+    other[7] = swap(own[7])
+    best = score(best, 12, 1, 14)
+    best = score(best, 14, 1, 15)
+    outbound = finish(order, own[7], other[7], flat, columns(14, 1)[0], best)
     returned = lax.all_to_all(outbound, axes, split_axis=0, concat_axis=0, tiled=True)
     sources = []
     for owner in range(8):
@@ -371,12 +415,12 @@
     arrived = jnp.roll(arrived.reshape(parts, size, width), -turn, axis=0)
     clusters = arrival_clusters(place_index, slot_cluster).reshape(parts, size)
     clusters = jnp.roll(clusters, -turn, axis=0)
-    column = jnp.broadcast_to(clusters[:news, :, None], (news, size, LANES))
+    column = jnp.broadcast_to(clusters[:news].reshape(1, -1, 1), (1, news * size, LANES))
     best = jnp.full((1, documents), -1.0, jnp.float32)
     tiles = tuple(range(documents // BLK))
-    passes = tuple((chunk, chunk, 0, 1, True, tiles) for chunk in range(news))
+    passes = ((0, news, 0, 1, True, tiles),)
     best = gram_best(
-        [arrived[i] for i in range(parts)], clusters.reshape(1, -1), column, best, passes, 0
+        [arrived[i] for i in range(parts)], clusters.reshape(1, -1), column, best, passes, tuple(range(news))
     )
     best = lax.all_gather(best[0, : news * size], "rep", axis=0, tiled=True)
     returned = lax.all_to_all(

time: 222 us -> 180 us (0.81)
  starting transfers between devices: 71.6 us -> 44.9 us
  waiting for transfers between devices: 37.4 us -> 26 us
  Pallas kernels: 96 us -> 88.3 us
  local copies, waits for them, and re-layouts: 14.1 us -> 18.5 us
    all_to_all x1, starting transfers between devices: 36.4 us -> 6.94 us  [hosted(): lax.all_to_all(outbound, axes, split_axis=0, concat_axis=0, tiled=True)]
    ppermute x1, waiting for transfers between devices: 12.1 us -> 0.01 us  [hosted(): lax.ppermute(arrival_clusters(place_index, slot_cluster), axes, metadata_...]
    pallas_call x7 -> x5, Pallas kernels: 61.1 us -> 50.4 us  [gram_best(): pl.pallas_call(functools.partial(gram_kernel, passes, count, size, first)...]
    squeeze x1 -> x3, local copies, waits for them, and re-layouts: 1.93 us -> 6.83 us  [the longest x1 3.12 us: hosted(): own[5] = go(5, tie(late[0], own[2]))]
    unnamed x32 -> x30, local copies, waits for them, and re-layouts: 4.37 us -> 0.76 us
    pallas_call x2, Pallas kernels: 28.6 us -> 31.6 us  [gather_rows(): pl.pallas_call(functools.partial(gather_kernel, count, size, sections), o...]
    broadcast_in_dim x2 -> x8, local copies, waits for them, and re-layouts: 2.4 us -> 5.08 us  [columns(): return jnp.broadcast_to(part, (1, news * size, LANES))]
    ppermute x15 -> x14, starting transfers between devices: 33.9 us -> 35 us  [the longest x7 28.1 us: go(): return lax.ppermute(chunk, axes, round_pairs(step - 1))]
  transfers between devices with their start and end apart: 17 -> 16, of which waited for: 4 -> 4; matrix products, arithmetic and copies ran while one was open for 3% -> 8% of each run, Pallas kernels for 28% -> 38%
where the time goes in v3:
time: 180 us; the launch traced here: 179 us
  Pallas kernels  88.3 us (49%)
  starting transfers between devices  44.9 us (25%)
  waiting for transfers between devices  26 us (14%)
  local copies, waits for them, and re-layouts  18.5 us (10%)
    pallas_call x5, Pallas kernels, gram_best(): pl.pallas_call(functools.partial(gram_kernel, passes, count, size, first)...  50.4 us
    pallas_call x2, Pallas kernels, gather_rows(): pl.pallas_call(functools.partial(gather_kernel, count, size, sections), o...  31.6 us
    ppermute x7, starting transfers between devices, go(): return lax.ppermute(chunk, axes, round_pairs(step - 1))  28.1 us
    ppermute x7, waiting for transfers between devices, go(): return lax.ppermute(chunk, axes, round_pairs(step - 1))  18.5 us
    all_to_all x1, waiting for transfers between devices, hosted(): lax.all_to_all(outbound, axes, split_axis=0, concat_axis=0, tiled=True)  7.5 us
    all_to_all x1, starting transfers between devices, hosted(): lax.all_to_all(outbound, axes, split_axis=0, concat_axis=0, tiled=True)  6.94 us
    ppermute x7, starting transfers between devices, swap(): return lax.ppermute(chunk, axes, SIBLINGS)  6.93 us
    broadcast_in_dim x8, local copies, waits for them, and re-layouts, columns(): return jnp.broadcast_to(part, (1, news * size, LANES))  5.08 us
  transfers between devices with their start and end apart: 16, of which 4 were waited for; matrix products, arithmetic and copies ran while one was open for 8% of the time, Pallas kernels for 38%

profile of v3, /device:TPU:0, one launch (start us, length us, event | category | flops | bytes accessed | tf_op | source)
XLA Modules:
  0.0 179.1 jit_solution(1098109145197476462)
XLA Ops:
  0.0 0.7 constant_dynamic-slice_fusion
  0.7 0.5 slice_bitcast_fusion.5.refs_0_
  1.2 14.0 %shard_map.64 = bf16[2,400,1024]{2,1,0:T(8,128)(2,1)} custom-call(s32[2]{0:T(128)} %slice_bitcast_fusion.5.refs_0_, s32[6400]{0:T(1024)} %refs_1_.3, bf16[6400,1024]{1,0:T(8,128)(2,1)} %refs_2_.3), custom_call_target="tpu_custom_call" | custom-call | tf_op jit(solution)/shard_map/pallas_call | solution.py:132
  15.2 2.8 %slice_bitcast_fusion.2 = (bf16[400,1024]{1,0:T(8,128)(2,1)}, bf16[400,1024]{1,0:T(8,128)(2,1)}) fusion(bf16[2,400,1024]{2,1,0:T(8,128)(2,1)} %shard_map.64), kind=kLoop, calls=%fused_computation.3 | loop fusion | bytes 3276800 | tf_op jit(solution)/shard_map/squeeze | solution.py:352
  18.0 6.0 %collective-permute-start = (bf16[400,1024]{1,0:T(8,128)(2,1)}, bf16[400,1024]{1,0:T(8,128)(2,1)S(1)}, u32[]{:S(2)}, u32[]{:S(2)}) collective-permute-start(bf16[400,1024]{1,0:T(8,128)(2,1)} %get-tuple-element.27), channel_id=1, source_target_pairs={{24,8},{28,12},{0,16},{4,20},{1,9},{5,13},{25,17},{29,21},{26,10},... | collective-permute-start | bytes 2457608 | tf_op jit(solution)/shard_map/ppermute | solution.py:344
  24.0 0.7 collective-permute-start.5
  24.9 0.2 select_reduce_fusion
  25.1 3.0 %collective-permute-start.3 = (s32[6400]{0:T(1024)S(1)}, s32[6400]{0:T(1024)S(1)}, u32[]{:S(2)}, u32[]{:S(2)}) collective-permute-start(s32[6400]{0:T(1024)S(1)} %select_reduce_fusion), channel_id=1, source_target_pairs={{0,8},{1,9},{4,12},{5,13},{10,10},{11,11},{14,14},{15,15},{16,16},... | collective-permute-start | bytes 76808 | tf_op jit(solution)/shard_map/ppermute | solution.py:339
  28.1 1.5 collective-permute-start.6
  29.7 0.7 fusion.2
  30.4 12.6 %collective-permute-done.refs_3_.refs_1_ = bf16[400,1024]{1,0:T(8,128)(2,1)S(1)} collective-permute-done((bf16[400,1024]{1,0:T(8,128)(2,1)}, bf16[400,1024]{1,0:T(8,128)(2,1)S(1)}, u32[]{:S(2)}, u32[]{:S(2)}) %collective-permute-start) | collective-permute-done | bytes 819232 | tf_op jit(solution)/shard_map/ppermute | solution.py:344
  42.9 0.7 collective-permute-start.2
  43.6 0.6 slice_bitcast_fusion.6.refs_0_
  44.4 0.6 gather_fusion
  45.0 0.7 reshape.70.refs_4_.refs_8_.refs_12_.refs_14_.refs_15_.clusters_ref
  45.8 1.5 collective-permute-start.1
  47.3 17.6 %shard_map.65 = bf16[3,400,1024]{2,1,0:T(8,128)(2,1)} custom-call(s32[3]{0:T(128)} %slice_bitcast_fusion.6.refs_0_, s32[6400]{0:T(1024)} %refs_1_.3, bf16[6400,1024]{1,0:T(8,128)(2,1)} %refs_2_.3, bf16[400,1024]{1,0:T(8,128)(2,1)} %copy-done.1), custom_call_target="tpu_custom_call" | custom-call | tf_op jit(solution)/shard_map/pallas_call | solution.py:132
  64.9 1.6 collective-permute-start.7
  66.5 3.1 %slice_bitcast_fusion = (bf16[400,1024]{1,0:T(8,128)(2,1)}, bf16[400,1024]{1,0:T(8,128)(2,1)}, bf16[400,1024]{1,0:T(8,128)(2,1)}) fusion(bf16[3,400,1024]{2,1,0:T(8,128)(2,1)} %shard_map.65), kind=kLoop, calls=%fused_computation.1 | loop fusion | bytes 4915200 | tf_op jit(solution)/shard_map/squeeze | solution.py:357
  69.7 1.0 broadcast_in_dim.62.refs_5_
  70.7 0.6 broadcast_in_dim.63.refs_6_
  71.3 6.9 %shard_map.66.refs_10_ = f32[1,6400]{1,0:T(1,128)} custom-call(bf16[400,1024]{1,0:T(8,128)(2,1)} %get-tuple-element.16.refs_0_, bf16[400,1024]{1,0:T(8,128)(2,1)} %copy-done.1, bf16[400,1024]{1,0:T(8,128)(2,1)} %get-tuple-element.24.refs_2_, bf16[400,1024]{1,0:T(8,128)(2,1)} %copy-done.2, ...), custom_call_target="tpu_custom_call" | custom-call | tf_op jit(solution)/shard_map/pallas_call | solution.py:231
  78.2 0.7 collective-permute-start.8
  79.0 10.3 %collective-permute-start.9 = (bf16[400,1024]{1,0:T(8,128)(2,1)}, bf16[400,1024]{1,0:T(8,128)(2,1)S(1)}, u32[]{:S(2)}, u32[]{:S(2)}) collective-permute-start(bf16[400,1024]{1,0:T(8,128)(2,1)} %get-tuple-element.21), channel_id=1, source_target_pairs={{0,8},{4,12},{24,16},{28,20},{25,9},{29,13},{1,17},{5,21},{2,10},{... | collective-permute-start | bytes 2457608 | tf_op jit(solution)/shard_map/ppermute | solution.py:344
  89.3 1.6 collective-permute-start.10
  91.0 1.6 collective-permute-start.13
  92.6 1.0 broadcast_in_dim.65.refs_9_
  93.6 10.1 %shard_map.67.refs_14_ = f32[1,6400]{1,0:T(1,128)} custom-call(bf16[400,1024]{1,0:T(8,128)(2,1)} %get-tuple-element.16.refs_0_, bf16[400,1024]{1,0:T(8,128)(2,1)} %copy-done.1, bf16[400,1024]{1,0:T(8,128)(2,1)} %get-tuple-element.24.refs_2_, bf16[400,1024]{1,0:T(8,128)(2,1)} %copy-done.2, bf16[400,1024]{1,0:T(8,128)(2,1)} %copy-done.3, ...), custom_call_target="tpu_custom_call" | custom-call | tf_op jit(solution)/shard_map/pallas_call | solution.py:231
  103.8 3.3 %collective-permute-done.9.refs_9_ = bf16[400,1024]{1,0:T(8,128)(2,1)S(1)} collective-permute-done((bf16[400,1024]{1,0:T(8,128)(2,1)}, bf16[400,1024]{1,0:T(8,128)(2,1)S(1)}, u32[]{:S(2)}, u32[]{:S(2)}) %collective-permute-start.9) | collective-permute-done | bytes 819232 | tf_op jit(solution)/shard_map/ppermute | solution.py:344
  107.0 0.7 collective-permute-start.11
  107.8 6.4 %collective-permute-start.4 = (bf16[400,1024]{1,0:T(8,128)(2,1)S(1)}, bf16[400,1024]{1,0:T(8,128)(2,1)S(1)}, u32[]{:S(2)}, u32[]{:S(2)}) collective-permute-start(bf16[400,1024]{1,0:T(8,128)(2,1)S(1)} %copy-done), channel_id=1, source_target_pairs={{4,8},{0,12},{28,16},{24,20},{29,9},{25,13},{5,17},{1,21},{6,10},{... | collective-permute-start | bytes 2457608 | tf_op jit(solution)/shard_map/ppermute | solution.py:344
  114.2 0.9 collective-permute-start.14
  115.1 1.0 broadcast_in_dim.67.refs_13_
  116.2 13.1 %shard_map.68.refs_16_ = f32[1,6400]{1,0:T(1,128)} custom-call(bf16[400,1024]{1,0:T(8,128)(2,1)} %get-tuple-element.16.refs_0_, bf16[400,1024]{1,0:T(8,128)(2,1)} %copy-done.1, bf16[400,1024]{1,0:T(8,128)(2,1)} %get-tuple-element.24.refs_2_, bf16[400,1024]{1,0:T(8,128)(2,1)} %copy-done.2, bf16[400,1024]{1,0:T(8,128)(2,1)} %copy-done.3, ...), custom_call_target="tpu_custom_call" | custom-call | tf_op jit(solution)/shard_map/pallas_call | solution.py:231
  129.3 2.7 %collective-permute-done.4.refs_14_.own_ref = bf16[400,1024]{1,0:T(8,128)(2,1)S(1)} collective-permute-done((bf16[400,1024]{1,0:T(8,128)(2,1)S(1)}, bf16[400,1024]{1,0:T(8,128)(2,1)S(1)}, u32[]{:S(2)}, u32[]{:S(2)}) %collective-permute-start.4) | collective-permute-done | bytes 819232 | tf_op jit(solution)/shard_map/ppermute | solution.py:344
  132.0 0.7 collective-permute-start.12
  132.7 1.2 fusion.3.order_ref
  133.9 1.0 broadcast_in_dim.71.refs_15_
  134.9 9.8 %shard_map.69.refs_17_ = f32[1,6400]{1,0:T(1,128)} custom-call(bf16[400,1024]{1,0:T(8,128)(2,1)} %get-tuple-element.16.refs_0_, bf16[400,1024]{1,0:T(8,128)(2,1)} %copy-done.1, bf16[400,1024]{1,0:T(8,128)(2,1)} %get-tuple-element.24.refs_2_, bf16[400,1024]{1,0:T(8,128)(2,1)} %copy-done.2, bf16[400,1024]{1,0:T(8,128)(2,1)} %copy-done.3, ...), custom_call_target="tpu_custom_call" | custom-call | tf_op jit(solution)/shard_map/pallas_call | solution.py:231
  144.7 0.8 broadcast_in_dim.69.refs_16_
  145.5 10.4 %shard_map.70.best_ref = f32[1,6400]{1,0:T(1,128)} custom-call(bf16[400,1024]{1,0:T(8,128)(2,1)} %get-tuple-element.16.refs_0_, bf16[400,1024]{1,0:T(8,128)(2,1)} %copy-done.1, bf16[400,1024]{1,0:T(8,128)(2,1)} %get-tuple-element.24.refs_2_, bf16[400,1024]{1,0:T(8,128)(2,1)} %copy-done.2, bf16[400,1024]{1,0:T(8,128)(2,1)} %copy-done.3, ...), custom_call_target="tpu_custom_call" | custom-call | tf_op jit(solution)/shard_map/pallas_call | solution.py:231
  155.9 0.9 squeeze.35.column_ref
  156.9 3.0 %shard_map.71 = f32[32,2,400]{2,1,0:T(2,128)} custom-call(s32[16]{0:T(128)} %fusion.3.order_ref, bf16[400,1024]{1,0:T(8,128)(2,1)} %copy-done.9, bf16[400,1024]{1,0:T(8,128)(2,1)} %copy-done.10, s32[1,6400]{1,0:T(1,128)} %reshape.70.refs_4_.refs_8_.refs_12_.refs_14_.refs_15_.clusters_ref, s32[400,128]{1,0:T(8,128)} %squeeze.35.column_ref, ...), custom_call_target="tpu_custom_call" | custom-call | tf_op jit(solution)/shard_map/pallas_call | solution.py:276
  160.0 6.9 %all-to-all-start = ((f32[32,2,400]{2,1,0:T(2,128)}), f32[32,2,400]{2,1,0:T(2,128)S(1)}, u32[]{:S(2)}, u32[]{:S(2)}) async-start(f32[32,2,400]{2,1,0:T(2,128)} %shard_map.71), calls=%async_computation | async-start | bytes 262144 | tf_op jit(solution)/shard_map/all_to_all | solution.py:393
  166.9 0.7 reshape.67.index_ref
  167.6 7.5 %all-to-all-done.values_ref = f32[32,2,400]{2,1,0:T(2,128)S(1)} async-done(((f32[32,2,400]{2,1,0:T(2,128)}), f32[32,2,400]{2,1,0:T(2,128)S(1)}, u32[]{:S(2)}, u32[]{:S(2)}) %all-to-all-start) | async-done | bytes 102432 | tf_op jit(solution)/shard_map/all_to_all | solution.py:393
  175.1 0.6 copy-done.11
  175.8 3.3 %shard_map.72 = f32[50,128]{1,0:T(8,128)} custom-call(s32[8,2,400]{2,1,0:T(2,128)} %reshape.67.index_ref, f32[32,2,400]{2,1,0:T(2,128)} %copy-done.11), custom_call_target="tpu_custom_call" | custom-call | tf_op jit(solution)/shard_map/pallas_call | solution.py:316
  (51 shorter events, 0.6 us)
Async XLA Ops:
  15.2 9.5 %copy-start.14 = (s32[6656]{0:T(1024)S(1)}, s32[6656]{0:T(1024)}, u32[]{:S(2)}) copy-start(s32[6656]{0:T(1024)} %param.10) | copy-start | bytes 79876
  15.2 9.5 %copy-start.13 = (s32[6400]{0:T(1024)S(1)}, s32[6400]{0:T(1024)}, u32[]{:S(2)}) copy-start(s32[6400]{0:T(1024)} %param.9) | copy-start | bytes 76804
  18.0 24.9 %collective-permute-start = (bf16[400,1024]{1,0:T(8,128)(2,1)}, bf16[400,1024]{1,0:T(8,128)(2,1)S(1)}, u32[]{:S(2)}, u32[]{:S(2)}) collective-permute-start(bf16[400,1024]{1,0:T(8,128)(2,1)} %get-tuple-element.27), channel_id=1, source_target_pairs={{24,8},{28,12},{0,16},{4,20},{1,9},{5,13},{25,17},{29,21},{26,10},... | collective-permute-start | bytes 2457608 | tf_op jit(solution)/shard_map/ppermute | solution.py:344
  24.0 40.9 %collective-permute-start.5 = (bf16[400,1024]{1,0:T(8,128)(2,1)}, bf16[400,1024]{1,0:T(8,128)(2,1)S(1)}, u32[]{:S(2)}, u32[]{:S(2)}) collective-permute-start(bf16[400,1024]{1,0:T(8,128)(2,1)} %get-tuple-element.27), channel_id=1, source_target_pairs={{16,8},{20,12},{8,16},{12,20},{13,9},{9,13},{21,17},{17,21},{18,10... | collective-permute-start | bytes 2457608 | tf_op jit(solution)/shard_map/ppermute | solution.py:344
  25.1 19.2 %collective-permute-start.3 = (s32[6400]{0:T(1024)S(1)}, s32[6400]{0:T(1024)S(1)}, u32[]{:S(2)}, u32[]{:S(2)}) collective-permute-start(s32[6400]{0:T(1024)S(1)} %select_reduce_fusion), channel_id=1, source_target_pairs={{0,8},{1,9},{4,12},{5,13},{10,10},{11,11},{14,14},{15,15},{16,16},... | collective-permute-start | bytes 76808 | tf_op jit(solution)/shard_map/ppermute | solution.py:339
  28.1 50.1 %collective-permute-start.6 = (bf16[400,1024]{1,0:T(8,128)(2,1)}, bf16[400,1024]{1,0:T(8,128)(2,1)S(1)}, u32[]{:S(2)}, u32[]{:S(2)}) collective-permute-start(bf16[400,1024]{1,0:T(8,128)(2,1)} %get-tuple-element.14), channel_id=1, source_target_pairs={{28,8},{24,12},{4,16},{0,20},{5,9},{1,13},{29,17},{25,21},{30,10},... | collective-permute-start | bytes 2457608 | tf_op jit(solution)/shard_map/ppermute | solution.py:344
  42.9 4.4 %copy-start.1 = (bf16[400,1024]{1,0:T(8,128)(2,1)}, bf16[400,1024]{1,0:T(8,128)(2,1)S(1)}, u32[]{:S(2)}) copy-start(bf16[400,1024]{1,0:T(8,128)(2,1)S(1)} %collective-permute-done.refs_3_.refs_1_) | copy-start | bytes 2457604
  42.9 26.7 %collective-permute-start.2 = (bf16[400,1024]{1,0:T(8,128)(2,1)S(1)}, bf16[400,1024]{1,0:T(8,128)(2,1)S(1)}, u32[]{:S(2)}, u32[]{:S(2)}) collective-permute-start(bf16[400,1024]{1,0:T(8,128)(2,1)S(1)} %collective-permute-done.refs_3_.refs_1_), channel_id=1, source_target_pairs={{8,9},{9,8},{10,11},{11,10},{12,13},{13,12},{14,15},{15,14},{16,17... | collective-permute-start | bytes 2457608 | tf_op jit(solution)/shard_map/ppermute | solution.py:347
  45.8 43.6 %collective-permute-start.1 = (bf16[400,1024]{1,0:T(8,128)(2,1)}, bf16[400,1024]{1,0:T(8,128)(2,1)}, u32[]{:S(2)}, u32[]{:S(2)}) collective-permute-start(bf16[400,1024]{1,0:T(8,128)(2,1)} %get-tuple-element.14), channel_id=1, source_target_pairs={{20,8},{16,12},{12,16},{8,20},{17,9},{21,13},{9,17},{13,21},{22,10... | collective-permute-start | bytes 2457608 | tf_op jit(solution)/shard_map/ppermute | solution.py:344
  64.9 4.7 %copy-start.3 = (bf16[400,1024]{1,0:T(8,128)(2,1)}, bf16[400,1024]{1,0:T(8,128)(2,1)S(1)}, u32[]{:S(2)}) copy-start(bf16[400,1024]{1,0:T(8,128)(2,1)S(1)} %collective-permute-done.5.refs_4_) | copy-start | bytes 2457604
  64.9 27.7 %collective-permute-start.7 = (bf16[400,1024]{1,0:T(8,128)(2,1)S(1)}, bf16[400,1024]{1,0:T(8,128)(2,1)}, u32[]{:S(2)}, u32[]{:S(2)}) collective-permute-start(bf16[400,1024]{1,0:T(8,128)(2,1)S(1)} %collective-permute-done.5.refs_4_), channel_id=1, source_target_pairs={{8,9},{9,8},{10,11},{11,10},{12,13},{13,12},{14,15},{15,14},{16,17... | collective-permute-start | bytes 2457608 | tf_op jit(solution)/shard_map/ppermute | solution.py:347
  69.6 1.7 copy-start.2
  78.2 14.4 %copy-start.4 = (bf16[400,1024]{1,0:T(8,128)(2,1)}, bf16[400,1024]{1,0:T(8,128)(2,1)S(1)}, u32[]{:S(2)}) copy-start(bf16[400,1024]{1,0:T(8,128)(2,1)S(1)} %collective-permute-done.6.refs_5_) | copy-start | bytes 2457604
  78.2 14.4 %collective-permute-start.8 = (bf16[400,1024]{1,0:T(8,128)(2,1)S(1)}, bf16[400,1024]{1,0:T(8,128)(2,1)S(1)}, u32[]{:S(2)}, u32[]{:S(2)}) collective-permute-start(bf16[400,1024]{1,0:T(8,128)(2,1)S(1)} %collective-permute-done.6.refs_5_), channel_id=1, source_target_pairs={{8,9},{9,8},{10,11},{11,10},{12,13},{13,12},{14,15},{15,14},{16,17... | collective-permute-start | bytes 2457608 | tf_op jit(solution)/shard_map/ppermute | solution.py:347
  79.0 28.1 %collective-permute-start.9 = (bf16[400,1024]{1,0:T(8,128)(2,1)}, bf16[400,1024]{1,0:T(8,128)(2,1)S(1)}, u32[]{:S(2)}, u32[]{:S(2)}) collective-permute-start(bf16[400,1024]{1,0:T(8,128)(2,1)} %get-tuple-element.21), channel_id=1, source_target_pairs={{0,8},{4,12},{24,16},{28,20},{25,9},{29,13},{1,17},{5,21},{2,10},{... | collective-permute-start | bytes 2457608 | tf_op jit(solution)/shard_map/ppermute | solution.py:344
  89.3 25.8 %collective-permute-start.10 = (bf16[400,1024]{1,0:T(8,128)(2,1)}, bf16[400,1024]{1,0:T(8,128)(2,1)}, u32[]{:S(2)}, u32[]{:S(2)}) collective-permute-start(bf16[400,1024]{1,0:T(8,128)(2,1)} %collective-permute-done.1.refs_8_), channel_id=1, source_target_pairs={{8,9},{9,8},{10,11},{11,10},{12,13},{13,12},{14,15},{15,14},{16,17... | collective-permute-start | bytes 2457608 | tf_op jit(solution)/shard_map/ppermute | solution.py:347
  91.0 23.2 %collective-permute-start.13 = (bf16[400,1024]{1,0:T(8,128)(2,1)}, bf16[400,1024]{1,0:T(8,128)(2,1)}, u32[]{:S(2)}, u32[]{:S(2)}) collective-permute-start(bf16[400,1024]{1,0:T(8,128)(2,1)} %get-tuple-element.21), channel_id=1, source_target_pairs={{12,8},{8,12},{20,16},{16,20},{21,9},{17,13},{13,17},{9,21},{14,10... | collective-permute-start | bytes 2457608 | tf_op jit(solution)/shard_map/ppermute | solution.py:344
  92.6 1.0 copy-start.5
  93.6 14.1 %copy-start = (bf16[400,1024]{1,0:T(8,128)(2,1)S(1)}, bf16[400,1024]{1,0:T(8,128)(2,1)}, u32[]{:S(2)}) copy-start(bf16[400,1024]{1,0:T(8,128)(2,1)} %get-tuple-element.16.refs_0_) | copy-start | bytes 2457604
  107.0 9.1 %copy-start.6 = (bf16[400,1024]{1,0:T(8,128)(2,1)}, bf16[400,1024]{1,0:T(8,128)(2,1)S(1)}, u32[]{:S(2)}) copy-start(bf16[400,1024]{1,0:T(8,128)(2,1)S(1)} %collective-permute-done.9.refs_9_) | copy-start | bytes 2457604
  107.0 8.1 %collective-permute-start.11 = (bf16[400,1024]{1,0:T(8,128)(2,1)S(1)}, bf16[400,1024]{1,0:T(8,128)(2,1)S(1)}, u32[]{:S(2)}, u32[]{:S(2)}) collective-permute-start(bf16[400,1024]{1,0:T(8,128)(2,1)S(1)} %collective-permute-done.9.refs_9_), channel_id=1, source_target_pairs={{8,9},{9,8},{10,11},{11,10},{12,13},{13,12},{14,15},{15,14},{16,17... | collective-permute-start | bytes 2457608 | tf_op jit(solution)/shard_map/ppermute | solution.py:347
  107.8 24.2 %collective-permute-start.4 = (bf16[400,1024]{1,0:T(8,128)(2,1)S(1)}, bf16[400,1024]{1,0:T(8,128)(2,1)S(1)}, u32[]{:S(2)}, u32[]{:S(2)}) collective-permute-start(bf16[400,1024]{1,0:T(8,128)(2,1)S(1)} %copy-done), channel_id=1, source_target_pairs={{4,8},{0,12},{28,16},{24,20},{29,9},{25,13},{5,17},{1,21},{6,10},{... | collective-permute-start | bytes 2457608 | tf_op jit(solution)/shard_map/ppermute | solution.py:344
  114.2 19.7 %collective-permute-start.14 = (bf16[400,1024]{1,0:T(8,128)(2,1)}, bf16[400,1024]{1,0:T(8,128)(2,1)S(1)}, u32[]{:S(2)}, u32[]{:S(2)}) collective-permute-start(bf16[400,1024]{1,0:T(8,128)(2,1)} %collective-permute-done.13.refs_12_), channel_id=1, source_target_pairs={{8,9},{9,8},{10,11},{11,10},{12,13},{13,12},{14,15},{15,14},{16,17... | collective-permute-start | bytes 2457608 | tf_op jit(solution)/shard_map/ppermute | solution.py:347
  115.1 1.0 copy-start.7
  132.0 13.5 %copy-start.9 = (bf16[400,1024]{1,0:T(8,128)(2,1)}, bf16[400,1024]{1,0:T(8,128)(2,1)S(1)}, u32[]{:S(2)}) copy-start(bf16[400,1024]{1,0:T(8,128)(2,1)S(1)} %collective-permute-done.4.refs_14_.own_ref) | copy-start | bytes 2457604
  132.0 23.9 %collective-permute-start.12 = (bf16[400,1024]{1,0:T(8,128)(2,1)S(1)}, bf16[400,1024]{1,0:T(8,128)(2,1)S(1)}, u32[]{:S(2)}, u32[]{:S(2)}) collective-permute-start(bf16[400,1024]{1,0:T(8,128)(2,1)S(1)} %collective-permute-done.4.refs_14_.own_ref), channel_id=1, source_target_pairs={{8,9},{9,8},{10,11},{11,10},{12,13},{13,12},{14,15},{15,14},{16,17... | collective-permute-start | bytes 2457608 | tf_op jit(solution)/shard_map/ppermute | solution.py:347
  133.9 1.0 copy-start.8
  155.9 11.0 %copy-start.12 = (s32[6400]{0:T(1024)S(1)}, s32[6400]{0:T(1024)}, u32[]{:S(2)}) copy-start(s32[6400]{0:T(1024)} %refs_1_.3) | copy-start | bytes 76804
  155.9 1.0 copy-start.10
  160.0 15.2 %all-to-all-start = ((f32[32,2,400]{2,1,0:T(2,128)}), f32[32,2,400]{2,1,0:T(2,128)S(1)}, u32[]{:S(2)}, u32[]{:S(2)}) async-start(f32[32,2,400]{2,1,0:T(2,128)} %shard_map.71), calls=%async_computation | async-start | bytes 262144 | tf_op jit(solution)/shard_map/all_to_all | solution.py:393
  175.1 0.7 copy-start.11

commit v4 on v3

--- a/solution.py
+++ b/solution.py
@@ -12,16 +12,17 @@
 LANES = 128
 NT = (((1,), (1,)), ((), ()))
 VMEM_LIMIT = 56 * 1024 * 1024
+LONG = 25_000_000_000
 
 HOSTS = (2, 3, 4, 5)
 ROUNDS = ((4, 6, 5, 7, 2, 1, 3), (2, 1, 3, 6, 4, 7, 5))
 
 
 CHUNKS = (
-    (0, 0), (1, 0), (0, 1), (1, 1),
-    (2, 0), (3, 0), (2, 1), (3, 1),
-    (4, 0), (5, 0), (4, 1), (5, 1),
-    (6, 0), (6, 1), (7, 0), (7, 1),
+    (0, 0), (1, 0), (2, 0), (0, 1), (1, 1), (2, 1),
+    (3, 0), (4, 0), (3, 1), (4, 1),
+    (5, 0), (6, 0), (5, 1), (6, 1),
+    (7, 0), (7, 1),
 )
 
 
@@ -90,7 +91,9 @@
 
 def gather_kernel(count, size, sections, *refs):
     table_ref, index_ref, rows_ref = refs[:3]
-    out_ref, raw, wide, picked, sems = refs[-5:]
+    outs, (raw, wide, picked, sems) = refs[-4 - count : -4], refs[-4:]
+    width = raw.shape[1]
+    tiles = width // LANES
     part = raw.shape[0] // sections
     copies = []
     for i in range(sections):
@@ -102,8 +105,10 @@
         copies[i].wait()
 
         def widen(j, _, i=i):
-            rows = pl.ds(pl.multiple_of(i * part + j * step, step), step)
-            wide[rows, :] = raw[rows, :].astype(jnp.float32)
+            first = i * part + j * step
+            rows = raw[pl.ds(pl.multiple_of(first, step), step), :].astype(jnp.float32)
+            for t in range(tiles):
+                wide[pl.ds(first * tiles + t, step, stride=tiles), :] = rows[:, t * LANES : (t + 1) * LANES]
             return 0
 
         lax.fori_loop(0, part // step, widen, 0)
@@ -113,11 +118,13 @@
 
         def pick(j, _, c=c, base=base):
             for t in range(group):
-                source = index_ref[base + j * group + t]
-                picked[pl.ds(t, 1), :] = wide[pl.ds(source, 1), :]
-            rows = picked[...]
+                source = pl.multiple_of(index_ref[base + j * group + t] * tiles, tiles)
+                picked[t * tiles : (t + 1) * tiles, :] = wide[pl.ds(source, tiles), :]
+            rows = jnp.concatenate(
+                [picked[pl.ds(t, group, stride=tiles), :] for t in range(tiles)], axis=1
+            )
             scale = lax.rsqrt(jnp.sum(rows * rows, axis=1, keepdims=True) + 1e-06)
-            out_ref[c, pl.ds(pl.multiple_of(j * group, group), group), :] = (rows * scale).astype(
+            outs[c][pl.ds(pl.multiple_of(j * group, group), group), :] = (rows * scale).astype(
                 jnp.bfloat16
             )
             return 0
@@ -125,28 +132,28 @@
         lax.fori_loop(0, size // group, pick, 0)
 
 
-def gather_rows(embeddings, index, starts, size, after=()):
+def gather_rows(embeddings, index, starts, size, work=0, after=()):
     documents, width = embeddings.shape
     count = starts.shape[0]
     sections = 8
     return pl.pallas_call(
         functools.partial(gather_kernel, count, size, sections),
-        out_shape=jax.ShapeDtypeStruct((count, size, width), jnp.bfloat16),
+        out_shape=[jax.ShapeDtypeStruct((size, width), jnp.bfloat16)] * count,
         in_specs=[
             pl.BlockSpec(memory_space=pltpu.SMEM),
             pl.BlockSpec(memory_space=pltpu.SMEM),
             pl.BlockSpec(memory_space=pl.ANY),
         ]
         + [pl.BlockSpec(memory_space=pl.ANY)] * len(after),
-        out_specs=pl.BlockSpec(memory_space=pltpu.VMEM),
+        out_specs=[pl.BlockSpec(memory_space=pltpu.VMEM)] * count,
         scratch_shapes=[
             pltpu.VMEM((documents, width), jnp.bfloat16),
-            pltpu.VMEM((documents, width), jnp.float32),
-            pltpu.VMEM((16, width), jnp.float32),
+            pltpu.VMEM((documents * width // LANES, LANES), jnp.float32),
+            pltpu.VMEM((16 * width // LANES, LANES), jnp.float32),
             pltpu.SemaphoreType.DMA((sections,)),
         ],
         compiler_params=pltpu.CompilerParams(vmem_limit_bytes=VMEM_LIMIT),
-        cost_estimate=pl.CostEstimate(flops=0, bytes_accessed=0, transcendentals=0),
+        cost_estimate=pl.CostEstimate(flops=work, bytes_accessed=0, transcendentals=0),
     )(starts, index, embeddings, *after)
 
 
@@ -154,9 +161,15 @@
     return jnp.max(jnp.transpose(acc), axis=0, keepdims=True)[:, :size]
 
 
+def as_column(row_ref, start, size):
+    wide = -(-size // LANES) * LANES
+    row = row_ref[:, start : start + wide]
+    return jnp.transpose(jnp.broadcast_to(row, (LANES, wide)))[:size]
+
+
 def gram_kernel(passes, count, size, first, *refs):
     chunks = refs[:count]
-    cluster_row, cluster_column, before_ref, best_ref, held, acc, sems = refs[count:]
+    cluster_row, before_ref, best_ref, held, acc, sems = refs[count:]
     limit = count * size
 
     def copy(i):
@@ -178,7 +191,7 @@
         height = news * size
         acc[...] = jnp.full_like(acc, -1.0)
         rows = held[chunk * size : chunk * size + height, :]
-        left = cluster_column[n]
+        left = as_column(cluster_row, chunk * size, height)
         left = jnp.concatenate([left, left], axis=1)
 
         def tile(start, special, chunk=chunk, height=height, rows=rows, left=left):
@@ -220,19 +233,18 @@
         best_ref[:, span] = jnp.maximum(best_ref[:, span], best_of_rows(acc[...], height))
 
 
-def gram_best(chunks, cluster_row, cluster_column, before, passes, first):
+def gram_best(chunks, cluster_row, before, passes, first):
     count = len(chunks)
     size, width = chunks[0].shape
     total = before.shape[1]
     held = -(-count * size // BLK) * BLK
     tall = max(news for _, news, *_ in passes) * size
     padded = -(-tall // LANES) * LANES
-    work = sum(news * (groups * group + len(last)) * BLK for _, news, groups, group, _, last in passes)
     return pl.pallas_call(
         functools.partial(gram_kernel, passes, count, size, first),
         out_shape=jax.ShapeDtypeStruct((1, total), jnp.float32),
         in_specs=[pl.BlockSpec(memory_space=pl.ANY)] * count
-        + [pl.BlockSpec(memory_space=pltpu.VMEM)] * 3,
+        + [pl.BlockSpec(memory_space=pltpu.VMEM)] * 2,
         out_specs=pl.BlockSpec(memory_space=pltpu.VMEM),
         scratch_shapes=[
             pltpu.VMEM((held, width), jnp.bfloat16),
@@ -241,7 +253,7 @@
         ],
         compiler_params=pltpu.CompilerParams(vmem_limit_bytes=VMEM_LIMIT),
         cost_estimate=pl.CostEstimate(flops=0, bytes_accessed=0, transcendentals=0),
-    )(*chunks, cluster_row, cluster_column, before)
+    )(*chunks, cluster_row, before)
 
 
 def one_pass(chunk, news, count, size):
@@ -251,9 +263,10 @@
     return ((chunk, news, groups, group, False, tuple(range(groups * group, tiles))),)
 
 
-def finish_kernel(size, order_ref, own_ref, other_ref, clusters_ref, column_ref, best_ref, out_ref, acc):
+def finish_kernel(size, order_ref, own_ref, other_ref, clusters_ref, best_ref, out_ref, acc):
     gram = lax.dot_general(own_ref[...], other_ref[...], NT, preferred_element_type=jnp.float32)
-    left = jnp.tile(column_ref[...], (1, -(-size // LANES)))[:, :size]
+    left = as_column(clusters_ref, 14 * size, size)
+    left = jnp.tile(left, (1, -(-size // LANES)))[:, :size]
     last = 15 * size
     values = jnp.where(left == clusters_ref[:, last : last + size], gram, jnp.float32(-1.0))
     acc[...] = jnp.full_like(acc, -1.0)
@@ -270,18 +283,18 @@
             out_ref[source * 4 + rep, pl.ds(half, 1), :] = found
 
 
-def finish(order, own, other, clusters, column, best):
+def finish(order, own, other, clusters, best):
     size = own.shape[0]
     padded = -(-size // LANES) * LANES
     return pl.pallas_call(
         functools.partial(finish_kernel, size),
         out_shape=jax.ShapeDtypeStruct((32, 2, size), jnp.float32),
         in_specs=[pl.BlockSpec(memory_space=pltpu.SMEM)]
-        + [pl.BlockSpec(memory_space=pltpu.VMEM)] * 5,
+        + [pl.BlockSpec(memory_space=pltpu.VMEM)] * 4,
         out_specs=pl.BlockSpec(memory_space=pltpu.VMEM),
         scratch_shapes=[pltpu.VMEM((padded, LANES), jnp.float32)],
         compiler_params=pltpu.CompilerParams(vmem_limit_bytes=VMEM_LIMIT),
-    )(order, own, other, clusters, column, best)
+    )(order, own, other, clusters, best)
 
 
 def settle_kernel(sources, size, high, index_ref, values_ref, out_ref, left_ref, right_ref):
@@ -347,49 +360,38 @@
         return lax.ppermute(chunk, axes, SIBLINGS)
 
     own, other = [None] * 8, [None] * 8
-    for step in (1, 2, 3):
+    for step in (1, 2, 3, 4):
         own[step] = go(step, early[(step - 1) // 2])
-    own[4] = go(4, tie(early[1], own[1]))
-    late = gather_rows(embeddings, send_index, starts[2:], size, (own[1],))
+    late = gather_rows(embeddings, send_index, starts[2:], size, LONG, (early[0],))
     own[0], other[0] = late[1], late[2]
-    other[1] = swap(own[1])
-    other[2] = swap(own[2])
-    own[5] = go(5, tie(late[0], own[2]))
-    def columns(chunk, news):
-        part = clusters[chunk : chunk + news].reshape(1, news * size, 1)
-        return jnp.broadcast_to(part, (1, news * size, LANES))
-
     flat = clusters.reshape(1, 16 * size)
-    best = jnp.full((1, 16 * size), -1.0, jnp.float32)
 
     def score(best, chunk, news, count):
         return gram_best(
             [(own, other)[side][r] for r, side in CHUNKS[:count]],
             flat,
-            columns(chunk, news),
             best,
             one_pass(chunk, news, count, size),
             tuple(range(chunk, chunk + news)),
         )
 
-    best = score(best, 0, 2, 4)
-    own[3] = tie(own[3], best)
-    other[3] = swap(own[3])
-    own[6] = go(6, tie(late[0], own[3]))
-    own[4] = tie(own[4], best)
-    other[4] = swap(own[4])
-    own[7] = go(7, tie(late[1], own[4]))
-    best = score(best, 4, 2, 8)
-    own[5] = tie(own[5], best)
-    other[5] = swap(own[5])
-    own[6] = tie(own[6], best)
-    other[6] = swap(own[6])
-    best = score(best, 8, 2, 12)
+    best = jnp.full((1, 16 * size), -1.0, jnp.float32)
+    own[1], own[2] = tie(own[1], late[0]), tie(own[2], late[0])
+    other[1], other[2] = swap(own[1]), swap(own[2])
+    own[5] = go(5, tie(late[0], own[1]))
+    own[6] = go(6, tie(late[0], own[2]))
+    best = score(best, 0, 3, 6)
+    own[3], own[4] = tie(own[3], best), tie(own[4], best)
+    other[3], other[4] = swap(own[3]), swap(own[4])
+    own[7] = go(7, tie(late[1], own[3]))
+    best = score(best, 6, 2, 10)
+    own[5], own[6] = tie(own[5], best), tie(own[6], best)
+    other[5], other[6] = swap(own[5]), swap(own[6])
+    best = score(best, 10, 2, 14)
     own[7] = tie(own[7], best)
     other[7] = swap(own[7])
-    best = score(best, 12, 1, 14)
     best = score(best, 14, 1, 15)
-    outbound = finish(order, own[7], other[7], flat, columns(14, 1)[0], best)
+    outbound = finish(order, own[7], other[7], flat, best)
     returned = lax.all_to_all(outbound, axes, split_axis=0, concat_axis=0, tiled=True)
     sources = []
     for owner in range(8):
@@ -415,12 +417,11 @@
     arrived = jnp.roll(arrived.reshape(parts, size, width), -turn, axis=0)
     clusters = arrival_clusters(place_index, slot_cluster).reshape(parts, size)
     clusters = jnp.roll(clusters, -turn, axis=0)
-    column = jnp.broadcast_to(clusters[:news].reshape(1, -1, 1), (1, news * size, LANES))
     best = jnp.full((1, documents), -1.0, jnp.float32)
     tiles = tuple(range(documents // BLK))
     passes = ((0, news, 0, 1, True, tiles),)
     best = gram_best(
-        [arrived[i] for i in range(parts)], clusters.reshape(1, -1), column, best, passes, tuple(range(news))
+        [arrived[i] for i in range(parts)], clusters.reshape(1, -1), best, passes, tuple(range(news))
     )
     best = lax.all_gather(best[0, : news * size], "rep", axis=0, tiled=True)
     returned = lax.all_to_all(

time: 180 us -> 178 us (0.989)
  local copies, waits for them, and re-layouts: 18.5 us -> 11.4 us
  starting transfers between devices: 44.9 us -> 47.4 us
  waiting for transfers between devices: 26 us -> 28.4 us
    ppermute x1, waiting for transfers between devices: 0.01 us -> 14.9 us  [hosted(): lax.ppermute(arrival_clusters(place_index, slot_cluster), axes, metadata_...]
    ppermute x7, waiting for transfers between devices: 18.5 us -> 5.97 us  [go(): return lax.ppermute(chunk, axes, round_pairs(step - 1))]
    squeeze x3 -> x0, local copies, waits for them, and re-layouts: 6.83 us -> none  [the longest x1 3.12 us: hosted(): own[5] = go(5, tie(late[0], own[2]))]
    ppermute x7, starting transfers between devices: 28.1 us -> 33.4 us  [go(): return lax.ppermute(chunk, axes, round_pairs(step - 1))]
    broadcast_in_dim x8 -> x0, local copies, waits for them, and re-layouts: 5.08 us -> none  [columns(): return jnp.broadcast_to(part, (1, news * size, LANES))]
    unnamed x30 -> x32, local copies, waits for them, and re-layouts: 0.76 us -> 5.43 us
    pallas_call x5 -> x4, Pallas kernels: 50.4 us -> 46.8 us  [gram_best(): pl.pallas_call(functools.partial(gram_kernel, passes, count, size, first)...]
    pallas_call x2, Pallas kernels: 31.6 us -> 34.9 us  [gather_rows(): pl.pallas_call(functools.partial(gather_kernel, count, size, sections), o...]
  transfers between devices with their start and end apart: 16 -> 16, of which waited for: 4 -> 4; matrix products, arithmetic and copies ran while one was open for 8% -> 3% of each run, Pallas kernels for 38% -> 37%
where the time goes in v4:
time: 178 us; the launch traced here: 176 us
  Pallas kernels  88 us (49%)
  starting transfers between devices  47.4 us (27%)
  waiting for transfers between devices  28.4 us (16%)
  local copies, waits for them, and re-layouts  11.4 us (6%)
    pallas_call x4, Pallas kernels, gram_best(): pl.pallas_call(functools.partial(gram_kernel, passes, count, size, first)...  46.8 us
    pallas_call x2, Pallas kernels, gather_rows(): pl.pallas_call(functools.partial(gather_kernel, count, size, sections), o...  34.9 us
    ppermute x7, starting transfers between devices, go(): return lax.ppermute(chunk, axes, round_pairs(step - 1))  33.4 us
    ppermute x1, waiting for transfers between devices, hosted(): lax.ppermute(arrival_clusters(place_index, slot_cluster), axes, metadata_...  14.9 us
    all_to_all x1, waiting for transfers between devices, hosted(): lax.all_to_all(outbound, axes, split_axis=0, concat_axis=0, tiled=True)  7.51 us
    all_to_all x1, starting transfers between devices, hosted(): lax.all_to_all(outbound, axes, split_axis=0, concat_axis=0, tiled=True)  6.74 us
    ppermute x7, waiting for transfers between devices, go(): return lax.ppermute(chunk, axes, round_pairs(step - 1))  5.97 us
    ppermute x7, starting transfers between devices, swap(): return lax.ppermute(chunk, axes, SIBLINGS)  5.95 us
  transfers between devices with their start and end apart: 16, of which 4 were waited for; matrix products, arithmetic and copies ran while one was open for 3% of the time, Pallas kernels for 37%

profile of v4, /device:TPU:0, one launch (start us, length us, event | category | flops | bytes accessed | tf_op | source)
XLA Modules:
  0.0 176.5 jit_solution(9882542529371711682)
XLA Ops:
  0.0 0.7 constant_dynamic-slice_fusion
  0.7 0.5 slice_bitcast_fusion.refs_0_
  1.2 15.7 %shard_map.64 = (bf16[400,1024]{1,0:T(8,128)(2,1)}, bf16[400,1024]{1,0:T(8,128)(2,1)}) custom-call(s32[2]{0:T(128)} %slice_bitcast_fusion.refs_0_, s32[6400]{0:T(1024)} %refs_1_.3, bf16[6400,1024]{1,0:T(8,128)(2,1)} %refs_2_.3), custom_call_target="tpu_custom_call" | custom-call | tf_op jit(solution)/shard_map/pallas_call | solution.py:139
  16.9 0.7 collective-permute-start.2
  17.6 7.6 %collective-permute-start.1 = (bf16[400,1024]{1,0:T(8,128)(2,1)}, bf16[400,1024]{1,0:T(8,128)(2,1)S(1)}, u32[]{:S(2)}, u32[]{:S(2)}) collective-permute-start(bf16[400,1024]{1,0:T(8,128)(2,1)} %get-tuple-element.20.refs_3_), channel_id=1, source_target_pairs={{24,8},{28,12},{0,16},{4,20},{1,9},{5,13},{25,17},{29,21},{26,10},... | collective-permute-start | bytes 2457608 | tf_op jit(solution)/shard_map/ppermute | solution.py:357
  25.2 0.6 slice_bitcast_fusion.1.refs_0_
  25.8 19.2 %shard_map.65 = (bf16[400,1024]{1,0:T(8,128)(2,1)}, bf16[400,1024]{1,0:T(8,128)(2,1)}, bf16[400,1024]{1,0:T(8,128)(2,1)}) custom-call(s32[3]{0:T(128)} %slice_bitcast_fusion.1.refs_0_, s32[6400]{0:T(1024)} %refs_1_.3, bf16[6400,1024]{1,0:T(8,128)(2,1)} %refs_2_.3, bf16[400,1024]{1,0:T(8,128)(2,1)} %get-tuple-element.20.refs_3_), custom_call_target="tpu_custom_call" | custom-call | flops 24999999488 | tf_op jit(solution)/shard_map/pallas_call | solution.py:139
  45.1 0.8 collective-permute-start.4
  45.9 1.6 collective-permute-start.3
  47.5 1.5 collective-permute-start.7
  49.1 7.1 %collective-permute-start = (bf16[400,1024]{1,0:T(8,128)(2,1)}, bf16[400,1024]{1,0:T(8,128)(2,1)}, u32[]{:S(2)}, u32[]{:S(2)}) collective-permute-start(bf16[400,1024]{1,0:T(8,128)(2,1)} %get-tuple-element.22), channel_id=1, source_target_pairs={{28,8},{24,12},{4,16},{0,20},{5,9},{1,13},{29,17},{25,21},{30,10},... | collective-permute-start | bytes 2457608 | tf_op jit(solution)/shard_map/ppermute | solution.py:357
  56.2 0.1 slice_reduce_fusion
  56.3 0.2 select_reduce_fusion
  56.5 1.3 collective-permute-start.5
  57.8 0.7 fusion.2
  58.5 14.9 %collective-permute-done.5 = s32[6400]{0:T(1024)S(1)} collective-permute-done((s32[6400]{0:T(1024)S(1)}, s32[6400]{0:T(1024)S(1)}, u32[]{:S(2)}, u32[]{:S(2)}) %collective-permute-start.5) | collective-permute-done | bytes 25632 | tf_op jit(solution)/shard_map/ppermute | solution.py:352
  73.4 0.1 reshape.48
  73.5 0.6 gather_fusion
  74.1 0.7 reshape.49.refs_6_.refs_10_.refs_14_.refs_15_.clusters_ref
  74.8 0.7 broadcast_in_dim.23.refs_7_
  75.5 0.2 copy-done.3
  75.7 10.7 %shard_map.66.refs_11_ = f32[1,6400]{1,0:T(1,128)} custom-call(bf16[400,1024]{1,0:T(8,128)(2,1)} %get-tuple-element.28.refs_0_, bf16[400,1024]{1,0:T(8,128)(2,1)} %copy-done.1, bf16[400,1024]{1,0:T(8,128)(2,1)} %copy-done, bf16[400,1024]{1,0:T(8,128)(2,1)} %get-tuple-element.26.refs_3_, bf16[400,1024]{1,0:T(8,128)(2,1)} %collective-permute-done.3.refs_4_, ...), custom_call_target="tpu_custom_call" | custom-call | tf_op jit(solution)/shard_map/pallas_call | solution.py:243
  86.4 0.7 collective-permute-start.9
  87.2 0.7 collective-permute-start.8
  87.9 0.7 collective-permute-start.11
  88.6 9.8 %collective-permute-start.10 = (bf16[400,1024]{1,0:T(8,128)(2,1)}, bf16[400,1024]{1,0:T(8,128)(2,1)S(1)}, u32[]{:S(2)}, u32[]{:S(2)}) collective-permute-start(bf16[400,1024]{1,0:T(8,128)(2,1)} %get-tuple-element.32), channel_id=1, source_target_pairs={{0,8},{4,12},{24,16},{28,20},{25,9},{29,13},{1,17},{5,21},{2,10},{... | collective-permute-start | bytes 2457608 | tf_op jit(solution)/shard_map/ppermute | solution.py:357
  98.5 0.9 copy-done.4
  99.4 0.9 copy-done.5
  100.3 11.4 %shard_map.67.refs_15_ = f32[1,6400]{1,0:T(1,128)} custom-call(bf16[400,1024]{1,0:T(8,128)(2,1)} %get-tuple-element.28.refs_0_, bf16[400,1024]{1,0:T(8,128)(2,1)} %copy-done.1, bf16[400,1024]{1,0:T(8,128)(2,1)} %copy-done, bf16[400,1024]{1,0:T(8,128)(2,1)} %get-tuple-element.26.refs_3_, bf16[400,1024]{1,0:T(8,128)(2,1)} %collective-permute-done.3.refs_4_, ...), custom_call_target="tpu_custom_call" | custom-call | tf_op jit(solution)/shard_map/pallas_call | solution.py:243
  111.7 0.0 copy-start.13
  111.8 0.7 collective-permute-start.13
  112.5 4.3 %collective-permute-done.10.refs_10_ = bf16[400,1024]{1,0:T(8,128)(2,1)S(1)} collective-permute-done((bf16[400,1024]{1,0:T(8,128)(2,1)}, bf16[400,1024]{1,0:T(8,128)(2,1)S(1)}, u32[]{:S(2)}, u32[]{:S(2)}) %collective-permute-start.10) | collective-permute-done | bytes 819232 | tf_op jit(solution)/shard_map/ppermute | solution.py:357
  116.8 0.7 collective-permute-start.12
  117.5 5.9 %collective-permute-start.6 = (bf16[400,1024]{1,0:T(8,128)(2,1)S(1)}, bf16[400,1024]{1,0:T(8,128)(2,1)S(1)}, u32[]{:S(2)}, u32[]{:S(2)}) collective-permute-start(bf16[400,1024]{1,0:T(8,128)(2,1)S(1)} %copy-done.2), channel_id=1, source_target_pairs={{4,8},{0,12},{28,16},{24,20},{29,9},{25,13},{5,17},{1,21},{6,10},{... | collective-permute-start | bytes 2457608 | tf_op jit(solution)/shard_map/ppermute | solution.py:357
  123.5 0.9 copy-done.8
  124.3 0.9 copy-done.9
  125.3 14.5 %shard_map.68.refs_16_ = f32[1,6400]{1,0:T(1,128)} custom-call(bf16[400,1024]{1,0:T(8,128)(2,1)} %get-tuple-element.28.refs_0_, bf16[400,1024]{1,0:T(8,128)(2,1)} %copy-done.1, bf16[400,1024]{1,0:T(8,128)(2,1)} %copy-done, bf16[400,1024]{1,0:T(8,128)(2,1)} %get-tuple-element.26.refs_3_, bf16[400,1024]{1,0:T(8,128)(2,1)} %collective-permute-done.3.refs_4_, ...), custom_call_target="tpu_custom_call" | custom-call | tf_op jit(solution)/shard_map/pallas_call | solution.py:243
  139.8 1.6 collective-permute-done.6.refs_14_.own_ref
  141.4 0.7 collective-permute-start.14
  142.1 1.3 fusion.3.order_ref
  143.4 10.2 %shard_map.69.best_ref = f32[1,6400]{1,0:T(1,128)} custom-call(bf16[400,1024]{1,0:T(8,128)(2,1)} %get-tuple-element.28.refs_0_, bf16[400,1024]{1,0:T(8,128)(2,1)} %copy-done.1, bf16[400,1024]{1,0:T(8,128)(2,1)} %copy-done, bf16[400,1024]{1,0:T(8,128)(2,1)} %get-tuple-element.26.refs_3_, bf16[400,1024]{1,0:T(8,128)(2,1)} %collective-permute-done.3.refs_4_, ...), custom_call_target="tpu_custom_call" | custom-call | tf_op jit(solution)/shard_map/pallas_call | solution.py:243
  153.7 0.9 copy-done.11
  154.6 3.0 %shard_map.70 = f32[32,2,400]{2,1,0:T(2,128)} custom-call(s32[16]{0:T(128)} %fusion.3.order_ref, bf16[400,1024]{1,0:T(8,128)(2,1)} %copy-done.10, bf16[400,1024]{1,0:T(8,128)(2,1)} %copy-done.11, s32[1,6400]{1,0:T(1,128)} %reshape.49.refs_6_.refs_10_.refs_14_.refs_15_.clusters_ref, f32[1,6400]{1,0:T(1,128)} %shard_map.69.best_ref), custom_call_target="tpu_custom_call" | custom-call | tf_op jit(solution)/shard_map/pallas_call | solution.py:289
  157.5 6.7 %all-to-all-start = ((f32[32,2,400]{2,1,0:T(2,128)}), f32[32,2,400]{2,1,0:T(2,128)S(1)}, u32[]{:S(2)}, u32[]{:S(2)}) async-start(f32[32,2,400]{2,1,0:T(2,128)} %shard_map.70), calls=%async_computation | async-start | bytes 262144 | tf_op jit(solution)/shard_map/all_to_all | solution.py:395
  164.3 0.7 reshape.46.index_ref
  165.0 7.5 %all-to-all-done.values_ref = f32[32,2,400]{2,1,0:T(2,128)S(1)} async-done(((f32[32,2,400]{2,1,0:T(2,128)}), f32[32,2,400]{2,1,0:T(2,128)S(1)}, u32[]{:S(2)}, u32[]{:S(2)}) %all-to-all-start) | async-done | bytes 102432 | tf_op jit(solution)/shard_map/all_to_all | solution.py:395
  172.5 0.6 copy-done.12
  173.2 3.3 %shard_map.71 = f32[50,128]{1,0:T(8,128)} custom-call(s32[8,2,400]{2,1,0:T(2,128)} %reshape.46.index_ref, f32[32,2,400]{2,1,0:T(2,128)} %copy-done.12), custom_call_target="tpu_custom_call" | custom-call | tf_op jit(solution)/shard_map/pallas_call | solution.py:329
  (39 shorter events, 0.1 us)
Async XLA Ops:
  16.9 28.2 %collective-permute-start.2 = (bf16[400,1024]{1,0:T(8,128)(2,1)}, bf16[400,1024]{1,0:T(8,128)(2,1)S(1)}, u32[]{:S(2)}, u32[]{:S(2)}) collective-permute-start(bf16[400,1024]{1,0:T(8,128)(2,1)} %get-tuple-element.20.refs_3_), channel_id=1, source_target_pairs={{16,8},{20,12},{8,16},{12,20},{13,9},{9,13},{21,17},{17,21},{18,10... | collective-permute-start | bytes 2457608 | tf_op jit(solution)/shard_map/ppermute | solution.py:357
  17.6 28.3 %collective-permute-start.1 = (bf16[400,1024]{1,0:T(8,128)(2,1)}, bf16[400,1024]{1,0:T(8,128)(2,1)S(1)}, u32[]{:S(2)}, u32[]{:S(2)}) collective-permute-start(bf16[400,1024]{1,0:T(8,128)(2,1)} %get-tuple-element.20.refs_3_), channel_id=1, source_target_pairs={{24,8},{28,12},{0,16},{4,20},{1,9},{5,13},{25,17},{29,21},{26,10},... | collective-permute-start | bytes 2457608 | tf_op jit(solution)/shard_map/ppermute | solution.py:357
  25.8 30.3 %copy-start.15 = (s32[6656]{0:T(1024)S(1)}, s32[6656]{0:T(1024)}, u32[]{:S(2)}) copy-start(s32[6656]{0:T(1024)} %param.10) | copy-start | bytes 79876
  25.8 30.4 %copy-start.14 = (s32[6400]{0:T(1024)S(1)}, s32[6400]{0:T(1024)}, u32[]{:S(2)}) copy-start(s32[6400]{0:T(1024)} %param.9) | copy-start | bytes 76804
  45.0 72.5 %copy-start.2 = (bf16[400,1024]{1,0:T(8,128)(2,1)S(1)}, bf16[400,1024]{1,0:T(8,128)(2,1)}, u32[]{:S(2)}) copy-start(bf16[400,1024]{1,0:T(8,128)(2,1)} %get-tuple-element.28.refs_0_) | copy-start | bytes 2457604
  45.1 30.4 %copy-start = (bf16[400,1024]{1,0:T(8,128)(2,1)}, bf16[400,1024]{1,0:T(8,128)(2,1)S(1)}, u32[]{:S(2)}) copy-start(bf16[400,1024]{1,0:T(8,128)(2,1)S(1)} %collective-permute-done.2.refs_2_) | copy-start | bytes 2457604
  45.1 29.7 %collective-permute-start.4 = (bf16[400,1024]{1,0:T(8,128)(2,1)S(1)}, bf16[400,1024]{1,0:T(8,128)(2,1)S(1)}, u32[]{:S(2)}, u32[]{:S(2)}) collective-permute-start(bf16[400,1024]{1,0:T(8,128)(2,1)S(1)} %collective-permute-done.2.refs_2_), channel_id=1, source_target_pairs={{8,9},{9,8},{10,11},{11,10},{12,13},{13,12},{14,15},{15,14},{16,17... | collective-permute-start | bytes 2457608 | tf_op jit(solution)/shard_map/ppermute | solution.py:360
  45.9 29.6 %copy-start.1 = (bf16[400,1024]{1,0:T(8,128)(2,1)}, bf16[400,1024]{1,0:T(8,128)(2,1)S(1)}, u32[]{:S(2)}) copy-start(bf16[400,1024]{1,0:T(8,128)(2,1)S(1)} %collective-permute-done.1.refs_1_) | copy-start | bytes 2457604
  45.9 28.9 %collective-permute-start.3 = (bf16[400,1024]{1,0:T(8,128)(2,1)S(1)}, bf16[400,1024]{1,0:T(8,128)(2,1)}, u32[]{:S(2)}, u32[]{:S(2)}) collective-permute-start(bf16[400,1024]{1,0:T(8,128)(2,1)S(1)} %collective-permute-done.1.refs_1_), channel_id=1, source_target_pairs={{8,9},{9,8},{10,11},{11,10},{12,13},{13,12},{14,15},{15,14},{16,17... | collective-permute-start | bytes 2457608 | tf_op jit(solution)/shard_map/ppermute | solution.py:360
  47.5 38.9 %collective-permute-start.7 = (bf16[400,1024]{1,0:T(8,128)(2,1)}, bf16[400,1024]{1,0:T(8,128)(2,1)}, u32[]{:S(2)}, u32[]{:S(2)}) collective-permute-start(bf16[400,1024]{1,0:T(8,128)(2,1)} %get-tuple-element.22), channel_id=1, source_target_pairs={{20,8},{16,12},{12,16},{8,20},{17,9},{21,13},{9,17},{13,21},{22,10... | collective-permute-start | bytes 2457608 | tf_op jit(solution)/shard_map/ppermute | solution.py:357
  49.1 38.1 %collective-permute-start = (bf16[400,1024]{1,0:T(8,128)(2,1)}, bf16[400,1024]{1,0:T(8,128)(2,1)}, u32[]{:S(2)}, u32[]{:S(2)}) collective-permute-start(bf16[400,1024]{1,0:T(8,128)(2,1)} %get-tuple-element.22), channel_id=1, source_target_pairs={{28,8},{24,12},{4,16},{0,20},{5,9},{1,13},{29,17},{25,21},{30,10},... | collective-permute-start | bytes 2457608 | tf_op jit(solution)/shard_map/ppermute | solution.py:357
  56.5 16.9 %collective-permute-start.5 = (s32[6400]{0:T(1024)S(1)}, s32[6400]{0:T(1024)S(1)}, u32[]{:S(2)}, u32[]{:S(2)}) collective-permute-start(s32[6400]{0:T(1024)S(1)} %select_reduce_fusion), channel_id=1, source_target_pairs={{0,8},{1,9},{4,12},{5,13},{10,10},{11,11},{14,14},{15,15},{16,16},... | collective-permute-start | bytes 76808 | tf_op jit(solution)/shard_map/ppermute | solution.py:352
  74.8 0.9 copy-start.3
  86.4 12.0 %collective-permute-start.9 = (bf16[400,1024]{1,0:T(8,128)(2,1)}, bf16[400,1024]{1,0:T(8,128)(2,1)S(1)}, u32[]{:S(2)}, u32[]{:S(2)}) collective-permute-start(bf16[400,1024]{1,0:T(8,128)(2,1)} %collective-permute-done.7.refs_7_), channel_id=1, source_target_pairs={{8,9},{9,8},{10,11},{11,10},{12,13},{13,12},{14,15},{15,14},{16,17... | collective-permute-start | bytes 2457608 | tf_op jit(solution)/shard_map/ppermute | solution.py:360
  87.2 11.3 %collective-permute-start.8 = (bf16[400,1024]{1,0:T(8,128)(2,1)}, bf16[400,1024]{1,0:T(8,128)(2,1)S(1)}, u32[]{:S(2)}, u32[]{:S(2)}) collective-permute-start(bf16[400,1024]{1,0:T(8,128)(2,1)} %collective-permute-done.refs_6_), channel_id=1, source_target_pairs={{8,9},{9,8},{10,11},{11,10},{12,13},{13,12},{14,15},{15,14},{16,17... | collective-permute-start | bytes 2457608 | tf_op jit(solution)/shard_map/ppermute | solution.py:360
  87.9 23.9 %collective-permute-start.11 = (bf16[400,1024]{1,0:T(8,128)(2,1)}, bf16[400,1024]{1,0:T(8,128)(2,1)S(1)}, u32[]{:S(2)}, u32[]{:S(2)}) collective-permute-start(bf16[400,1024]{1,0:T(8,128)(2,1)} %get-tuple-element.32), channel_id=1, source_target_pairs={{12,8},{8,12},{20,16},{16,20},{21,9},{17,13},{13,17},{9,21},{14,10... | collective-permute-start | bytes 2457608 | tf_op jit(solution)/shard_map/ppermute | solution.py:357
  88.6 28.2 %collective-permute-start.10 = (bf16[400,1024]{1,0:T(8,128)(2,1)}, bf16[400,1024]{1,0:T(8,128)(2,1)S(1)}, u32[]{:S(2)}, u32[]{:S(2)}) collective-permute-start(bf16[400,1024]{1,0:T(8,128)(2,1)} %get-tuple-element.32), channel_id=1, source_target_pairs={{0,8},{4,12},{24,16},{28,20},{25,9},{29,13},{1,17},{5,21},{2,10},{... | collective-permute-start | bytes 2457608 | tf_op jit(solution)/shard_map/ppermute | solution.py:357
  98.5 1.0 copy-start.4
  99.4 0.9 copy-start.5
  111.7 52.6 %copy-start.13 = (s32[6400]{0:T(1024)S(1)}, s32[6400]{0:T(1024)}, u32[]{:S(2)}) copy-start(s32[6400]{0:T(1024)} %refs_1_.3) | copy-start | bytes 76804
  111.7 11.7 %copy-start.6 = (bf16[400,1024]{1,0:T(8,128)(2,1)}, bf16[400,1024]{1,0:T(8,128)(2,1)S(1)}, u32[]{:S(2)}) copy-start(bf16[400,1024]{1,0:T(8,128)(2,1)S(1)} %collective-permute-done.11.refs_11_) | copy-start | bytes 2457604
  111.8 11.7 %collective-permute-start.13 = (bf16[400,1024]{1,0:T(8,128)(2,1)S(1)}, bf16[400,1024]{1,0:T(8,128)(2,1)S(1)}, u32[]{:S(2)}, u32[]{:S(2)}) collective-permute-start(bf16[400,1024]{1,0:T(8,128)(2,1)S(1)} %collective-permute-done.11.refs_11_), channel_id=1, source_target_pairs={{8,9},{9,8},{10,11},{11,10},{12,13},{13,12},{14,15},{15,14},{16,17... | collective-permute-start | bytes 2457608 | tf_op jit(solution)/shard_map/ppermute | solution.py:360
  116.8 6.6 %copy-start.7 = (bf16[400,1024]{1,0:T(8,128)(2,1)}, bf16[400,1024]{1,0:T(8,128)(2,1)S(1)}, u32[]{:S(2)}) copy-start(bf16[400,1024]{1,0:T(8,128)(2,1)S(1)} %collective-permute-done.10.refs_10_) | copy-start | bytes 2457604
  116.8 6.6 %collective-permute-start.12 = (bf16[400,1024]{1,0:T(8,128)(2,1)S(1)}, bf16[400,1024]{1,0:T(8,128)(2,1)S(1)}, u32[]{:S(2)}, u32[]{:S(2)}) collective-permute-start(bf16[400,1024]{1,0:T(8,128)(2,1)S(1)} %collective-permute-done.10.refs_10_), channel_id=1, source_target_pairs={{8,9},{9,8},{10,11},{11,10},{12,13},{13,12},{14,15},{15,14},{16,17... | collective-permute-start | bytes 2457608 | tf_op jit(solution)/shard_map/ppermute | solution.py:360
  117.5 23.9 %collective-permute-start.6 = (bf16[400,1024]{1,0:T(8,128)(2,1)S(1)}, bf16[400,1024]{1,0:T(8,128)(2,1)S(1)}, u32[]{:S(2)}, u32[]{:S(2)}) collective-permute-start(bf16[400,1024]{1,0:T(8,128)(2,1)S(1)} %copy-done.2), channel_id=1, source_target_pairs={{4,8},{0,12},{28,16},{24,20},{29,9},{25,13},{5,17},{1,21},{6,10},{... | collective-permute-start | bytes 2457608 | tf_op jit(solution)/shard_map/ppermute | solution.py:357
  123.4 0.9 copy-start.8
  124.3 0.9 copy-start.9
  141.4 2.0 %copy-start.10 = (bf16[400,1024]{1,0:T(8,128)(2,1)}, bf16[400,1024]{1,0:T(8,128)(2,1)S(1)}, u32[]{:S(2)}) copy-start(bf16[400,1024]{1,0:T(8,128)(2,1)S(1)} %collective-permute-done.6.refs_14_.own_ref) | copy-start | bytes 2457604
  141.4 12.2 %collective-permute-start.14 = (bf16[400,1024]{1,0:T(8,128)(2,1)S(1)}, bf16[400,1024]{1,0:T(8,128)(2,1)S(1)}, u32[]{:S(2)}, u32[]{:S(2)}) collective-permute-start(bf16[400,1024]{1,0:T(8,128)(2,1)S(1)} %collective-permute-done.6.refs_14_.own_ref), channel_id=1, source_target_pairs={{8,9},{9,8},{10,11},{11,10},{12,13},{13,12},{14,15},{15,14},{16,17... | collective-permute-start | bytes 2457608 | tf_op jit(solution)/shard_map/ppermute | solution.py:360
  153.7 0.9 copy-start.11
  157.5 15.0 %all-to-all-start = ((f32[32,2,400]{2,1,0:T(2,128)}), f32[32,2,400]{2,1,0:T(2,128)S(1)}, u32[]{:S(2)}, u32[]{:S(2)}) async-start(f32[32,2,400]{2,1,0:T(2,128)} %shard_map.70), calls=%async_computation | async-start | bytes 262144 | tf_op jit(solution)/shard_map/all_to_all | solution.py:395
  172.5 0.7 copy-start.12

commit v5 on v4

--- a/solution.py
+++ b/solution.py
@@ -19,10 +19,10 @@
 
 
 CHUNKS = (
-    (0, 0), (1, 0), (2, 0), (0, 1), (1, 1), (2, 1),
-    (3, 0), (4, 0), (3, 1), (4, 1),
-    (5, 0), (6, 0), (5, 1), (6, 1),
-    (7, 0), (7, 1),
+    (0, 0), (1, 0), (2, 0), (0, 1),
+    (1, 1), (2, 1), (3, 0), (4, 0),
+    (3, 1), (4, 1), (5, 0), (6, 0),
+    (5, 1), (6, 1), (7, 0), (7, 1),
 )
 
 
@@ -35,6 +35,7 @@
     owner_at = {host_of(owner): owner for owner in range(8)}
     sends = np.zeros((8, 4, 4), np.int32)
     order = np.zeros((8, 4, 16), np.int32)
+    hosts = np.zeros((8, 4), np.int32)
     for s in range(8):
         for rep in range(4):
             y, core = divmod(rep, 2)
@@ -43,12 +44,13 @@
             targets = [s ^ k for _, k in steps]
             if s in HOSTS:
                 targets.append(s)
+                hosts[s, rep] = owner_at[s, y]
             sends[s, rep] = [owner_at[target, y] for target in targets]
             for side in range(2):
                 half = core ^ side
                 for step, k in enumerate((0,) + ROUNDS[half]):
                     order[s, rep, CHUNKS.index((step, side))] = (s ^ k) * 2 + half
-    return sends, order
+    return sends, order, hosts
 
 
 def round_pairs(step):
@@ -62,15 +64,6 @@
 SIBLINGS = [(host * 4 + rep, host * 4 + (rep ^ 1)) for host in HOSTS for rep in range(4)]
 
 
-def metadata_pairs():
-    pairs = []
-    for owner in range(8):
-        host, y = host_of(owner)
-        for core in range(2):
-            pairs.append((owner * 4 + y * 2 + core, host * 4 + y * 2 + core))
-    return pairs
-
-
 def tie(value, *after):
     return lax.optimization_barrier((value, *after))[0]
 
@@ -89,9 +82,10 @@
     return jnp.sum(jnp.where(hit, heads[:, None], 0), axis=0)
 
 
-def gather_kernel(count, size, sections, *refs):
+def gather_kernel(count, size, group, sections, named, *refs):
     table_ref, index_ref, rows_ref = refs[:3]
-    outs, (raw, wide, picked, sems) = refs[-4 - count : -4], refs[-4:]
+    raw, wide, picked, sems = refs[-4:]
+    outs = refs[-4 - count : -4]
     width = raw.shape[1]
     tiles = width // LANES
     part = raw.shape[0] // sections
@@ -100,6 +94,13 @@
         rows = pl.ds(i * part, part)
         copies.append(pltpu.make_async_copy(rows_ref.at[rows], raw.at[rows], sems.at[i]))
         copies[-1].start()
+    if named:
+        place_ref, slots_ref = refs[3:5]
+        block = place_ref[...] // BLK
+        found = jnp.zeros_like(block)
+        for i in range(slots_ref.shape[0] // BLK):
+            found = jnp.where(block == i, slots_ref[i * BLK], found)
+        refs[-5 - count][...] = found
     step = 80
     for i in range(sections):
         copies[i].wait()
@@ -112,7 +113,6 @@
             return 0
 
         lax.fori_loop(0, part // step, widen, 0)
-    group = 16
     for c in range(count):
         base = table_ref[c]
 
@@ -120,41 +120,50 @@
             for t in range(group):
                 source = pl.multiple_of(index_ref[base + j * group + t] * tiles, tiles)
                 picked[t * tiles : (t + 1) * tiles, :] = wide[pl.ds(source, tiles), :]
-            rows = jnp.concatenate(
-                [picked[pl.ds(t, group, stride=tiles), :] for t in range(tiles)], axis=1
-            )
-            scale = lax.rsqrt(jnp.sum(rows * rows, axis=1, keepdims=True) + 1e-06)
-            outs[c][pl.ds(pl.multiple_of(j * group, group), group), :] = (rows * scale).astype(
-                jnp.bfloat16
-            )
+            for first in range(0, group, 16):
+                rows = jnp.concatenate(
+                    [picked[pl.ds(first * tiles + t, 16, stride=tiles), :] for t in range(tiles)],
+                    axis=1,
+                )
+                scale = lax.rsqrt(jnp.sum(rows * rows, axis=1, keepdims=True) + 1e-06)
+                outs[c][pl.ds(pl.multiple_of(j * group + first, 16), 16), :] = (rows * scale).astype(
+                    jnp.bfloat16
+                )
             return 0
 
         lax.fori_loop(0, size // group, pick, 0)
 
 
-def gather_rows(embeddings, index, starts, size, work=0, after=()):
+def gather_rows(embeddings, index, starts, size, work=0, names=(), after=()):
     documents, width = embeddings.shape
     count = starts.shape[0]
     sections = 8
+    group = 80
+    extra = []
+    if names:
+        places = names[0].reshape(-1, LANES)
+        names = (places, names[1])
+        extra = [jax.ShapeDtypeStruct(places.shape, jnp.int32)]
     return pl.pallas_call(
-        functools.partial(gather_kernel, count, size, sections),
-        out_shape=[jax.ShapeDtypeStruct((size, width), jnp.bfloat16)] * count,
+        functools.partial(gather_kernel, count, size, group, sections, bool(names)),
+        out_shape=extra + [jax.ShapeDtypeStruct((size, width), jnp.bfloat16)] * count,
         in_specs=[
             pl.BlockSpec(memory_space=pltpu.SMEM),
             pl.BlockSpec(memory_space=pltpu.SMEM),
             pl.BlockSpec(memory_space=pl.ANY),
         ]
+        + [pl.BlockSpec(memory_space=pltpu.VMEM), pl.BlockSpec(memory_space=pltpu.SMEM)][: len(names)]
         + [pl.BlockSpec(memory_space=pl.ANY)] * len(after),
-        out_specs=[pl.BlockSpec(memory_space=pltpu.VMEM)] * count,
+        out_specs=[pl.BlockSpec(memory_space=pltpu.VMEM)] * (count + len(extra)),
         scratch_shapes=[
             pltpu.VMEM((documents, width), jnp.bfloat16),
             pltpu.VMEM((documents * width // LANES, LANES), jnp.float32),
-            pltpu.VMEM((16 * width // LANES, LANES), jnp.float32),
+            pltpu.VMEM((group * width // LANES, LANES), jnp.float32),
             pltpu.SemaphoreType.DMA((sections,)),
         ],
         compiler_params=pltpu.CompilerParams(vmem_limit_bytes=VMEM_LIMIT),
         cost_estimate=pl.CostEstimate(flops=work, bytes_accessed=0, transcendentals=0),
-    )(starts, index, embeddings, *after)
+    )(starts, index, embeddings, *names, *after)
 
 
 def best_of_rows(acc, size):
@@ -167,13 +176,14 @@
     return jnp.transpose(jnp.broadcast_to(row, (LANES, wide)))[:size]
 
 
-def gram_kernel(passes, count, size, first, *refs):
-    chunks = refs[:count]
-    cluster_row, before_ref, best_ref, held, acc, sems = refs[count:]
-    limit = count * size
+def gram_kernel(passes, loads, size, limit, *refs):
+    chunks = refs[: len(loads)]
+    cluster_row, before_ref, best_ref, held, acc, sems = refs[-6:]
+    first = range(passes[0][0], passes[0][0] + passes[0][1])
 
     def copy(i):
-        return pltpu.make_async_copy(chunks[i], held.at[pl.ds(i * size, size)], sems.at[i])
+        rows = held.at[pl.ds(i * size, size)]
+        return pltpu.make_async_copy(chunks[loads.index(i)], rows, sems.at[i])
 
     def arrive(i):
         rows = held.at[pl.ds(0, size)]
@@ -181,7 +191,7 @@
 
     for i in first:
         copy(i).start()
-    for i in range(count):
+    for i in loads:
         if i not in first:
             copy(i).start()
     best_ref[...] = before_ref[...]
@@ -224,7 +234,7 @@
 
         lax.fori_loop(0, groups, visit, 0)
         if n == 0:
-            for i in range(count):
+            for i in loads:
                 if i not in first and not i < min(2 * groups, first[0]):
                     arrive(i)
         for t in last:
@@ -233,34 +243,39 @@
         best_ref[:, span] = jnp.maximum(best_ref[:, span], best_of_rows(acc[...], height))
 
 
-def gram_best(chunks, cluster_row, before, passes, first):
-    count = len(chunks)
-    size, width = chunks[0].shape
+def gram_best(chunks, loads, size, cluster_row, before, passes, after=()):
+    width = chunks[0].shape[1]
     total = before.shape[1]
-    held = -(-count * size // BLK) * BLK
+    limit = (max(loads) + 1) * size
+    held = -(-limit // BLK) * BLK
     tall = max(news for _, news, *_ in passes) * size
     padded = -(-tall // LANES) * LANES
     return pl.pallas_call(
-        functools.partial(gram_kernel, passes, count, size, first),
+        functools.partial(gram_kernel, passes, loads, size, limit),
         out_shape=jax.ShapeDtypeStruct((1, total), jnp.float32),
-        in_specs=[pl.BlockSpec(memory_space=pl.ANY)] * count
+        in_specs=[pl.BlockSpec(memory_space=pltpu.HBM)] * len(loads)
+        + [pl.BlockSpec(memory_space=pl.ANY)] * len(after)
         + [pl.BlockSpec(memory_space=pltpu.VMEM)] * 2,
         out_specs=pl.BlockSpec(memory_space=pltpu.VMEM),
         scratch_shapes=[
             pltpu.VMEM((held, width), jnp.bfloat16),
             pltpu.VMEM((padded, LANES), jnp.float32),
-            pltpu.SemaphoreType.DMA((count,)),
+            pltpu.SemaphoreType.DMA((max(loads) + 1,)),
         ],
         compiler_params=pltpu.CompilerParams(vmem_limit_bytes=VMEM_LIMIT),
         cost_estimate=pl.CostEstimate(flops=0, bytes_accessed=0, transcendentals=0),
-    )(*chunks, cluster_row, before)
-
-
-def one_pass(chunk, news, count, size):
+    )(*chunks, *after, cluster_row, before)
+
+
+def new_pass(chunk, news, count, size):
     group = 3
     groups = chunk * size // (group * BLK)
     tiles = -(-count * size // BLK)
-    return ((chunk, news, groups, group, False, tuple(range(groups * group, tiles))),)
+    return (chunk, news, groups, group, False, tuple(range(groups * group, tiles)))
+
+
+def late_pass(chunk, news, low, high, size):
+    return (chunk, news, 0, 1, True, tuple(range(low * size // BLK, -(-high * size // BLK))))
 
 
 def finish_kernel(size, order_ref, own_ref, other_ref, clusters_ref, best_ref, out_ref, acc):
@@ -344,14 +359,17 @@
     size = share // 2
     s, rep = lax.axis_index("shard"), lax.axis_index("rep")
     axes = ("shard", "rep")
-    sends, order = plan()
+    sends, order, hosts = plan()
     halves = np.arange(4)[:, None] % 2 ^ np.array([0, 0, 0, 0, 1])
     starts = sends[:, :, [0, 1, 2, 3, 3]] * share + (halves * size).astype(np.int32)
     starts = jnp.asarray(starts)[s, rep]
     order = jnp.asarray(order)[s, rep]
-    clusters = lax.ppermute(arrival_clusters(place_index, slot_cluster), axes, metadata_pairs())
+    clusters, early = gather_rows(
+        embeddings, send_index, starts[:1], size, names=(place_index, slot_cluster)
+    )
+    clusters = lax.all_gather(clusters, "shard")[jnp.asarray(hosts)[s, rep]]
     clusters = clusters.reshape(16, size)[order]
-    early = gather_rows(embeddings, send_index, starts[:2], size)
+    index = send_index.reshape(8, 2, size)
 
     def go(step, chunk):
         return lax.ppermute(chunk, axes, round_pairs(step - 1))
@@ -360,37 +378,33 @@
         return lax.ppermute(chunk, axes, SIBLINGS)
 
     own, other = [None] * 8, [None] * 8
-    for step in (1, 2, 3, 4):
-        own[step] = go(step, early[(step - 1) // 2])
-    late = gather_rows(embeddings, send_index, starts[2:], size, LONG, (early[0],))
-    own[0], other[0] = late[1], late[2]
+    own[1], own[2] = go(1, early), go(2, early)
+    late = gather_rows(embeddings, send_index, starts[1:], size, LONG, after=(early,))
+    own[0], other[0] = late[2:]
+    own[3], own[4] = go(3, late[0]), go(4, late[0])
     flat = clusters.reshape(1, 16 * size)
 
-    def score(best, chunk, news, count):
-        return gram_best(
-            [(own, other)[side][r] for r, side in CHUNKS[:count]],
-            flat,
-            best,
-            one_pass(chunk, news, count, size),
-            tuple(range(chunk, chunk + news)),
-        )
-
+    def score(best, loads, passes, after=()):
+        chunks = [(own, other)[side][r] for r, side in [CHUNKS[i] for i in loads]]
+        return gram_best(chunks, tuple(loads), size, flat, best, passes, after)
+
+    own[1], own[2] = tie(own[1], late[0]), tie(own[2], late[0])
+    own[5] = go(5, tie(late[1], own[1]))
+    own[6] = go(6, tie(late[1], own[2]))
     best = jnp.full((1, 16 * size), -1.0, jnp.float32)
-    own[1], own[2] = tie(own[1], late[0]), tie(own[2], late[0])
-    other[1], other[2] = swap(own[1]), swap(own[2])
-    own[5] = go(5, tie(late[0], own[1]))
-    own[6] = go(6, tie(late[0], own[2]))
-    best = score(best, 0, 3, 6)
+    best = score(best, range(4), (new_pass(0, 3, 4, size),), (order, index))
+    other[1], other[2] = swap(tie(own[1], best)), swap(tie(own[2], best))
     own[3], own[4] = tie(own[3], best), tie(own[4], best)
-    other[3], other[4] = swap(own[3]), swap(own[4])
-    own[7] = go(7, tie(late[1], own[3]))
-    best = score(best, 6, 2, 10)
+    own[7] = go(7, tie(late[2], own[3]))
+    best = score(best, range(8), (new_pass(6, 2, 8, size), late_pass(1, 2, 4, 6, size)))
+    other[3], other[4] = swap(tie(own[3], best)), swap(tie(own[4], best))
     own[5], own[6] = tie(own[5], best), tie(own[6], best)
     other[5], other[6] = swap(own[5]), swap(own[6])
-    best = score(best, 10, 2, 14)
+    best = score(best, range(12), (new_pass(10, 2, 12, size), late_pass(6, 2, 8, 10, size)))
+    best = score(best, range(10, 14), (late_pass(10, 2, 12, 14, size),))
     own[7] = tie(own[7], best)
     other[7] = swap(own[7])
-    best = score(best, 14, 1, 15)
+    best = score(best, range(15), (new_pass(14, 1, 15, size),))
     outbound = finish(order, own[7], other[7], flat, best)
     returned = lax.all_to_all(outbound, axes, split_axis=0, concat_axis=0, tiled=True)
     sources = []
@@ -398,7 +412,7 @@
         host, y = host_of(owner)
         for half in range(2):
             sources.append(tuple((host * 4 + y * 2 + core, half) for core in range(2)))
-    return settle(send_index.reshape(8, 2, size), returned, tuple(sources), documents)
+    return settle(index, returned, tuple(sources), documents)
 
 
 def gathered(embeddings, send_index, place_index, slot_cluster):
@@ -420,9 +434,8 @@
     best = jnp.full((1, documents), -1.0, jnp.float32)
     tiles = tuple(range(documents // BLK))
     passes = ((0, news, 0, 1, True, tiles),)
-    best = gram_best(
-        [arrived[i] for i in range(parts)], clusters.reshape(1, -1), best, passes, tuple(range(news))
-    )
+    chunks = [arrived[i] for i in range(parts)]
+    best = gram_best(chunks, tuple(range(parts)), size, clusters.reshape(1, -1), best, passes)
     best = lax.all_gather(best[0, : news * size], "rep", axis=0, tiled=True)
     returned = lax.all_to_all(
         best.reshape(owners, share), "shard", split_axis=0, concat_axis=0, tiled=True

time: 178 us -> 204 us (1.15)
  blocking collectives: 0 us -> 61.1 us
  waiting for transfers between devices: 28.4 us -> 4.36 us
  starting transfers between devices: 47.4 us -> 36.8 us
  Pallas kernels: 88 us -> 83.7 us
  local copies, waits for them, and re-layouts: 11.4 us -> 14.2 us
    all_gather x0 -> x1, blocking collectives: none -> 47.8 us  [hosted(): clusters = lax.all_gather(clusters, 'shard')[jnp.asarray(hosts)[s, rep]]]
    ppermute x1 -> x0, waiting for transfers between devices: 14.9 us -> none  [hosted(): lax.ppermute(arrival_clusters(place_index, slot_cluster), axes, metadata_...]
    all_to_all x0 -> x1, blocking collectives: none -> 13.3 us  [hosted(): lax.all_to_all(outbound, axes, split_axis=0, concat_axis=0, tiled=True)]
    all_to_all x1 -> x0, waiting for transfers between devices: 7.51 us -> none  [hosted(): lax.all_to_all(outbound, axes, split_axis=0, concat_axis=0, tiled=True)]
    all_to_all x1 -> x0, starting transfers between devices: 6.74 us -> none  [hosted(): lax.all_to_all(outbound, axes, split_axis=0, concat_axis=0, tiled=True)]
    pallas_call x6 -> x7, Pallas kernels: 81.7 us -> 77.4 us  [the longest x5 50.9 us: gram_best(): pl.pallas_call(functools.partial(gram_kernel, passes, loads, size, limit)...]
    unnamed x32 -> x34, local copies, waits for them, and re-layouts: 5.43 us -> 7.12 us
  transfers between devices with their start and end apart: 16 -> 14, of which waited for: 4 -> 1; matrix products, arithmetic and copies ran while one was open for 3% -> 3% of each run, Pallas kernels for 37% -> 32%
where the time goes in v5:
time: 204 us; the launch traced here: 203 us
  Pallas kernels  83.7 us (41%)
  blocking collectives  61.1 us (30%)
  starting transfers between devices  36.8 us (18%)
  local copies, waits for them, and re-layouts  14.2 us (7%)
  waiting for transfers between devices  4.36 us (2%)
  between operations  2.29 us (1%)
    pallas_call x5, Pallas kernels, gram_best(): pl.pallas_call(functools.partial(gram_kernel, passes, loads, size, limit)...  50.9 us
    all_gather x1, blocking collectives, hosted(): clusters = lax.all_gather(clusters, 'shard')[jnp.asarray(hosts)[s, rep]]  47.8 us
    ppermute x7, starting transfers between devices, go(): return lax.ppermute(chunk, axes, round_pairs(step - 1))  31.6 us
    pallas_call x2, Pallas kernels, gather_rows(): pl.pallas_call(functools.partial(gather_kernel, count, size, group, secti...  26.4 us
    all_to_all x1, blocking collectives, hosted(): lax.all_to_all(outbound, axes, split_axis=0, concat_axis=0, tiled=True)  13.3 us
    unnamed x34, local copies, waits for them, and re-layouts  7.12 us
    ppermute x7, starting transfers between devices, swap(): return lax.ppermute(chunk, axes, SIBLINGS)  5.2 us
    ppermute x7, waiting for transfers between devices, go(): return lax.ppermute(chunk, axes, round_pairs(step - 1))  4.35 us
  transfers between devices with their start and end apart: 14, of which 1 were waited for; matrix products, arithmetic and copies ran while one was open for 3% of the time, Pallas kernels for 32%

profile of v5, /device:TPU:0, one launch (start us, length us, event | category | flops | bytes accessed | tf_op | source)
XLA Modules:
  0.0 203.1 jit_solution(9029503485360871095)
XLA Ops:
  0.0 1.2 constant_dynamic-slice_fusion.1
  1.2 11.8 %shard_map.73 = (s32[50,128]{1,0:T(8,128)}, bf16[400,1024]{1,0:T(8,128)(2,1)}) custom-call(s32[1]{0:T(128)} %bitcast.16, s32[6400]{0:T(1024)} %refs_1_.3, bf16[6400,1024]{1,0:T(8,128)(2,1)} %refs_2_.3, s32[50,128]{1,0:T(8,128)} %bitcast.14, s32[6656]{0:T(1024)} %refs_4_.1), custom_call_target="tpu_custom_call" | custom-call | tf_op jit(solution)/shard_map/pallas_call | solution.py:147
  13.0 0.7 collective-permute-start.2
  13.7 7.6 %collective-permute-start.1 = (bf16[400,1024]{1,0:T(8,128)(2,1)}, bf16[400,1024]{1,0:T(8,128)(2,1)S(1)}, u32[]{:S(2)}, u32[]{:S(2)}) collective-permute-start(bf16[400,1024]{1,0:T(8,128)(2,1)} %get-tuple-element.25.refs_3_), channel_id=1, source_target_pairs={{24,8},{28,12},{0,16},{4,20},{1,9},{5,13},{25,17},{29,21},{26,10},... | collective-permute-start | bytes 2457608 | tf_op jit(solution)/shard_map/ppermute | solution.py:375
  21.3 0.6 slice_bitcast_fusion.refs_0_
  21.9 14.7 %shard_map.74 = (bf16[400,1024]{1,0:T(8,128)(2,1)}, bf16[400,1024]{1,0:T(8,128)(2,1)}, bf16[400,1024]{1,0:T(8,128)(2,1)}, bf16[400,1024]{1,0:T(8,128)(2,1)}) custom-call(s32[4]{0:T(128)} %slice_bitcast_fusion.refs_0_, s32[6400]{0:T(1024)} %refs_1_.3, bf16[6400,1024]{1,0:T(8,128)(2,1)} %refs_2_.3, bf16[400,1024]{1,0:T(8,128)(2,1)} %get-tuple-element.25.refs_3_), custom_call_target="tpu_custom_call" | custom-call | flops 24999999488 | tf_op jit(solution)/shard_map/pallas_call | solution.py:147
  36.6 0.7 collective-permute-start.7
  37.3 5.0 %collective-permute-start = (bf16[400,1024]{1,0:T(8,128)(2,1)}, bf16[400,1024]{1,0:T(8,128)(2,1)S(1)}, u32[]{:S(2)}, u32[]{:S(2)}) collective-permute-start(bf16[400,1024]{1,0:T(8,128)(2,1)} %get-tuple-element.27), channel_id=1, source_target_pairs={{28,8},{24,12},{4,16},{0,20},{5,9},{1,13},{29,17},{25,21},{30,10},... | collective-permute-start | bytes 2457608 | tf_op jit(solution)/shard_map/ppermute | solution.py:375
  42.3 1.3 dynamic_slice.14
  44.9 0.7 reshape.42.refs_5_.index_ref
  46.2 47.8 %all-gather.1 = s32[8,50,128]{2,1,0:T(8,128)S(1)} all-gather(s32[1,50,128]{2,1,0:T(8,128)S(1)} %bitcast.15), channel_id=2, replica_groups=mesh['shard'=8,'rep'=4] {'shard'}, dimensions={0}, use_global_device_ids=true | all-gather | bytes 230400 | tf_op jit(solution)/shard_map/all_gather | solution.py:370
  94.0 0.1 reshape_squeeze.3
  94.1 0.7 fusion
  94.8 0.6 gather_fusion
  95.4 0.7 reshape.44.refs_6_.refs_8_.refs_12_.refs_4_.refs_15_.clusters_ref
  96.1 1.2 fusion.1.refs_4_.order_ref
  97.3 0.0 collective-permute-done.2.refs_2_
  97.3 0.0 collective-permute-done.1.refs_1_
  97.3 0.7 broadcast_in_dim.4.refs_7_
  98.0 0.2 copy-done
  98.2 0.3 copy-done.1
  98.5 8.3 %shard_map.75.refs_9_ = f32[1,6400]{1,0:T(1,128)} custom-call(bf16[400,1024]{1,0:T(8,128)(2,1)} %get-tuple-element.33.refs_0_, bf16[400,1024]{1,0:T(8,128)(2,1)} %copy-done.1, bf16[400,1024]{1,0:T(8,128)(2,1)} %copy-done, bf16[400,1024]{1,0:T(8,128)(2,1)} %get-tuple-element.30.refs_3_, s32[16]{0:T(128)} %fusion.1.refs_4_.order_ref, ...), custom_call_target="tpu_custom_call" | custom-call | tf_op jit(solution)/shard_map/pallas_call | solution.py:253
  106.8 0.7 collective-permute-start.5
  107.5 0.7 collective-permute-start.6
  108.3 0.7 collective-permute-start.8
  109.0 7.8 %collective-permute-start.4 = (bf16[400,1024]{1,0:T(8,128)(2,1)}, bf16[400,1024]{1,0:T(8,128)(2,1)S(1)}, u32[]{:S(2)}, u32[]{:S(2)}) collective-permute-start(bf16[400,1024]{1,0:T(8,128)(2,1)} %get-tuple-element.40), channel_id=1, source_target_pairs={{0,8},{4,12},{24,16},{28,20},{25,9},{29,13},{1,17},{5,21},{2,10},{... | collective-permute-start | bytes 2457608 | tf_op jit(solution)/shard_map/ppermute | solution.py:375
  116.8 0.8 copy-done.5
  117.7 0.3 copy-done.6
  118.0 0.9 copy-done.7
  118.9 11.9 %shard_map.76.refs_13_ = f32[1,6400]{1,0:T(1,128)} custom-call(bf16[400,1024]{1,0:T(8,128)(2,1)} %get-tuple-element.33.refs_0_, bf16[400,1024]{1,0:T(8,128)(2,1)} %copy-done.1, bf16[400,1024]{1,0:T(8,128)(2,1)} %copy-done, bf16[400,1024]{1,0:T(8,128)(2,1)} %get-tuple-element.30.refs_3_, bf16[400,1024]{1,0:T(8,128)(2,1)} %copy-done.6, ...), custom_call_target="tpu_custom_call" | custom-call | tf_op jit(solution)/shard_map/pallas_call | solution.py:253
  130.8 4.3 %collective-permute-done.4.refs_10_.refs_0_ = bf16[400,1024]{1,0:T(8,128)(2,1)S(1)} collective-permute-done((bf16[400,1024]{1,0:T(8,128)(2,1)}, bf16[400,1024]{1,0:T(8,128)(2,1)S(1)}, u32[]{:S(2)}, u32[]{:S(2)}) %collective-permute-start.4) | collective-permute-done | bytes 819232 | tf_op jit(solution)/shard_map/ppermute | solution.py:375
  135.2 0.7 collective-permute-start.11
  135.9 0.7 collective-permute-start.12
  136.6 0.7 collective-permute-start.9
  137.3 0.7 collective-permute-start.10
  138.0 9.1 %collective-permute-start.3 = (bf16[400,1024]{1,0:T(8,128)(2,1)}, bf16[400,1024]{1,0:T(8,128)(2,1)S(1)}, u32[]{:S(2)}, u32[]{:S(2)}) collective-permute-start(bf16[400,1024]{1,0:T(8,128)(2,1)} %get-tuple-element.33.refs_0_), channel_id=1, source_target_pairs={{4,8},{0,12},{28,16},{24,20},{29,9},{25,13},{5,17},{1,21},{6,10},{... | collective-permute-start | bytes 2457608 | tf_op jit(solution)/shard_map/ppermute | solution.py:375
  147.2 0.9 copy-done.8
  148.1 0.9 copy-done.9
  149.0 15.0 %shard_map.77.refs_5_ = f32[1,6400]{1,0:T(1,128)} custom-call(bf16[400,1024]{1,0:T(8,128)(2,1)} %get-tuple-element.33.refs_0_, bf16[400,1024]{1,0:T(8,128)(2,1)} %copy-done.1, bf16[400,1024]{1,0:T(8,128)(2,1)} %copy-done, bf16[400,1024]{1,0:T(8,128)(2,1)} %get-tuple-element.30.refs_3_, bf16[400,1024]{1,0:T(8,128)(2,1)} %copy-done.6, ...), custom_call_target="tpu_custom_call" | custom-call | tf_op jit(solution)/shard_map/pallas_call | solution.py:253
  164.1 0.9 copy-done.11
  165.0 0.9 copy-done.12
  165.9 5.5 %shard_map.78.refs_16_ = f32[1,6400]{1,0:T(1,128)} custom-call(bf16[400,1024]{1,0:T(8,128)(2,1)} %copy-done.3, bf16[400,1024]{1,0:T(8,128)(2,1)} %copy-done.2, bf16[400,1024]{1,0:T(8,128)(2,1)} %copy-done.11, bf16[400,1024]{1,0:T(8,128)(2,1)} %copy-done.12, s32[1,6400]{1,0:T(1,128)} %reshape.44.refs_6_.refs_8_.refs_12_.refs_4_.refs_15_.clusters_ref, ...), custom_call_target="tpu_custom_call" | custom-call | tf_op jit(solution)/shard_map/pallas_call | solution.py:253
  171.4 0.9 collective-permute-start.13
  172.4 10.3 %shard_map.79.best_ref = f32[1,6400]{1,0:T(1,128)} custom-call(bf16[400,1024]{1,0:T(8,128)(2,1)} %get-tuple-element.33.refs_0_, bf16[400,1024]{1,0:T(8,128)(2,1)} %copy-done.1, bf16[400,1024]{1,0:T(8,128)(2,1)} %copy-done, bf16[400,1024]{1,0:T(8,128)(2,1)} %get-tuple-element.30.refs_3_, bf16[400,1024]{1,0:T(8,128)(2,1)} %copy-done.6, ...), custom_call_target="tpu_custom_call" | custom-call | tf_op jit(solution)/shard_map/pallas_call | solution.py:253
  182.6 0.9 copy-done.13
  183.5 3.0 %shard_map.80 = f32[32,2,400]{2,1,0:T(2,128)} custom-call(s32[16]{0:T(128)} %fusion.1.refs_4_.order_ref, bf16[400,1024]{1,0:T(8,128)(2,1)} %copy-done.10, bf16[400,1024]{1,0:T(8,128)(2,1)} %copy-done.13, s32[1,6400]{1,0:T(1,128)} %reshape.44.refs_6_.refs_8_.refs_12_.refs_4_.refs_15_.clusters_ref, f32[1,6400]{1,0:T(1,128)} %shard_map.79.best_ref), custom_call_target="tpu_custom_call" | custom-call | tf_op jit(solution)/shard_map/pallas_call | solution.py:304
  186.6 13.3 %all_to_all.5.values_ref = f32[32,2,400]{2,1,0:T(2,128)} all-to-all(f32[32,2,400]{2,1,0:T(2,128)} %shard_map.80), channel_id=1, replica_groups=mesh['shard'=8,'rep'=4] {'shard','rep'}, dimensions={0} | all-to-all | bytes 204800 | tf_op jit(solution)/shard_map/all_to_all | solution.py:409
  199.8 3.3 %shard_map.81 = f32[50,128]{1,0:T(8,128)} custom-call(s32[8,2,400]{2,1,0:T(2,128)} %reshape.42.refs_5_.index_ref, f32[32,2,400]{2,1,0:T(2,128)} %all_to_all.5.values_ref), custom_call_target="tpu_custom_call" | custom-call | tf_op jit(solution)/shard_map/pallas_call | solution.py:344
  (37 shorter events, 0.1 us)
Async XLA Ops:
  1.2 20.1 %copy-start.16 = (s32[1,1,5]{2,1,0:T(1,128)S(1)}, s32[1,1,5]{2,1,0:T(1,128)}, u32[]{:S(2)}) copy-start(s32[1,1,5]{2,1,0:T(1,128)} %constant_dynamic-slice_fusion.1) | copy-start | bytes 64
  13.0 84.4 %collective-permute-start.2 = (bf16[400,1024]{1,0:T(8,128)(2,1)}, bf16[400,1024]{1,0:T(8,128)(2,1)S(1)}, u32[]{:S(2)}, u32[]{:S(2)}) collective-permute-start(bf16[400,1024]{1,0:T(8,128)(2,1)} %get-tuple-element.25.refs_3_), channel_id=1, source_target_pairs={{16,8},{20,12},{8,16},{12,20},{13,9},{9,13},{21,17},{17,21},{18,10... | collective-permute-start | bytes 2457608 | tf_op jit(solution)/shard_map/ppermute | solution.py:375
  13.7 83.6 %collective-permute-start.1 = (bf16[400,1024]{1,0:T(8,128)(2,1)}, bf16[400,1024]{1,0:T(8,128)(2,1)S(1)}, u32[]{:S(2)}, u32[]{:S(2)}) collective-permute-start(bf16[400,1024]{1,0:T(8,128)(2,1)} %get-tuple-element.25.refs_3_), channel_id=1, source_target_pairs={{24,8},{28,12},{0,16},{4,20},{1,9},{5,13},{25,17},{29,21},{26,10},... | collective-permute-start | bytes 2457608 | tf_op jit(solution)/shard_map/ppermute | solution.py:375
  21.9 22.9 %copy-start.14 = (s32[6400]{0:T(1024)S(1)}, s32[6400]{0:T(1024)}, u32[]{:S(2)}) copy-start(s32[6400]{0:T(1024)} %refs_1_.3) | copy-start | bytes 76804
  21.9 24.3 %copy-start.15 = (s32[50,128]{1,0:T(8,128)S(1)}, s32[50,128]{1,0:T(8,128)}, u32[]{:S(2)}) copy-start(s32[50,128]{1,0:T(8,128)} %get-tuple-element.31) | copy-start | bytes 76804
  36.6 72.4 %collective-permute-start.7 = (bf16[400,1024]{1,0:T(8,128)(2,1)}, bf16[400,1024]{1,0:T(8,128)(2,1)S(1)}, u32[]{:S(2)}, u32[]{:S(2)}) collective-permute-start(bf16[400,1024]{1,0:T(8,128)(2,1)} %get-tuple-element.27), channel_id=1, source_target_pairs={{20,8},{16,12},{12,16},{8,20},{17,9},{21,13},{9,17},{13,21},{22,10... | collective-permute-start | bytes 2457608 | tf_op jit(solution)/shard_map/ppermute | solution.py:375
  37.3 79.4 %collective-permute-start = (bf16[400,1024]{1,0:T(8,128)(2,1)}, bf16[400,1024]{1,0:T(8,128)(2,1)S(1)}, u32[]{:S(2)}, u32[]{:S(2)}) collective-permute-start(bf16[400,1024]{1,0:T(8,128)(2,1)} %get-tuple-element.27), channel_id=1, source_target_pairs={{28,8},{24,12},{4,16},{0,20},{5,9},{1,13},{29,17},{25,21},{30,10},... | collective-permute-start | bytes 2457608 | tf_op jit(solution)/shard_map/ppermute | solution.py:375
  97.3 0.9 copy-start
  97.3 1.2 copy-start.1
  106.8 10.0 %collective-permute-start.5 = (bf16[400,1024]{1,0:T(8,128)(2,1)}, bf16[400,1024]{1,0:T(8,128)(2,1)S(1)}, u32[]{:S(2)}, u32[]{:S(2)}) collective-permute-start(bf16[400,1024]{1,0:T(8,128)(2,1)} %copy-done.1), channel_id=1, source_target_pairs={{8,9},{9,8},{10,11},{11,10},{12,13},{13,12},{14,15},{15,14},{16,17... | collective-permute-start | bytes 2457608 | tf_op jit(solution)/shard_map/ppermute | solution.py:378
  107.5 9.3 %collective-permute-start.6 = (bf16[400,1024]{1,0:T(8,128)(2,1)}, bf16[400,1024]{1,0:T(8,128)(2,1)S(1)}, u32[]{:S(2)}, u32[]{:S(2)}) collective-permute-start(bf16[400,1024]{1,0:T(8,128)(2,1)} %copy-done), channel_id=1, source_target_pairs={{8,9},{9,8},{10,11},{11,10},{12,13},{13,12},{14,15},{15,14},{16,17... | collective-permute-start | bytes 2457608 | tf_op jit(solution)/shard_map/ppermute | solution.py:378
  108.3 22.5 %collective-permute-start.8 = (bf16[400,1024]{1,0:T(8,128)(2,1)}, bf16[400,1024]{1,0:T(8,128)(2,1)S(1)}, u32[]{:S(2)}, u32[]{:S(2)}) collective-permute-start(bf16[400,1024]{1,0:T(8,128)(2,1)} %get-tuple-element.40), channel_id=1, source_target_pairs={{12,8},{8,12},{20,16},{16,20},{21,9},{17,13},{13,17},{9,21},{14,10... | collective-permute-start | bytes 2457608 | tf_op jit(solution)/shard_map/ppermute | solution.py:375
  109.0 7.9 %copy-start.4 = (bf16[400,1024]{1,0:T(8,128)(2,1)}, bf16[400,1024]{1,0:T(8,128)(2,1)S(1)}, u32[]{:S(2)}) copy-start(bf16[400,1024]{1,0:T(8,128)(2,1)S(1)} %collective-permute-done.7.refs_7_) | copy-start | bytes 2457604
  109.0 26.2 %collective-permute-start.4 = (bf16[400,1024]{1,0:T(8,128)(2,1)}, bf16[400,1024]{1,0:T(8,128)(2,1)S(1)}, u32[]{:S(2)}, u32[]{:S(2)}) collective-permute-start(bf16[400,1024]{1,0:T(8,128)(2,1)} %get-tuple-element.40), channel_id=1, source_target_pairs={{0,8},{4,12},{24,16},{28,20},{25,9},{29,13},{1,17},{5,21},{2,10},{... | collective-permute-start | bytes 2457608 | tf_op jit(solution)/shard_map/ppermute | solution.py:375
  116.8 0.9 copy-start.5
  116.8 1.2 copy-start.6
  118.0 0.9 copy-start.7
  130.8 16.4 %copy-start.2 = (bf16[400,1024]{1,0:T(8,128)(2,1)}, bf16[400,1024]{1,0:T(8,128)(2,1)S(1)}, u32[]{:S(2)}) copy-start(bf16[400,1024]{1,0:T(8,128)(2,1)S(1)} %collective-permute-done.8.refs_11_.refs_1_) | copy-start | bytes 2457604
  135.2 12.0 %copy-start.3 = (bf16[400,1024]{1,0:T(8,128)(2,1)}, bf16[400,1024]{1,0:T(8,128)(2,1)S(1)}, u32[]{:S(2)}) copy-start(bf16[400,1024]{1,0:T(8,128)(2,1)S(1)} %collective-permute-done.4.refs_10_.refs_0_) | copy-start | bytes 2457604
  135.2 12.0 %collective-permute-start.11 = (bf16[400,1024]{1,0:T(8,128)(2,1)}, bf16[400,1024]{1,0:T(8,128)(2,1)S(1)}, u32[]{:S(2)}, u32[]{:S(2)}) collective-permute-start(bf16[400,1024]{1,0:T(8,128)(2,1)} %copy-done.5), channel_id=1, source_target_pairs={{8,9},{9,8},{10,11},{11,10},{12,13},{13,12},{14,15},{15,14},{16,17... | collective-permute-start | bytes 2457608 | tf_op jit(solution)/shard_map/ppermute | solution.py:378
  135.9 11.3 %collective-permute-start.12 = (bf16[400,1024]{1,0:T(8,128)(2,1)}, bf16[400,1024]{1,0:T(8,128)(2,1)S(1)}, u32[]{:S(2)}, u32[]{:S(2)}) collective-permute-start(bf16[400,1024]{1,0:T(8,128)(2,1)} %copy-done.4), channel_id=1, source_target_pairs={{8,9},{9,8},{10,11},{11,10},{12,13},{13,12},{14,15},{15,14},{16,17... | collective-permute-start | bytes 2457608 | tf_op jit(solution)/shard_map/ppermute | solution.py:378
  136.6 27.5 %collective-permute-start.9 = (bf16[400,1024]{1,0:T(8,128)(2,1)S(1)}, bf16[400,1024]{1,0:T(8,128)(2,1)S(1)}, u32[]{:S(2)}, u32[]{:S(2)}) collective-permute-start(bf16[400,1024]{1,0:T(8,128)(2,1)S(1)} %collective-permute-done.4.refs_10_.refs_0_), channel_id=1, source_target_pairs={{8,9},{9,8},{10,11},{11,10},{12,13},{13,12},{14,15},{15,14},{16,17... | collective-permute-start | bytes 2457608 | tf_op jit(solution)/shard_map/ppermute | solution.py:378
  137.3 26.8 %collective-permute-start.10 = (bf16[400,1024]{1,0:T(8,128)(2,1)S(1)}, bf16[400,1024]{1,0:T(8,128)(2,1)S(1)}, u32[]{:S(2)}, u32[]{:S(2)}) collective-permute-start(bf16[400,1024]{1,0:T(8,128)(2,1)S(1)} %collective-permute-done.8.refs_11_.refs_1_), channel_id=1, source_target_pairs={{8,9},{9,8},{10,11},{11,10},{12,13},{13,12},{14,15},{15,14},{16,17... | collective-permute-start | bytes 2457608 | tf_op jit(solution)/shard_map/ppermute | solution.py:378
  138.0 33.4 %collective-permute-start.3 = (bf16[400,1024]{1,0:T(8,128)(2,1)}, bf16[400,1024]{1,0:T(8,128)(2,1)S(1)}, u32[]{:S(2)}, u32[]{:S(2)}) collective-permute-start(bf16[400,1024]{1,0:T(8,128)(2,1)} %get-tuple-element.33.refs_0_), channel_id=1, source_target_pairs={{4,8},{0,12},{28,16},{24,20},{29,9},{25,13},{5,17},{1,21},{6,10},{... | collective-permute-start | bytes 2457608 | tf_op jit(solution)/shard_map/ppermute | solution.py:375
  147.2 1.0 copy-start.8
  148.1 0.9 copy-start.9
  164.1 0.9 copy-start.11
  165.0 0.9 copy-start.12
  171.4 1.0 copy-start.10
  171.4 11.2 %collective-permute-start.13 = (bf16[400,1024]{1,0:T(8,128)(2,1)S(1)}, bf16[400,1024]{1,0:T(8,128)(2,1)S(1)}, u32[]{:S(2)}, u32[]{:S(2)}) collective-permute-start(bf16[400,1024]{1,0:T(8,128)(2,1)S(1)} %collective-permute-done.3.refs_14_.own_ref), channel_id=1, source_target_pairs={{8,9},{9,8},{10,11},{11,10},{12,13},{13,12},{14,15},{15,14},{16,17... | collective-permute-start | bytes 2457608 | tf_op jit(solution)/shard_map/ppermute | solution.py:378
  182.6 0.9 copy-start.13

commit v6 on v5

--- a/solution.py
+++ b/solution.py
@@ -11,7 +11,7 @@
 BLK = 256
 LANES = 128
 NT = (((1,), (1,)), ((), ()))
-VMEM_LIMIT = 56 * 1024 * 1024
+MIB = 1024 * 1024
 LONG = 25_000_000_000
 
 HOSTS = (2, 3, 4, 5)
@@ -35,7 +35,6 @@
     owner_at = {host_of(owner): owner for owner in range(8)}
     sends = np.zeros((8, 4, 4), np.int32)
     order = np.zeros((8, 4, 16), np.int32)
-    hosts = np.zeros((8, 4), np.int32)
     for s in range(8):
         for rep in range(4):
             y, core = divmod(rep, 2)
@@ -44,13 +43,12 @@
             targets = [s ^ k for _, k in steps]
             if s in HOSTS:
                 targets.append(s)
-                hosts[s, rep] = owner_at[s, y]
             sends[s, rep] = [owner_at[target, y] for target in targets]
             for side in range(2):
                 half = core ^ side
                 for step, k in enumerate((0,) + ROUNDS[half]):
                     order[s, rep, CHUNKS.index((step, side))] = (s ^ k) * 2 + half
-    return sends, order, hosts
+    return sends, order
 
 
 def round_pairs(step):
@@ -64,6 +62,15 @@
 SIBLINGS = [(host * 4 + rep, host * 4 + (rep ^ 1)) for host in HOSTS for rep in range(4)]
 
 
+def metadata_pairs():
+    pairs = []
+    for owner in range(8):
+        host, y = host_of(owner)
+        for core in range(2):
+            pairs.append((owner * 4 + y * 2 + core, host * 4 + y * 2 + core))
+    return pairs
+
+
 def tie(value, *after):
     return lax.optimization_barrier((value, *after))[0]
 
@@ -75,14 +82,23 @@
     )
 
 
-def arrival_clusters(place_index, slot_cluster):
-    heads = slot_cluster.reshape(-1, BLK)[:, 0]
-    block = place_index // BLK
-    hit = block[None, :] == jnp.arange(heads.shape[0], dtype=jnp.int32)[:, None]
-    return jnp.sum(jnp.where(hit, heads[:, None], 0), axis=0)
-
-
-def gather_kernel(count, size, group, sections, named, *refs):
+def names_kernel(place_ref, slots_ref, out_ref):
+    block = place_ref[...] // BLK
+    found = jnp.zeros_like(block)
+    for i in range(slots_ref.shape[0] * LANES // BLK):
+        row = i * BLK // LANES
+        found = jnp.where(block == i, slots_ref[row : row + 1, 0:1], found)
+    out_ref[...] = found
+
+
+def arrival_names(place_index, slot_cluster):
+    places = place_index.reshape(-1, LANES)
+    return pl.pallas_call(
+        names_kernel, out_shape=jax.ShapeDtypeStruct(places.shape, jnp.int32)
+    )(places, slot_cluster.reshape(-1, LANES))
+
+
+def gather_kernel(count, size, group, sections, *refs):
     table_ref, index_ref, rows_ref = refs[:3]
     raw, wide, picked, sems = refs[-4:]
     outs = refs[-4 - count : -4]
@@ -94,14 +110,7 @@
         rows = pl.ds(i * part, part)
         copies.append(pltpu.make_async_copy(rows_ref.at[rows], raw.at[rows], sems.at[i]))
         copies[-1].start()
-    if named:
-        place_ref, slots_ref = refs[3:5]
-        block = place_ref[...] // BLK
-        found = jnp.zeros_like(block)
-        for i in range(slots_ref.shape[0] // BLK):
-            found = jnp.where(block == i, slots_ref[i * BLK], found)
-        refs[-5 - count][...] = found
-    step = 80
+    step = 160
     for i in range(sections):
         copies[i].wait()
 
@@ -134,36 +143,30 @@
         lax.fori_loop(0, size // group, pick, 0)
 
 
-def gather_rows(embeddings, index, starts, size, work=0, names=(), after=()):
+def gather_rows(embeddings, index, starts, size, after=()):
     documents, width = embeddings.shape
     count = starts.shape[0]
-    sections = 8
+    sections = 10
     group = 80
-    extra = []
-    if names:
-        places = names[0].reshape(-1, LANES)
-        names = (places, names[1])
-        extra = [jax.ShapeDtypeStruct(places.shape, jnp.int32)]
     return pl.pallas_call(
-        functools.partial(gather_kernel, count, size, group, sections, bool(names)),
-        out_shape=extra + [jax.ShapeDtypeStruct((size, width), jnp.bfloat16)] * count,
+        functools.partial(gather_kernel, count, size, group, sections),
+        out_shape=[jax.ShapeDtypeStruct((size, width), jnp.bfloat16)] * count,
         in_specs=[
             pl.BlockSpec(memory_space=pltpu.SMEM),
             pl.BlockSpec(memory_space=pltpu.SMEM),
             pl.BlockSpec(memory_space=pl.ANY),
         ]
-        + [pl.BlockSpec(memory_space=pltpu.VMEM), pl.BlockSpec(memory_space=pltpu.SMEM)][: len(names)]
         + [pl.BlockSpec(memory_space=pl.ANY)] * len(after),
-        out_specs=[pl.BlockSpec(memory_space=pltpu.VMEM)] * (count + len(extra)),
+        out_specs=[pl.BlockSpec(memory_space=pltpu.VMEM)] * count,
         scratch_shapes=[
             pltpu.VMEM((documents, width), jnp.bfloat16),
             pltpu.VMEM((documents * width // LANES, LANES), jnp.float32),
             pltpu.VMEM((group * width // LANES, LANES), jnp.float32),
             pltpu.SemaphoreType.DMA((sections,)),
         ],
-        compiler_params=pltpu.CompilerParams(vmem_limit_bytes=VMEM_LIMIT),
-        cost_estimate=pl.CostEstimate(flops=work, bytes_accessed=0, transcendentals=0),
-    )(starts, index, embeddings, *names, *after)
+        compiler_params=pltpu.CompilerParams(vmem_limit_bytes=45 * MIB),
+        cost_estimate=pl.CostEstimate(flops=LONG, bytes_accessed=0, transcendentals=0),
+    )(starts, index, embeddings, *after)
 
 
 def best_of_rows(acc, size):
@@ -243,7 +246,8 @@
         best_ref[:, span] = jnp.maximum(best_ref[:, span], best_of_rows(acc[...], height))
 
 
-def gram_best(chunks, loads, size, cluster_row, before, passes, after=()):
+def gram_best(chunks, size, cluster_row, before, passes, after=()):
+    loads = tuple(range(len(chunks)))
     width = chunks[0].shape[1]
     total = before.shape[1]
     limit = (max(loads) + 1) * size
@@ -253,7 +257,7 @@
     return pl.pallas_call(
         functools.partial(gram_kernel, passes, loads, size, limit),
         out_shape=jax.ShapeDtypeStruct((1, total), jnp.float32),
-        in_specs=[pl.BlockSpec(memory_space=pltpu.HBM)] * len(loads)
+        in_specs=[pl.BlockSpec(memory_space=pl.ANY)] * len(loads)
         + [pl.BlockSpec(memory_space=pl.ANY)] * len(after)
         + [pl.BlockSpec(memory_space=pltpu.VMEM)] * 2,
         out_specs=pl.BlockSpec(memory_space=pltpu.VMEM),
@@ -262,7 +266,7 @@
             pltpu.VMEM((padded, LANES), jnp.float32),
             pltpu.SemaphoreType.DMA((max(loads) + 1,)),
         ],
-        compiler_params=pltpu.CompilerParams(vmem_limit_bytes=VMEM_LIMIT),
+        compiler_params=pltpu.CompilerParams(vmem_limit_bytes=24 * MIB),
         cost_estimate=pl.CostEstimate(flops=0, bytes_accessed=0, transcendentals=0),
     )(*chunks, *after, cluster_row, before)
 
@@ -308,7 +312,7 @@
         + [pl.BlockSpec(memory_space=pltpu.VMEM)] * 4,
         out_specs=pl.BlockSpec(memory_space=pltpu.VMEM),
         scratch_shapes=[pltpu.VMEM((padded, LANES), jnp.float32)],
-        compiler_params=pltpu.CompilerParams(vmem_limit_bytes=VMEM_LIMIT),
+        compiler_params=pltpu.CompilerParams(vmem_limit_bytes=16 * MIB),
     )(order, own, other, clusters, best)
 
 
@@ -348,7 +352,7 @@
             pltpu.VMEM((3 * high, wide), jnp.bfloat16),
             pltpu.VMEM((LANES, wide), jnp.bfloat16),
         ],
-        compiler_params=pltpu.CompilerParams(vmem_limit_bytes=VMEM_LIMIT),
+        compiler_params=pltpu.CompilerParams(vmem_limit_bytes=16 * MIB),
     )(index, values)
     return out.reshape(-1)
 
@@ -359,16 +363,16 @@
     size = share // 2
     s, rep = lax.axis_index("shard"), lax.axis_index("rep")
     axes = ("shard", "rep")
-    sends, order, hosts = plan()
+    sends, order = plan()
     halves = np.arange(4)[:, None] % 2 ^ np.array([0, 0, 0, 0, 1])
     starts = sends[:, :, [0, 1, 2, 3, 3]] * share + (halves * size).astype(np.int32)
     starts = jnp.asarray(starts)[s, rep]
     order = jnp.asarray(order)[s, rep]
-    clusters, early = gather_rows(
-        embeddings, send_index, starts[:1], size, names=(place_index, slot_cluster)
-    )
-    clusters = lax.all_gather(clusters, "shard")[jnp.asarray(hosts)[s, rep]]
-    clusters = clusters.reshape(16, size)[order]
+    named = arrival_names(place_index, slot_cluster)
+    (early,) = gather_rows(embeddings, send_index, starts[:1], size, (named,))
+    named = lax.ppermute(named, axes, metadata_pairs())
+    early = tie(early, named)
+    clusters = named.reshape(16, size)[order]
     index = send_index.reshape(8, 2, size)
 
     def go(step, chunk):
@@ -379,32 +383,31 @@
 
     own, other = [None] * 8, [None] * 8
     own[1], own[2] = go(1, early), go(2, early)
-    late = gather_rows(embeddings, send_index, starts[1:], size, LONG, after=(early,))
+    late = gather_rows(embeddings, send_index, starts[1:], size, (early,))
     own[0], other[0] = late[2:]
     own[3], own[4] = go(3, late[0]), go(4, late[0])
     flat = clusters.reshape(1, 16 * size)
 
-    def score(best, loads, passes, after=()):
-        chunks = [(own, other)[side][r] for r, side in [CHUNKS[i] for i in loads]]
-        return gram_best(chunks, tuple(loads), size, flat, best, passes, after)
+    def score(best, count, passes, after=()):
+        chunks = [(own, other)[side][r] for r, side in CHUNKS[:count]]
+        return gram_best(chunks, size, flat, best, passes, after)
 
     own[1], own[2] = tie(own[1], late[0]), tie(own[2], late[0])
+    other[1], other[2] = swap(own[1]), swap(own[2])
     own[5] = go(5, tie(late[1], own[1]))
     own[6] = go(6, tie(late[1], own[2]))
     best = jnp.full((1, 16 * size), -1.0, jnp.float32)
-    best = score(best, range(4), (new_pass(0, 3, 4, size),), (order, index))
-    other[1], other[2] = swap(tie(own[1], best)), swap(tie(own[2], best))
+    best = score(best, 6, (new_pass(0, 3, 6, size),), (order, index))
     own[3], own[4] = tie(own[3], best), tie(own[4], best)
+    other[3], other[4] = swap(own[3]), swap(own[4])
     own[7] = go(7, tie(late[2], own[3]))
-    best = score(best, range(8), (new_pass(6, 2, 8, size), late_pass(1, 2, 4, 6, size)))
-    other[3], other[4] = swap(tie(own[3], best)), swap(tie(own[4], best))
+    best = score(best, 8, (new_pass(6, 2, 8, size),))
     own[5], own[6] = tie(own[5], best), tie(own[6], best)
     other[5], other[6] = swap(own[5]), swap(own[6])
-    best = score(best, range(12), (new_pass(10, 2, 12, size), late_pass(6, 2, 8, 10, size)))
-    best = score(best, range(10, 14), (late_pass(10, 2, 12, 14, size),))
+    best = score(best, 12, (new_pass(10, 2, 12, size), late_pass(6, 2, 8, 10, size)))
     own[7] = tie(own[7], best)
     other[7] = swap(own[7])
-    best = score(best, range(15), (new_pass(14, 1, 15, size),))
+    best = score(best, 15, (new_pass(14, 1, 15, size), late_pass(10, 2, 12, 14, size)))
     outbound = finish(order, own[7], other[7], flat, best)
     returned = lax.all_to_all(outbound, axes, split_axis=0, concat_axis=0, tiled=True)
     sources = []
@@ -429,13 +432,13 @@
     news = parts // reps
     turn = lax.axis_index("rep") * news
     arrived = jnp.roll(arrived.reshape(parts, size, width), -turn, axis=0)
-    clusters = arrival_clusters(place_index, slot_cluster).reshape(parts, size)
+    clusters = arrival_names(place_index, slot_cluster).reshape(parts, size)
     clusters = jnp.roll(clusters, -turn, axis=0)
     best = jnp.full((1, documents), -1.0, jnp.float32)
     tiles = tuple(range(documents // BLK))
     passes = ((0, news, 0, 1, True, tiles),)
     chunks = [arrived[i] for i in range(parts)]
-    best = gram_best(chunks, tuple(range(parts)), size, clusters.reshape(1, -1), best, passes)
+    best = gram_best(chunks, size, clusters.reshape(1, -1), best, passes)
     best = lax.all_gather(best[0, : news * size], "rep", axis=0, tiled=True)
     returned = lax.all_to_all(
         best.reshape(owners, share), "shard", split_axis=0, concat_axis=0, tiled=True

time: 204 us -> 153 us (0.75)
  blocking collectives: 61.1 us -> 14.4 us
  starting transfers between devices: 36.8 us -> 56.8 us
  Pallas kernels: 83.7 us -> 70.1 us
  local copies, waits for them, and re-layouts: 14.2 us -> 4.74 us
    all_gather x1 -> x0, blocking collectives: 47.8 us -> none  [hosted(): clusters = lax.all_gather(clusters, 'shard')[jnp.asarray(hosts)[s, rep]]]
    ppermute x7, starting transfers between devices: 31.6 us -> 45.2 us  [go(): return lax.ppermute(chunk, axes, round_pairs(step - 1))]
    pallas_call x5 -> x4, Pallas kernels: 50.9 us -> 40.7 us  [gram_best(): pl.pallas_call(functools.partial(gram_kernel, passes, loads, size, limit)...]
    ppermute x0 -> x1, starting transfers between devices: none -> 4.92 us  [hosted(): named = lax.ppermute(named, axes, metadata_pairs())]
    unnamed x34 -> x8, local copies, waits for them, and re-layouts: 7.12 us -> 2.4 us
    pallas_call x2, Pallas kernels: 26.4 us -> 24 us  [gather_rows(): pl.pallas_call(functools.partial(gather_kernel, count, size, group, secti...]
  transfers between devices with their start and end apart: 14 -> 15, of which waited for: 1 -> 2; matrix products, arithmetic and copies ran while one was open for 3% -> 2% of each run, Pallas kernels for 32% -> 42%
where the time goes in v6:
time: 153 us; the launch traced here: 152 us
  Pallas kernels  70.1 us (46%)
  starting transfers between devices  56.8 us (37%)
  blocking collectives  14.4 us (9%)
  waiting for transfers between devices  5.5 us (4%)
  local copies, waits for them, and re-layouts  4.74 us (3%)
    ppermute x7, starting transfers between devices, go(): return lax.ppermute(chunk, axes, round_pairs(step - 1))  45.2 us
    pallas_call x4, Pallas kernels, gram_best(): pl.pallas_call(functools.partial(gram_kernel, passes, loads, size, limit)...  40.7 us
    pallas_call x2, Pallas kernels, gather_rows(): pl.pallas_call(functools.partial(gather_kernel, count, size, group, secti...  24 us
    all_to_all x1, blocking collectives, hosted(): lax.all_to_all(outbound, axes, split_axis=0, concat_axis=0, tiled=True)  14.4 us
    ppermute x7, starting transfers between devices, swap(): return lax.ppermute(chunk, axes, SIBLINGS)  6.7 us
    ppermute x7, waiting for transfers between devices, go(): return lax.ppermute(chunk, axes, round_pairs(step - 1))  5.47 us
    ppermute x1, starting transfers between devices, hosted(): named = lax.ppermute(named, axes, metadata_pairs())  4.92 us
  transfers between devices with their start and end apart: 15, of which 2 were waited for; matrix products, arithmetic and copies ran while one was open for 2% of the time, Pallas kernels for 42%

profile of v6, /device:TPU:0, one launch (start us, length us, event | category | flops | bytes accessed | tf_op | source)
XLA Modules:
  0.0 152.5 jit_solution(47295051118902550)
XLA Ops:
  0.0 1.5 shard_map.64.refs_3_
  1.5 4.9 %collective-permute-start = (s32[50,128]{1,0:T(8,128)}, s32[50,128]{1,0:T(8,128)S(1)}, u32[]{:S(2)}, u32[]{:S(2)}) collective-permute-start(s32[50,128]{1,0:T(8,128)} %shard_map.64.refs_3_), channel_id=1, source_target_pairs={{0,8},{1,9},{4,12},{5,13},{10,10},{11,11},{14,14},{15,15},{16,16},... | collective-permute-start | bytes 76808 | tf_op jit(solution)/shard_map/ppermute | solution.py:373
  6.4 0.7 constant_dynamic-slice_fusion
  7.1 0.7 copy-done
  7.8 0.7 copy-done.2
  8.6 9.9 %shard_map.65.refs_3_ = bf16[400,1024]{1,0:T(8,128)(2,1)S(1)} custom-call(s32[1]{0:T(128)S(1)} %bitcast.13, s32[6400]{0:T(1024)S(1)} %copy-done, bf16[6400,1024]{1,0:T(8,128)(2,1)} %refs_2_.3, s32[50,128]{1,0:T(8,128)S(1)} %copy-done.2), custom_call_target="tpu_custom_call" | custom-call | flops 24999999488 | tf_op jit(solution)/shard_map/pallas_call | solution.py:151
  18.5 0.1 slice_bitcast_fusion.refs_0_
  18.6 0.0 collective-permute-done
  18.6 0.7 collective-permute-start.3
  19.3 4.0 %collective-permute-start.2 = (bf16[400,1024]{1,0:T(8,128)(2,1)S(1)}, bf16[400,1024]{1,0:T(8,128)(2,1)S(1)}, u32[]{:S(2)}, u32[]{:S(2)}) collective-permute-start(bf16[400,1024]{1,0:T(8,128)(2,1)S(1)} %shard_map.65.refs_3_), channel_id=1, source_target_pairs={{24,8},{28,12},{0,16},{4,20},{1,9},{5,13},{25,17},{29,21},{26,10},... | collective-permute-start | bytes 2457608 | tf_op jit(solution)/shard_map/ppermute | solution.py:379
  23.3 14.1 %shard_map.66 = (bf16[400,1024]{1,0:T(8,128)(2,1)}, bf16[400,1024]{1,0:T(8,128)(2,1)S(1)}, bf16[400,1024]{1,0:T(8,128)(2,1)S(1)}, bf16[400,1024]{1,0:T(8,128)(2,1)S(1)}) custom-call(s32[4]{0:T(128)S(1)} %slice_bitcast_fusion.refs_0_, s32[6400]{0:T(1024)S(1)} %copy-done.1, bf16[6400,1024]{1,0:T(8,128)(2,1)} %refs_2_.3, bf16[400,1024]{1,0:T(8,128)(2,1)S(1)} %shard_map.65.refs_3_), custom_call_target="tpu_custom_call" | custom-call | flops 24999999488 | tf_op jit(solution)/shard_map/pallas_call | solution.py:151
  37.4 0.9 copy-done.3
  38.3 2.2 %collective-permute-done.2.refs_1_ = bf16[400,1024]{1,0:T(8,128)(2,1)S(1)} collective-permute-done((bf16[400,1024]{1,0:T(8,128)(2,1)S(1)}, bf16[400,1024]{1,0:T(8,128)(2,1)S(1)}, u32[]{:S(2)}, u32[]{:S(2)}) %collective-permute-start.2) | collective-permute-done | bytes 819232 | tf_op jit(solution)/shard_map/ppermute | solution.py:379
  40.5 1.6 %collective-permute-start.4 = (bf16[400,1024]{1,0:T(8,128)(2,1)S(1)}, bf16[400,1024]{1,0:T(8,128)(2,1)}, u32[]{:S(2)}, u32[]{:S(2)}) collective-permute-start(bf16[400,1024]{1,0:T(8,128)(2,1)S(1)} %collective-permute-done.2.refs_1_), channel_id=1, source_target_pairs={{8,9},{9,8},{10,11},{11,10},{12,13},{13,12},{14,15},{15,14},{16,17... | collective-permute-start | bytes 2457608 | tf_op jit(solution)/shard_map/ppermute | solution.py:382
  42.1 0.0 collective-permute-done.3.refs_2_
  42.1 1.6 %collective-permute-start.5 = (bf16[400,1024]{1,0:T(8,128)(2,1)S(1)}, bf16[400,1024]{1,0:T(8,128)(2,1)}, u32[]{:S(2)}, u32[]{:S(2)}) collective-permute-start(bf16[400,1024]{1,0:T(8,128)(2,1)S(1)} %collective-permute-done.3.refs_2_), channel_id=1, source_target_pairs={{8,9},{9,8},{10,11},{11,10},{12,13},{13,12},{14,15},{15,14},{16,17... | collective-permute-start | bytes 2457608 | tf_op jit(solution)/shard_map/ppermute | solution.py:382
  43.7 7.4 %collective-permute-start.1 = (bf16[400,1024]{1,0:T(8,128)(2,1)}, bf16[400,1024]{1,0:T(8,128)(2,1)}, u32[]{:S(2)}, u32[]{:S(2)}) collective-permute-start(bf16[400,1024]{1,0:T(8,128)(2,1)} %get-tuple-element.22), channel_id=1, source_target_pairs={{28,8},{24,12},{4,16},{0,20},{5,9},{1,13},{29,17},{25,21},{30,10},... | collective-permute-start | bytes 2457608 | tf_op jit(solution)/shard_map/ppermute | solution.py:379
  51.0 1.6 %collective-permute-start.7 = (bf16[400,1024]{1,0:T(8,128)(2,1)}, bf16[400,1024]{1,0:T(8,128)(2,1)}, u32[]{:S(2)}, u32[]{:S(2)}) collective-permute-start(bf16[400,1024]{1,0:T(8,128)(2,1)} %get-tuple-element.22), channel_id=1, source_target_pairs={{20,8},{16,12},{12,16},{8,20},{17,9},{21,13},{9,17},{13,21},{22,10... | collective-permute-start | bytes 2457608 | tf_op jit(solution)/shard_map/ppermute | solution.py:379
  52.6 0.1 reshape.48.refs_7_.index_ref
  52.7 0.7 fusion.1.refs_6_.order_ref
  53.4 0.7 fusion
  54.1 0.1 reshape.51
  54.2 0.6 gather_fusion
  54.8 0.1 reshape.52.refs_8_.refs_12_.refs_15_.clusters_ref
  54.9 1.3 collective-permute-start.10
  56.2 0.0 collective-permute-done.4.refs_4_
  56.2 0.7 collective-permute-start.11
  57.0 0.0 collective-permute-done.5.refs_5_
  57.0 8.8 %shard_map.67.refs_9_ = f32[1,6400]{1,0:T(1,128)S(1)} custom-call(bf16[400,1024]{1,0:T(8,128)(2,1)S(1)} %get-tuple-element.27.refs_0_, bf16[400,1024]{1,0:T(8,128)(2,1)S(1)} %collective-permute-done.2.refs_1_, bf16[400,1024]{1,0:T(8,128)(2,1)S(1)} %collective-permute-done.3.refs_2_, bf16[400,1024]{1,0:T(8,128)(2,1)S(1)} %get-tuple-element.25.refs_3_, ...), custom_call_target="tpu_custom_call" | custom-call | tf_op jit(solution)/shard_map/pallas_call | solution.py:257
  65.8 3.3 %collective-permute-done.1.refs_6_ = bf16[400,1024]{1,0:T(8,128)(2,1)} collective-permute-done((bf16[400,1024]{1,0:T(8,128)(2,1)}, bf16[400,1024]{1,0:T(8,128)(2,1)}, u32[]{:S(2)}, u32[]{:S(2)}) %collective-permute-start.1) | collective-permute-done | bytes 819232 | tf_op jit(solution)/shard_map/ppermute | solution.py:379
  69.1 0.7 collective-permute-start.8
  69.8 0.0 collective-permute-done.7.refs_7_
  69.8 0.7 collective-permute-start.9
  70.5 29.5 %collective-permute-start.6 = (bf16[400,1024]{1,0:T(8,128)(2,1)S(1)}, bf16[400,1024]{1,0:T(8,128)(2,1)S(1)}, u32[]{:S(2)}, u32[]{:S(2)}) collective-permute-start(bf16[400,1024]{1,0:T(8,128)(2,1)S(1)} %get-tuple-element.27.refs_0_), channel_id=1, source_target_pairs={{4,8},{0,12},{28,16},{24,20},{29,9},{25,13},{5,17},{1,21},{6,10},{... | collective-permute-start | bytes 2457608 | tf_op jit(solution)/shard_map/ppermute | solution.py:379
  100.0 8.6 %shard_map.68.refs_13_ = f32[1,6400]{1,0:T(1,128)S(1)} custom-call(bf16[400,1024]{1,0:T(8,128)(2,1)S(1)} %get-tuple-element.27.refs_0_, bf16[400,1024]{1,0:T(8,128)(2,1)S(1)} %collective-permute-done.2.refs_1_, bf16[400,1024]{1,0:T(8,128)(2,1)S(1)} %collective-permute-done.3.refs_2_, bf16[400,1024]{1,0:T(8,128)(2,1)S(1)} %get-tuple-element.25.refs_3_, ...), custom_call_target="tpu_custom_call" | custom-call | tf_op jit(solution)/shard_map/pallas_call | solution.py:257
  108.6 0.0 collective-permute-done.11.refs_11_
  108.7 0.7 collective-permute-start.13
  109.4 0.7 collective-permute-start.14
  110.1 0.0 collective-permute-done.9.refs_9_
  110.1 12.9 %shard_map.69.refs_16_ = f32[1,6400]{1,0:T(1,128)S(1)} custom-call(bf16[400,1024]{1,0:T(8,128)(2,1)S(1)} %get-tuple-element.27.refs_0_, bf16[400,1024]{1,0:T(8,128)(2,1)S(1)} %collective-permute-done.2.refs_1_, bf16[400,1024]{1,0:T(8,128)(2,1)S(1)} %collective-permute-done.3.refs_2_, bf16[400,1024]{1,0:T(8,128)(2,1)S(1)} %get-tuple-element.25.refs_3_, ...), custom_call_target="tpu_custom_call" | custom-call | tf_op jit(solution)/shard_map/pallas_call | solution.py:257
  123.1 0.0 collective-permute-done.6.refs_14_.own_ref
  123.1 0.7 collective-permute-start.12
  123.8 0.0 collective-permute-done.13.refs_12_
  123.8 0.0 collective-permute-done.14.refs_13_
  123.8 10.3 %shard_map.70.best_ref = f32[1,6400]{1,0:T(1,128)S(1)} custom-call(bf16[400,1024]{1,0:T(8,128)(2,1)S(1)} %get-tuple-element.27.refs_0_, bf16[400,1024]{1,0:T(8,128)(2,1)S(1)} %collective-permute-done.2.refs_1_, bf16[400,1024]{1,0:T(8,128)(2,1)S(1)} %collective-permute-done.3.refs_2_, bf16[400,1024]{1,0:T(8,128)(2,1)S(1)} %get-tuple-element.25.refs_3_, ...), custom_call_target="tpu_custom_call" | custom-call | tf_op jit(solution)/shard_map/pallas_call | solution.py:257
  134.2 1.5 shard_map.71
  135.7 14.4 %all_to_all.5.values_ref = f32[32,2,400]{2,1,0:T(2,128)S(1)} all-to-all(f32[32,2,400]{2,1,0:T(2,128)S(1)} %shard_map.71), channel_id=1, replica_groups=mesh['shard'=8,'rep'=4] {'shard','rep'}, dimensions={0} | all-to-all | bytes 204800 | tf_op jit(solution)/shard_map/all_to_all | solution.py:412
  150.1 2.4 %shard_map.72 = f32[50,128]{1,0:T(8,128)} custom-call(s32[8,2,400]{2,1,0:T(2,128)S(1)} %reshape.48.refs_7_.index_ref, f32[32,2,400]{2,1,0:T(2,128)S(1)} %all_to_all.5.values_ref), custom_call_target="tpu_custom_call" | custom-call | tf_op jit(solution)/shard_map/pallas_call | solution.py:348
  (10 shorter events, 0.0 us)
Async XLA Ops:
  1.5 17.2 %collective-permute-start = (s32[50,128]{1,0:T(8,128)}, s32[50,128]{1,0:T(8,128)S(1)}, u32[]{:S(2)}, u32[]{:S(2)}) collective-permute-start(s32[50,128]{1,0:T(8,128)} %shard_map.64.refs_3_), channel_id=1, source_target_pairs={{0,8},{1,9},{4,12},{5,13},{10,10},{11,11},{14,14},{15,15},{16,16},... | collective-permute-start | bytes 76808 | tf_op jit(solution)/shard_map/ppermute | solution.py:373
  7.1 0.7 copy-start
  7.8 0.7 copy-start.2
  8.6 14.8 %copy-start.1 = (s32[6400]{0:T(1024)S(1)}, s32[6400]{0:T(1024)}, u32[]{:S(2)}) copy-start(s32[6400]{0:T(1024)} %refs_1_.3) | copy-start | bytes 76804
  18.6 23.5 %collective-permute-start.3 = (bf16[400,1024]{1,0:T(8,128)(2,1)S(1)}, bf16[400,1024]{1,0:T(8,128)(2,1)S(1)}, u32[]{:S(2)}, u32[]{:S(2)}) collective-permute-start(bf16[400,1024]{1,0:T(8,128)(2,1)S(1)} %shard_map.65.refs_3_), channel_id=1, source_target_pairs={{16,8},{20,12},{8,16},{12,20},{13,9},{9,13},{21,17},{17,21},{18,10... | collective-permute-start | bytes 2457608 | tf_op jit(solution)/shard_map/ppermute | solution.py:379
  19.3 21.2 %collective-permute-start.2 = (bf16[400,1024]{1,0:T(8,128)(2,1)S(1)}, bf16[400,1024]{1,0:T(8,128)(2,1)S(1)}, u32[]{:S(2)}, u32[]{:S(2)}) collective-permute-start(bf16[400,1024]{1,0:T(8,128)(2,1)S(1)} %shard_map.65.refs_3_), channel_id=1, source_target_pairs={{24,8},{28,12},{0,16},{4,20},{1,9},{5,13},{25,17},{29,21},{26,10},... | collective-permute-start | bytes 2457608 | tf_op jit(solution)/shard_map/ppermute | solution.py:379
  37.4 0.9 copy-start.3
  40.5 15.7 %collective-permute-start.4 = (bf16[400,1024]{1,0:T(8,128)(2,1)S(1)}, bf16[400,1024]{1,0:T(8,128)(2,1)}, u32[]{:S(2)}, u32[]{:S(2)}) collective-permute-start(bf16[400,1024]{1,0:T(8,128)(2,1)S(1)} %collective-permute-done.2.refs_1_), channel_id=1, source_target_pairs={{8,9},{9,8},{10,11},{11,10},{12,13},{13,12},{14,15},{15,14},{16,17... | collective-permute-start | bytes 2457608 | tf_op jit(solution)/shard_map/ppermute | solution.py:382
  42.1 14.9 %collective-permute-start.5 = (bf16[400,1024]{1,0:T(8,128)(2,1)S(1)}, bf16[400,1024]{1,0:T(8,128)(2,1)}, u32[]{:S(2)}, u32[]{:S(2)}) collective-permute-start(bf16[400,1024]{1,0:T(8,128)(2,1)S(1)} %collective-permute-done.3.refs_2_), channel_id=1, source_target_pairs={{8,9},{9,8},{10,11},{11,10},{12,13},{13,12},{14,15},{15,14},{16,17... | collective-permute-start | bytes 2457608 | tf_op jit(solution)/shard_map/ppermute | solution.py:382
  43.7 25.4 %collective-permute-start.1 = (bf16[400,1024]{1,0:T(8,128)(2,1)}, bf16[400,1024]{1,0:T(8,128)(2,1)}, u32[]{:S(2)}, u32[]{:S(2)}) collective-permute-start(bf16[400,1024]{1,0:T(8,128)(2,1)} %get-tuple-element.22), channel_id=1, source_target_pairs={{28,8},{24,12},{4,16},{0,20},{5,9},{1,13},{29,17},{25,21},{30,10},... | collective-permute-start | bytes 2457608 | tf_op jit(solution)/shard_map/ppermute | solution.py:379
  51.0 18.7 %collective-permute-start.7 = (bf16[400,1024]{1,0:T(8,128)(2,1)}, bf16[400,1024]{1,0:T(8,128)(2,1)}, u32[]{:S(2)}, u32[]{:S(2)}) collective-permute-start(bf16[400,1024]{1,0:T(8,128)(2,1)} %get-tuple-element.22), channel_id=1, source_target_pairs={{20,8},{16,12},{12,16},{8,20},{17,9},{21,13},{9,17},{13,21},{22,10... | collective-permute-start | bytes 2457608 | tf_op jit(solution)/shard_map/ppermute | solution.py:379
  54.9 53.8 %collective-permute-start.10 = (bf16[400,1024]{1,0:T(8,128)(2,1)}, bf16[400,1024]{1,0:T(8,128)(2,1)S(1)}, u32[]{:S(2)}, u32[]{:S(2)}) collective-permute-start(bf16[400,1024]{1,0:T(8,128)(2,1)} %copy-done.3), channel_id=1, source_target_pairs={{0,8},{4,12},{24,16},{28,20},{25,9},{29,13},{1,17},{5,21},{2,10},{... | collective-permute-start | bytes 2457608 | tf_op jit(solution)/shard_map/ppermute | solution.py:379
  56.2 52.4 %collective-permute-start.11 = (bf16[400,1024]{1,0:T(8,128)(2,1)}, bf16[400,1024]{1,0:T(8,128)(2,1)S(1)}, u32[]{:S(2)}, u32[]{:S(2)}) collective-permute-start(bf16[400,1024]{1,0:T(8,128)(2,1)} %copy-done.3), channel_id=1, source_target_pairs={{12,8},{8,12},{20,16},{16,20},{21,9},{17,13},{13,17},{9,21},{14,10... | collective-permute-start | bytes 2457608 | tf_op jit(solution)/shard_map/ppermute | solution.py:379
  69.1 41.1 %collective-permute-start.8 = (bf16[400,1024]{1,0:T(8,128)(2,1)}, bf16[400,1024]{1,0:T(8,128)(2,1)S(1)}, u32[]{:S(2)}, u32[]{:S(2)}) collective-permute-start(bf16[400,1024]{1,0:T(8,128)(2,1)} %collective-permute-done.1.refs_6_), channel_id=1, source_target_pairs={{8,9},{9,8},{10,11},{11,10},{12,13},{13,12},{14,15},{15,14},{16,17... | collective-permute-start | bytes 2457608 | tf_op jit(solution)/shard_map/ppermute | solution.py:382
  69.8 40.3 %collective-permute-start.9 = (bf16[400,1024]{1,0:T(8,128)(2,1)}, bf16[400,1024]{1,0:T(8,128)(2,1)S(1)}, u32[]{:S(2)}, u32[]{:S(2)}) collective-permute-start(bf16[400,1024]{1,0:T(8,128)(2,1)} %collective-permute-done.7.refs_7_), channel_id=1, source_target_pairs={{8,9},{9,8},{10,11},{11,10},{12,13},{13,12},{14,15},{15,14},{16,17... | collective-permute-start | bytes 2457608 | tf_op jit(solution)/shard_map/ppermute | solution.py:382
  70.5 52.6 %collective-permute-start.6 = (bf16[400,1024]{1,0:T(8,128)(2,1)S(1)}, bf16[400,1024]{1,0:T(8,128)(2,1)S(1)}, u32[]{:S(2)}, u32[]{:S(2)}) collective-permute-start(bf16[400,1024]{1,0:T(8,128)(2,1)S(1)} %get-tuple-element.27.refs_0_), channel_id=1, source_target_pairs={{4,8},{0,12},{28,16},{24,20},{29,9},{25,13},{5,17},{1,21},{6,10},{... | collective-permute-start | bytes 2457608 | tf_op jit(solution)/shard_map/ppermute | solution.py:379
  108.7 15.1 %collective-permute-start.13 = (bf16[400,1024]{1,0:T(8,128)(2,1)S(1)}, bf16[400,1024]{1,0:T(8,128)(2,1)S(1)}, u32[]{:S(2)}, u32[]{:S(2)}) collective-permute-start(bf16[400,1024]{1,0:T(8,128)(2,1)S(1)} %collective-permute-done.10.refs_10_), channel_id=1, source_target_pairs={{8,9},{9,8},{10,11},{11,10},{12,13},{13,12},{14,15},{15,14},{16,17... | collective-permute-start | bytes 2457608 | tf_op jit(solution)/shard_map/ppermute | solution.py:382
  109.4 14.4 %collective-permute-start.14 = (bf16[400,1024]{1,0:T(8,128)(2,1)S(1)}, bf16[400,1024]{1,0:T(8,128)(2,1)S(1)}, u32[]{:S(2)}, u32[]{:S(2)}) collective-permute-start(bf16[400,1024]{1,0:T(8,128)(2,1)S(1)} %collective-permute-done.11.refs_11_), channel_id=1, source_target_pairs={{8,9},{9,8},{10,11},{11,10},{12,13},{13,12},{14,15},{15,14},{16,17... | collective-permute-start | bytes 2457608 | tf_op jit(solution)/shard_map/ppermute | solution.py:382
  123.1 11.1 %collective-permute-start.12 = (bf16[400,1024]{1,0:T(8,128)(2,1)S(1)}, bf16[400,1024]{1,0:T(8,128)(2,1)S(1)}, u32[]{:S(2)}, u32[]{:S(2)}) collective-permute-start(bf16[400,1024]{1,0:T(8,128)(2,1)S(1)} %collective-permute-done.6.refs_14_.own_ref), channel_id=1, source_target_pairs={{8,9},{9,8},{10,11},{11,10},{12,13},{13,12},{14,15},{15,14},{16,17... | collective-permute-start | bytes 2457608 | tf_op jit(solution)/shard_map/ppermute | solution.py:382

commit v7 on v6

--- a/solution.py
+++ b/solution.py
@@ -15,7 +15,7 @@
 LONG = 25_000_000_000
 
 HOSTS = (2, 3, 4, 5)
-ROUNDS = ((4, 6, 5, 7, 2, 1, 3), (2, 1, 3, 6, 4, 7, 5))
+ROUNDS = ((2, 6, 5, 1, 3, 7, 4), (3, 7, 2, 6, 4, 1, 5))
 
 
 CHUNKS = (
@@ -31,24 +31,14 @@
     return (1 if z < 2 else 2) * 2 + x, z % 2
 
 
-def plan():
-    owner_at = {host_of(owner): owner for owner in range(8)}
-    sends = np.zeros((8, 4, 4), np.int32)
+def chunk_order():
     order = np.zeros((8, 4, 16), np.int32)
     for s in range(8):
         for rep in range(4):
-            y, core = divmod(rep, 2)
-            steps = [(step, k) for step, k in enumerate(ROUNDS[core]) if s ^ k in HOSTS]
-            assert [step // 2 for step, _ in steps] == list(range(len(steps)))
-            targets = [s ^ k for _, k in steps]
-            if s in HOSTS:
-                targets.append(s)
-            sends[s, rep] = [owner_at[target, y] for target in targets]
-            for side in range(2):
-                half = core ^ side
-                for step, k in enumerate((0,) + ROUNDS[half]):
-                    order[s, rep, CHUNKS.index((step, side))] = (s ^ k) * 2 + half
-    return sends, order
+            for i, (step, side) in enumerate(CHUNKS):
+                half = rep % 2 ^ side
+                order[s, rep, i] = (s ^ ((0,) + ROUNDS[half])[step]) * 2 + half
+    return order
 
 
 def round_pairs(step):
@@ -98,10 +88,26 @@
     )(places, slot_cluster.reshape(-1, LANES))
 
 
-def gather_kernel(count, size, group, sections, *refs):
-    table_ref, index_ref, rows_ref = refs[:3]
-    raw, wide, picked, sems = refs[-4:]
-    outs = refs[-4 - count : -4]
+def chunk_start(slot, size):
+    s, rep = lax.axis_index("shard"), lax.axis_index("rep")
+    y, core = rep // 2, rep % 2
+    inner = (s >= HOSTS[0]) & (s <= HOSTS[-1])
+    turn = min(slot, 3)
+    steps = [(order[2 * turn], (order + (0,))[2 * turn + 1]) for order in ROUNDS]
+    outer_step = jnp.where(core == 0, steps[0][0], steps[1][0])
+    inner_step = jnp.where(core == 0, steps[0][1], steps[1][1])
+    target = s ^ jnp.where(inner, inner_step, outer_step)
+    owner = (2 * (target // 2 - 1) + y) * 2 + target % 2
+    half = 1 - core if slot == 4 else core
+    return owner * (2 * size) + half * size
+
+
+def gather_kernel(slots, size, group, sections, *refs):
+    index_hbm, rows_ref = refs[:2]
+    index_ref, raw, wide, picked, sems = refs[-5:]
+    outs = refs[-5 - len(slots) : -5]
+    listed = pltpu.make_async_copy(index_hbm, index_ref, sems.at[sections])
+    listed.start()
     width = raw.shape[1]
     tiles = width // LANES
     part = raw.shape[0] // sections
@@ -122,8 +128,9 @@
             return 0
 
         lax.fori_loop(0, part // step, widen, 0)
-    for c in range(count):
-        base = table_ref[c]
+    listed.wait()
+    for c, slot in enumerate(slots):
+        base = chunk_start(slot, size)
 
         def pick(j, _, c=c, base=base):
             for t in range(group):
@@ -143,30 +150,27 @@
         lax.fori_loop(0, size // group, pick, 0)
 
 
-def gather_rows(embeddings, index, starts, size, after=()):
+def gather_rows(embeddings, index, slots, size, after=()):
     documents, width = embeddings.shape
-    count = starts.shape[0]
+    count = len(slots)
     sections = 10
     group = 80
     return pl.pallas_call(
-        functools.partial(gather_kernel, count, size, group, sections),
+        functools.partial(gather_kernel, slots, size, group, sections),
         out_shape=[jax.ShapeDtypeStruct((size, width), jnp.bfloat16)] * count,
-        in_specs=[
-            pl.BlockSpec(memory_space=pltpu.SMEM),
-            pl.BlockSpec(memory_space=pltpu.SMEM),
-            pl.BlockSpec(memory_space=pl.ANY),
-        ]
+        in_specs=[pl.BlockSpec(memory_space=pltpu.HBM)] * 2
         + [pl.BlockSpec(memory_space=pl.ANY)] * len(after),
         out_specs=[pl.BlockSpec(memory_space=pltpu.VMEM)] * count,
         scratch_shapes=[
+            pltpu.SMEM(index.shape, jnp.int32),
             pltpu.VMEM((documents, width), jnp.bfloat16),
             pltpu.VMEM((documents * width // LANES, LANES), jnp.float32),
             pltpu.VMEM((group * width // LANES, LANES), jnp.float32),
-            pltpu.SemaphoreType.DMA((sections,)),
+            pltpu.SemaphoreType.DMA((sections + 1,)),
         ],
         compiler_params=pltpu.CompilerParams(vmem_limit_bytes=45 * MIB),
         cost_estimate=pl.CostEstimate(flops=LONG, bytes_accessed=0, transcendentals=0),
-    )(starts, index, embeddings, *after)
+    )(index, embeddings, *after)
 
 
 def best_of_rows(acc, size):
@@ -359,17 +363,12 @@
 
 def hosted(embeddings, send_index, place_index, slot_cluster):
     documents = embeddings.shape[0]
-    share = send_index.shape[0] // 8
-    size = share // 2
+    size = send_index.shape[0] // 16
     s, rep = lax.axis_index("shard"), lax.axis_index("rep")
     axes = ("shard", "rep")
-    sends, order = plan()
-    halves = np.arange(4)[:, None] % 2 ^ np.array([0, 0, 0, 0, 1])
-    starts = sends[:, :, [0, 1, 2, 3, 3]] * share + (halves * size).astype(np.int32)
-    starts = jnp.asarray(starts)[s, rep]
-    order = jnp.asarray(order)[s, rep]
+    order = jnp.asarray(chunk_order())[s, rep]
     named = arrival_names(place_index, slot_cluster)
-    (early,) = gather_rows(embeddings, send_index, starts[:1], size, (named,))
+    (early,) = gather_rows(embeddings, send_index, (0,), size, (named,))
     named = lax.ppermute(named, axes, metadata_pairs())
     early = tie(early, named)
     clusters = named.reshape(16, size)[order]
@@ -383,7 +382,7 @@
 
     own, other = [None] * 8, [None] * 8
     own[1], own[2] = go(1, early), go(2, early)
-    late = gather_rows(embeddings, send_index, starts[1:], size, (early,))
+    late = gather_rows(embeddings, send_index, (1, 2, 3, 4), size, (early,))
     own[0], other[0] = late[2:]
     own[3], own[4] = go(3, late[0]), go(4, late[0])
     flat = clusters.reshape(1, 16 * size)
@@ -393,15 +392,15 @@
         return gram_best(chunks, size, flat, best, passes, after)
 
     own[1], own[2] = tie(own[1], late[0]), tie(own[2], late[0])
-    other[1], other[2] = swap(own[1]), swap(own[2])
     own[5] = go(5, tie(late[1], own[1]))
     own[6] = go(6, tie(late[1], own[2]))
     best = jnp.full((1, 16 * size), -1.0, jnp.float32)
-    best = score(best, 6, (new_pass(0, 3, 6, size),), (order, index))
+    best = score(best, 4, (new_pass(0, 3, 4, size),), (order, index))
+    other[1], other[2] = swap(tie(own[1], best)), swap(tie(own[2], best))
     own[3], own[4] = tie(own[3], best), tie(own[4], best)
     other[3], other[4] = swap(own[3]), swap(own[4])
     own[7] = go(7, tie(late[2], own[3]))
-    best = score(best, 8, (new_pass(6, 2, 8, size),))
+    best = score(best, 8, (new_pass(6, 2, 8, size), late_pass(1, 2, 4, 6, size)))
     own[5], own[6] = tie(own[5], best), tie(own[6], best)
     other[5], other[6] = swap(own[5]), swap(own[6])
     best = score(best, 12, (new_pass(10, 2, 12, size), late_pass(6, 2, 8, 10, size)))

time: 153 us -> 148 us (0.967)
  starting transfers between devices: 56.8 us -> 39.9 us
  blocking collectives: 14.4 us -> 30.7 us
  waiting for transfers between devices: 5.5 us -> 3.43 us
  Pallas kernels: 70.1 us -> 68.5 us
    all_to_all x1, blocking collectives: 14.4 us -> 30.7 us  [hosted(): lax.all_to_all(outbound, axes, split_axis=0, concat_axis=0, tiled=True)]
    ppermute x7, starting transfers between devices: 45.2 us -> 29.8 us  [go(): return lax.ppermute(chunk, axes, round_pairs(step - 1))]
    ppermute x7, waiting for transfers between devices: 5.47 us -> 3.41 us  [go(): return lax.ppermute(chunk, axes, round_pairs(step - 1))]
  transfers between devices with their start and end apart: 15 -> 15, of which waited for: 2 -> 1; matrix products, arithmetic and copies ran while one was open for 2% -> 2% of each run, Pallas kernels for 42% -> 43%
where the time goes in v7:
time: 148 us
  Pallas kernels  68.5 us (46%)
  starting transfers between devices  39.9 us (27%)
  blocking collectives  30.7 us (21%)
  local copies, waits for them, and re-layouts  3.96 us (3%)
  waiting for transfers between devices  3.43 us (2%)
    pallas_call x4, Pallas kernels, gram_best(): pl.pallas_call(functools.partial(gram_kernel, passes, loads, size, limit)...  39.9 us
    all_to_all x1, blocking collectives, hosted(): lax.all_to_all(outbound, axes, split_axis=0, concat_axis=0, tiled=True)  30.7 us
    ppermute x7, starting transfers between devices, go(): return lax.ppermute(chunk, axes, round_pairs(step - 1))  29.8 us
    pallas_call x2, Pallas kernels, gather_rows(): pl.pallas_call(functools.partial(gather_kernel, slots, size, group, secti...  23.2 us
    ppermute x7, starting transfers between devices, swap(): return lax.ppermute(chunk, axes, SIBLINGS)  5.21 us
    ppermute x1, starting transfers between devices, hosted(): named = lax.ppermute(named, axes, metadata_pairs())  4.92 us
    ppermute x7, waiting for transfers between devices, go(): return lax.ppermute(chunk, axes, round_pairs(step - 1))  3.41 us
  transfers between devices with their start and end apart: 15, of which 1 were waited for; matrix products, arithmetic and copies ran while one was open for 2% of the time, Pallas kernels for 43%

profile of v7, /device:TPU:0, one launch (start us, length us, event | category | flops | bytes accessed | tf_op | source)
XLA Modules:
  0.0 147.5 jit_solution(2724803661847485302)
XLA Ops:
  0.0 1.5 shard_map.55.refs_2_
  1.5 4.9 %collective-permute-start = (s32[50,128]{1,0:T(8,128)}, s32[50,128]{1,0:T(8,128)S(1)}, u32[]{:S(2)}, u32[]{:S(2)}) collective-permute-start(s32[50,128]{1,0:T(8,128)} %shard_map.55.refs_2_), channel_id=1, source_target_pairs={{0,8},{1,9},{4,12},{5,13},{10,10},{11,11},{14,14},{15,15},{16,16},... | collective-permute-start | bytes 76808 | tf_op jit(solution)/shard_map/ppermute | solution.py:372
  6.4 0.7 fusion
  7.1 0.0 copy-start
  7.1 0.7 copy-done
  7.8 0.7 copy-done.2
  8.6 9.9 %shard_map.56.refs_2_ = bf16[400,1024]{1,0:T(8,128)(2,1)} custom-call(s32[6400]{0:T(1024)S(1)} %copy-done, bf16[6400,1024]{1,0:T(8,128)(2,1)} %refs_1_.3, s32[50,128]{1,0:T(8,128)S(1)} %copy-done.2), custom_call_target="tpu_custom_call" | custom-call | flops 24999999488 | tf_op jit(solution)/shard_map/pallas_call | solution.py:158
  18.5 0.7 fusion.1.refs_4_.order_ref
  19.2 0.1 reshape.46.refs_5_.index_ref
  19.3 0.0 collective-permute-done
  19.3 0.7 collective-permute-start.3
  20.0 4.2 %collective-permute-start.2 = (bf16[400,1024]{1,0:T(8,128)(2,1)}, bf16[400,1024]{1,0:T(8,128)(2,1)S(1)}, u32[]{:S(2)}, u32[]{:S(2)}) collective-permute-start(bf16[400,1024]{1,0:T(8,128)(2,1)} %shard_map.56.refs_2_), channel_id=1, source_target_pairs={{0,8},{4,12},{24,16},{28,20},{5,9},{1,13},{29,17},{25,21},{2,10},{... | collective-permute-start | bytes 2457608 | tf_op jit(solution)/shard_map/ppermute | solution.py:378
  24.2 13.3 %shard_map.57 = (bf16[400,1024]{1,0:T(8,128)(2,1)}, bf16[400,1024]{1,0:T(8,128)(2,1)S(1)}, bf16[400,1024]{1,0:T(8,128)(2,1)S(1)}, bf16[400,1024]{1,0:T(8,128)(2,1)S(1)}) custom-call(s32[6400]{0:T(1024)S(1)} %copy-done.1, bf16[6400,1024]{1,0:T(8,128)(2,1)} %refs_1_.3, bf16[400,1024]{1,0:T(8,128)(2,1)} %shard_map.56.refs_2_), custom_call_target="tpu_custom_call" | custom-call | flops 24999999488 | tf_op jit(solution)/shard_map/pallas_call | solution.py:158
  37.5 0.9 copy-done.3
  38.4 1.6 %collective-permute-start.7 = (bf16[400,1024]{1,0:T(8,128)(2,1)}, bf16[400,1024]{1,0:T(8,128)(2,1)}, u32[]{:S(2)}, u32[]{:S(2)}) collective-permute-start(bf16[400,1024]{1,0:T(8,128)(2,1)} %get-tuple-element.24), channel_id=1, source_target_pairs={{12,8},{8,12},{20,16},{16,20},{17,9},{21,13},{9,17},{13,21},{14,10... | collective-permute-start | bytes 2457608 | tf_op jit(solution)/shard_map/ppermute | solution.py:378
  40.0 3.7 %collective-permute-start.1 = (bf16[400,1024]{1,0:T(8,128)(2,1)}, bf16[400,1024]{1,0:T(8,128)(2,1)}, u32[]{:S(2)}, u32[]{:S(2)}) collective-permute-start(bf16[400,1024]{1,0:T(8,128)(2,1)} %get-tuple-element.24), channel_id=1, source_target_pairs={{28,8},{24,12},{4,16},{0,20},{1,9},{5,13},{25,17},{29,21},{30,10},... | collective-permute-start | bytes 2457608 | tf_op jit(solution)/shard_map/ppermute | solution.py:378
  43.7 0.1 reshape.49
  43.8 0.6 gather_fusion
  44.4 0.1 reshape.50.refs_6_.refs_8_.refs_12_.refs_15_.clusters_ref
  44.5 0.0 collective-permute-done.3.refs_2_
  44.5 0.0 collective-permute-done.2.refs_1_
  44.5 5.7 %shard_map.58.refs_9_ = f32[1,6400]{1,0:T(1,128)S(1)} custom-call(bf16[400,1024]{1,0:T(8,128)(2,1)S(1)} %get-tuple-element.29.refs_0_, bf16[400,1024]{1,0:T(8,128)(2,1)S(1)} %collective-permute-done.2.refs_1_, bf16[400,1024]{1,0:T(8,128)(2,1)S(1)} %collective-permute-done.3.refs_2_, bf16[400,1024]{1,0:T(8,128)(2,1)S(1)} %get-tuple-element.27.refs_3_, ...), custom_call_target="tpu_custom_call" | custom-call | tf_op jit(solution)/shard_map/pallas_call | solution.py:261
  50.3 0.7 collective-permute-start.5
  51.0 0.7 collective-permute-start.6
  51.7 6.7 %collective-permute-start.10 = (bf16[400,1024]{1,0:T(8,128)(2,1)}, bf16[400,1024]{1,0:T(8,128)(2,1)S(1)}, u32[]{:S(2)}, u32[]{:S(2)}) collective-permute-start(bf16[400,1024]{1,0:T(8,128)(2,1)} %copy-done.3), channel_id=1, source_target_pairs={{4,8},{0,12},{28,16},{24,20},{25,9},{29,13},{1,17},{5,21},{6,10},{... | collective-permute-start | bytes 2457608 | tf_op jit(solution)/shard_map/ppermute | solution.py:378
  58.4 3.4 %collective-permute-done.1.refs_6_ = bf16[400,1024]{1,0:T(8,128)(2,1)} collective-permute-done((bf16[400,1024]{1,0:T(8,128)(2,1)}, bf16[400,1024]{1,0:T(8,128)(2,1)}, u32[]{:S(2)}, u32[]{:S(2)}) %collective-permute-start.1) | collective-permute-done | bytes 819232 | tf_op jit(solution)/shard_map/ppermute | solution.py:378
  61.8 0.7 collective-permute-start.11
  62.5 0.0 collective-permute-done.7.refs_7_
  62.5 0.7 collective-permute-start.8
  63.3 0.0 collective-permute-done.5.refs_4_
  63.3 0.7 collective-permute-start.9
  64.0 0.0 collective-permute-done.6.refs_5_
  64.0 12.2 %collective-permute-start.4 = (bf16[400,1024]{1,0:T(8,128)(2,1)S(1)}, bf16[400,1024]{1,0:T(8,128)(2,1)S(1)}, u32[]{:S(2)}, u32[]{:S(2)}) collective-permute-start(bf16[400,1024]{1,0:T(8,128)(2,1)S(1)} %get-tuple-element.29.refs_0_), channel_id=1, source_target_pairs={{24,8},{28,12},{0,16},{4,20},{29,9},{25,13},{5,17},{1,21},{26,10},... | collective-permute-start | bytes 2457608 | tf_op jit(solution)/shard_map/ppermute | solution.py:378
  76.2 10.4 %shard_map.59.refs_13_ = f32[1,6400]{1,0:T(1,128)S(1)} custom-call(bf16[400,1024]{1,0:T(8,128)(2,1)S(1)} %get-tuple-element.29.refs_0_, bf16[400,1024]{1,0:T(8,128)(2,1)S(1)} %collective-permute-done.2.refs_1_, bf16[400,1024]{1,0:T(8,128)(2,1)S(1)} %collective-permute-done.3.refs_2_, bf16[400,1024]{1,0:T(8,128)(2,1)S(1)} %get-tuple-element.27.refs_3_, ...), custom_call_target="tpu_custom_call" | custom-call | tf_op jit(solution)/shard_map/pallas_call | solution.py:261
  86.6 0.0 collective-permute-done.11.refs_11_
  86.6 0.0 collective-permute-done.10.refs_10_
  86.6 0.7 collective-permute-start.13
  87.4 0.7 collective-permute-start.14
  88.1 0.0 collective-permute-done.9.refs_9_
  88.1 0.0 collective-permute-done.8.refs_8_
  88.1 13.2 %shard_map.60.refs_16_ = f32[1,6400]{1,0:T(1,128)S(1)} custom-call(bf16[400,1024]{1,0:T(8,128)(2,1)S(1)} %get-tuple-element.29.refs_0_, bf16[400,1024]{1,0:T(8,128)(2,1)S(1)} %collective-permute-done.2.refs_1_, bf16[400,1024]{1,0:T(8,128)(2,1)S(1)} %collective-permute-done.3.refs_2_, bf16[400,1024]{1,0:T(8,128)(2,1)S(1)} %get-tuple-element.27.refs_3_, ...), custom_call_target="tpu_custom_call" | custom-call | tf_op jit(solution)/shard_map/pallas_call | solution.py:261
  101.3 0.9 collective-permute-start.12
  102.3 0.0 collective-permute-done.13.refs_12_
  102.3 0.0 collective-permute-done.14.refs_13_
  102.3 10.6 %shard_map.61.best_ref = f32[1,6400]{1,0:T(1,128)S(1)} custom-call(bf16[400,1024]{1,0:T(8,128)(2,1)S(1)} %get-tuple-element.29.refs_0_, bf16[400,1024]{1,0:T(8,128)(2,1)S(1)} %collective-permute-done.2.refs_1_, bf16[400,1024]{1,0:T(8,128)(2,1)S(1)} %collective-permute-done.3.refs_2_, bf16[400,1024]{1,0:T(8,128)(2,1)S(1)} %get-tuple-element.27.refs_3_, ...), custom_call_target="tpu_custom_call" | custom-call | tf_op jit(solution)/shard_map/pallas_call | solution.py:261
  112.9 1.5 %shard_map.62 = f32[32,2,400]{2,1,0:T(2,128)S(1)} custom-call(s32[16]{0:T(128)S(1)} %fusion.1.refs_4_.order_ref, bf16[400,1024]{1,0:T(8,128)(2,1)S(1)} %collective-permute-done.4.refs_14_.own_ref, bf16[400,1024]{1,0:T(8,128)(2,1)S(1)} %collective-permute-done.12.other_ref, s32[1,6400]{1,0:T(1,128)S(1)} %reshape.50.refs_6_.refs_8_.refs_12_.refs_15_.clusters_ref, ...), custom_call_target="tpu_custom_call" | custom-call | tf_op jit(solution)/shard_map/pallas_call | solution.py:312
  114.4 30.7 %all_to_all.5.values_ref = f32[32,2,400]{2,1,0:T(2,128)S(1)} all-to-all(f32[32,2,400]{2,1,0:T(2,128)S(1)} %shard_map.62), channel_id=1, replica_groups=mesh['shard'=8,'rep'=4] {'shard','rep'}, dimensions={0} | all-to-all | bytes 204800 | tf_op jit(solution)/shard_map/all_to_all | solution.py:411
  145.1 2.4 %shard_map.63 = f32[50,128]{1,0:T(8,128)} custom-call(s32[8,2,400]{2,1,0:T(2,128)S(1)} %reshape.46.refs_5_.index_ref, f32[32,2,400]{2,1,0:T(2,128)S(1)} %all_to_all.5.values_ref), custom_call_target="tpu_custom_call" | custom-call | tf_op jit(solution)/shard_map/pallas_call | solution.py:352
  (8 shorter events, 0.0 us)
Async XLA Ops:
  1.5 17.8 %collective-permute-start = (s32[50,128]{1,0:T(8,128)}, s32[50,128]{1,0:T(8,128)S(1)}, u32[]{:S(2)}, u32[]{:S(2)}) collective-permute-start(s32[50,128]{1,0:T(8,128)} %shard_map.55.refs_2_), channel_id=1, source_target_pairs={{0,8},{1,9},{4,12},{5,13},{10,10},{11,11},{14,14},{15,15},{16,16},... | collective-permute-start | bytes 76808 | tf_op jit(solution)/shard_map/ppermute | solution.py:372
  7.1 0.7 copy-start
  7.8 0.7 copy-start.2
  8.6 10.6 %copy-start.1 = (s32[6400]{0:T(1024)S(1)}, s32[6400]{0:T(1024)}, u32[]{:S(2)}) copy-start(s32[6400]{0:T(1024)} %refs_0_.3) | copy-start | bytes 76804
  19.3 25.2 %collective-permute-start.3 = (bf16[400,1024]{1,0:T(8,128)(2,1)}, bf16[400,1024]{1,0:T(8,128)(2,1)S(1)}, u32[]{:S(2)}, u32[]{:S(2)}) collective-permute-start(bf16[400,1024]{1,0:T(8,128)(2,1)} %shard_map.56.refs_2_), channel_id=1, source_target_pairs={{16,8},{20,12},{8,16},{12,20},{21,9},{17,13},{13,17},{9,21},{18,10... | collective-permute-start | bytes 2457608 | tf_op jit(solution)/shard_map/ppermute | solution.py:378
  20.0 24.5 %collective-permute-start.2 = (bf16[400,1024]{1,0:T(8,128)(2,1)}, bf16[400,1024]{1,0:T(8,128)(2,1)S(1)}, u32[]{:S(2)}, u32[]{:S(2)}) collective-permute-start(bf16[400,1024]{1,0:T(8,128)(2,1)} %shard_map.56.refs_2_), channel_id=1, source_target_pairs={{0,8},{4,12},{24,16},{28,20},{5,9},{1,13},{29,17},{25,21},{2,10},{... | collective-permute-start | bytes 2457608 | tf_op jit(solution)/shard_map/ppermute | solution.py:378
  37.5 0.9 copy-start.3
  38.4 24.1 %collective-permute-start.7 = (bf16[400,1024]{1,0:T(8,128)(2,1)}, bf16[400,1024]{1,0:T(8,128)(2,1)}, u32[]{:S(2)}, u32[]{:S(2)}) collective-permute-start(bf16[400,1024]{1,0:T(8,128)(2,1)} %get-tuple-element.24), channel_id=1, source_target_pairs={{12,8},{8,12},{20,16},{16,20},{17,9},{21,13},{9,17},{13,21},{14,10... | collective-permute-start | bytes 2457608 | tf_op jit(solution)/shard_map/ppermute | solution.py:378
  40.0 21.8 %collective-permute-start.1 = (bf16[400,1024]{1,0:T(8,128)(2,1)}, bf16[400,1024]{1,0:T(8,128)(2,1)}, u32[]{:S(2)}, u32[]{:S(2)}) collective-permute-start(bf16[400,1024]{1,0:T(8,128)(2,1)} %get-tuple-element.24), channel_id=1, source_target_pairs={{28,8},{24,12},{4,16},{0,20},{1,9},{5,13},{25,17},{29,21},{30,10},... | collective-permute-start | bytes 2457608 | tf_op jit(solution)/shard_map/ppermute | solution.py:378
  50.3 13.0 %collective-permute-start.5 = (bf16[400,1024]{1,0:T(8,128)(2,1)S(1)}, bf16[400,1024]{1,0:T(8,128)(2,1)S(1)}, u32[]{:S(2)}, u32[]{:S(2)}) collective-permute-start(bf16[400,1024]{1,0:T(8,128)(2,1)S(1)} %collective-permute-done.2.refs_1_), channel_id=1, source_target_pairs={{8,9},{9,8},{10,11},{11,10},{12,13},{13,12},{14,15},{15,14},{16,17... | collective-permute-start | bytes 2457608 | tf_op jit(solution)/shard_map/ppermute | solution.py:381
  51.0 13.0 %collective-permute-start.6 = (bf16[400,1024]{1,0:T(8,128)(2,1)S(1)}, bf16[400,1024]{1,0:T(8,128)(2,1)S(1)}, u32[]{:S(2)}, u32[]{:S(2)}) collective-permute-start(bf16[400,1024]{1,0:T(8,128)(2,1)S(1)} %collective-permute-done.3.refs_2_), channel_id=1, source_target_pairs={{8,9},{9,8},{10,11},{11,10},{12,13},{13,12},{14,15},{15,14},{16,17... | collective-permute-start | bytes 2457608 | tf_op jit(solution)/shard_map/ppermute | solution.py:381
  51.7 34.9 %collective-permute-start.10 = (bf16[400,1024]{1,0:T(8,128)(2,1)}, bf16[400,1024]{1,0:T(8,128)(2,1)S(1)}, u32[]{:S(2)}, u32[]{:S(2)}) collective-permute-start(bf16[400,1024]{1,0:T(8,128)(2,1)} %copy-done.3), channel_id=1, source_target_pairs={{4,8},{0,12},{28,16},{24,20},{25,9},{29,13},{1,17},{5,21},{6,10},{... | collective-permute-start | bytes 2457608 | tf_op jit(solution)/shard_map/ppermute | solution.py:378
  61.8 24.8 %collective-permute-start.11 = (bf16[400,1024]{1,0:T(8,128)(2,1)}, bf16[400,1024]{1,0:T(8,128)(2,1)S(1)}, u32[]{:S(2)}, u32[]{:S(2)}) collective-permute-start(bf16[400,1024]{1,0:T(8,128)(2,1)} %copy-done.3), channel_id=1, source_target_pairs={{20,8},{16,12},{12,16},{8,20},{13,9},{9,13},{21,17},{17,21},{22,10... | collective-permute-start | bytes 2457608 | tf_op jit(solution)/shard_map/ppermute | solution.py:378
  62.5 25.6 %collective-permute-start.8 = (bf16[400,1024]{1,0:T(8,128)(2,1)}, bf16[400,1024]{1,0:T(8,128)(2,1)S(1)}, u32[]{:S(2)}, u32[]{:S(2)}) collective-permute-start(bf16[400,1024]{1,0:T(8,128)(2,1)} %collective-permute-done.1.refs_6_), channel_id=1, source_target_pairs={{8,9},{9,8},{10,11},{11,10},{12,13},{13,12},{14,15},{15,14},{16,17... | collective-permute-start | bytes 2457608 | tf_op jit(solution)/shard_map/ppermute | solution.py:381
  63.3 24.8 %collective-permute-start.9 = (bf16[400,1024]{1,0:T(8,128)(2,1)}, bf16[400,1024]{1,0:T(8,128)(2,1)S(1)}, u32[]{:S(2)}, u32[]{:S(2)}) collective-permute-start(bf16[400,1024]{1,0:T(8,128)(2,1)} %collective-permute-done.7.refs_7_), channel_id=1, source_target_pairs={{8,9},{9,8},{10,11},{11,10},{12,13},{13,12},{14,15},{15,14},{16,17... | collective-permute-start | bytes 2457608 | tf_op jit(solution)/shard_map/ppermute | solution.py:381
  64.0 37.3 %collective-permute-start.4 = (bf16[400,1024]{1,0:T(8,128)(2,1)S(1)}, bf16[400,1024]{1,0:T(8,128)(2,1)S(1)}, u32[]{:S(2)}, u32[]{:S(2)}) collective-permute-start(bf16[400,1024]{1,0:T(8,128)(2,1)S(1)} %get-tuple-element.29.refs_0_), channel_id=1, source_target_pairs={{24,8},{28,12},{0,16},{4,20},{29,9},{25,13},{5,17},{1,21},{26,10},... | collective-permute-start | bytes 2457608 | tf_op jit(solution)/shard_map/ppermute | solution.py:378
  86.6 15.6 %collective-permute-start.13 = (bf16[400,1024]{1,0:T(8,128)(2,1)S(1)}, bf16[400,1024]{1,0:T(8,128)(2,1)S(1)}, u32[]{:S(2)}, u32[]{:S(2)}) collective-permute-start(bf16[400,1024]{1,0:T(8,128)(2,1)S(1)} %collective-permute-done.10.refs_10_), channel_id=1, source_target_pairs={{8,9},{9,8},{10,11},{11,10},{12,13},{13,12},{14,15},{15,14},{16,17... | collective-permute-start | bytes 2457608 | tf_op jit(solution)/shard_map/ppermute | solution.py:381
  87.4 14.9 %collective-permute-start.14 = (bf16[400,1024]{1,0:T(8,128)(2,1)S(1)}, bf16[400,1024]{1,0:T(8,128)(2,1)S(1)}, u32[]{:S(2)}, u32[]{:S(2)}) collective-permute-start(bf16[400,1024]{1,0:T(8,128)(2,1)S(1)} %collective-permute-done.11.refs_11_), channel_id=1, source_target_pairs={{8,9},{9,8},{10,11},{11,10},{12,13},{13,12},{14,15},{15,14},{16,17... | collective-permute-start | bytes 2457608 | tf_op jit(solution)/shard_map/ppermute | solution.py:381
  101.3 11.6 %collective-permute-start.12 = (bf16[400,1024]{1,0:T(8,128)(2,1)S(1)}, bf16[400,1024]{1,0:T(8,128)(2,1)S(1)}, u32[]{:S(2)}, u32[]{:S(2)}) collective-permute-start(bf16[400,1024]{1,0:T(8,128)(2,1)S(1)} %collective-permute-done.4.refs_14_.own_ref), channel_id=1, source_target_pairs={{8,9},{9,8},{10,11},{11,10},{12,13},{13,12},{14,15},{15,14},{16,17... | collective-permute-start | bytes 2457608 | tf_op jit(solution)/shard_map/ppermute | solution.py:381

commit v8 on v7

--- a/solution.py
+++ b/solution.py
@@ -150,7 +150,7 @@
         lax.fori_loop(0, size // group, pick, 0)
 
 
-def gather_rows(embeddings, index, slots, size, after=()):
+def gather_rows(embeddings, index, slots, size):
     documents, width = embeddings.shape
     count = len(slots)
     sections = 10
@@ -158,8 +158,7 @@
     return pl.pallas_call(
         functools.partial(gather_kernel, slots, size, group, sections),
         out_shape=[jax.ShapeDtypeStruct((size, width), jnp.bfloat16)] * count,
-        in_specs=[pl.BlockSpec(memory_space=pltpu.HBM)] * 2
-        + [pl.BlockSpec(memory_space=pl.ANY)] * len(after),
+        in_specs=[pl.BlockSpec(memory_space=pltpu.HBM)] * 2,
         out_specs=[pl.BlockSpec(memory_space=pltpu.VMEM)] * count,
         scratch_shapes=[
             pltpu.SMEM(index.shape, jnp.int32),
@@ -170,7 +169,7 @@
         ],
         compiler_params=pltpu.CompilerParams(vmem_limit_bytes=45 * MIB),
         cost_estimate=pl.CostEstimate(flops=LONG, bytes_accessed=0, transcendentals=0),
-    )(index, embeddings, *after)
+    )(index, embeddings)
 
 
 def best_of_rows(acc, size):
@@ -183,14 +182,22 @@
     return jnp.transpose(jnp.broadcast_to(row, (LANES, wide)))[:size]
 
 
-def gram_kernel(passes, loads, size, limit, *refs):
-    chunks = refs[: len(loads)]
-    cluster_row, before_ref, best_ref, held, acc, sems = refs[-6:]
+def gram_kernel(passes, loads, carry, size, limit, *refs):
+    cluster_row, before_ref, best_ref, pair_ref, held, acc, sems = refs[-7:]
+    count = len(loads)
     first = range(passes[0][0], passes[0][0] + passes[0][1])
 
+    def source(i):
+        array, place = loads[i]
+        return refs[array].at[pl.ds(place * size, size)]
+
     def copy(i):
-        rows = held.at[pl.ds(i * size, size)]
-        return pltpu.make_async_copy(chunks[loads.index(i)], rows, sems.at[i])
+        return pltpu.make_async_copy(source(i), held.at[pl.ds(i * size, size)], sems.at[i])
+
+    handed = [
+        pltpu.make_async_copy(source(i), pair_ref.at[pl.ds(n * size, size)], sems.at[count + n])
+        for n, i in enumerate(carry)
+    ]
 
     def arrive(i):
         rows = held.at[pl.ds(0, size)]
@@ -198,9 +205,11 @@
 
     for i in first:
         copy(i).start()
-    for i in loads:
+    for i in range(count):
         if i not in first:
             copy(i).start()
+    for item in handed:
+        item.start()
     best_ref[...] = before_ref[...]
     for i in first:
         copy(i).wait()
@@ -241,38 +250,65 @@
 
         lax.fori_loop(0, groups, visit, 0)
         if n == 0:
-            for i in loads:
+            for i in range(count):
                 if i not in first and not i < min(2 * groups, first[0]):
                     arrive(i)
         for t in last:
             tile(t * BLK, True)
         span = slice(chunk * size, chunk * size + height)
         best_ref[:, span] = jnp.maximum(best_ref[:, span], best_of_rows(acc[...], height))
-
-
-def gram_best(chunks, size, cluster_row, before, passes, after=()):
-    loads = tuple(range(len(chunks)))
-    width = chunks[0].shape[1]
-    total = before.shape[1]
-    limit = (max(loads) + 1) * size
+    for item in handed:
+        item.wait()
+
+
+def gram_best(arrays, loads, size, cluster_row, before, passes, carry=(), after=()):
+    width = arrays[0].shape[1]
+    limit = len(loads) * size
     held = -(-limit // BLK) * BLK
     tall = max(news for _, news, *_ in passes) * size
     padded = -(-tall // LANES) * LANES
     return pl.pallas_call(
-        functools.partial(gram_kernel, passes, loads, size, limit),
-        out_shape=jax.ShapeDtypeStruct((1, total), jnp.float32),
-        in_specs=[pl.BlockSpec(memory_space=pl.ANY)] * len(loads)
-        + [pl.BlockSpec(memory_space=pl.ANY)] * len(after)
+        functools.partial(gram_kernel, passes, loads, carry, size, limit),
+        out_shape=[
+            jax.ShapeDtypeStruct(before.shape, jnp.float32),
+            jax.ShapeDtypeStruct((max(1, len(carry)) * size, width), jnp.bfloat16),
+        ],
+        in_specs=[pl.BlockSpec(memory_space=pl.ANY)] * (len(arrays) + len(after))
         + [pl.BlockSpec(memory_space=pltpu.VMEM)] * 2,
-        out_specs=pl.BlockSpec(memory_space=pltpu.VMEM),
+        out_specs=[pl.BlockSpec(memory_space=pltpu.VMEM), pl.BlockSpec(memory_space=pl.ANY)],
         scratch_shapes=[
             pltpu.VMEM((held, width), jnp.bfloat16),
             pltpu.VMEM((padded, LANES), jnp.float32),
-            pltpu.SemaphoreType.DMA((max(loads) + 1,)),
+            pltpu.SemaphoreType.DMA((len(loads) + len(carry),)),
         ],
         compiler_params=pltpu.CompilerParams(vmem_limit_bytes=24 * MIB),
         cost_estimate=pl.CostEstimate(flops=0, bytes_accessed=0, transcendentals=0),
-    )(*chunks, *after, cluster_row, before)
+    )(*arrays, *after, cluster_row, before)
+
+
+def join_kernel(first_ref, second_ref, out_ref, sems):
+    size = first_ref.shape[0]
+    copies = [
+        pltpu.make_async_copy(ref, out_ref.at[pl.ds(i * size, size)], sems.at[i])
+        for i, ref in enumerate((first_ref, second_ref))
+    ]
+    for copy in copies:
+        copy.start()
+    for copy in copies:
+        copy.wait()
+
+
+def join(first, second, work):
+    size, width = first.shape
+    return pl.pallas_call(
+        join_kernel,
+        out_shape=jax.ShapeDtypeStruct((2 * size, width), first.dtype),
+        in_specs=[pl.BlockSpec(memory_space=pl.ANY)] * 2,
+        out_specs=pl.BlockSpec(memory_space=pl.ANY),
+        scratch_shapes=[pltpu.SemaphoreType.DMA((2,))],
+        compiler_params=pltpu.CompilerParams(vmem_limit_bytes=MIB),
+        cost_estimate=pl.CostEstimate(flops=work, bytes_accessed=0, transcendentals=0),
+    )(first, second)
 
 
 def new_pass(chunk, news, count, size):
@@ -364,14 +400,12 @@
 def hosted(embeddings, send_index, place_index, slot_cluster):
     documents = embeddings.shape[0]
     size = send_index.shape[0] // 16
-    s, rep = lax.axis_index("shard"), lax.axis_index("rep")
     axes = ("shard", "rep")
-    order = jnp.asarray(chunk_order())[s, rep]
     named = arrival_names(place_index, slot_cluster)
-    (early,) = gather_rows(embeddings, send_index, (0,), size, (named,))
+    embeddings = tie(embeddings, named)
+    (early,) = gather_rows(embeddings, send_index, (0,), size)
     named = lax.ppermute(named, axes, metadata_pairs())
     early = tie(early, named)
-    clusters = named.reshape(16, size)[order]
     index = send_index.reshape(8, 2, size)
 
     def go(step, chunk):
@@ -382,31 +416,45 @@
 
     own, other = [None] * 8, [None] * 8
     own[1], own[2] = go(1, early), go(2, early)
-    late = gather_rows(embeddings, send_index, (1, 2, 3, 4), size, (early,))
+    late = gather_rows(tie(embeddings, early), send_index, (1, 2, 3, 4), size)
     own[0], other[0] = late[2:]
     own[3], own[4] = go(3, late[0]), go(4, late[0])
-    flat = clusters.reshape(1, 16 * size)
-
-    def score(best, count, passes, after=()):
-        chunks = [(own, other)[side][r] for r, side in CHUNKS[:count]]
-        return gram_best(chunks, size, flat, best, passes, after)
-
     own[1], own[2] = tie(own[1], late[0]), tie(own[2], late[0])
     own[5] = go(5, tie(late[1], own[1]))
     own[6] = go(6, tie(late[1], own[2]))
+
+    named, table = tie(named, late[0]), tie(jnp.asarray(chunk_order()), late[0])
+    order = table[lax.axis_index("shard"), lax.axis_index("rep")]
+    flat = named.reshape(16, size)[order].reshape(1, 16 * size)
+
+    def score(best, count, passes, carry=(), after=()):
+        arrays, loads = [], []
+        for r, side in CHUNKS[:count]:
+            chunk = (own, other)[side][r]
+            array, place = chunk if isinstance(chunk, tuple) else (chunk, 0)
+            if not any(array is known for known in arrays):
+                arrays.append(array)
+            loads.append(([array is known for known in arrays].index(True), place))
+        return gram_best(arrays, tuple(loads), size, flat, best, passes, carry, after)
+
     best = jnp.full((1, 16 * size), -1.0, jnp.float32)
-    best = score(best, 4, (new_pass(0, 3, 4, size),), (order, index))
-    other[1], other[2] = swap(tie(own[1], best)), swap(tie(own[2], best))
-    own[3], own[4] = tie(own[3], best), tie(own[4], best)
-    other[3], other[4] = swap(own[3]), swap(own[4])
+    best, pair = score(best, 4, (new_pass(0, 3, 4, size),), (1, 2), (order, index))
+    pair = swap(pair)
+    other[1], other[2] = (pair, 0), (pair, 1)
+    early_pair = join(tie(own[3], best), tie(own[4], best), LONG // 2)
     own[7] = go(7, tie(late[2], own[3]))
-    best = score(best, 8, (new_pass(6, 2, 8, size), late_pass(1, 2, 4, 6, size)))
-    own[5], own[6] = tie(own[5], best), tie(own[6], best)
-    other[5], other[6] = swap(own[5]), swap(own[6])
-    best = score(best, 12, (new_pass(10, 2, 12, size), late_pass(6, 2, 8, 10, size)))
+    pair = swap(early_pair)
+    own[3], own[4] = (early_pair, 0), (early_pair, 1)
+    best, _ = score(best, 8, (new_pass(6, 2, 8, size), late_pass(1, 2, 4, 6, size)))
+    other[3], other[4] = (pair, 0), (pair, 1)
+    late_pair = join(tie(own[5], best), tie(own[6], best), LONG // 2)
+    pair = swap(late_pair)
+    own[5], own[6] = (late_pair, 0), (late_pair, 1)
+    best, _ = score(best, 12, (new_pass(10, 2, 12, size), late_pass(6, 2, 8, 10, size)))
+    other[5], other[6] = (pair, 0), (pair, 1)
     own[7] = tie(own[7], best)
     other[7] = swap(own[7])
-    best = score(best, 15, (new_pass(14, 1, 15, size), late_pass(10, 2, 12, 14, size)))
+    best, _ = score(best, 15, (new_pass(14, 1, 15, size), late_pass(10, 2, 12, 14, size)))
     outbound = finish(order, own[7], other[7], flat, best)
     returned = lax.all_to_all(outbound, axes, split_axis=0, concat_axis=0, tiled=True)
     sources = []
@@ -437,7 +485,8 @@
     tiles = tuple(range(documents // BLK))
     passes = ((0, news, 0, 1, True, tiles),)
     chunks = [arrived[i] for i in range(parts)]
-    best = gram_best(chunks, size, clusters.reshape(1, -1), best, passes)
+    loads = tuple((i, 0) for i in range(parts))
+    best, _ = gram_best(chunks, loads, size, clusters.reshape(1, -1), best, passes)
     best = lax.all_gather(best[0, : news * size], "rep", axis=0, tiled=True)
     returned = lax.all_to_all(
         best.reshape(owners, share), "shard", split_axis=0, concat_axis=0, tiled=True

time: 148 us -> 149 us (level)
  starting transfers between devices: 39.9 us -> 30.8 us
  waiting for transfers between devices: 3.43 us -> 10.2 us
  blocking collectives: 30.7 us -> 33.2 us
    ppermute x7, starting transfers between devices: 29.8 us -> 22.7 us  [go(): return lax.ppermute(chunk, axes, round_pairs(step - 1))]
    ppermute x7, waiting for transfers between devices: 3.41 us -> 10.2 us  [go(): return lax.ppermute(chunk, axes, round_pairs(step - 1))]
    all_to_all x1, blocking collectives: 30.7 us -> 33.2 us  [hosted(): lax.all_to_all(outbound, axes, split_axis=0, concat_axis=0, tiled=True)]
    ppermute x7 -> x4, starting transfers between devices: 5.21 us -> 3.23 us  [swap(): return lax.ppermute(chunk, axes, SIBLINGS)]
    pallas_call x4 -> x6, Pallas kernels: 39.9 us -> 41.3 us  [the longest x4 39.7 us: gram_best(): pl.pallas_call(functools.partial(gram_kernel, passes, loads, carry, size,...]
  transfers between devices with their start and end apart: 15 -> 12, of which waited for: 1 -> 2; matrix products, arithmetic and copies ran while one was open for 2% -> 2% of each run, Pallas kernels for 43% -> 43%
where the time goes in v8:
time: 149 us; the launch traced here: 148 us
  Pallas kernels  69.8 us (47%)
  blocking collectives  33.2 us (22%)
  starting transfers between devices  30.8 us (21%)
  waiting for transfers between devices  10.2 us (7%)
  local copies, waits for them, and re-layouts  3.21 us (2%)
    pallas_call x4, Pallas kernels, gram_best(): pl.pallas_call(functools.partial(gram_kernel, passes, loads, carry, size,...  39.7 us
    all_to_all x1, blocking collectives, hosted(): lax.all_to_all(outbound, axes, split_axis=0, concat_axis=0, tiled=True)  33.2 us
    pallas_call x2, Pallas kernels, gather_rows(): pl.pallas_call(functools.partial(gather_kernel, slots, size, group, secti...  23.2 us
    ppermute x7, starting transfers between devices, go(): return lax.ppermute(chunk, axes, round_pairs(step - 1))  22.7 us
    ppermute x7, waiting for transfers between devices, go(): return lax.ppermute(chunk, axes, round_pairs(step - 1))  10.2 us
    ppermute x1, starting transfers between devices, hosted(): named = lax.ppermute(named, axes, metadata_pairs())  4.92 us
    ppermute x4, starting transfers between devices, swap(): return lax.ppermute(chunk, axes, SIBLINGS)  3.23 us
  transfers between devices with their start and end apart: 12, of which 2 were waited for; matrix products, arithmetic and copies ran while one was open for 2% of the time, Pallas kernels for 43%

profile of v8, /device:TPU:0, one launch (start us, length us, event | category | flops | bytes accessed | tf_op | source)
XLA Modules:
  0.0 148.3 jit_solution(13534153390234311326)
XLA Ops:
  0.0 1.5 shard_map.55
  1.5 4.9 %collective-permute-start = (s32[50,128]{1,0:T(8,128)}, s32[50,128]{1,0:T(8,128)S(1)}, u32[]{:S(2)}, u32[]{:S(2)}) collective-permute-start(s32[50,128]{1,0:T(8,128)} %shard_map.55), channel_id=1, source_target_pairs={{0,8},{1,9},{4,12},{5,13},{10,10},{11,11},{14,14},{15,15},{16,16},... | collective-permute-start | bytes 76808 | tf_op jit(solution)/shard_map/ppermute | solution.py:407
  6.4 0.0 copy-start
  6.4 0.7 copy-done
  7.1 9.9 %shard_map.56 = bf16[400,1024]{1,0:T(8,128)(2,1)} custom-call(s32[6400]{0:T(1024)S(1)} %copy-done, bf16[6400,1024]{1,0:T(8,128)(2,1)} %refs_1_.1), custom_call_target="tpu_custom_call" | custom-call | flops 24999999488 | tf_op jit(solution)/shard_map/pallas_call | solution.py:158
  17.1 0.0 copy-start.1
  17.1 0.0 collective-permute-done
  17.1 1.3 collective-permute-start.3
  18.5 0.7 collective-permute-start.4
  19.2 13.2 %shard_map.57 = (bf16[400,1024]{1,0:T(8,128)(2,1)}, bf16[400,1024]{1,0:T(8,128)(2,1)S(1)}, bf16[400,1024]{1,0:T(8,128)(2,1)S(1)}, bf16[400,1024]{1,0:T(8,128)(2,1)S(1)}) custom-call(s32[6400]{0:T(1024)S(1)} %copy-done, bf16[6400,1024]{1,0:T(8,128)(2,1)} %refs_1_.1), custom_call_target="tpu_custom_call" | custom-call | flops 24999999488 | tf_op jit(solution)/shard_map/pallas_call | solution.py:158
  32.4 0.0 copy-start.2
  32.4 0.9 copy-done.2
  33.3 1.6 %collective-permute-start.6 = (bf16[400,1024]{1,0:T(8,128)(2,1)}, bf16[400,1024]{1,0:T(8,128)(2,1)}, u32[]{:S(2)}, u32[]{:S(2)}) collective-permute-start(bf16[400,1024]{1,0:T(8,128)(2,1)} %get-tuple-element.32), channel_id=1, source_target_pairs={{12,8},{8,12},{20,16},{16,20},{17,9},{21,13},{9,17},{13,21},{14,10... | collective-permute-start | bytes 2457608 | tf_op jit(solution)/shard_map/ppermute | solution.py:412
  34.9 6.6 %collective-permute-start.1 = (bf16[400,1024]{1,0:T(8,128)(2,1)}, bf16[400,1024]{1,0:T(8,128)(2,1)}, u32[]{:S(2)}, u32[]{:S(2)}) collective-permute-start(bf16[400,1024]{1,0:T(8,128)(2,1)} %get-tuple-element.32), channel_id=1, source_target_pairs={{28,8},{24,12},{4,16},{0,20},{1,9},{5,13},{25,17},{29,21},{30,10},... | collective-permute-start | bytes 2457608 | tf_op jit(solution)/shard_map/ppermute | solution.py:412
  41.5 0.0 copy-done.1
  41.5 0.1 reshape.46.refs_5_.index_ref
  41.6 0.1 reshape.49
  41.7 0.7 fusion
  42.4 0.6 gather_fusion
  42.9 0.1 reshape.50.refs_6_.refs_8_.refs_10_.clusters_ref
  43.1 0.7 fusion.1.refs_4_.order_ref
  43.8 0.0 collective-permute-done.3.refs_1_
  43.8 0.0 collective-permute-done.4.refs_2_
  43.8 5.9 %shard_map.58 = (f32[1,6400]{1,0:T(1,128)S(1)}, bf16[800,1024]{1,0:T(8,128)(2,1)S(1)}) custom-call(bf16[400,1024]{1,0:T(8,128)(2,1)S(1)} %get-tuple-element.35.refs_0_, bf16[400,1024]{1,0:T(8,128)(2,1)S(1)} %collective-permute-done.3.refs_1_, bf16[400,1024]{1,0:T(8,128)(2,1)S(1)} %collective-permute-done.4.refs_2_, ...), custom_call_target="tpu_custom_call" | custom-call | tf_op jit(solution)/shard_map/pallas_call | solution.py:270
  49.7 0.8 collective-permute-start.5
  50.5 0.0 collective-permute-done.6.second_ref
  50.5 7.3 %collective-permute-done.1.first_ref = bf16[400,1024]{1,0:T(8,128)(2,1)} collective-permute-done((bf16[400,1024]{1,0:T(8,128)(2,1)}, bf16[400,1024]{1,0:T(8,128)(2,1)}, u32[]{:S(2)}, u32[]{:S(2)}) %collective-permute-start.1) | collective-permute-done | bytes 819232 | tf_op jit(solution)/shard_map/ppermute | solution.py:412
  57.8 0.7 collective-permute-start.9
  58.5 8.0 %collective-permute-start.8 = (bf16[400,1024]{1,0:T(8,128)(2,1)S(1)}, bf16[400,1024]{1,0:T(8,128)(2,1)S(1)}, u32[]{:S(2)}, u32[]{:S(2)}) collective-permute-start(bf16[400,1024]{1,0:T(8,128)(2,1)S(1)} %copy-done.3), channel_id=1, source_target_pairs={{4,8},{0,12},{28,16},{24,20},{25,9},{29,13},{1,17},{5,21},{6,10},{... | collective-permute-start | bytes 2457608 | tf_op jit(solution)/shard_map/ppermute | solution.py:412
  66.5 1.4 shard_map.59.refs_5_
  67.9 0.8 collective-permute-start.7
  68.7 3.8 %collective-permute-start.2 = (bf16[400,1024]{1,0:T(8,128)(2,1)S(1)}, bf16[400,1024]{1,0:T(8,128)(2,1)S(1)}, u32[]{:S(2)}, u32[]{:S(2)}) collective-permute-start(bf16[400,1024]{1,0:T(8,128)(2,1)S(1)} %get-tuple-element.35.refs_0_), channel_id=1, source_target_pairs={{24,8},{28,12},{0,16},{4,20},{29,9},{25,13},{5,17},{1,21},{26,10},... | collective-permute-start | bytes 2457608 | tf_op jit(solution)/shard_map/ppermute | solution.py:412
  72.5 0.0 collective-permute-done.5.refs_4_
  72.5 9.7 %shard_map.60 = (f32[1,6400]{1,0:T(1,128)S(1)}, bf16[400,1024]{1,0:T(8,128)(2,1)}) custom-call(bf16[400,1024]{1,0:T(8,128)(2,1)S(1)} %get-tuple-element.35.refs_0_, bf16[400,1024]{1,0:T(8,128)(2,1)S(1)} %collective-permute-done.3.refs_1_, bf16[400,1024]{1,0:T(8,128)(2,1)S(1)} %collective-permute-done.4.refs_2_, ...), custom_call_target="tpu_custom_call" | custom-call | tf_op jit(solution)/shard_map/pallas_call | solution.py:270
  82.3 0.0 collective-permute-done.9.second_ref
  82.3 2.9 %collective-permute-done.8.first_ref = bf16[400,1024]{1,0:T(8,128)(2,1)S(1)} collective-permute-done((bf16[400,1024]{1,0:T(8,128)(2,1)S(1)}, bf16[400,1024]{1,0:T(8,128)(2,1)S(1)}, u32[]{:S(2)}, u32[]{:S(2)}) %collective-permute-start.8) | collective-permute-done | bytes 819232 | tf_op jit(solution)/shard_map/ppermute | solution.py:412
  85.2 0.2 shard_map.61.refs_7_
  85.4 0.8 collective-permute-start.11
  86.1 0.0 collective-permute-done.7.refs_6_
  86.2 13.3 %shard_map.62 = (f32[1,6400]{1,0:T(1,128)S(1)}, bf16[400,1024]{1,0:T(8,128)(2,1)}) custom-call(bf16[400,1024]{1,0:T(8,128)(2,1)S(1)} %get-tuple-element.35.refs_0_, bf16[400,1024]{1,0:T(8,128)(2,1)S(1)} %collective-permute-done.3.refs_1_, bf16[400,1024]{1,0:T(8,128)(2,1)S(1)} %collective-permute-done.4.refs_2_, ...), custom_call_target="tpu_custom_call" | custom-call | tf_op jit(solution)/shard_map/pallas_call | solution.py:270
  99.5 0.0 collective-permute-done.2.refs_9_.own_ref
  99.5 0.9 collective-permute-start.10
  100.4 0.0 collective-permute-done.11.refs_8_
  100.5 10.7 %shard_map.63 = (f32[1,6400]{1,0:T(1,128)S(1)}, bf16[400,1024]{1,0:T(8,128)(2,1)}) custom-call(bf16[400,1024]{1,0:T(8,128)(2,1)S(1)} %get-tuple-element.35.refs_0_, bf16[400,1024]{1,0:T(8,128)(2,1)S(1)} %collective-permute-done.3.refs_1_, bf16[400,1024]{1,0:T(8,128)(2,1)S(1)} %collective-permute-done.4.refs_2_, ...), custom_call_target="tpu_custom_call" | custom-call | tf_op jit(solution)/shard_map/pallas_call | solution.py:270
  111.2 0.0 collective-permute-done.10.other_ref
  111.2 1.5 %shard_map.64 = f32[32,2,400]{2,1,0:T(2,128)S(1)} custom-call(s32[16]{0:T(128)S(1)} %fusion.1.refs_4_.order_ref, bf16[400,1024]{1,0:T(8,128)(2,1)S(1)} %collective-permute-done.2.refs_9_.own_ref, bf16[400,1024]{1,0:T(8,128)(2,1)S(1)} %collective-permute-done.10.other_ref, s32[1,6400]{1,0:T(1,128)S(1)} %reshape.50.refs_6_.refs_8_.refs_10_.clusters_ref, ...), custom_call_target="tpu_custom_call" | custom-call | tf_op jit(solution)/shard_map/pallas_call | solution.py:348
  112.7 33.2 %all_to_all.5.values_ref = f32[32,2,400]{2,1,0:T(2,128)S(1)} all-to-all(f32[32,2,400]{2,1,0:T(2,128)S(1)} %shard_map.64), channel_id=1, replica_groups=mesh['shard'=8,'rep'=4] {'shard','rep'}, dimensions={0} | all-to-all | bytes 204800 | tf_op jit(solution)/shard_map/all_to_all | solution.py:459
  145.9 2.4 %shard_map.65 = f32[50,128]{1,0:T(8,128)} custom-call(s32[8,2,400]{2,1,0:T(2,128)S(1)} %reshape.46.refs_5_.index_ref, f32[32,2,400]{2,1,0:T(2,128)S(1)} %all_to_all.5.values_ref), custom_call_target="tpu_custom_call" | custom-call | tf_op jit(solution)/shard_map/pallas_call | solution.py:388
  (4 shorter events, 0.0 us)
Async XLA Ops:
  1.5 15.6 %collective-permute-start = (s32[50,128]{1,0:T(8,128)}, s32[50,128]{1,0:T(8,128)S(1)}, u32[]{:S(2)}, u32[]{:S(2)}) collective-permute-start(s32[50,128]{1,0:T(8,128)} %shard_map.55), channel_id=1, source_target_pairs={{0,8},{1,9},{4,12},{5,13},{10,10},{11,11},{14,14},{15,15},{16,16},... | collective-permute-start | bytes 76808 | tf_op jit(solution)/shard_map/ppermute | solution.py:407
  6.4 0.8 copy-start
  17.1 24.4 %copy-start.1 = (s32[6400]{0:T(1024)S(1)}, s32[6400]{0:T(1024)}, u32[]{:S(2)}) copy-start(s32[6400]{0:T(1024)} %refs_0_.3) | copy-start | bytes 76804
  17.1 26.7 %collective-permute-start.3 = (bf16[400,1024]{1,0:T(8,128)(2,1)}, bf16[400,1024]{1,0:T(8,128)(2,1)S(1)}, u32[]{:S(2)}, u32[]{:S(2)}) collective-permute-start(bf16[400,1024]{1,0:T(8,128)(2,1)} %shard_map.56), channel_id=1, source_target_pairs={{0,8},{4,12},{24,16},{28,20},{5,9},{1,13},{29,17},{25,21},{2,10},{... | collective-permute-start | bytes 2457608 | tf_op jit(solution)/shard_map/ppermute | solution.py:412
  18.5 25.3 %collective-permute-start.4 = (bf16[400,1024]{1,0:T(8,128)(2,1)}, bf16[400,1024]{1,0:T(8,128)(2,1)S(1)}, u32[]{:S(2)}, u32[]{:S(2)}) collective-permute-start(bf16[400,1024]{1,0:T(8,128)(2,1)} %shard_map.56), channel_id=1, source_target_pairs={{16,8},{20,12},{8,16},{12,20},{21,9},{17,13},{13,17},{9,21},{18,10... | collective-permute-start | bytes 2457608 | tf_op jit(solution)/shard_map/ppermute | solution.py:412
  32.4 0.9 copy-start.2
  33.3 17.2 %collective-permute-start.6 = (bf16[400,1024]{1,0:T(8,128)(2,1)}, bf16[400,1024]{1,0:T(8,128)(2,1)}, u32[]{:S(2)}, u32[]{:S(2)}) collective-permute-start(bf16[400,1024]{1,0:T(8,128)(2,1)} %get-tuple-element.32), channel_id=1, source_target_pairs={{12,8},{8,12},{20,16},{16,20},{17,9},{21,13},{9,17},{13,21},{14,10... | collective-permute-start | bytes 2457608 | tf_op jit(solution)/shard_map/ppermute | solution.py:412
  34.9 23.0 %collective-permute-start.1 = (bf16[400,1024]{1,0:T(8,128)(2,1)}, bf16[400,1024]{1,0:T(8,128)(2,1)}, u32[]{:S(2)}, u32[]{:S(2)}) collective-permute-start(bf16[400,1024]{1,0:T(8,128)(2,1)} %get-tuple-element.32), channel_id=1, source_target_pairs={{28,8},{24,12},{4,16},{0,20},{1,9},{5,13},{25,17},{29,21},{30,10},... | collective-permute-start | bytes 2457608 | tf_op jit(solution)/shard_map/ppermute | solution.py:412
  43.8 14.1 %copy-start.3 = (bf16[400,1024]{1,0:T(8,128)(2,1)S(1)}, bf16[400,1024]{1,0:T(8,128)(2,1)}, u32[]{:S(2)}) copy-start(bf16[400,1024]{1,0:T(8,128)(2,1)} %copy-done.2) | copy-start | bytes 2457604
  49.7 22.8 %collective-permute-start.5 = (bf16[800,1024]{1,0:T(8,128)(2,1)S(1)}, bf16[800,1024]{1,0:T(8,128)(2,1)S(1)}, u32[]{:S(2)}, u32[]{:S(2)}) collective-permute-start(bf16[800,1024]{1,0:T(8,128)(2,1)S(1)} %get-tuple-element.40), channel_id=1, source_target_pairs={{8,9},{9,8},{10,11},{11,10},{12,13},{13,12},{14,15},{15,14},{16,17... | collective-permute-start | bytes 4915208 | tf_op jit(solution)/shard_map/ppermute | solution.py:415
  57.8 24.4 %collective-permute-start.9 = (bf16[400,1024]{1,0:T(8,128)(2,1)S(1)}, bf16[400,1024]{1,0:T(8,128)(2,1)S(1)}, u32[]{:S(2)}, u32[]{:S(2)}) collective-permute-start(bf16[400,1024]{1,0:T(8,128)(2,1)S(1)} %copy-done.3), channel_id=1, source_target_pairs={{20,8},{16,12},{12,16},{8,20},{13,9},{9,13},{21,17},{17,21},{22,10... | collective-permute-start | bytes 2457608 | tf_op jit(solution)/shard_map/ppermute | solution.py:412
  58.5 26.6 %collective-permute-start.8 = (bf16[400,1024]{1,0:T(8,128)(2,1)S(1)}, bf16[400,1024]{1,0:T(8,128)(2,1)S(1)}, u32[]{:S(2)}, u32[]{:S(2)}) collective-permute-start(bf16[400,1024]{1,0:T(8,128)(2,1)S(1)} %copy-done.3), channel_id=1, source_target_pairs={{4,8},{0,12},{28,16},{24,20},{25,9},{29,13},{1,17},{5,21},{6,10},{... | collective-permute-start | bytes 2457608 | tf_op jit(solution)/shard_map/ppermute | solution.py:412
  67.9 18.2 %collective-permute-start.7 = (bf16[800,1024]{1,0:T(8,128)(2,1)S(1)}, bf16[800,1024]{1,0:T(8,128)(2,1)S(1)}, u32[]{:S(2)}, u32[]{:S(2)}) collective-permute-start(bf16[800,1024]{1,0:T(8,128)(2,1)S(1)} %shard_map.59.refs_5_), channel_id=1, source_target_pairs={{8,9},{9,8},{10,11},{11,10},{12,13},{13,12},{14,15},{15,14},{16,17... | collective-permute-start | bytes 4915208 | tf_op jit(solution)/shard_map/ppermute | solution.py:415
  68.7 30.8 %collective-permute-start.2 = (bf16[400,1024]{1,0:T(8,128)(2,1)S(1)}, bf16[400,1024]{1,0:T(8,128)(2,1)S(1)}, u32[]{:S(2)}, u32[]{:S(2)}) collective-permute-start(bf16[400,1024]{1,0:T(8,128)(2,1)S(1)} %get-tuple-element.35.refs_0_), channel_id=1, source_target_pairs={{24,8},{28,12},{0,16},{4,20},{29,9},{25,13},{5,17},{1,21},{26,10},... | collective-permute-start | bytes 2457608 | tf_op jit(solution)/shard_map/ppermute | solution.py:412
  85.4 15.1 %collective-permute-start.11 = (bf16[800,1024]{1,0:T(8,128)(2,1)S(1)}, bf16[800,1024]{1,0:T(8,128)(2,1)S(1)}, u32[]{:S(2)}, u32[]{:S(2)}) collective-permute-start(bf16[800,1024]{1,0:T(8,128)(2,1)S(1)} %shard_map.61.refs_7_), channel_id=1, source_target_pairs={{8,9},{9,8},{10,11},{11,10},{12,13},{13,12},{14,15},{15,14},{16,17... | collective-permute-start | bytes 4915208 | tf_op jit(solution)/shard_map/ppermute | solution.py:415
  99.5 11.7 %collective-permute-start.10 = (bf16[400,1024]{1,0:T(8,128)(2,1)S(1)}, bf16[400,1024]{1,0:T(8,128)(2,1)S(1)}, u32[]{:S(2)}, u32[]{:S(2)}) collective-permute-start(bf16[400,1024]{1,0:T(8,128)(2,1)S(1)} %collective-permute-done.2.refs_9_.own_ref), channel_id=1, source_target_pairs={{8,9},{9,8},{10,11},{11,10},{12,13},{13,12},{14,15},{15,14},{16,17... | collective-permute-start | bytes 2457608 | tf_op jit(solution)/shard_map/ppermute | solution.py:415

commit v9 on v8

--- a/solution.py
+++ b/solution.py
@@ -12,16 +12,17 @@
 LANES = 128
 NT = (((1,), (1,)), ((), ()))
 MIB = 1024 * 1024
-LONG = 25_000_000_000
+LONG = 40_000_000_000
+SHORT = 2_000_000_000
 
 HOSTS = (2, 3, 4, 5)
-ROUNDS = ((2, 6, 5, 1, 3, 7, 4), (3, 7, 2, 6, 4, 1, 5))
+ROUNDS = ((2, 6, 3, 7, 4, 1, 5), (3, 7, 2, 6, 5, 1, 4))
 
 
 CHUNKS = (
-    (0, 0), (1, 0), (2, 0), (0, 1),
-    (1, 1), (2, 1), (3, 0), (4, 0),
-    (3, 1), (4, 1), (5, 0), (6, 0),
+    (0, 1), (0, 0), (1, 0), (2, 0),
+    (3, 0), (4, 0), (1, 1),
+    (2, 1), (3, 1), (4, 1), (5, 0), (6, 0),
     (5, 1), (6, 1), (7, 0), (7, 1),
 )
 
@@ -182,8 +183,8 @@
     return jnp.transpose(jnp.broadcast_to(row, (LANES, wide)))[:size]
 
 
-def gram_kernel(passes, loads, carry, size, limit, *refs):
-    cluster_row, before_ref, best_ref, pair_ref, held, acc, sems = refs[-7:]
+def gram_kernel(passes, loads, size, limit, *refs):
+    cluster_row, before_ref, best_ref, held, acc, sems = refs[-6:]
     count = len(loads)
     first = range(passes[0][0], passes[0][0] + passes[0][1])
 
@@ -193,11 +194,6 @@
 
     def copy(i):
         return pltpu.make_async_copy(source(i), held.at[pl.ds(i * size, size)], sems.at[i])
-
-    handed = [
-        pltpu.make_async_copy(source(i), pair_ref.at[pl.ds(n * size, size)], sems.at[count + n])
-        for n, i in enumerate(carry)
-    ]
 
     def arrive(i):
         rows = held.at[pl.ds(0, size)]
@@ -208,8 +204,6 @@
     for i in range(count):
         if i not in first:
             copy(i).start()
-    for item in handed:
-        item.start()
     best_ref[...] = before_ref[...]
     for i in first:
         copy(i).wait()
@@ -257,40 +251,35 @@
             tile(t * BLK, True)
         span = slice(chunk * size, chunk * size + height)
         best_ref[:, span] = jnp.maximum(best_ref[:, span], best_of_rows(acc[...], height))
-    for item in handed:
-        item.wait()
-
-
-def gram_best(arrays, loads, size, cluster_row, before, passes, carry=(), after=()):
+
+
+def gram_best(arrays, loads, size, cluster_row, before, passes, after=()):
     width = arrays[0].shape[1]
     limit = len(loads) * size
     held = -(-limit // BLK) * BLK
     tall = max(news for _, news, *_ in passes) * size
     padded = -(-tall // LANES) * LANES
     return pl.pallas_call(
-        functools.partial(gram_kernel, passes, loads, carry, size, limit),
-        out_shape=[
-            jax.ShapeDtypeStruct(before.shape, jnp.float32),
-            jax.ShapeDtypeStruct((max(1, len(carry)) * size, width), jnp.bfloat16),
-        ],
+        functools.partial(gram_kernel, passes, loads, size, limit),
+        out_shape=jax.ShapeDtypeStruct(before.shape, jnp.float32),
         in_specs=[pl.BlockSpec(memory_space=pl.ANY)] * (len(arrays) + len(after))
         + [pl.BlockSpec(memory_space=pltpu.VMEM)] * 2,
-        out_specs=[pl.BlockSpec(memory_space=pltpu.VMEM), pl.BlockSpec(memory_space=pl.ANY)],
+        out_specs=pl.BlockSpec(memory_space=pltpu.VMEM),
         scratch_shapes=[
             pltpu.VMEM((held, width), jnp.bfloat16),
             pltpu.VMEM((padded, LANES), jnp.float32),
-            pltpu.SemaphoreType.DMA((len(loads) + len(carry),)),
+            pltpu.SemaphoreType.DMA((len(loads),)),
         ],
         compiler_params=pltpu.CompilerParams(vmem_limit_bytes=24 * MIB),
         cost_estimate=pl.CostEstimate(flops=0, bytes_accessed=0, transcendentals=0),
     )(*arrays, *after, cluster_row, before)
 
 
-def join_kernel(first_ref, second_ref, out_ref, sems):
-    size = first_ref.shape[0]
+def join_kernel(size, *refs):
+    out_ref, sems = refs[-2:]
     copies = [
         pltpu.make_async_copy(ref, out_ref.at[pl.ds(i * size, size)], sems.at[i])
-        for i, ref in enumerate((first_ref, second_ref))
+        for i, ref in enumerate(refs[:-2])
     ]
     for copy in copies:
         copy.start()
@@ -298,17 +287,17 @@
         copy.wait()
 
 
-def join(first, second, work):
-    size, width = first.shape
+def join(chunks, work):
+    size, width = chunks[0].shape
     return pl.pallas_call(
-        join_kernel,
-        out_shape=jax.ShapeDtypeStruct((2 * size, width), first.dtype),
-        in_specs=[pl.BlockSpec(memory_space=pl.ANY)] * 2,
+        functools.partial(join_kernel, size),
+        out_shape=jax.ShapeDtypeStruct((len(chunks) * size, width), chunks[0].dtype),
+        in_specs=[pl.BlockSpec(memory_space=pl.ANY)] * len(chunks),
         out_specs=pl.BlockSpec(memory_space=pl.ANY),
-        scratch_shapes=[pltpu.SemaphoreType.DMA((2,))],
+        scratch_shapes=[pltpu.SemaphoreType.DMA((len(chunks),))],
         compiler_params=pltpu.CompilerParams(vmem_limit_bytes=MIB),
         cost_estimate=pl.CostEstimate(flops=work, bytes_accessed=0, transcendentals=0),
-    )(first, second)
+    )(*chunks)
 
 
 def new_pass(chunk, news, count, size):
@@ -427,7 +416,7 @@
     order = table[lax.axis_index("shard"), lax.axis_index("rep")]
     flat = named.reshape(16, size)[order].reshape(1, 16 * size)
 
-    def score(best, count, passes, carry=(), after=()):
+    def score(best, count, passes, after=()):
         arrays, loads = [], []
         for r, side in CHUNKS[:count]:
             chunk = (own, other)[side][r]
@@ -435,26 +424,25 @@
             if not any(array is known for known in arrays):
                 arrays.append(array)
             loads.append(([array is known for known in arrays].index(True), place))
-        return gram_best(arrays, tuple(loads), size, flat, best, passes, carry, after)
+        return gram_best(arrays, tuple(loads), size, flat, best, passes, after)
 
     best = jnp.full((1, 16 * size), -1.0, jnp.float32)
-    best, pair = score(best, 4, (new_pass(0, 3, 4, size),), (1, 2), (order, index))
-    pair = swap(pair)
-    other[1], other[2] = (pair, 0), (pair, 1)
-    early_pair = join(tie(own[3], best), tie(own[4], best), LONG // 2)
+    best = score(best, 4, (new_pass(1, 3, 4, size),), (order, index))
+    other[1] = swap(tie(own[1], best))
+    joined = join([own[2], tie(own[3], best), tie(own[4], best)], SHORT)
     own[7] = go(7, tie(late[2], own[3]))
-    pair = swap(early_pair)
-    own[3], own[4] = (early_pair, 0), (early_pair, 1)
-    best, _ = score(best, 8, (new_pass(6, 2, 8, size), late_pass(1, 2, 4, 6, size)))
-    other[3], other[4] = (pair, 0), (pair, 1)
-    late_pair = join(tie(own[5], best), tie(own[6], best), LONG // 2)
-    pair = swap(late_pair)
-    own[5], own[6] = (late_pair, 0), (late_pair, 1)
-    best, _ = score(best, 12, (new_pass(10, 2, 12, size), late_pass(6, 2, 8, 10, size)))
-    other[5], other[6] = (pair, 0), (pair, 1)
+    swapped = swap(joined)
+    own[3], own[4] = (joined, 1), (joined, 2)
+    best = score(best, 7, (new_pass(4, 2, 7, size), late_pass(2, 2, 6, 7, size)))
+    other[2], other[3], other[4] = (swapped, 0), (swapped, 1), (swapped, 2)
+    joined = join([tie(own[5], best), tie(own[6], best)], LONG)
+    swapped = swap(joined)
+    own[5], own[6] = (joined, 0), (joined, 1)
+    best = score(best, 12, (new_pass(10, 2, 12, size), late_pass(3, 3, 7, 10, size)))
+    other[5], other[6] = (swapped, 0), (swapped, 1)
     own[7] = tie(own[7], best)
     other[7] = swap(own[7])
-    best, _ = score(best, 15, (new_pass(14, 1, 15, size), late_pass(10, 2, 12, 14, size)))
+    best = score(best, 15, (new_pass(14, 1, 15, size), late_pass(10, 2, 12, 14, size)))
     outbound = finish(order, own[7], other[7], flat, best)
     returned = lax.all_to_all(outbound, axes, split_axis=0, concat_axis=0, tiled=True)
     sources = []
@@ -486,7 +474,7 @@
     passes = ((0, news, 0, 1, True, tiles),)
     chunks = [arrived[i] for i in range(parts)]
     loads = tuple((i, 0) for i in range(parts))
-    best, _ = gram_best(chunks, loads, size, clusters.reshape(1, -1), best, passes)
+    best = gram_best(chunks, loads, size, clusters.reshape(1, -1), best, passes)
     best = lax.all_gather(best[0, : news * size], "rep", axis=0, tiled=True)
     returned = lax.all_to_all(
         best.reshape(owners, share), "shard", split_axis=0, concat_axis=0, tiled=True

time: 149 us -> 141 us (0.946)
  waiting for transfers between devices: 10.2 us -> 4.16 us
  blocking collectives: 33.2 us -> 31.4 us
    ppermute x7, waiting for transfers between devices: 10.2 us -> 4.15 us  [go(): return lax.ppermute(chunk, axes, round_pairs(step - 1))]
    all_to_all x1, blocking collectives: 33.2 us -> 31.4 us  [hosted(): lax.all_to_all(outbound, axes, split_axis=0, concat_axis=0, tiled=True)]
  transfers between devices with their start and end apart: 12 -> 12, of which waited for: 2 -> 2; matrix products, arithmetic and copies ran while one was open for 2% -> 2% of each run, Pallas kernels for 43% -> 46%
where the time goes in v9:
time: 141 us; the launch traced here: 140 us
  Pallas kernels  70.1 us (50%)
  blocking collectives  31.4 us (22%)
  starting transfers between devices  30.5 us (22%)
  waiting for transfers between devices  4.16 us (3%)
  local copies, waits for them, and re-layouts  3.3 us (2%)
    pallas_call x4, Pallas kernels, gram_best(): pl.pallas_call(functools.partial(gram_kernel, passes, loads, size, limit)...  39.8 us
    all_to_all x1, blocking collectives, hosted(): lax.all_to_all(outbound, axes, split_axis=0, concat_axis=0, tiled=True)  31.4 us
    pallas_call x2, Pallas kernels, gather_rows(): pl.pallas_call(functools.partial(gather_kernel, slots, size, group, secti...  23.2 us
    ppermute x7, starting transfers between devices, go(): return lax.ppermute(chunk, axes, round_pairs(step - 1))  22.1 us
    ppermute x1, starting transfers between devices, hosted(): named = lax.ppermute(named, axes, metadata_pairs())  4.92 us
    ppermute x7, waiting for transfers between devices, go(): return lax.ppermute(chunk, axes, round_pairs(step - 1))  4.15 us
    ppermute x4, starting transfers between devices, swap(): return lax.ppermute(chunk, axes, SIBLINGS)  3.41 us
  transfers between devices with their start and end apart: 12, of which 2 were waited for; matrix products, arithmetic and copies ran while one was open for 2% of the time, Pallas kernels for 46%

profile of v9, /device:TPU:0, one launch (start us, length us, event | category | flops | bytes accessed | tf_op | source)
XLA Modules:
  0.0 140.4 jit_solution(3419480864661132373)
XLA Ops:
  0.0 1.5 %shard_map.55 = s32[50,128]{1,0:T(8,128)} custom-call(s32[50,128]{1,0:T(8,128)} %bitcast.9, s32[52,128]{1,0:T(8,128)} %bitcast.10), custom_call_target="tpu_custom_call" | custom-call | tf_op jit(solution)/shard_map/pallas_call | solution.py:87
  1.5 4.9 %collective-permute-start = (s32[50,128]{1,0:T(8,128)}, s32[50,128]{1,0:T(8,128)S(1)}, u32[]{:S(2)}, u32[]{:S(2)}) collective-permute-start(s32[50,128]{1,0:T(8,128)} %shard_map.55), channel_id=1, source_target_pairs={{0,8},{1,9},{4,12},{5,13},{10,10},{11,11},{14,14},{15,15},{16,16},... | collective-permute-start | bytes 76808 | tf_op jit(solution)/shard_map/ppermute | solution.py:396
  6.4 0.0 copy-start
  6.4 0.7 copy-done
  7.1 9.9 %shard_map.56 = bf16[400,1024]{1,0:T(8,128)(2,1)} custom-call(s32[6400]{0:T(1024)S(1)} %copy-done, bf16[6400,1024]{1,0:T(8,128)(2,1)} %refs_1_.1), custom_call_target="tpu_custom_call" | custom-call | flops 40000000000 | tf_op jit(solution)/shard_map/pallas_call | solution.py:159
  17.1 0.0 copy-done.1
  17.1 0.1 reshape.46.refs_5_.index_ref
  17.2 0.0 collective-permute-done
  17.2 0.7 collective-permute-start.4
  17.9 4.2 %collective-permute-start.3 = (bf16[400,1024]{1,0:T(8,128)(2,1)}, bf16[400,1024]{1,0:T(8,128)(2,1)S(1)}, u32[]{:S(2)}, u32[]{:S(2)}) collective-permute-start(bf16[400,1024]{1,0:T(8,128)(2,1)} %shard_map.56), channel_id=1, source_target_pairs={{0,8},{4,12},{24,16},{28,20},{5,9},{1,13},{29,17},{25,21},{2,10},{... | collective-permute-start | bytes 2457608 | tf_op jit(solution)/shard_map/ppermute | solution.py:401
  22.2 13.2 %shard_map.57 = (bf16[400,1024]{1,0:T(8,128)(2,1)}, bf16[400,1024]{1,0:T(8,128)(2,1)S(1)}, bf16[400,1024]{1,0:T(8,128)(2,1)S(1)}, bf16[400,1024]{1,0:T(8,128)(2,1)S(1)}) custom-call(s32[6400]{0:T(1024)S(1)} %copy-done.1, bf16[6400,1024]{1,0:T(8,128)(2,1)} %refs_1_.1), custom_call_target="tpu_custom_call" | custom-call | flops 40000000000 | tf_op jit(solution)/shard_map/pallas_call | solution.py:159
  35.4 0.9 copy-done.2
  36.3 1.6 %collective-permute-start.5 = (bf16[400,1024]{1,0:T(8,128)(2,1)}, bf16[400,1024]{1,0:T(8,128)(2,1)}, u32[]{:S(2)}, u32[]{:S(2)}) collective-permute-start(bf16[400,1024]{1,0:T(8,128)(2,1)} %get-tuple-element.28), channel_id=1, source_target_pairs={{20,8},{16,12},{12,16},{8,20},{17,9},{21,13},{9,17},{13,21},{22,10... | collective-permute-start | bytes 2457608 | tf_op jit(solution)/shard_map/ppermute | solution.py:401
  37.9 3.7 %collective-permute-start.1 = (bf16[400,1024]{1,0:T(8,128)(2,1)}, bf16[400,1024]{1,0:T(8,128)(2,1)}, u32[]{:S(2)}, u32[]{:S(2)}) collective-permute-start(bf16[400,1024]{1,0:T(8,128)(2,1)} %get-tuple-element.28), channel_id=1, source_target_pairs={{4,8},{0,12},{28,16},{24,20},{1,9},{5,13},{25,17},{29,21},{6,10},{... | collective-permute-start | bytes 2457608 | tf_op jit(solution)/shard_map/ppermute | solution.py:401
  41.6 0.1 reshape.49
  41.7 0.7 fusion
  42.4 0.6 gather_fusion
  43.0 0.1 reshape.50.refs_6_.refs_8_.refs_10_.clusters_ref
  43.1 0.0 copy-start.3
  43.1 0.8 fusion.1.refs_4_.order_ref
  43.9 0.0 collective-permute-done.4.refs_3_.refs_0_
  43.9 0.0 collective-permute-done.3.refs_2_
  43.9 5.9 %shard_map.58.refs_7_ = f32[1,6400]{1,0:T(1,128)S(1)} custom-call(bf16[400,1024]{1,0:T(8,128)(2,1)S(1)} %get-tuple-element.32.refs_0_, bf16[400,1024]{1,0:T(8,128)(2,1)S(1)} %get-tuple-element.31.refs_1_, bf16[400,1024]{1,0:T(8,128)(2,1)S(1)} %collective-permute-done.3.refs_2_, bf16[400,1024]{1,0:T(8,128)(2,1)S(1)} %collective-permute-done.4.refs_3_.refs_0_, ...), custom_call_target="tpu_custom_call" | custom-call | tf_op jit(solution)/shard_map/pallas_call | solution.py:262
  49.8 0.7 collective-permute-start.6
  50.5 0.0 copy-done.3
  50.5 0.7 collective-permute-start.9
  51.2 4.7 %collective-permute-start.8 = (bf16[400,1024]{1,0:T(8,128)(2,1)S(1)}, bf16[400,1024]{1,0:T(8,128)(2,1)S(1)}, u32[]{:S(2)}, u32[]{:S(2)}) collective-permute-start(bf16[400,1024]{1,0:T(8,128)(2,1)S(1)} %copy-done.3), channel_id=1, source_target_pairs={{24,8},{28,12},{0,16},{4,20},{29,9},{25,13},{5,17},{1,21},{26,10},... | collective-permute-start | bytes 2457608 | tf_op jit(solution)/shard_map/ppermute | solution.py:401
  55.9 0.0 collective-permute-done.5.refs_2_
  55.9 3.4 %collective-permute-done.1.refs_1_ = bf16[400,1024]{1,0:T(8,128)(2,1)} collective-permute-done((bf16[400,1024]{1,0:T(8,128)(2,1)}, bf16[400,1024]{1,0:T(8,128)(2,1)}, u32[]{:S(2)}, u32[]{:S(2)}) %collective-permute-start.1) | collective-permute-done | bytes 819232 | tf_op jit(solution)/shard_map/ppermute | solution.py:401
  59.4 6.5 %collective-permute-start.2 = (bf16[400,1024]{1,0:T(8,128)(2,1)S(1)}, bf16[400,1024]{1,0:T(8,128)(2,1)S(1)}, u32[]{:S(2)}, u32[]{:S(2)}) collective-permute-start(bf16[400,1024]{1,0:T(8,128)(2,1)S(1)} %get-tuple-element.31.refs_1_), channel_id=1, source_target_pairs={{28,8},{24,12},{4,16},{0,20},{25,9},{29,13},{1,17},{5,21},{30,10},... | collective-permute-start | bytes 2457608 | tf_op jit(solution)/shard_map/ppermute | solution.py:401
  65.9 1.5 %shard_map.59.refs_4_ = bf16[1200,1024]{1,0:T(8,128)(2,1)S(1)} custom-call(bf16[400,1024]{1,0:T(8,128)(2,1)S(1)} %collective-permute-done.4.refs_3_.refs_0_, bf16[400,1024]{1,0:T(8,128)(2,1)} %collective-permute-done.1.refs_1_, bf16[400,1024]{1,0:T(8,128)(2,1)} %collective-permute-done.5.refs_2_), custom_call_target="tpu_custom_call" | custom-call | flops 2000000000 | tf_op jit(solution)/shard_map/pallas_call | solution.py:292
  67.4 1.0 collective-permute-start.7
  68.5 0.0 collective-permute-done.6.refs_5_
  68.5 7.7 %shard_map.60.refs_9_ = f32[1,6400]{1,0:T(1,128)S(1)} custom-call(bf16[400,1024]{1,0:T(8,128)(2,1)S(1)} %get-tuple-element.32.refs_0_, bf16[400,1024]{1,0:T(8,128)(2,1)S(1)} %get-tuple-element.31.refs_1_, bf16[400,1024]{1,0:T(8,128)(2,1)S(1)} %collective-permute-done.3.refs_2_, bf16[400,1024]{1,0:T(8,128)(2,1)S(1)} %collective-permute-done.4.refs_3_.refs_0_, ...), custom_call_target="tpu_custom_call" | custom-call | tf_op jit(solution)/shard_map/pallas_call | solution.py:262
  76.1 0.0 collective-permute-done.9.refs_1_
  76.1 0.7 collective-permute-done.8.refs_0_
  76.8 0.2 shard_map.61.refs_7_
  77.0 0.8 collective-permute-start.11
  77.8 0.0 collective-permute-done.7.refs_6_
  77.8 15.6 %shard_map.62.refs_11_ = f32[1,6400]{1,0:T(1,128)S(1)} custom-call(bf16[400,1024]{1,0:T(8,128)(2,1)S(1)} %get-tuple-element.32.refs_0_, bf16[400,1024]{1,0:T(8,128)(2,1)S(1)} %get-tuple-element.31.refs_1_, bf16[400,1024]{1,0:T(8,128)(2,1)S(1)} %collective-permute-done.3.refs_2_, bf16[400,1024]{1,0:T(8,128)(2,1)S(1)} %collective-permute-done.4.refs_3_.refs_0_, ...), custom_call_target="tpu_custom_call" | custom-call | tf_op jit(solution)/shard_map/pallas_call | solution.py:262
  93.4 0.0 collective-permute-done.2.refs_9_.own_ref
  93.4 0.9 collective-permute-start.10
  94.3 0.0 collective-permute-done.11.refs_8_
  94.4 10.7 %shard_map.63.best_ref = f32[1,6400]{1,0:T(1,128)S(1)} custom-call(bf16[400,1024]{1,0:T(8,128)(2,1)S(1)} %get-tuple-element.32.refs_0_, bf16[400,1024]{1,0:T(8,128)(2,1)S(1)} %get-tuple-element.31.refs_1_, bf16[400,1024]{1,0:T(8,128)(2,1)S(1)} %collective-permute-done.3.refs_2_, bf16[400,1024]{1,0:T(8,128)(2,1)S(1)} %collective-permute-done.4.refs_3_.refs_0_, ...), custom_call_target="tpu_custom_call" | custom-call | tf_op jit(solution)/shard_map/pallas_call | solution.py:262
  105.1 0.0 collective-permute-done.10.other_ref
  105.1 1.5 %shard_map.64 = f32[32,2,400]{2,1,0:T(2,128)S(1)} custom-call(s32[16]{0:T(128)S(1)} %fusion.1.refs_4_.order_ref, bf16[400,1024]{1,0:T(8,128)(2,1)S(1)} %collective-permute-done.2.refs_9_.own_ref, bf16[400,1024]{1,0:T(8,128)(2,1)S(1)} %collective-permute-done.10.other_ref, s32[1,6400]{1,0:T(1,128)S(1)} %reshape.50.refs_6_.refs_8_.refs_10_.clusters_ref, ...), custom_call_target="tpu_custom_call" | custom-call | tf_op jit(solution)/shard_map/pallas_call | solution.py:337
  106.6 31.4 %all_to_all.5.values_ref = f32[32,2,400]{2,1,0:T(2,128)S(1)} all-to-all(f32[32,2,400]{2,1,0:T(2,128)S(1)} %shard_map.64), channel_id=1, replica_groups=mesh['shard'=8,'rep'=4] {'shard','rep'}, dimensions={0} | all-to-all | bytes 204800 | tf_op jit(solution)/shard_map/all_to_all | solution.py:447
  138.0 2.4 %shard_map.65 = f32[50,128]{1,0:T(8,128)} custom-call(s32[8,2,400]{2,1,0:T(2,128)S(1)} %reshape.46.refs_5_.index_ref, f32[32,2,400]{2,1,0:T(2,128)S(1)} %all_to_all.5.values_ref), custom_call_target="tpu_custom_call" | custom-call | tf_op jit(solution)/shard_map/pallas_call | solution.py:377
  (4 shorter events, 0.0 us)
Async XLA Ops:
  1.5 15.7 %collective-permute-start = (s32[50,128]{1,0:T(8,128)}, s32[50,128]{1,0:T(8,128)S(1)}, u32[]{:S(2)}, u32[]{:S(2)}) collective-permute-start(s32[50,128]{1,0:T(8,128)} %shard_map.55), channel_id=1, source_target_pairs={{0,8},{1,9},{4,12},{5,13},{10,10},{11,11},{14,14},{15,15},{16,16},... | collective-permute-start | bytes 76808 | tf_op jit(solution)/shard_map/ppermute | solution.py:396
  6.4 0.8 copy-start
  7.1 10.0 %copy-start.1 = (s32[6400]{0:T(1024)S(1)}, s32[6400]{0:T(1024)}, u32[]{:S(2)}) copy-start(s32[6400]{0:T(1024)} %refs_0_.3) | copy-start | bytes 76804
  17.2 26.6 %collective-permute-start.4 = (bf16[400,1024]{1,0:T(8,128)(2,1)}, bf16[400,1024]{1,0:T(8,128)(2,1)S(1)}, u32[]{:S(2)}, u32[]{:S(2)}) collective-permute-start(bf16[400,1024]{1,0:T(8,128)(2,1)} %shard_map.56), channel_id=1, source_target_pairs={{16,8},{20,12},{8,16},{12,20},{21,9},{17,13},{13,17},{9,21},{18,10... | collective-permute-start | bytes 2457608 | tf_op jit(solution)/shard_map/ppermute | solution.py:401
  17.9 25.9 %collective-permute-start.3 = (bf16[400,1024]{1,0:T(8,128)(2,1)}, bf16[400,1024]{1,0:T(8,128)(2,1)S(1)}, u32[]{:S(2)}, u32[]{:S(2)}) collective-permute-start(bf16[400,1024]{1,0:T(8,128)(2,1)} %shard_map.56), channel_id=1, source_target_pairs={{0,8},{4,12},{24,16},{28,20},{5,9},{1,13},{29,17},{25,21},{2,10},{... | collective-permute-start | bytes 2457608 | tf_op jit(solution)/shard_map/ppermute | solution.py:401
  35.4 0.9 copy-start.2
  36.3 19.6 %collective-permute-start.5 = (bf16[400,1024]{1,0:T(8,128)(2,1)}, bf16[400,1024]{1,0:T(8,128)(2,1)}, u32[]{:S(2)}, u32[]{:S(2)}) collective-permute-start(bf16[400,1024]{1,0:T(8,128)(2,1)} %get-tuple-element.28), channel_id=1, source_target_pairs={{20,8},{16,12},{12,16},{8,20},{17,9},{21,13},{9,17},{13,21},{22,10... | collective-permute-start | bytes 2457608 | tf_op jit(solution)/shard_map/ppermute | solution.py:401
  37.9 21.5 %collective-permute-start.1 = (bf16[400,1024]{1,0:T(8,128)(2,1)}, bf16[400,1024]{1,0:T(8,128)(2,1)}, u32[]{:S(2)}, u32[]{:S(2)}) collective-permute-start(bf16[400,1024]{1,0:T(8,128)(2,1)} %get-tuple-element.28), channel_id=1, source_target_pairs={{4,8},{0,12},{28,16},{24,20},{1,9},{5,13},{25,17},{29,21},{6,10},{... | collective-permute-start | bytes 2457608 | tf_op jit(solution)/shard_map/ppermute | solution.py:401
  43.1 7.4 %copy-start.3 = (bf16[400,1024]{1,0:T(8,128)(2,1)S(1)}, bf16[400,1024]{1,0:T(8,128)(2,1)}, u32[]{:S(2)}) copy-start(bf16[400,1024]{1,0:T(8,128)(2,1)} %copy-done.2) | copy-start | bytes 2457604
  49.8 18.7 %collective-permute-start.6 = (bf16[400,1024]{1,0:T(8,128)(2,1)S(1)}, bf16[400,1024]{1,0:T(8,128)(2,1)S(1)}, u32[]{:S(2)}, u32[]{:S(2)}) collective-permute-start(bf16[400,1024]{1,0:T(8,128)(2,1)S(1)} %collective-permute-done.3.refs_2_), channel_id=1, source_target_pairs={{8,9},{9,8},{10,11},{11,10},{12,13},{13,12},{14,15},{15,14},{16,17... | collective-permute-start | bytes 2457608 | tf_op jit(solution)/shard_map/ppermute | solution.py:404
  50.5 25.6 %collective-permute-start.9 = (bf16[400,1024]{1,0:T(8,128)(2,1)S(1)}, bf16[400,1024]{1,0:T(8,128)(2,1)S(1)}, u32[]{:S(2)}, u32[]{:S(2)}) collective-permute-start(bf16[400,1024]{1,0:T(8,128)(2,1)S(1)} %copy-done.3), channel_id=1, source_target_pairs={{12,8},{8,12},{20,16},{16,20},{13,9},{9,13},{21,17},{17,21},{14,10... | collective-permute-start | bytes 2457608 | tf_op jit(solution)/shard_map/ppermute | solution.py:401
  51.2 25.6 %collective-permute-start.8 = (bf16[400,1024]{1,0:T(8,128)(2,1)S(1)}, bf16[400,1024]{1,0:T(8,128)(2,1)S(1)}, u32[]{:S(2)}, u32[]{:S(2)}) collective-permute-start(bf16[400,1024]{1,0:T(8,128)(2,1)S(1)} %copy-done.3), channel_id=1, source_target_pairs={{24,8},{28,12},{0,16},{4,20},{29,9},{25,13},{5,17},{1,21},{26,10},... | collective-permute-start | bytes 2457608 | tf_op jit(solution)/shard_map/ppermute | solution.py:401
  59.4 34.0 %collective-permute-start.2 = (bf16[400,1024]{1,0:T(8,128)(2,1)S(1)}, bf16[400,1024]{1,0:T(8,128)(2,1)S(1)}, u32[]{:S(2)}, u32[]{:S(2)}) collective-permute-start(bf16[400,1024]{1,0:T(8,128)(2,1)S(1)} %get-tuple-element.31.refs_1_), channel_id=1, source_target_pairs={{28,8},{24,12},{4,16},{0,20},{25,9},{29,13},{1,17},{5,21},{30,10},... | collective-permute-start | bytes 2457608 | tf_op jit(solution)/shard_map/ppermute | solution.py:401
  67.4 10.4 %collective-permute-start.7 = (bf16[1200,1024]{1,0:T(8,128)(2,1)S(1)}, bf16[1200,1024]{1,0:T(8,128)(2,1)S(1)}, u32[]{:S(2)}, u32[]{:S(2)}) collective-permute-start(bf16[1200,1024]{1,0:T(8,128)(2,1)S(1)} %shard_map.59.refs_4_), channel_id=1, source_target_pairs={{8,9},{9,8},{10,11},{11,10},{12,13},{13,12},{14,15},{15,14},{16,17... | collective-permute-start | bytes 7372808 | tf_op jit(solution)/shard_map/ppermute | solution.py:404
  77.0 17.3 %collective-permute-start.11 = (bf16[800,1024]{1,0:T(8,128)(2,1)S(1)}, bf16[800,1024]{1,0:T(8,128)(2,1)S(1)}, u32[]{:S(2)}, u32[]{:S(2)}) collective-permute-start(bf16[800,1024]{1,0:T(8,128)(2,1)S(1)} %shard_map.61.refs_7_), channel_id=1, source_target_pairs={{8,9},{9,8},{10,11},{11,10},{12,13},{13,12},{14,15},{15,14},{16,17... | collective-permute-start | bytes 4915208 | tf_op jit(solution)/shard_map/ppermute | solution.py:404
  93.4 11.7 %collective-permute-start.10 = (bf16[400,1024]{1,0:T(8,128)(2,1)S(1)}, bf16[400,1024]{1,0:T(8,128)(2,1)S(1)}, u32[]{:S(2)}, u32[]{:S(2)}) collective-permute-start(bf16[400,1024]{1,0:T(8,128)(2,1)S(1)} %collective-permute-done.2.refs_9_.own_ref), channel_id=1, source_target_pairs={{8,9},{9,8},{10,11},{11,10},{12,13},{13,12},{14,15},{15,14},{16,17... | collective-permute-start | bytes 2457608 | tf_op jit(solution)/shard_map/ppermute | solution.py:404

commit v10 on v9

--- a/solution.py
+++ b/solution.py
@@ -430,10 +430,10 @@
     best = score(best, 4, (new_pass(1, 3, 4, size),), (order, index))
     other[1] = swap(tie(own[1], best))
     joined = join([own[2], tie(own[3], best), tie(own[4], best)], SHORT)
-    own[7] = go(7, tie(late[2], own[3]))
     swapped = swap(joined)
     own[3], own[4] = (joined, 1), (joined, 2)
     best = score(best, 7, (new_pass(4, 2, 7, size), late_pass(2, 2, 6, 7, size)))
+    own[7] = go(7, tie(late[2], best))
     other[2], other[3], other[4] = (swapped, 0), (swapped, 1), (swapped, 2)
     joined = join([tie(own[5], best), tie(own[6], best)], LONG)
     swapped = swap(joined)

time: 141 us -> 139 us (0.986)
  blocking collectives: 31.4 us -> 14.9 us
  starting transfers between devices: 30.5 us -> 38.7 us
  waiting for transfers between devices: 4.16 us -> 10.3 us
    all_to_all x1, blocking collectives: 31.4 us -> 14.9 us  [hosted(): lax.all_to_all(outbound, axes, split_axis=0, concat_axis=0, tiled=True)]
    ppermute x7, starting transfers between devices: 22.1 us -> 30.4 us  [go(): return lax.ppermute(chunk, axes, round_pairs(step - 1))]
    ppermute x7, waiting for transfers between devices: 4.15 us -> 10.3 us  [go(): return lax.ppermute(chunk, axes, round_pairs(step - 1))]
  transfers between devices with their start and end apart: 12 -> 12, of which waited for: 2 -> 3; matrix products, arithmetic and copies ran while one was open for 2% -> 2% of each run, Pallas kernels for 46% -> 47%
where the time goes in v10:
time: 139 us; the launch traced here: 138 us
  Pallas kernels  70 us (50%)
  starting transfers between devices  38.7 us (28%)
  blocking collectives  14.9 us (11%)
  waiting for transfers between devices  10.3 us (7%)
  local copies, waits for them, and re-layouts  3.3 us (2%)
    pallas_call x4, Pallas kernels, gram_best(): pl.pallas_call(functools.partial(gram_kernel, passes, loads, size, limit)...  39.8 us
    ppermute x7, starting transfers between devices, go(): return lax.ppermute(chunk, axes, round_pairs(step - 1))  30.4 us
    pallas_call x2, Pallas kernels, gather_rows(): pl.pallas_call(functools.partial(gather_kernel, slots, size, group, secti...  23.2 us
    all_to_all x1, blocking collectives, hosted(): lax.all_to_all(outbound, axes, split_axis=0, concat_axis=0, tiled=True)  14.9 us
    ppermute x7, waiting for transfers between devices, go(): return lax.ppermute(chunk, axes, round_pairs(step - 1))  10.3 us
    ppermute x1, starting transfers between devices, hosted(): named = lax.ppermute(named, axes, metadata_pairs())  4.92 us
    ppermute x4, starting transfers between devices, swap(): return lax.ppermute(chunk, axes, SIBLINGS)  3.4 us
  transfers between devices with their start and end apart: 12, of which 3 were waited for; matrix products, arithmetic and copies ran while one was open for 2% of the time, Pallas kernels for 47%

profile of v10, /device:TPU:0, one launch (start us, length us, event | category | flops | bytes accessed | tf_op | source)
XLA Modules:
  0.0 138.3 jit_solution(4499928089210311865)
XLA Ops:
  0.0 1.5 %shard_map.55 = s32[50,128]{1,0:T(8,128)} custom-call(s32[50,128]{1,0:T(8,128)} %bitcast.9, s32[52,128]{1,0:T(8,128)} %bitcast.10), custom_call_target="tpu_custom_call" | custom-call | tf_op jit(solution)/shard_map/pallas_call | solution.py:87
  1.5 4.9 %collective-permute-start = (s32[50,128]{1,0:T(8,128)}, s32[50,128]{1,0:T(8,128)S(1)}, u32[]{:S(2)}, u32[]{:S(2)}) collective-permute-start(s32[50,128]{1,0:T(8,128)} %shard_map.55), channel_id=1, source_target_pairs={{0,8},{1,9},{4,12},{5,13},{10,10},{11,11},{14,14},{15,15},{16,16},... | collective-permute-start | bytes 76808 | tf_op jit(solution)/shard_map/ppermute | solution.py:396
  6.4 0.0 copy-start
  6.4 0.7 copy-done
  7.1 9.9 %shard_map.56 = bf16[400,1024]{1,0:T(8,128)(2,1)} custom-call(s32[6400]{0:T(1024)S(1)} %copy-done, bf16[6400,1024]{1,0:T(8,128)(2,1)} %refs_1_.1), custom_call_target="tpu_custom_call" | custom-call | flops 40000000000 | tf_op jit(solution)/shard_map/pallas_call | solution.py:159
  17.1 0.0 copy-done.1
  17.1 0.1 reshape.46.refs_5_.index_ref
  17.2 0.0 collective-permute-done
  17.2 0.7 collective-permute-start.2
  17.9 4.2 %collective-permute-start.1 = (bf16[400,1024]{1,0:T(8,128)(2,1)}, bf16[400,1024]{1,0:T(8,128)(2,1)S(1)}, u32[]{:S(2)}, u32[]{:S(2)}) collective-permute-start(bf16[400,1024]{1,0:T(8,128)(2,1)} %shard_map.56), channel_id=1, source_target_pairs={{0,8},{4,12},{24,16},{28,20},{5,9},{1,13},{29,17},{25,21},{2,10},{... | collective-permute-start | bytes 2457608 | tf_op jit(solution)/shard_map/ppermute | solution.py:401
  22.2 13.2 %shard_map.57 = (bf16[400,1024]{1,0:T(8,128)(2,1)}, bf16[400,1024]{1,0:T(8,128)(2,1)S(1)}, bf16[400,1024]{1,0:T(8,128)(2,1)S(1)}, bf16[400,1024]{1,0:T(8,128)(2,1)S(1)}) custom-call(s32[6400]{0:T(1024)S(1)} %copy-done.1, bf16[6400,1024]{1,0:T(8,128)(2,1)} %refs_1_.1), custom_call_target="tpu_custom_call" | custom-call | flops 40000000000 | tf_op jit(solution)/shard_map/pallas_call | solution.py:159
  35.4 0.0 copy-start.2
  35.4 0.9 copy-done.2
  36.3 1.6 %collective-permute-start.4 = (bf16[400,1024]{1,0:T(8,128)(2,1)}, bf16[400,1024]{1,0:T(8,128)(2,1)}, u32[]{:S(2)}, u32[]{:S(2)}) collective-permute-start(bf16[400,1024]{1,0:T(8,128)(2,1)} %get-tuple-element.28), channel_id=1, source_target_pairs={{20,8},{16,12},{12,16},{8,20},{17,9},{21,13},{9,17},{13,21},{22,10... | collective-permute-start | bytes 2457608 | tf_op jit(solution)/shard_map/ppermute | solution.py:401
  37.9 3.7 %collective-permute-start.3 = (bf16[400,1024]{1,0:T(8,128)(2,1)}, bf16[400,1024]{1,0:T(8,128)(2,1)}, u32[]{:S(2)}, u32[]{:S(2)}) collective-permute-start(bf16[400,1024]{1,0:T(8,128)(2,1)} %get-tuple-element.28), channel_id=1, source_target_pairs={{4,8},{0,12},{28,16},{24,20},{1,9},{5,13},{25,17},{29,21},{6,10},{... | collective-permute-start | bytes 2457608 | tf_op jit(solution)/shard_map/ppermute | solution.py:401
  41.6 0.1 reshape.49
  41.7 0.7 fusion
  42.4 0.6 gather_fusion
  43.0 0.1 reshape.50.refs_6_.refs_8_.refs_10_.clusters_ref
  43.1 0.0 copy-start.3
  43.1 0.8 fusion.1.refs_4_.order_ref
  43.9 0.0 collective-permute-done.2.refs_3_.refs_0_
  43.9 0.0 collective-permute-done.1.refs_2_
  43.9 5.9 %shard_map.58.refs_7_ = f32[1,6400]{1,0:T(1,128)S(1)} custom-call(bf16[400,1024]{1,0:T(8,128)(2,1)S(1)} %get-tuple-element.31.refs_0_, bf16[400,1024]{1,0:T(8,128)(2,1)S(1)} %get-tuple-element.38.refs_1_, bf16[400,1024]{1,0:T(8,128)(2,1)S(1)} %collective-permute-done.1.refs_2_, bf16[400,1024]{1,0:T(8,128)(2,1)S(1)} %collective-permute-done.2.refs_3_.refs_0_, ...), custom_call_target="tpu_custom_call" | custom-call | tf_op jit(solution)/shard_map/pallas_call | solution.py:262
  49.8 0.7 collective-permute-start.5
  50.5 0.7 collective-permute-start.9
  51.2 4.7 %collective-permute-start.8 = (bf16[400,1024]{1,0:T(8,128)(2,1)S(1)}, bf16[400,1024]{1,0:T(8,128)(2,1)S(1)}, u32[]{:S(2)}, u32[]{:S(2)}) collective-permute-start(bf16[400,1024]{1,0:T(8,128)(2,1)S(1)} %copy-done.3), channel_id=1, source_target_pairs={{24,8},{28,12},{0,16},{4,20},{29,9},{25,13},{5,17},{1,21},{26,10},... | collective-permute-start | bytes 2457608 | tf_op jit(solution)/shard_map/ppermute | solution.py:401
  55.9 0.0 collective-permute-done.4.refs_2_
  55.9 3.4 %collective-permute-done.3.refs_1_ = bf16[400,1024]{1,0:T(8,128)(2,1)} collective-permute-done((bf16[400,1024]{1,0:T(8,128)(2,1)}, bf16[400,1024]{1,0:T(8,128)(2,1)}, u32[]{:S(2)}, u32[]{:S(2)}) %collective-permute-start.3) | collective-permute-done | bytes 819232 | tf_op jit(solution)/shard_map/ppermute | solution.py:401
  59.4 1.5 %shard_map.59.refs_4_ = bf16[1200,1024]{1,0:T(8,128)(2,1)S(1)} custom-call(bf16[400,1024]{1,0:T(8,128)(2,1)S(1)} %collective-permute-done.2.refs_3_.refs_0_, bf16[400,1024]{1,0:T(8,128)(2,1)} %collective-permute-done.3.refs_1_, bf16[400,1024]{1,0:T(8,128)(2,1)} %collective-permute-done.4.refs_2_), custom_call_target="tpu_custom_call" | custom-call | flops 2000000000 | tf_op jit(solution)/shard_map/pallas_call | solution.py:292
  60.9 1.0 collective-permute-start.7
  61.9 0.0 collective-permute-done.5.refs_5_
  61.9 7.6 %shard_map.60.refs_9_ = f32[1,6400]{1,0:T(1,128)S(1)} custom-call(bf16[400,1024]{1,0:T(8,128)(2,1)S(1)} %get-tuple-element.31.refs_0_, bf16[400,1024]{1,0:T(8,128)(2,1)S(1)} %get-tuple-element.38.refs_1_, bf16[400,1024]{1,0:T(8,128)(2,1)S(1)} %collective-permute-done.1.refs_2_, bf16[400,1024]{1,0:T(8,128)(2,1)S(1)} %collective-permute-done.2.refs_3_.refs_0_, ...), custom_call_target="tpu_custom_call" | custom-call | tf_op jit(solution)/shard_map/pallas_call | solution.py:262
  69.6 0.0 collective-permute-done.9.refs_1_
  69.6 6.2 %collective-permute-done.8.refs_0_ = bf16[400,1024]{1,0:T(8,128)(2,1)S(1)} collective-permute-done((bf16[400,1024]{1,0:T(8,128)(2,1)S(1)}, bf16[400,1024]{1,0:T(8,128)(2,1)S(1)}, u32[]{:S(2)}, u32[]{:S(2)}) %collective-permute-start.8) | collective-permute-done | bytes 819232 | tf_op jit(solution)/shard_map/ppermute | solution.py:401
  75.8 14.8 %collective-permute-start.6 = (bf16[400,1024]{1,0:T(8,128)(2,1)S(1)}, bf16[400,1024]{1,0:T(8,128)(2,1)S(1)}, u32[]{:S(2)}, u32[]{:S(2)}) collective-permute-start(bf16[400,1024]{1,0:T(8,128)(2,1)S(1)} %get-tuple-element.38.refs_1_), channel_id=1, source_target_pairs={{28,8},{24,12},{4,16},{0,20},{25,9},{29,13},{1,17},{5,21},{30,10},... | collective-permute-start | bytes 2457608 | tf_op jit(solution)/shard_map/ppermute | solution.py:401
  90.6 0.2 shard_map.61.refs_7_
  90.8 0.8 collective-permute-start.11
  91.6 0.0 collective-permute-done.7.refs_6_
  91.6 15.5 %shard_map.62.refs_11_ = f32[1,6400]{1,0:T(1,128)S(1)} custom-call(bf16[400,1024]{1,0:T(8,128)(2,1)S(1)} %get-tuple-element.31.refs_0_, bf16[400,1024]{1,0:T(8,128)(2,1)S(1)} %get-tuple-element.38.refs_1_, bf16[400,1024]{1,0:T(8,128)(2,1)S(1)} %collective-permute-done.1.refs_2_, bf16[400,1024]{1,0:T(8,128)(2,1)S(1)} %collective-permute-done.2.refs_3_.refs_0_, ...), custom_call_target="tpu_custom_call" | custom-call | tf_op jit(solution)/shard_map/pallas_call | solution.py:262
  107.2 0.7 collective-permute-done.6.refs_9_.own_ref
  107.8 0.9 collective-permute-start.10
  108.7 0.0 collective-permute-done.11.refs_8_
  108.8 10.7 %shard_map.63.best_ref = f32[1,6400]{1,0:T(1,128)S(1)} custom-call(bf16[400,1024]{1,0:T(8,128)(2,1)S(1)} %get-tuple-element.31.refs_0_, bf16[400,1024]{1,0:T(8,128)(2,1)S(1)} %get-tuple-element.38.refs_1_, bf16[400,1024]{1,0:T(8,128)(2,1)S(1)} %collective-permute-done.1.refs_2_, bf16[400,1024]{1,0:T(8,128)(2,1)S(1)} %collective-permute-done.2.refs_3_.refs_0_, ...), custom_call_target="tpu_custom_call" | custom-call | tf_op jit(solution)/shard_map/pallas_call | solution.py:262
  119.5 0.0 collective-permute-done.10.other_ref
  119.5 1.5 %shard_map.64 = f32[32,2,400]{2,1,0:T(2,128)S(1)} custom-call(s32[16]{0:T(128)S(1)} %fusion.1.refs_4_.order_ref, bf16[400,1024]{1,0:T(8,128)(2,1)S(1)} %collective-permute-done.6.refs_9_.own_ref, bf16[400,1024]{1,0:T(8,128)(2,1)S(1)} %collective-permute-done.10.other_ref, s32[1,6400]{1,0:T(1,128)S(1)} %reshape.50.refs_6_.refs_8_.refs_10_.clusters_ref, ...), custom_call_target="tpu_custom_call" | custom-call | tf_op jit(solution)/shard_map/pallas_call | solution.py:337
  121.0 14.9 %all_to_all.5.values_ref = f32[32,2,400]{2,1,0:T(2,128)S(1)} all-to-all(f32[32,2,400]{2,1,0:T(2,128)S(1)} %shard_map.64), channel_id=1, replica_groups=mesh['shard'=8,'rep'=4] {'shard','rep'}, dimensions={0} | all-to-all | bytes 204800 | tf_op jit(solution)/shard_map/all_to_all | solution.py:447
  135.9 2.4 %shard_map.65 = f32[50,128]{1,0:T(8,128)} custom-call(s32[8,2,400]{2,1,0:T(2,128)S(1)} %reshape.46.refs_5_.index_ref, f32[32,2,400]{2,1,0:T(2,128)S(1)} %all_to_all.5.values_ref), custom_call_target="tpu_custom_call" | custom-call | tf_op jit(solution)/shard_map/pallas_call | solution.py:377
  (4 shorter events, 0.0 us)
Async XLA Ops:
  1.5 15.7 %collective-permute-start = (s32[50,128]{1,0:T(8,128)}, s32[50,128]{1,0:T(8,128)S(1)}, u32[]{:S(2)}, u32[]{:S(2)}) collective-permute-start(s32[50,128]{1,0:T(8,128)} %shard_map.55), channel_id=1, source_target_pairs={{0,8},{1,9},{4,12},{5,13},{10,10},{11,11},{14,14},{15,15},{16,16},... | collective-permute-start | bytes 76808 | tf_op jit(solution)/shard_map/ppermute | solution.py:396
  6.4 0.8 copy-start
  7.1 10.0 %copy-start.1 = (s32[6400]{0:T(1024)S(1)}, s32[6400]{0:T(1024)}, u32[]{:S(2)}) copy-start(s32[6400]{0:T(1024)} %refs_0_.3) | copy-start | bytes 76804
  17.2 26.6 %collective-permute-start.2 = (bf16[400,1024]{1,0:T(8,128)(2,1)}, bf16[400,1024]{1,0:T(8,128)(2,1)S(1)}, u32[]{:S(2)}, u32[]{:S(2)}) collective-permute-start(bf16[400,1024]{1,0:T(8,128)(2,1)} %shard_map.56), channel_id=1, source_target_pairs={{16,8},{20,12},{8,16},{12,20},{21,9},{17,13},{13,17},{9,21},{18,10... | collective-permute-start | bytes 2457608 | tf_op jit(solution)/shard_map/ppermute | solution.py:401
  17.9 25.9 %collective-permute-start.1 = (bf16[400,1024]{1,0:T(8,128)(2,1)}, bf16[400,1024]{1,0:T(8,128)(2,1)S(1)}, u32[]{:S(2)}, u32[]{:S(2)}) collective-permute-start(bf16[400,1024]{1,0:T(8,128)(2,1)} %shard_map.56), channel_id=1, source_target_pairs={{0,8},{4,12},{24,16},{28,20},{5,9},{1,13},{29,17},{25,21},{2,10},{... | collective-permute-start | bytes 2457608 | tf_op jit(solution)/shard_map/ppermute | solution.py:401
  35.4 0.9 copy-start.2
  36.3 19.6 %collective-permute-start.4 = (bf16[400,1024]{1,0:T(8,128)(2,1)}, bf16[400,1024]{1,0:T(8,128)(2,1)}, u32[]{:S(2)}, u32[]{:S(2)}) collective-permute-start(bf16[400,1024]{1,0:T(8,128)(2,1)} %get-tuple-element.28), channel_id=1, source_target_pairs={{20,8},{16,12},{12,16},{8,20},{17,9},{21,13},{9,17},{13,21},{22,10... | collective-permute-start | bytes 2457608 | tf_op jit(solution)/shard_map/ppermute | solution.py:401
  37.9 21.5 %collective-permute-start.3 = (bf16[400,1024]{1,0:T(8,128)(2,1)}, bf16[400,1024]{1,0:T(8,128)(2,1)}, u32[]{:S(2)}, u32[]{:S(2)}) collective-permute-start(bf16[400,1024]{1,0:T(8,128)(2,1)} %get-tuple-element.28), channel_id=1, source_target_pairs={{4,8},{0,12},{28,16},{24,20},{1,9},{5,13},{25,17},{29,21},{6,10},{... | collective-permute-start | bytes 2457608 | tf_op jit(solution)/shard_map/ppermute | solution.py:401
  43.1 7.4 %copy-start.3 = (bf16[400,1024]{1,0:T(8,128)(2,1)S(1)}, bf16[400,1024]{1,0:T(8,128)(2,1)}, u32[]{:S(2)}) copy-start(bf16[400,1024]{1,0:T(8,128)(2,1)} %copy-done.2) | copy-start | bytes 2457604
  49.8 12.1 %collective-permute-start.5 = (bf16[400,1024]{1,0:T(8,128)(2,1)S(1)}, bf16[400,1024]{1,0:T(8,128)(2,1)S(1)}, u32[]{:S(2)}, u32[]{:S(2)}) collective-permute-start(bf16[400,1024]{1,0:T(8,128)(2,1)S(1)} %collective-permute-done.1.refs_2_), channel_id=1, source_target_pairs={{8,9},{9,8},{10,11},{11,10},{12,13},{13,12},{14,15},{15,14},{16,17... | collective-permute-start | bytes 2457608 | tf_op jit(solution)/shard_map/ppermute | solution.py:404
  50.5 19.0 %collective-permute-start.9 = (bf16[400,1024]{1,0:T(8,128)(2,1)S(1)}, bf16[400,1024]{1,0:T(8,128)(2,1)S(1)}, u32[]{:S(2)}, u32[]{:S(2)}) collective-permute-start(bf16[400,1024]{1,0:T(8,128)(2,1)S(1)} %copy-done.3), channel_id=1, source_target_pairs={{12,8},{8,12},{20,16},{16,20},{13,9},{9,13},{21,17},{17,21},{14,10... | collective-permute-start | bytes 2457608 | tf_op jit(solution)/shard_map/ppermute | solution.py:401
  51.2 24.5 %collective-permute-start.8 = (bf16[400,1024]{1,0:T(8,128)(2,1)S(1)}, bf16[400,1024]{1,0:T(8,128)(2,1)S(1)}, u32[]{:S(2)}, u32[]{:S(2)}) collective-permute-start(bf16[400,1024]{1,0:T(8,128)(2,1)S(1)} %copy-done.3), channel_id=1, source_target_pairs={{24,8},{28,12},{0,16},{4,20},{29,9},{25,13},{5,17},{1,21},{26,10},... | collective-permute-start | bytes 2457608 | tf_op jit(solution)/shard_map/ppermute | solution.py:401
  60.9 30.7 %collective-permute-start.7 = (bf16[1200,1024]{1,0:T(8,128)(2,1)S(1)}, bf16[1200,1024]{1,0:T(8,128)(2,1)S(1)}, u32[]{:S(2)}, u32[]{:S(2)}) collective-permute-start(bf16[1200,1024]{1,0:T(8,128)(2,1)S(1)} %shard_map.59.refs_4_), channel_id=1, source_target_pairs={{8,9},{9,8},{10,11},{11,10},{12,13},{13,12},{14,15},{15,14},{16,17... | collective-permute-start | bytes 7372808 | tf_op jit(solution)/shard_map/ppermute | solution.py:404
  75.8 32.0 %collective-permute-start.6 = (bf16[400,1024]{1,0:T(8,128)(2,1)S(1)}, bf16[400,1024]{1,0:T(8,128)(2,1)S(1)}, u32[]{:S(2)}, u32[]{:S(2)}) collective-permute-start(bf16[400,1024]{1,0:T(8,128)(2,1)S(1)} %get-tuple-element.38.refs_1_), channel_id=1, source_target_pairs={{28,8},{24,12},{4,16},{0,20},{25,9},{29,13},{1,17},{5,21},{30,10},... | collective-permute-start | bytes 2457608 | tf_op jit(solution)/shard_map/ppermute | solution.py:401
  90.8 17.9 %collective-permute-start.11 = (bf16[800,1024]{1,0:T(8,128)(2,1)S(1)}, bf16[800,1024]{1,0:T(8,128)(2,1)S(1)}, u32[]{:S(2)}, u32[]{:S(2)}) collective-permute-start(bf16[800,1024]{1,0:T(8,128)(2,1)S(1)} %shard_map.61.refs_7_), channel_id=1, source_target_pairs={{8,9},{9,8},{10,11},{11,10},{12,13},{13,12},{14,15},{15,14},{16,17... | collective-permute-start | bytes 4915208 | tf_op jit(solution)/shard_map/ppermute | solution.py:404
  107.8 11.7 %collective-permute-start.10 = (bf16[400,1024]{1,0:T(8,128)(2,1)S(1)}, bf16[400,1024]{1,0:T(8,128)(2,1)S(1)}, u32[]{:S(2)}, u32[]{:S(2)}) collective-permute-start(bf16[400,1024]{1,0:T(8,128)(2,1)S(1)} %collective-permute-done.6.refs_9_.own_ref), channel_id=1, source_target_pairs={{8,9},{9,8},{10,11},{11,10},{12,13},{13,12},{14,15},{15,14},{16,17... | collective-permute-start | bytes 2457608 | tf_op jit(solution)/shard_map/ppermute | solution.py:404

commit v11 on v10

--- a/solution.py
+++ b/solution.py
@@ -16,7 +16,7 @@
 SHORT = 2_000_000_000
 
 HOSTS = (2, 3, 4, 5)
-ROUNDS = ((2, 6, 3, 7, 4, 1, 5), (3, 7, 2, 6, 5, 1, 4))
+ROUNDS = ((2, 6, 3, 7, 4, 1, 5), (3, 7, 2, 6, 4, 1, 5))
 
 
 CHUNKS = (

time: 139 us -> 131 us (0.942)
  starting transfers between devices: 38.7 us -> 30.2 us
    ppermute x7, starting transfers between devices: 30.4 us -> 21.9 us  [go(): return lax.ppermute(chunk, axes, round_pairs(step - 1))]
  transfers between devices with their start and end apart: 12 -> 12, of which waited for: 3 -> 3; matrix products, arithmetic and copies ran while one was open for 2% -> 2% of each run, Pallas kernels for 47% -> 50%
where the time goes in v11:
time: 131 us; the launch traced here: 130 us
  Pallas kernels  70.1 us (54%)
  starting transfers between devices  30.2 us (23%)
  blocking collectives  14.9 us (11%)
  waiting for transfers between devices  10.5 us (8%)
  local copies, waits for them, and re-layouts  3.3 us (3%)
    pallas_call x4, Pallas kernels, gram_best(): pl.pallas_call(functools.partial(gram_kernel, passes, loads, size, limit)...  39.8 us
    pallas_call x2, Pallas kernels, gather_rows(): pl.pallas_call(functools.partial(gather_kernel, slots, size, group, secti...  23.2 us
    ppermute x7, starting transfers between devices, go(): return lax.ppermute(chunk, axes, round_pairs(step - 1))  21.9 us
    all_to_all x1, blocking collectives, hosted(): lax.all_to_all(outbound, axes, split_axis=0, concat_axis=0, tiled=True)  14.9 us
    ppermute x7, waiting for transfers between devices, go(): return lax.ppermute(chunk, axes, round_pairs(step - 1))  10.5 us
    ppermute x1, starting transfers between devices, hosted(): named = lax.ppermute(named, axes, metadata_pairs())  4.92 us
    ppermute x4, starting transfers between devices, swap(): return lax.ppermute(chunk, axes, SIBLINGS)  3.4 us
  transfers between devices with their start and end apart: 12, of which 3 were waited for; matrix products, arithmetic and copies ran while one was open for 2% of the time, Pallas kernels for 50%

profile of v11, /device:TPU:0, one launch (start us, length us, event | category | flops | bytes accessed | tf_op | source)
XLA Modules:
  0.0 130.0 jit_solution(2224779084532214208)
XLA Ops:
  0.0 1.5 %shard_map.55 = s32[50,128]{1,0:T(8,128)} custom-call(s32[50,128]{1,0:T(8,128)} %bitcast.9, s32[52,128]{1,0:T(8,128)} %bitcast.10), custom_call_target="tpu_custom_call" | custom-call | tf_op jit(solution)/shard_map/pallas_call | solution.py:87
  1.5 4.9 %collective-permute-start = (s32[50,128]{1,0:T(8,128)}, s32[50,128]{1,0:T(8,128)S(1)}, u32[]{:S(2)}, u32[]{:S(2)}) collective-permute-start(s32[50,128]{1,0:T(8,128)} %shard_map.55), channel_id=1, source_target_pairs={{0,8},{1,9},{4,12},{5,13},{10,10},{11,11},{14,14},{15,15},{16,16},... | collective-permute-start | bytes 76808 | tf_op jit(solution)/shard_map/ppermute | solution.py:396
  6.4 0.0 copy-start
  6.4 0.7 copy-done
  7.1 9.9 %shard_map.56 = bf16[400,1024]{1,0:T(8,128)(2,1)} custom-call(s32[6400]{0:T(1024)S(1)} %copy-done, bf16[6400,1024]{1,0:T(8,128)(2,1)} %refs_1_.1), custom_call_target="tpu_custom_call" | custom-call | flops 40000000000 | tf_op jit(solution)/shard_map/pallas_call | solution.py:159
  17.1 0.0 copy-done.1
  17.1 0.1 reshape.46.refs_5_.index_ref
  17.2 0.0 collective-permute-done
  17.2 0.7 collective-permute-start.2
  17.9 4.2 %collective-permute-start.1 = (bf16[400,1024]{1,0:T(8,128)(2,1)}, bf16[400,1024]{1,0:T(8,128)(2,1)S(1)}, u32[]{:S(2)}, u32[]{:S(2)}) collective-permute-start(bf16[400,1024]{1,0:T(8,128)(2,1)} %shard_map.56), channel_id=1, source_target_pairs={{0,8},{4,12},{24,16},{28,20},{5,9},{1,13},{29,17},{25,21},{2,10},{... | collective-permute-start | bytes 2457608 | tf_op jit(solution)/shard_map/ppermute | solution.py:401
  22.2 13.2 %shard_map.57 = (bf16[400,1024]{1,0:T(8,128)(2,1)}, bf16[400,1024]{1,0:T(8,128)(2,1)S(1)}, bf16[400,1024]{1,0:T(8,128)(2,1)S(1)}, bf16[400,1024]{1,0:T(8,128)(2,1)S(1)}) custom-call(s32[6400]{0:T(1024)S(1)} %copy-done.1, bf16[6400,1024]{1,0:T(8,128)(2,1)} %refs_1_.1), custom_call_target="tpu_custom_call" | custom-call | flops 40000000000 | tf_op jit(solution)/shard_map/pallas_call | solution.py:159
  35.4 0.0 copy-start.2
  35.4 0.9 copy-done.2
  36.3 1.6 %collective-permute-start.4 = (bf16[400,1024]{1,0:T(8,128)(2,1)}, bf16[400,1024]{1,0:T(8,128)(2,1)}, u32[]{:S(2)}, u32[]{:S(2)}) collective-permute-start(bf16[400,1024]{1,0:T(8,128)(2,1)} %get-tuple-element.28), channel_id=1, source_target_pairs={{20,8},{16,12},{12,16},{8,20},{17,9},{21,13},{9,17},{13,21},{22,10... | collective-permute-start | bytes 2457608 | tf_op jit(solution)/shard_map/ppermute | solution.py:401
  37.9 3.7 %collective-permute-start.3 = (bf16[400,1024]{1,0:T(8,128)(2,1)}, bf16[400,1024]{1,0:T(8,128)(2,1)}, u32[]{:S(2)}, u32[]{:S(2)}) collective-permute-start(bf16[400,1024]{1,0:T(8,128)(2,1)} %get-tuple-element.28), channel_id=1, source_target_pairs={{4,8},{0,12},{28,16},{24,20},{1,9},{5,13},{25,17},{29,21},{6,10},{... | collective-permute-start | bytes 2457608 | tf_op jit(solution)/shard_map/ppermute | solution.py:401
  41.6 0.1 reshape.49
  41.7 0.7 fusion
  42.4 0.6 gather_fusion
  43.0 0.1 reshape.50.refs_6_.refs_8_.refs_10_.clusters_ref
  43.1 0.0 copy-start.3
  43.1 0.8 fusion.1.refs_4_.order_ref
  43.9 0.0 collective-permute-done.2.refs_3_.refs_0_
  43.9 0.0 collective-permute-done.1.refs_2_
  43.9 5.9 %shard_map.58.refs_7_ = f32[1,6400]{1,0:T(1,128)S(1)} custom-call(bf16[400,1024]{1,0:T(8,128)(2,1)S(1)} %get-tuple-element.31.refs_0_, bf16[400,1024]{1,0:T(8,128)(2,1)S(1)} %get-tuple-element.38.refs_1_, bf16[400,1024]{1,0:T(8,128)(2,1)S(1)} %collective-permute-done.1.refs_2_, bf16[400,1024]{1,0:T(8,128)(2,1)S(1)} %collective-permute-done.2.refs_3_.refs_0_, ...), custom_call_target="tpu_custom_call" | custom-call | tf_op jit(solution)/shard_map/pallas_call | solution.py:262
  49.8 0.7 collective-permute-start.5
  50.5 0.7 collective-permute-start.9
  51.2 4.7 %collective-permute-start.8 = (bf16[400,1024]{1,0:T(8,128)(2,1)S(1)}, bf16[400,1024]{1,0:T(8,128)(2,1)S(1)}, u32[]{:S(2)}, u32[]{:S(2)}) collective-permute-start(bf16[400,1024]{1,0:T(8,128)(2,1)S(1)} %copy-done.3), channel_id=1, source_target_pairs={{24,8},{28,12},{0,16},{4,20},{25,9},{29,13},{1,17},{5,21},{26,10},... | collective-permute-start | bytes 2457608 | tf_op jit(solution)/shard_map/ppermute | solution.py:401
  55.9 0.0 collective-permute-done.4.refs_2_
  55.9 3.8 %collective-permute-done.3.refs_1_ = bf16[400,1024]{1,0:T(8,128)(2,1)} collective-permute-done((bf16[400,1024]{1,0:T(8,128)(2,1)}, bf16[400,1024]{1,0:T(8,128)(2,1)}, u32[]{:S(2)}, u32[]{:S(2)}) %collective-permute-start.3) | collective-permute-done | bytes 819232 | tf_op jit(solution)/shard_map/ppermute | solution.py:401
  59.7 1.5 %shard_map.59.refs_4_ = bf16[1200,1024]{1,0:T(8,128)(2,1)S(1)} custom-call(bf16[400,1024]{1,0:T(8,128)(2,1)S(1)} %collective-permute-done.2.refs_3_.refs_0_, bf16[400,1024]{1,0:T(8,128)(2,1)} %collective-permute-done.3.refs_1_, bf16[400,1024]{1,0:T(8,128)(2,1)} %collective-permute-done.4.refs_2_), custom_call_target="tpu_custom_call" | custom-call | flops 2000000000 | tf_op jit(solution)/shard_map/pallas_call | solution.py:292
  61.2 1.0 collective-permute-start.7
  62.2 0.0 collective-permute-done.5.refs_5_
  62.2 7.7 %shard_map.60.refs_9_ = f32[1,6400]{1,0:T(1,128)S(1)} custom-call(bf16[400,1024]{1,0:T(8,128)(2,1)S(1)} %get-tuple-element.31.refs_0_, bf16[400,1024]{1,0:T(8,128)(2,1)S(1)} %get-tuple-element.38.refs_1_, bf16[400,1024]{1,0:T(8,128)(2,1)S(1)} %collective-permute-done.1.refs_2_, bf16[400,1024]{1,0:T(8,128)(2,1)S(1)} %collective-permute-done.2.refs_3_.refs_0_, ...), custom_call_target="tpu_custom_call" | custom-call | tf_op jit(solution)/shard_map/pallas_call | solution.py:262
  69.9 0.0 collective-permute-done.9.refs_1_
  69.9 5.6 %collective-permute-done.8.refs_0_ = bf16[400,1024]{1,0:T(8,128)(2,1)S(1)} collective-permute-done((bf16[400,1024]{1,0:T(8,128)(2,1)S(1)}, bf16[400,1024]{1,0:T(8,128)(2,1)S(1)}, u32[]{:S(2)}, u32[]{:S(2)}) %collective-permute-start.8) | collective-permute-done | bytes 819232 | tf_op jit(solution)/shard_map/ppermute | solution.py:401
  75.5 6.3 %collective-permute-start.6 = (bf16[400,1024]{1,0:T(8,128)(2,1)S(1)}, bf16[400,1024]{1,0:T(8,128)(2,1)S(1)}, u32[]{:S(2)}, u32[]{:S(2)}) collective-permute-start(bf16[400,1024]{1,0:T(8,128)(2,1)S(1)} %get-tuple-element.38.refs_1_), channel_id=1, source_target_pairs={{28,8},{24,12},{4,16},{0,20},{29,9},{25,13},{5,17},{1,21},{30,10},... | collective-permute-start | bytes 2457608 | tf_op jit(solution)/shard_map/ppermute | solution.py:401
  81.8 0.2 shard_map.61.refs_7_
  82.0 0.8 collective-permute-start.11
  82.8 0.0 collective-permute-done.7.refs_6_
  82.8 15.6 %shard_map.62.refs_11_ = f32[1,6400]{1,0:T(1,128)S(1)} custom-call(bf16[400,1024]{1,0:T(8,128)(2,1)S(1)} %get-tuple-element.31.refs_0_, bf16[400,1024]{1,0:T(8,128)(2,1)S(1)} %get-tuple-element.38.refs_1_, bf16[400,1024]{1,0:T(8,128)(2,1)S(1)} %collective-permute-done.1.refs_2_, bf16[400,1024]{1,0:T(8,128)(2,1)S(1)} %collective-permute-done.2.refs_3_.refs_0_, ...), custom_call_target="tpu_custom_call" | custom-call | tf_op jit(solution)/shard_map/pallas_call | solution.py:262
  98.4 1.1 collective-permute-done.6.refs_9_.own_ref
  99.5 0.9 collective-permute-start.10
  100.4 0.0 collective-permute-done.11.refs_8_
  100.4 10.7 %shard_map.63.best_ref = f32[1,6400]{1,0:T(1,128)S(1)} custom-call(bf16[400,1024]{1,0:T(8,128)(2,1)S(1)} %get-tuple-element.31.refs_0_, bf16[400,1024]{1,0:T(8,128)(2,1)S(1)} %get-tuple-element.38.refs_1_, bf16[400,1024]{1,0:T(8,128)(2,1)S(1)} %collective-permute-done.1.refs_2_, bf16[400,1024]{1,0:T(8,128)(2,1)S(1)} %collective-permute-done.2.refs_3_.refs_0_, ...), custom_call_target="tpu_custom_call" | custom-call | tf_op jit(solution)/shard_map/pallas_call | solution.py:262
  111.2 0.0 collective-permute-done.10.other_ref
  111.2 1.5 %shard_map.64 = f32[32,2,400]{2,1,0:T(2,128)S(1)} custom-call(s32[16]{0:T(128)S(1)} %fusion.1.refs_4_.order_ref, bf16[400,1024]{1,0:T(8,128)(2,1)S(1)} %collective-permute-done.6.refs_9_.own_ref, bf16[400,1024]{1,0:T(8,128)(2,1)S(1)} %collective-permute-done.10.other_ref, s32[1,6400]{1,0:T(1,128)S(1)} %reshape.50.refs_6_.refs_8_.refs_10_.clusters_ref, ...), custom_call_target="tpu_custom_call" | custom-call | tf_op jit(solution)/shard_map/pallas_call | solution.py:337
  112.7 14.9 %all_to_all.5.values_ref = f32[32,2,400]{2,1,0:T(2,128)S(1)} all-to-all(f32[32,2,400]{2,1,0:T(2,128)S(1)} %shard_map.64), channel_id=1, replica_groups=mesh['shard'=8,'rep'=4] {'shard','rep'}, dimensions={0} | all-to-all | bytes 204800 | tf_op jit(solution)/shard_map/all_to_all | solution.py:447
  127.6 2.4 %shard_map.65 = f32[50,128]{1,0:T(8,128)} custom-call(s32[8,2,400]{2,1,0:T(2,128)S(1)} %reshape.46.refs_5_.index_ref, f32[32,2,400]{2,1,0:T(2,128)S(1)} %all_to_all.5.values_ref), custom_call_target="tpu_custom_call" | custom-call | tf_op jit(solution)/shard_map/pallas_call | solution.py:377
  (4 shorter events, 0.0 us)
Async XLA Ops:
  1.5 15.7 %collective-permute-start = (s32[50,128]{1,0:T(8,128)}, s32[50,128]{1,0:T(8,128)S(1)}, u32[]{:S(2)}, u32[]{:S(2)}) collective-permute-start(s32[50,128]{1,0:T(8,128)} %shard_map.55), channel_id=1, source_target_pairs={{0,8},{1,9},{4,12},{5,13},{10,10},{11,11},{14,14},{15,15},{16,16},... | collective-permute-start | bytes 76808 | tf_op jit(solution)/shard_map/ppermute | solution.py:396
  6.4 0.8 copy-start
  7.1 10.0 %copy-start.1 = (s32[6400]{0:T(1024)S(1)}, s32[6400]{0:T(1024)}, u32[]{:S(2)}) copy-start(s32[6400]{0:T(1024)} %refs_0_.3) | copy-start | bytes 76804
  17.2 26.6 %collective-permute-start.2 = (bf16[400,1024]{1,0:T(8,128)(2,1)}, bf16[400,1024]{1,0:T(8,128)(2,1)S(1)}, u32[]{:S(2)}, u32[]{:S(2)}) collective-permute-start(bf16[400,1024]{1,0:T(8,128)(2,1)} %shard_map.56), channel_id=1, source_target_pairs={{16,8},{20,12},{8,16},{12,20},{21,9},{17,13},{13,17},{9,21},{18,10... | collective-permute-start | bytes 2457608 | tf_op jit(solution)/shard_map/ppermute | solution.py:401
  17.9 25.9 %collective-permute-start.1 = (bf16[400,1024]{1,0:T(8,128)(2,1)}, bf16[400,1024]{1,0:T(8,128)(2,1)S(1)}, u32[]{:S(2)}, u32[]{:S(2)}) collective-permute-start(bf16[400,1024]{1,0:T(8,128)(2,1)} %shard_map.56), channel_id=1, source_target_pairs={{0,8},{4,12},{24,16},{28,20},{5,9},{1,13},{29,17},{25,21},{2,10},{... | collective-permute-start | bytes 2457608 | tf_op jit(solution)/shard_map/ppermute | solution.py:401
  35.4 0.9 copy-start.2
  36.3 19.6 %collective-permute-start.4 = (bf16[400,1024]{1,0:T(8,128)(2,1)}, bf16[400,1024]{1,0:T(8,128)(2,1)}, u32[]{:S(2)}, u32[]{:S(2)}) collective-permute-start(bf16[400,1024]{1,0:T(8,128)(2,1)} %get-tuple-element.28), channel_id=1, source_target_pairs={{20,8},{16,12},{12,16},{8,20},{17,9},{21,13},{9,17},{13,21},{22,10... | collective-permute-start | bytes 2457608 | tf_op jit(solution)/shard_map/ppermute | solution.py:401
  37.9 21.8 %collective-permute-start.3 = (bf16[400,1024]{1,0:T(8,128)(2,1)}, bf16[400,1024]{1,0:T(8,128)(2,1)}, u32[]{:S(2)}, u32[]{:S(2)}) collective-permute-start(bf16[400,1024]{1,0:T(8,128)(2,1)} %get-tuple-element.28), channel_id=1, source_target_pairs={{4,8},{0,12},{28,16},{24,20},{1,9},{5,13},{25,17},{29,21},{6,10},{... | collective-permute-start | bytes 2457608 | tf_op jit(solution)/shard_map/ppermute | solution.py:401
  43.1 7.4 %copy-start.3 = (bf16[400,1024]{1,0:T(8,128)(2,1)S(1)}, bf16[400,1024]{1,0:T(8,128)(2,1)}, u32[]{:S(2)}) copy-start(bf16[400,1024]{1,0:T(8,128)(2,1)} %copy-done.2) | copy-start | bytes 2457604
  49.8 12.4 %collective-permute-start.5 = (bf16[400,1024]{1,0:T(8,128)(2,1)S(1)}, bf16[400,1024]{1,0:T(8,128)(2,1)S(1)}, u32[]{:S(2)}, u32[]{:S(2)}) collective-permute-start(bf16[400,1024]{1,0:T(8,128)(2,1)S(1)} %collective-permute-done.1.refs_2_), channel_id=1, source_target_pairs={{8,9},{9,8},{10,11},{11,10},{12,13},{13,12},{14,15},{15,14},{16,17... | collective-permute-start | bytes 2457608 | tf_op jit(solution)/shard_map/ppermute | solution.py:404
  50.5 19.4 %collective-permute-start.9 = (bf16[400,1024]{1,0:T(8,128)(2,1)S(1)}, bf16[400,1024]{1,0:T(8,128)(2,1)S(1)}, u32[]{:S(2)}, u32[]{:S(2)}) collective-permute-start(bf16[400,1024]{1,0:T(8,128)(2,1)S(1)} %copy-done.3), channel_id=1, source_target_pairs={{12,8},{8,12},{20,16},{16,20},{13,9},{9,13},{21,17},{17,21},{14,10... | collective-permute-start | bytes 2457608 | tf_op jit(solution)/shard_map/ppermute | solution.py:401
  51.2 24.3 %collective-permute-start.8 = (bf16[400,1024]{1,0:T(8,128)(2,1)S(1)}, bf16[400,1024]{1,0:T(8,128)(2,1)S(1)}, u32[]{:S(2)}, u32[]{:S(2)}) collective-permute-start(bf16[400,1024]{1,0:T(8,128)(2,1)S(1)} %copy-done.3), channel_id=1, source_target_pairs={{24,8},{28,12},{0,16},{4,20},{25,9},{29,13},{1,17},{5,21},{26,10},... | collective-permute-start | bytes 2457608 | tf_op jit(solution)/shard_map/ppermute | solution.py:401
  61.2 21.6 %collective-permute-start.7 = (bf16[1200,1024]{1,0:T(8,128)(2,1)S(1)}, bf16[1200,1024]{1,0:T(8,128)(2,1)S(1)}, u32[]{:S(2)}, u32[]{:S(2)}) collective-permute-start(bf16[1200,1024]{1,0:T(8,128)(2,1)S(1)} %shard_map.59.refs_4_), channel_id=1, source_target_pairs={{8,9},{9,8},{10,11},{11,10},{12,13},{13,12},{14,15},{15,14},{16,17... | collective-permute-start | bytes 7372808 | tf_op jit(solution)/shard_map/ppermute | solution.py:404
  75.5 24.0 %collective-permute-start.6 = (bf16[400,1024]{1,0:T(8,128)(2,1)S(1)}, bf16[400,1024]{1,0:T(8,128)(2,1)S(1)}, u32[]{:S(2)}, u32[]{:S(2)}) collective-permute-start(bf16[400,1024]{1,0:T(8,128)(2,1)S(1)} %get-tuple-element.38.refs_1_), channel_id=1, source_target_pairs={{28,8},{24,12},{4,16},{0,20},{29,9},{25,13},{5,17},{1,21},{30,10},... | collective-permute-start | bytes 2457608 | tf_op jit(solution)/shard_map/ppermute | solution.py:401
  82.0 18.4 %collective-permute-start.11 = (bf16[800,1024]{1,0:T(8,128)(2,1)S(1)}, bf16[800,1024]{1,0:T(8,128)(2,1)S(1)}, u32[]{:S(2)}, u32[]{:S(2)}) collective-permute-start(bf16[800,1024]{1,0:T(8,128)(2,1)S(1)} %shard_map.61.refs_7_), channel_id=1, source_target_pairs={{8,9},{9,8},{10,11},{11,10},{12,13},{13,12},{14,15},{15,14},{16,17... | collective-permute-start | bytes 4915208 | tf_op jit(solution)/shard_map/ppermute | solution.py:404
  99.5 11.7 %collective-permute-start.10 = (bf16[400,1024]{1,0:T(8,128)(2,1)S(1)}, bf16[400,1024]{1,0:T(8,128)(2,1)S(1)}, u32[]{:S(2)}, u32[]{:S(2)}) collective-permute-start(bf16[400,1024]{1,0:T(8,128)(2,1)S(1)} %collective-permute-done.6.refs_9_.own_ref), channel_id=1, source_target_pairs={{8,9},{9,8},{10,11},{11,10},{12,13},{13,12},{14,15},{15,14},{16,17... | collective-permute-start | bytes 2457608 | tf_op jit(solution)/shard_map/ppermute | solution.py:404

commit v12 on v11

--- a/solution.py
+++ b/solution.py
@@ -248,7 +248,9 @@
                 if i not in first and not i < min(2 * groups, first[0]):
                     arrive(i)
         for t in last:
-            tile(t * BLK, True)
+            start, stop = t * BLK, (t + 1) * BLK
+            meets = start < chunk * size + height and stop > chunk * size
+            tile(start, meets or stop > limit)
         span = slice(chunk * size, chunk * size + height)
         best_ref[:, span] = jnp.maximum(best_ref[:, span], best_of_rows(acc[...], height))
 
@@ -390,11 +392,9 @@
     documents = embeddings.shape[0]
     size = send_index.shape[0] // 16
     axes = ("shard", "rep")
-    named = arrival_names(place_index, slot_cluster)
-    embeddings = tie(embeddings, named)
     (early,) = gather_rows(embeddings, send_index, (0,), size)
+    named = arrival_names(tie(place_index, early), slot_cluster)
     named = lax.ppermute(named, axes, metadata_pairs())
-    early = tie(early, named)
     index = send_index.reshape(8, 2, size)
 
     def go(step, chunk):
@@ -407,7 +407,7 @@
     own[1], own[2] = go(1, early), go(2, early)
     late = gather_rows(tie(embeddings, early), send_index, (1, 2, 3, 4), size)
     own[0], other[0] = late[2:]
-    own[3], own[4] = go(3, late[0]), go(4, late[0])
+    own[3], own[4] = go(3, late[0]), go(4, tie(late[0], named))
     own[1], own[2] = tie(own[1], late[0]), tie(own[2], late[0])
     own[5] = go(5, tie(late[1], own[1]))
     own[6] = go(6, tie(late[1], own[2]))
@@ -430,10 +430,10 @@
     best = score(best, 4, (new_pass(1, 3, 4, size),), (order, index))
     other[1] = swap(tie(own[1], best))
     joined = join([own[2], tie(own[3], best), tie(own[4], best)], SHORT)
+    own[7] = go(7, tie(late[2], own[3]))
     swapped = swap(joined)
     own[3], own[4] = (joined, 1), (joined, 2)
     best = score(best, 7, (new_pass(4, 2, 7, size), late_pass(2, 2, 6, 7, size)))
-    own[7] = go(7, tie(late[2], best))
     other[2], other[3], other[4] = (swapped, 0), (swapped, 1), (swapped, 2)
     joined = join([tie(own[5], best), tie(own[6], best)], LONG)
     swapped = swap(joined)

time: 131 us -> 155 us (1.18)
  blocking collectives: 14.9 us -> 44.8 us
  waiting for transfers between devices: 10.5 us -> 5.15 us
    all_to_all x1, blocking collectives: 14.9 us -> 44.8 us  [hosted(): lax.all_to_all(outbound, axes, split_axis=0, concat_axis=0, tiled=True)]
    ppermute x7, waiting for transfers between devices: 10.5 us -> 5.14 us  [go(): return lax.ppermute(chunk, axes, round_pairs(step - 1))]
    ppermute x1, starting transfers between devices: 4.92 us -> 1.28 us  [hosted(): named = lax.ppermute(named, axes, metadata_pairs())]
    ppermute x7, starting transfers between devices: 21.9 us -> 25.4 us  [go(): return lax.ppermute(chunk, axes, round_pairs(step - 1))]
  transfers between devices with their start and end apart: 12 -> 12, of which waited for: 3 -> 2; matrix products, arithmetic and copies ran while one was open for 2% -> 1% of each run, Pallas kernels for 50% -> 37%
where the time goes in v12:
time: 155 us; the launch traced here: 154 us
  Pallas kernels  70.2 us (45%)
  blocking collectives  44.8 us (29%)
  starting transfers between devices  30 us (19%)
  waiting for transfers between devices  5.15 us (3%)
  local copies, waits for them, and re-layouts  3.22 us (2%)
    all_to_all x1, blocking collectives, hosted(): lax.all_to_all(outbound, axes, split_axis=0, concat_axis=0, tiled=True)  44.8 us
    pallas_call x4, Pallas kernels, gram_best(): pl.pallas_call(functools.partial(gram_kernel, passes, loads, size, limit)...  40 us
    ppermute x7, starting transfers between devices, go(): return lax.ppermute(chunk, axes, round_pairs(step - 1))  25.4 us
    pallas_call x2, Pallas kernels, gather_rows(): pl.pallas_call(functools.partial(gather_kernel, slots, size, group, secti...  23.2 us
    ppermute x7, waiting for transfers between devices, go(): return lax.ppermute(chunk, axes, round_pairs(step - 1))  5.14 us
    ppermute x4, starting transfers between devices, swap(): return lax.ppermute(chunk, axes, SIBLINGS)  3.4 us
  transfers between devices with their start and end apart: 12, of which 2 were waited for; matrix products, arithmetic and copies ran while one was open for 1% of the time, Pallas kernels for 37%

profile of v12, /device:TPU:0, one launch (start us, length us, event | category | flops | bytes accessed | tf_op | source)
XLA Modules:
  0.0 154.4 jit_solution(326139749136530690)
XLA Ops:
  0.0 0.7 copy-done
  0.8 9.9 %shard_map.55 = bf16[400,1024]{1,0:T(8,128)(2,1)} custom-call(s32[6400]{0:T(1024)S(1)} %copy-done, bf16[6400,1024]{1,0:T(8,128)(2,1)} %refs_1_.2), custom_call_target="tpu_custom_call" | custom-call | flops 40000000000 | tf_op jit(solution)/shard_map/pallas_call | solution.py:159
  10.7 0.7 collective-permute-start.3
  11.4 7.8 %collective-permute-start.2 = (bf16[400,1024]{1,0:T(8,128)(2,1)}, bf16[400,1024]{1,0:T(8,128)(2,1)S(1)}, u32[]{:S(2)}, u32[]{:S(2)}) collective-permute-start(bf16[400,1024]{1,0:T(8,128)(2,1)} %shard_map.55), channel_id=1, source_target_pairs={{0,8},{4,12},{24,16},{28,20},{5,9},{1,13},{29,17},{25,21},{2,10},{... | collective-permute-start | bytes 2457608 | tf_op jit(solution)/shard_map/ppermute | solution.py:401
  19.2 1.5 shard_map.57
  20.6 1.3 collective-permute-start.4
  21.9 0.0 copy-done.1
  21.9 13.2 %shard_map.56 = (bf16[400,1024]{1,0:T(8,128)(2,1)}, bf16[400,1024]{1,0:T(8,128)(2,1)S(1)}, bf16[400,1024]{1,0:T(8,128)(2,1)S(1)}, bf16[400,1024]{1,0:T(8,128)(2,1)S(1)}) custom-call(s32[6400]{0:T(1024)S(1)} %copy-done.1, bf16[6400,1024]{1,0:T(8,128)(2,1)} %refs_1_.2), custom_call_target="tpu_custom_call" | custom-call | flops 40000000000 | tf_op jit(solution)/shard_map/pallas_call | solution.py:159
  35.2 0.0 copy-start.2
  35.2 0.9 copy-done.2
  36.1 3.1 %collective-permute-start = (bf16[400,1024]{1,0:T(8,128)(2,1)}, bf16[400,1024]{1,0:T(8,128)(2,1)}, u32[]{:S(2)}, u32[]{:S(2)}) collective-permute-start(bf16[400,1024]{1,0:T(8,128)(2,1)} %get-tuple-element.36), channel_id=1, source_target_pairs={{4,8},{0,12},{28,16},{24,20},{1,9},{5,13},{25,17},{29,21},{6,10},{... | collective-permute-start | bytes 2457608 | tf_op jit(solution)/shard_map/ppermute | solution.py:401
  39.1 0.7 fusion.1.refs_4_.order_ref
  39.8 0.1 reshape.46.refs_5_.index_ref
  39.9 0.0 collective-permute-done.4
  39.9 1.6 %collective-permute-start.5 = (bf16[400,1024]{1,0:T(8,128)(2,1)}, bf16[400,1024]{1,0:T(8,128)(2,1)}, u32[]{:S(2)}, u32[]{:S(2)}) collective-permute-start(bf16[400,1024]{1,0:T(8,128)(2,1)} %get-tuple-element.36), channel_id=1, source_target_pairs={{20,8},{16,12},{12,16},{8,20},{17,9},{21,13},{9,17},{13,21},{22,10... | collective-permute-start | bytes 2457608 | tf_op jit(solution)/shard_map/ppermute | solution.py:401
  41.5 0.7 fusion
  42.2 0.1 reshape.49
  42.3 0.6 gather_fusion
  42.9 0.1 reshape.50.refs_6_.refs_8_.refs_10_.clusters_ref
  43.0 0.0 copy-start.3
  43.0 0.0 collective-permute-done.3.refs_3_.refs_0_
  43.0 0.0 collective-permute-done.2.refs_2_
  43.0 5.9 %shard_map.58.refs_7_ = f32[1,6400]{1,0:T(1,128)S(1)} custom-call(bf16[400,1024]{1,0:T(8,128)(2,1)S(1)} %get-tuple-element.30.refs_0_, bf16[400,1024]{1,0:T(8,128)(2,1)S(1)} %get-tuple-element.29.refs_1_, bf16[400,1024]{1,0:T(8,128)(2,1)S(1)} %collective-permute-done.2.refs_2_, bf16[400,1024]{1,0:T(8,128)(2,1)S(1)} %collective-permute-done.3.refs_3_.refs_0_, ...), custom_call_target="tpu_custom_call" | custom-call | tf_op jit(solution)/shard_map/pallas_call | solution.py:264
  48.9 0.7 collective-permute-start.6
  49.7 0.0 copy-done.3
  49.7 0.7 collective-permute-start.9
  50.4 8.2 %collective-permute-start.8 = (bf16[400,1024]{1,0:T(8,128)(2,1)S(1)}, bf16[400,1024]{1,0:T(8,128)(2,1)S(1)}, u32[]{:S(2)}, u32[]{:S(2)}) collective-permute-start(bf16[400,1024]{1,0:T(8,128)(2,1)S(1)} %copy-done.3), channel_id=1, source_target_pairs={{24,8},{28,12},{0,16},{4,20},{25,9},{29,13},{1,17},{5,21},{26,10},... | collective-permute-start | bytes 2457608 | tf_op jit(solution)/shard_map/ppermute | solution.py:401
  58.6 0.0 collective-permute-done.refs_1_
  58.6 3.3 %collective-permute-start.1 = (bf16[400,1024]{1,0:T(8,128)(2,1)S(1)}, bf16[400,1024]{1,0:T(8,128)(2,1)S(1)}, u32[]{:S(2)}, u32[]{:S(2)}) collective-permute-start(bf16[400,1024]{1,0:T(8,128)(2,1)S(1)} %get-tuple-element.29.refs_1_), channel_id=1, source_target_pairs={{28,8},{24,12},{4,16},{0,20},{29,9},{25,13},{5,17},{1,21},{30,10},... | collective-permute-start | bytes 2457608 | tf_op jit(solution)/shard_map/ppermute | solution.py:401
  62.0 0.0 collective-permute-done.5.refs_2_
  62.0 1.5 shard_map.59.refs_4_
  63.5 1.0 collective-permute-start.7
  64.5 0.0 collective-permute-done.6.refs_5_
  64.5 7.7 %shard_map.60.refs_9_ = f32[1,6400]{1,0:T(1,128)S(1)} custom-call(bf16[400,1024]{1,0:T(8,128)(2,1)S(1)} %get-tuple-element.30.refs_0_, bf16[400,1024]{1,0:T(8,128)(2,1)S(1)} %get-tuple-element.29.refs_1_, bf16[400,1024]{1,0:T(8,128)(2,1)S(1)} %collective-permute-done.2.refs_2_, bf16[400,1024]{1,0:T(8,128)(2,1)S(1)} %collective-permute-done.3.refs_3_.refs_0_, ...), custom_call_target="tpu_custom_call" | custom-call | tf_op jit(solution)/shard_map/pallas_call | solution.py:264
  72.2 0.0 collective-permute-done.9.refs_1_
  72.2 4.9 %collective-permute-done.8.refs_0_ = bf16[400,1024]{1,0:T(8,128)(2,1)S(1)} collective-permute-done((bf16[400,1024]{1,0:T(8,128)(2,1)S(1)}, bf16[400,1024]{1,0:T(8,128)(2,1)S(1)}, u32[]{:S(2)}, u32[]{:S(2)}) %collective-permute-start.8) | collective-permute-done | bytes 819232 | tf_op jit(solution)/shard_map/ppermute | solution.py:401
  77.2 0.2 shard_map.61.refs_7_
  77.4 0.8 collective-permute-start.11
  78.1 0.0 collective-permute-done.7.refs_6_
  78.2 15.6 %shard_map.62.refs_11_ = f32[1,6400]{1,0:T(1,128)S(1)} custom-call(bf16[400,1024]{1,0:T(8,128)(2,1)S(1)} %get-tuple-element.30.refs_0_, bf16[400,1024]{1,0:T(8,128)(2,1)S(1)} %get-tuple-element.29.refs_1_, bf16[400,1024]{1,0:T(8,128)(2,1)S(1)} %collective-permute-done.2.refs_2_, bf16[400,1024]{1,0:T(8,128)(2,1)S(1)} %collective-permute-done.3.refs_3_.refs_0_, ...), custom_call_target="tpu_custom_call" | custom-call | tf_op jit(solution)/shard_map/pallas_call | solution.py:264
  93.8 0.2 collective-permute-done.1.refs_9_.own_ref
  94.0 0.9 collective-permute-start.10
  94.9 0.0 collective-permute-done.11.refs_8_
  94.9 10.8 %shard_map.63.best_ref = f32[1,6400]{1,0:T(1,128)S(1)} custom-call(bf16[400,1024]{1,0:T(8,128)(2,1)S(1)} %get-tuple-element.30.refs_0_, bf16[400,1024]{1,0:T(8,128)(2,1)S(1)} %get-tuple-element.29.refs_1_, bf16[400,1024]{1,0:T(8,128)(2,1)S(1)} %collective-permute-done.2.refs_2_, bf16[400,1024]{1,0:T(8,128)(2,1)S(1)} %collective-permute-done.3.refs_3_.refs_0_, ...), custom_call_target="tpu_custom_call" | custom-call | tf_op jit(solution)/shard_map/pallas_call | solution.py:264
  105.7 0.0 collective-permute-done.10.other_ref
  105.7 1.5 shard_map.64
  107.2 44.8 %all_to_all.5.values_ref = f32[32,2,400]{2,1,0:T(2,128)S(1)} all-to-all(f32[32,2,400]{2,1,0:T(2,128)S(1)} %shard_map.64), channel_id=1, replica_groups=mesh['shard'=8,'rep'=4] {'shard','rep'}, dimensions={0} | all-to-all | bytes 204800 | tf_op jit(solution)/shard_map/all_to_all | solution.py:447
  152.0 2.4 %shard_map.65 = f32[50,128]{1,0:T(8,128)} custom-call(s32[8,2,400]{2,1,0:T(2,128)S(1)} %reshape.46.refs_5_.index_ref, f32[32,2,400]{2,1,0:T(2,128)S(1)} %all_to_all.5.values_ref), custom_call_target="tpu_custom_call" | custom-call | tf_op jit(solution)/shard_map/pallas_call | solution.py:379
  (4 shorter events, 0.0 us)
Async XLA Ops:
  0.0 0.7 copy-start
  0.7 21.2 %copy-start.1 = (s32[6400]{0:T(1024)S(1)}, s32[6400]{0:T(1024)}, u32[]{:S(2)}) copy-start(s32[6400]{0:T(1024)} %refs_0_.3) | copy-start | bytes 76804
  10.7 32.3 %collective-permute-start.3 = (bf16[400,1024]{1,0:T(8,128)(2,1)}, bf16[400,1024]{1,0:T(8,128)(2,1)S(1)}, u32[]{:S(2)}, u32[]{:S(2)}) collective-permute-start(bf16[400,1024]{1,0:T(8,128)(2,1)} %shard_map.55), channel_id=1, source_target_pairs={{16,8},{20,12},{8,16},{12,20},{21,9},{17,13},{13,17},{9,21},{18,10... | collective-permute-start | bytes 2457608 | tf_op jit(solution)/shard_map/ppermute | solution.py:401
  11.4 31.6 %collective-permute-start.2 = (bf16[400,1024]{1,0:T(8,128)(2,1)}, bf16[400,1024]{1,0:T(8,128)(2,1)S(1)}, u32[]{:S(2)}, u32[]{:S(2)}) collective-permute-start(bf16[400,1024]{1,0:T(8,128)(2,1)} %shard_map.55), channel_id=1, source_target_pairs={{0,8},{4,12},{24,16},{28,20},{5,9},{1,13},{29,17},{25,21},{2,10},{... | collective-permute-start | bytes 2457608 | tf_op jit(solution)/shard_map/ppermute | solution.py:401
  20.6 19.3 %collective-permute-start.4 = (s32[50,128]{1,0:T(8,128)}, s32[50,128]{1,0:T(8,128)S(1)}, u32[]{:S(2)}, u32[]{:S(2)}) collective-permute-start(s32[50,128]{1,0:T(8,128)} %shard_map.57), channel_id=1, source_target_pairs={{0,8},{1,9},{4,12},{5,13},{10,10},{11,11},{14,14},{15,15},{16,16},... | collective-permute-start | bytes 76808 | tf_op jit(solution)/shard_map/ppermute | solution.py:397
  35.2 0.9 copy-start.2
  36.1 22.6 %collective-permute-start = (bf16[400,1024]{1,0:T(8,128)(2,1)}, bf16[400,1024]{1,0:T(8,128)(2,1)}, u32[]{:S(2)}, u32[]{:S(2)}) collective-permute-start(bf16[400,1024]{1,0:T(8,128)(2,1)} %get-tuple-element.36), channel_id=1, source_target_pairs={{4,8},{0,12},{28,16},{24,20},{1,9},{5,13},{25,17},{29,21},{6,10},{... | collective-permute-start | bytes 2457608 | tf_op jit(solution)/shard_map/ppermute | solution.py:401
  39.9 22.0 %collective-permute-start.5 = (bf16[400,1024]{1,0:T(8,128)(2,1)}, bf16[400,1024]{1,0:T(8,128)(2,1)}, u32[]{:S(2)}, u32[]{:S(2)}) collective-permute-start(bf16[400,1024]{1,0:T(8,128)(2,1)} %get-tuple-element.36), channel_id=1, source_target_pairs={{20,8},{16,12},{12,16},{8,20},{17,9},{21,13},{9,17},{13,21},{22,10... | collective-permute-start | bytes 2457608 | tf_op jit(solution)/shard_map/ppermute | solution.py:401
  43.0 6.7 %copy-start.3 = (bf16[400,1024]{1,0:T(8,128)(2,1)S(1)}, bf16[400,1024]{1,0:T(8,128)(2,1)}, u32[]{:S(2)}) copy-start(bf16[400,1024]{1,0:T(8,128)(2,1)} %copy-done.2) | copy-start | bytes 2457604
  48.9 15.6 %collective-permute-start.6 = (bf16[400,1024]{1,0:T(8,128)(2,1)S(1)}, bf16[400,1024]{1,0:T(8,128)(2,1)S(1)}, u32[]{:S(2)}, u32[]{:S(2)}) collective-permute-start(bf16[400,1024]{1,0:T(8,128)(2,1)S(1)} %collective-permute-done.2.refs_2_), channel_id=1, source_target_pairs={{8,9},{9,8},{10,11},{11,10},{12,13},{13,12},{14,15},{15,14},{16,17... | collective-permute-start | bytes 2457608 | tf_op jit(solution)/shard_map/ppermute | solution.py:404
  49.7 22.6 %collective-permute-start.9 = (bf16[400,1024]{1,0:T(8,128)(2,1)S(1)}, bf16[400,1024]{1,0:T(8,128)(2,1)S(1)}, u32[]{:S(2)}, u32[]{:S(2)}) collective-permute-start(bf16[400,1024]{1,0:T(8,128)(2,1)S(1)} %copy-done.3), channel_id=1, source_target_pairs={{12,8},{8,12},{20,16},{16,20},{13,9},{9,13},{21,17},{17,21},{14,10... | collective-permute-start | bytes 2457608 | tf_op jit(solution)/shard_map/ppermute | solution.py:401
  50.4 26.8 %collective-permute-start.8 = (bf16[400,1024]{1,0:T(8,128)(2,1)S(1)}, bf16[400,1024]{1,0:T(8,128)(2,1)S(1)}, u32[]{:S(2)}, u32[]{:S(2)}) collective-permute-start(bf16[400,1024]{1,0:T(8,128)(2,1)S(1)} %copy-done.3), channel_id=1, source_target_pairs={{24,8},{28,12},{0,16},{4,20},{25,9},{29,13},{1,17},{5,21},{26,10},... | collective-permute-start | bytes 2457608 | tf_op jit(solution)/shard_map/ppermute | solution.py:401
  58.6 35.4 %collective-permute-start.1 = (bf16[400,1024]{1,0:T(8,128)(2,1)S(1)}, bf16[400,1024]{1,0:T(8,128)(2,1)S(1)}, u32[]{:S(2)}, u32[]{:S(2)}) collective-permute-start(bf16[400,1024]{1,0:T(8,128)(2,1)S(1)} %get-tuple-element.29.refs_1_), channel_id=1, source_target_pairs={{28,8},{24,12},{4,16},{0,20},{29,9},{25,13},{5,17},{1,21},{30,10},... | collective-permute-start | bytes 2457608 | tf_op jit(solution)/shard_map/ppermute | solution.py:401
  63.5 14.6 %collective-permute-start.7 = (bf16[1200,1024]{1,0:T(8,128)(2,1)S(1)}, bf16[1200,1024]{1,0:T(8,128)(2,1)S(1)}, u32[]{:S(2)}, u32[]{:S(2)}) collective-permute-start(bf16[1200,1024]{1,0:T(8,128)(2,1)S(1)} %shard_map.59.refs_4_), channel_id=1, source_target_pairs={{8,9},{9,8},{10,11},{11,10},{12,13},{13,12},{14,15},{15,14},{16,17... | collective-permute-start | bytes 7372808 | tf_op jit(solution)/shard_map/ppermute | solution.py:404
  77.4 17.6 %collective-permute-start.11 = (bf16[800,1024]{1,0:T(8,128)(2,1)S(1)}, bf16[800,1024]{1,0:T(8,128)(2,1)S(1)}, u32[]{:S(2)}, u32[]{:S(2)}) collective-permute-start(bf16[800,1024]{1,0:T(8,128)(2,1)S(1)} %shard_map.61.refs_7_), channel_id=1, source_target_pairs={{8,9},{9,8},{10,11},{11,10},{12,13},{13,12},{14,15},{15,14},{16,17... | collective-permute-start | bytes 4915208 | tf_op jit(solution)/shard_map/ppermute | solution.py:404
  94.0 11.7 %collective-permute-start.10 = (bf16[400,1024]{1,0:T(8,128)(2,1)S(1)}, bf16[400,1024]{1,0:T(8,128)(2,1)S(1)}, u32[]{:S(2)}, u32[]{:S(2)}) collective-permute-start(bf16[400,1024]{1,0:T(8,128)(2,1)S(1)} %collective-permute-done.1.refs_9_.own_ref), channel_id=1, source_target_pairs={{8,9},{9,8},{10,11},{11,10},{12,13},{13,12},{14,15},{15,14},{16,17... | collective-permute-start | bytes 2457608 | tf_op jit(solution)/shard_map/ppermute | solution.py:404

commit v13 on v12

--- a/solution.py
+++ b/solution.py
@@ -392,9 +392,11 @@
     documents = embeddings.shape[0]
     size = send_index.shape[0] // 16
     axes = ("shard", "rep")
+    named = arrival_names(place_index, slot_cluster)
+    embeddings = tie(embeddings, named)
     (early,) = gather_rows(embeddings, send_index, (0,), size)
-    named = arrival_names(tie(place_index, early), slot_cluster)
     named = lax.ppermute(named, axes, metadata_pairs())
+    early = tie(early, named)
     index = send_index.reshape(8, 2, size)
 
     def go(step, chunk):
@@ -407,9 +409,9 @@
     own[1], own[2] = go(1, early), go(2, early)
     late = gather_rows(tie(embeddings, early), send_index, (1, 2, 3, 4), size)
     own[0], other[0] = late[2:]
-    own[3], own[4] = go(3, late[0]), go(4, tie(late[0], named))
+    own[3], own[4] = go(3, late[0]), go(4, late[0])
     own[1], own[2] = tie(own[1], late[0]), tie(own[2], late[0])
-    own[5] = go(5, tie(late[1], own[1]))
+    own[5] = go(5, tie(late[1], own[4]))
     own[6] = go(6, tie(late[1], own[2]))
 
     named, table = tie(named, late[0]), tie(jnp.asarray(chunk_order()), late[0])

time: 155 us -> 129 us (0.83)
  blocking collectives: 44.8 us -> 16.6 us
  starting transfers between devices: 30 us -> 32.5 us
    all_to_all x1, blocking collectives: 44.8 us -> 16.6 us  [hosted(): lax.all_to_all(outbound, axes, split_axis=0, concat_axis=0, tiled=True)]
    ppermute x1, starting transfers between devices: 1.28 us -> 4.92 us  [hosted(): named = lax.ppermute(named, axes, metadata_pairs())]
  transfers between devices with their start and end apart: 12 -> 12, of which waited for: 2 -> 1; matrix products, arithmetic and copies ran while one was open for 1% -> 2% of each run, Pallas kernels for 37% -> 50%
where the time goes in v13:
time: 129 us; the launch traced here: 128 us
  Pallas kernels  70 us (54%)
  starting transfers between devices  32.5 us (25%)
  blocking collectives  16.6 us (13%)
  waiting for transfers between devices  5.05 us (4%)
  local copies, waits for them, and re-layouts  3.3 us (3%)
    pallas_call x4, Pallas kernels, gram_best(): pl.pallas_call(functools.partial(gram_kernel, passes, loads, size, limit)...  39.8 us
    ppermute x7, starting transfers between devices, go(): return lax.ppermute(chunk, axes, round_pairs(step - 1))  24.1 us
    pallas_call x2, Pallas kernels, gather_rows(): pl.pallas_call(functools.partial(gather_kernel, slots, size, group, secti...  23.2 us
    all_to_all x1, blocking collectives, hosted(): lax.all_to_all(outbound, axes, split_axis=0, concat_axis=0, tiled=True)  16.6 us
    ppermute x7, waiting for transfers between devices, go(): return lax.ppermute(chunk, axes, round_pairs(step - 1))  5.04 us
    ppermute x1, starting transfers between devices, hosted(): named = lax.ppermute(named, axes, metadata_pairs())  4.92 us
    ppermute x4, starting transfers between devices, swap(): return lax.ppermute(chunk, axes, SIBLINGS)  3.41 us
  transfers between devices with their start and end apart: 12, of which 1 were waited for; matrix products, arithmetic and copies ran while one was open for 2% of the time, Pallas kernels for 50%

profile of v13, /device:TPU:0, one launch (start us, length us, event | category | flops | bytes accessed | tf_op | source)
XLA Modules:
  0.0 128.5 jit_solution(16445706673618512092)
XLA Ops:
  0.0 1.5 %shard_map.55 = s32[50,128]{1,0:T(8,128)} custom-call(s32[50,128]{1,0:T(8,128)} %bitcast.9, s32[52,128]{1,0:T(8,128)} %bitcast.10), custom_call_target="tpu_custom_call" | custom-call | tf_op jit(solution)/shard_map/pallas_call | solution.py:87
  1.5 4.9 %collective-permute-start = (s32[50,128]{1,0:T(8,128)}, s32[50,128]{1,0:T(8,128)S(1)}, u32[]{:S(2)}, u32[]{:S(2)}) collective-permute-start(s32[50,128]{1,0:T(8,128)} %shard_map.55), channel_id=1, source_target_pairs={{0,8},{1,9},{4,12},{5,13},{10,10},{11,11},{14,14},{15,15},{16,16},... | collective-permute-start | bytes 76808 | tf_op jit(solution)/shard_map/ppermute | solution.py:398
  6.4 0.0 copy-start
  6.4 0.7 copy-done
  7.1 9.9 %shard_map.56 = bf16[400,1024]{1,0:T(8,128)(2,1)} custom-call(s32[6400]{0:T(1024)S(1)} %copy-done, bf16[6400,1024]{1,0:T(8,128)(2,1)} %refs_1_.1), custom_call_target="tpu_custom_call" | custom-call | flops 40000000000 | tf_op jit(solution)/shard_map/pallas_call | solution.py:159
  17.1 0.0 copy-start.1
  17.1 0.0 collective-permute-done
  17.1 0.7 collective-permute-start.4
  17.8 4.2 %collective-permute-start.3 = (bf16[400,1024]{1,0:T(8,128)(2,1)}, bf16[400,1024]{1,0:T(8,128)(2,1)S(1)}, u32[]{:S(2)}, u32[]{:S(2)}) collective-permute-start(bf16[400,1024]{1,0:T(8,128)(2,1)} %shard_map.56), channel_id=1, source_target_pairs={{0,8},{4,12},{24,16},{28,20},{5,9},{1,13},{29,17},{25,21},{2,10},{... | collective-permute-start | bytes 2457608 | tf_op jit(solution)/shard_map/ppermute | solution.py:403
  22.1 13.2 %shard_map.57 = (bf16[400,1024]{1,0:T(8,128)(2,1)}, bf16[400,1024]{1,0:T(8,128)(2,1)S(1)}, bf16[400,1024]{1,0:T(8,128)(2,1)S(1)}, bf16[400,1024]{1,0:T(8,128)(2,1)S(1)}) custom-call(s32[6400]{0:T(1024)S(1)} %copy-done, bf16[6400,1024]{1,0:T(8,128)(2,1)} %refs_1_.1), custom_call_target="tpu_custom_call" | custom-call | flops 40000000000 | tf_op jit(solution)/shard_map/pallas_call | solution.py:159
  35.3 0.0 copy-start.2
  35.3 0.9 copy-done.2
  36.2 1.6 %collective-permute-start.5 = (bf16[400,1024]{1,0:T(8,128)(2,1)}, bf16[400,1024]{1,0:T(8,128)(2,1)}, u32[]{:S(2)}, u32[]{:S(2)}) collective-permute-start(bf16[400,1024]{1,0:T(8,128)(2,1)} %get-tuple-element.28), channel_id=1, source_target_pairs={{20,8},{16,12},{12,16},{8,20},{17,9},{21,13},{9,17},{13,21},{22,10... | collective-permute-start | bytes 2457608 | tf_op jit(solution)/shard_map/ppermute | solution.py:403
  37.8 0.0 copy-done.1
  37.8 0.1 reshape.46.refs_5_.index_ref
  37.9 3.7 %collective-permute-start.1 = (bf16[400,1024]{1,0:T(8,128)(2,1)}, bf16[400,1024]{1,0:T(8,128)(2,1)}, u32[]{:S(2)}, u32[]{:S(2)}) collective-permute-start(bf16[400,1024]{1,0:T(8,128)(2,1)} %get-tuple-element.28), channel_id=1, source_target_pairs={{4,8},{0,12},{28,16},{24,20},{1,9},{5,13},{25,17},{29,21},{6,10},{... | collective-permute-start | bytes 2457608 | tf_op jit(solution)/shard_map/ppermute | solution.py:403
  41.6 0.1 reshape.49
  41.7 0.7 fusion
  42.4 0.6 gather_fusion
  43.0 0.1 reshape.50.refs_6_.refs_8_.refs_10_.clusters_ref
  43.1 0.8 fusion.1.refs_4_.order_ref
  43.9 0.0 collective-permute-done.4.refs_3_.refs_0_
  43.9 0.0 collective-permute-done.3.refs_2_
  43.9 5.9 %shard_map.58.refs_7_ = f32[1,6400]{1,0:T(1,128)S(1)} custom-call(bf16[400,1024]{1,0:T(8,128)(2,1)S(1)} %get-tuple-element.32.refs_0_, bf16[400,1024]{1,0:T(8,128)(2,1)S(1)} %get-tuple-element.31.refs_1_, bf16[400,1024]{1,0:T(8,128)(2,1)S(1)} %collective-permute-done.3.refs_2_, bf16[400,1024]{1,0:T(8,128)(2,1)S(1)} %collective-permute-done.4.refs_3_.refs_0_, ...), custom_call_target="tpu_custom_call" | custom-call | tf_op jit(solution)/shard_map/pallas_call | solution.py:264
  49.8 0.7 collective-permute-start.6
  50.5 0.7 collective-permute-start.9
  51.3 0.0 collective-permute-done.5.refs_2_
  51.3 9.8 %collective-permute-start.8 = (bf16[400,1024]{1,0:T(8,128)(2,1)S(1)}, bf16[400,1024]{1,0:T(8,128)(2,1)S(1)}, u32[]{:S(2)}, u32[]{:S(2)}) collective-permute-start(bf16[400,1024]{1,0:T(8,128)(2,1)S(1)} %copy-done.3), channel_id=1, source_target_pairs={{24,8},{28,12},{0,16},{4,20},{25,9},{29,13},{1,17},{5,21},{26,10},... | collective-permute-start | bytes 2457608 | tf_op jit(solution)/shard_map/ppermute | solution.py:403
  61.1 0.0 collective-permute-done.1.refs_1_
  61.1 3.4 %collective-permute-start.2 = (bf16[400,1024]{1,0:T(8,128)(2,1)S(1)}, bf16[400,1024]{1,0:T(8,128)(2,1)S(1)}, u32[]{:S(2)}, u32[]{:S(2)}) collective-permute-start(bf16[400,1024]{1,0:T(8,128)(2,1)S(1)} %get-tuple-element.31.refs_1_), channel_id=1, source_target_pairs={{28,8},{24,12},{4,16},{0,20},{29,9},{25,13},{5,17},{1,21},{30,10},... | collective-permute-start | bytes 2457608 | tf_op jit(solution)/shard_map/ppermute | solution.py:403
  64.5 1.5 %shard_map.59.refs_4_ = bf16[1200,1024]{1,0:T(8,128)(2,1)S(1)} custom-call(bf16[400,1024]{1,0:T(8,128)(2,1)S(1)} %collective-permute-done.4.refs_3_.refs_0_, bf16[400,1024]{1,0:T(8,128)(2,1)} %collective-permute-done.1.refs_1_, bf16[400,1024]{1,0:T(8,128)(2,1)} %collective-permute-done.5.refs_2_), custom_call_target="tpu_custom_call" | custom-call | flops 2000000000 | tf_op jit(solution)/shard_map/pallas_call | solution.py:294
  66.0 1.0 collective-permute-start.7
  67.0 0.0 collective-permute-done.6.refs_5_
  67.0 7.6 %shard_map.60.refs_9_ = f32[1,6400]{1,0:T(1,128)S(1)} custom-call(bf16[400,1024]{1,0:T(8,128)(2,1)S(1)} %get-tuple-element.32.refs_0_, bf16[400,1024]{1,0:T(8,128)(2,1)S(1)} %get-tuple-element.31.refs_1_, bf16[400,1024]{1,0:T(8,128)(2,1)S(1)} %collective-permute-done.3.refs_2_, bf16[400,1024]{1,0:T(8,128)(2,1)S(1)} %collective-permute-done.4.refs_3_.refs_0_, ...), custom_call_target="tpu_custom_call" | custom-call | tf_op jit(solution)/shard_map/pallas_call | solution.py:264
  74.7 0.0 collective-permute-done.9.refs_1_
  74.7 5.0 %collective-permute-done.8.refs_0_ = bf16[400,1024]{1,0:T(8,128)(2,1)S(1)} collective-permute-done((bf16[400,1024]{1,0:T(8,128)(2,1)S(1)}, bf16[400,1024]{1,0:T(8,128)(2,1)S(1)}, u32[]{:S(2)}, u32[]{:S(2)}) %collective-permute-start.8) | collective-permute-done | bytes 819232 | tf_op jit(solution)/shard_map/ppermute | solution.py:403
  79.7 0.2 shard_map.61.refs_7_
  79.9 0.8 collective-permute-start.11
  80.7 0.0 collective-permute-done.7.refs_6_
  80.7 15.6 %shard_map.62.refs_11_ = f32[1,6400]{1,0:T(1,128)S(1)} custom-call(bf16[400,1024]{1,0:T(8,128)(2,1)S(1)} %get-tuple-element.32.refs_0_, bf16[400,1024]{1,0:T(8,128)(2,1)S(1)} %get-tuple-element.31.refs_1_, bf16[400,1024]{1,0:T(8,128)(2,1)S(1)} %collective-permute-done.3.refs_2_, bf16[400,1024]{1,0:T(8,128)(2,1)S(1)} %collective-permute-done.4.refs_3_.refs_0_, ...), custom_call_target="tpu_custom_call" | custom-call | tf_op jit(solution)/shard_map/pallas_call | solution.py:264
  96.3 0.0 collective-permute-done.2.refs_9_.own_ref
  96.3 0.9 collective-permute-start.10
  97.2 0.0 collective-permute-done.11.refs_8_
  97.2 10.7 %shard_map.63.best_ref = f32[1,6400]{1,0:T(1,128)S(1)} custom-call(bf16[400,1024]{1,0:T(8,128)(2,1)S(1)} %get-tuple-element.32.refs_0_, bf16[400,1024]{1,0:T(8,128)(2,1)S(1)} %get-tuple-element.31.refs_1_, bf16[400,1024]{1,0:T(8,128)(2,1)S(1)} %collective-permute-done.3.refs_2_, bf16[400,1024]{1,0:T(8,128)(2,1)S(1)} %collective-permute-done.4.refs_3_.refs_0_, ...), custom_call_target="tpu_custom_call" | custom-call | tf_op jit(solution)/shard_map/pallas_call | solution.py:264
  108.0 0.0 collective-permute-done.10.other_ref
  108.0 1.5 %shard_map.64 = f32[32,2,400]{2,1,0:T(2,128)S(1)} custom-call(s32[16]{0:T(128)S(1)} %fusion.1.refs_4_.order_ref, bf16[400,1024]{1,0:T(8,128)(2,1)S(1)} %collective-permute-done.2.refs_9_.own_ref, bf16[400,1024]{1,0:T(8,128)(2,1)S(1)} %collective-permute-done.10.other_ref, s32[1,6400]{1,0:T(1,128)S(1)} %reshape.50.refs_6_.refs_8_.refs_10_.clusters_ref, ...), custom_call_target="tpu_custom_call" | custom-call | tf_op jit(solution)/shard_map/pallas_call | solution.py:339
  109.5 16.6 %all_to_all.5.values_ref = f32[32,2,400]{2,1,0:T(2,128)S(1)} all-to-all(f32[32,2,400]{2,1,0:T(2,128)S(1)} %shard_map.64), channel_id=1, replica_groups=mesh['shard'=8,'rep'=4] {'shard','rep'}, dimensions={0} | all-to-all | bytes 204800 | tf_op jit(solution)/shard_map/all_to_all | solution.py:449
  126.1 2.4 %shard_map.65 = f32[50,128]{1,0:T(8,128)} custom-call(s32[8,2,400]{2,1,0:T(2,128)S(1)} %reshape.46.refs_5_.index_ref, f32[32,2,400]{2,1,0:T(2,128)S(1)} %all_to_all.5.values_ref), custom_call_target="tpu_custom_call" | custom-call | tf_op jit(solution)/shard_map/pallas_call | solution.py:379
  (4 shorter events, 0.0 us)
Async XLA Ops:
  1.5 15.6 %collective-permute-start = (s32[50,128]{1,0:T(8,128)}, s32[50,128]{1,0:T(8,128)S(1)}, u32[]{:S(2)}, u32[]{:S(2)}) collective-permute-start(s32[50,128]{1,0:T(8,128)} %shard_map.55), channel_id=1, source_target_pairs={{0,8},{1,9},{4,12},{5,13},{10,10},{11,11},{14,14},{15,15},{16,16},... | collective-permute-start | bytes 76808 | tf_op jit(solution)/shard_map/ppermute | solution.py:398
  6.4 0.8 copy-start
  17.1 20.7 %copy-start.1 = (s32[6400]{0:T(1024)S(1)}, s32[6400]{0:T(1024)}, u32[]{:S(2)}) copy-start(s32[6400]{0:T(1024)} %refs_0_.3) | copy-start | bytes 76804
  17.1 26.8 %collective-permute-start.4 = (bf16[400,1024]{1,0:T(8,128)(2,1)}, bf16[400,1024]{1,0:T(8,128)(2,1)S(1)}, u32[]{:S(2)}, u32[]{:S(2)}) collective-permute-start(bf16[400,1024]{1,0:T(8,128)(2,1)} %shard_map.56), channel_id=1, source_target_pairs={{16,8},{20,12},{8,16},{12,20},{21,9},{17,13},{13,17},{9,21},{18,10... | collective-permute-start | bytes 2457608 | tf_op jit(solution)/shard_map/ppermute | solution.py:403
  17.8 26.1 %collective-permute-start.3 = (bf16[400,1024]{1,0:T(8,128)(2,1)}, bf16[400,1024]{1,0:T(8,128)(2,1)S(1)}, u32[]{:S(2)}, u32[]{:S(2)}) collective-permute-start(bf16[400,1024]{1,0:T(8,128)(2,1)} %shard_map.56), channel_id=1, source_target_pairs={{0,8},{4,12},{24,16},{28,20},{5,9},{1,13},{29,17},{25,21},{2,10},{... | collective-permute-start | bytes 2457608 | tf_op jit(solution)/shard_map/ppermute | solution.py:403
  35.3 0.9 copy-start.2
  36.2 15.1 %collective-permute-start.5 = (bf16[400,1024]{1,0:T(8,128)(2,1)}, bf16[400,1024]{1,0:T(8,128)(2,1)}, u32[]{:S(2)}, u32[]{:S(2)}) collective-permute-start(bf16[400,1024]{1,0:T(8,128)(2,1)} %get-tuple-element.28), channel_id=1, source_target_pairs={{20,8},{16,12},{12,16},{8,20},{17,9},{21,13},{9,17},{13,21},{22,10... | collective-permute-start | bytes 2457608 | tf_op jit(solution)/shard_map/ppermute | solution.py:403
  37.9 23.2 %collective-permute-start.1 = (bf16[400,1024]{1,0:T(8,128)(2,1)}, bf16[400,1024]{1,0:T(8,128)(2,1)}, u32[]{:S(2)}, u32[]{:S(2)}) collective-permute-start(bf16[400,1024]{1,0:T(8,128)(2,1)} %get-tuple-element.28), channel_id=1, source_target_pairs={{4,8},{0,12},{28,16},{24,20},{1,9},{5,13},{25,17},{29,21},{6,10},{... | collective-permute-start | bytes 2457608 | tf_op jit(solution)/shard_map/ppermute | solution.py:403
  43.1 7.4 %copy-start.3 = (bf16[400,1024]{1,0:T(8,128)(2,1)S(1)}, bf16[400,1024]{1,0:T(8,128)(2,1)}, u32[]{:S(2)}) copy-start(bf16[400,1024]{1,0:T(8,128)(2,1)} %copy-done.2) | copy-start | bytes 2457604
  49.8 17.2 %collective-permute-start.6 = (bf16[400,1024]{1,0:T(8,128)(2,1)S(1)}, bf16[400,1024]{1,0:T(8,128)(2,1)S(1)}, u32[]{:S(2)}, u32[]{:S(2)}) collective-permute-start(bf16[400,1024]{1,0:T(8,128)(2,1)S(1)} %collective-permute-done.3.refs_2_), channel_id=1, source_target_pairs={{8,9},{9,8},{10,11},{11,10},{12,13},{13,12},{14,15},{15,14},{16,17... | collective-permute-start | bytes 2457608 | tf_op jit(solution)/shard_map/ppermute | solution.py:406
  50.5 24.1 %collective-permute-start.9 = (bf16[400,1024]{1,0:T(8,128)(2,1)S(1)}, bf16[400,1024]{1,0:T(8,128)(2,1)S(1)}, u32[]{:S(2)}, u32[]{:S(2)}) collective-permute-start(bf16[400,1024]{1,0:T(8,128)(2,1)S(1)} %copy-done.3), channel_id=1, source_target_pairs={{12,8},{8,12},{20,16},{16,20},{13,9},{9,13},{21,17},{17,21},{14,10... | collective-permute-start | bytes 2457608 | tf_op jit(solution)/shard_map/ppermute | solution.py:403
  51.3 28.4 %collective-permute-start.8 = (bf16[400,1024]{1,0:T(8,128)(2,1)S(1)}, bf16[400,1024]{1,0:T(8,128)(2,1)S(1)}, u32[]{:S(2)}, u32[]{:S(2)}) collective-permute-start(bf16[400,1024]{1,0:T(8,128)(2,1)S(1)} %copy-done.3), channel_id=1, source_target_pairs={{24,8},{28,12},{0,16},{4,20},{25,9},{29,13},{1,17},{5,21},{26,10},... | collective-permute-start | bytes 2457608 | tf_op jit(solution)/shard_map/ppermute | solution.py:403
  61.1 35.2 %collective-permute-start.2 = (bf16[400,1024]{1,0:T(8,128)(2,1)S(1)}, bf16[400,1024]{1,0:T(8,128)(2,1)S(1)}, u32[]{:S(2)}, u32[]{:S(2)}) collective-permute-start(bf16[400,1024]{1,0:T(8,128)(2,1)S(1)} %get-tuple-element.31.refs_1_), channel_id=1, source_target_pairs={{28,8},{24,12},{4,16},{0,20},{29,9},{25,13},{5,17},{1,21},{30,10},... | collective-permute-start | bytes 2457608 | tf_op jit(solution)/shard_map/ppermute | solution.py:403
  66.0 14.7 %collective-permute-start.7 = (bf16[1200,1024]{1,0:T(8,128)(2,1)S(1)}, bf16[1200,1024]{1,0:T(8,128)(2,1)S(1)}, u32[]{:S(2)}, u32[]{:S(2)}) collective-permute-start(bf16[1200,1024]{1,0:T(8,128)(2,1)S(1)} %shard_map.59.refs_4_), channel_id=1, source_target_pairs={{8,9},{9,8},{10,11},{11,10},{12,13},{13,12},{14,15},{15,14},{16,17... | collective-permute-start | bytes 7372808 | tf_op jit(solution)/shard_map/ppermute | solution.py:406
  79.9 17.3 %collective-permute-start.11 = (bf16[800,1024]{1,0:T(8,128)(2,1)S(1)}, bf16[800,1024]{1,0:T(8,128)(2,1)S(1)}, u32[]{:S(2)}, u32[]{:S(2)}) collective-permute-start(bf16[800,1024]{1,0:T(8,128)(2,1)S(1)} %shard_map.61.refs_7_), channel_id=1, source_target_pairs={{8,9},{9,8},{10,11},{11,10},{12,13},{13,12},{14,15},{15,14},{16,17... | collective-permute-start | bytes 4915208 | tf_op jit(solution)/shard_map/ppermute | solution.py:406
  96.3 11.7 %collective-permute-start.10 = (bf16[400,1024]{1,0:T(8,128)(2,1)S(1)}, bf16[400,1024]{1,0:T(8,128)(2,1)S(1)}, u32[]{:S(2)}, u32[]{:S(2)}) collective-permute-start(bf16[400,1024]{1,0:T(8,128)(2,1)S(1)} %collective-permute-done.2.refs_9_.own_ref), channel_id=1, source_target_pairs={{8,9},{9,8},{10,11},{11,10},{12,13},{13,12},{14,15},{15,14},{16,17... | collective-permute-start | bytes 2457608 | tf_op jit(solution)/shard_map/ppermute | solution.py:406

commit v14 on v13

--- a/solution.py
+++ b/solution.py
@@ -112,23 +112,23 @@
     width = raw.shape[1]
     tiles = width // LANES
     part = raw.shape[0] // sections
-    copies = []
+
+    def load(i):
+        rows = pl.ds(pl.multiple_of(i * part, part), part)
+        return pltpu.make_async_copy(rows_ref.at[rows], raw.at[rows], sems.at[i])
+
     for i in range(sections):
-        rows = pl.ds(i * part, part)
-        copies.append(pltpu.make_async_copy(rows_ref.at[rows], raw.at[rows], sems.at[i]))
-        copies[-1].start()
-    step = 160
-    for i in range(sections):
-        copies[i].wait()
-
-        def widen(j, _, i=i):
-            first = i * part + j * step
-            rows = raw[pl.ds(pl.multiple_of(first, step), step), :].astype(jnp.float32)
-            for t in range(tiles):
-                wide[pl.ds(first * tiles + t, step, stride=tiles), :] = rows[:, t * LANES : (t + 1) * LANES]
-            return 0
-
-        lax.fori_loop(0, part // step, widen, 0)
+        load(i).start()
+
+    def widen(i, _):
+        load(i).wait()
+        first = pl.multiple_of(i * part, part)
+        rows = raw[pl.ds(first, part), :].astype(jnp.float32)
+        for t in range(tiles):
+            wide[pl.ds(first * tiles + t, part, stride=tiles), :] = rows[:, t * LANES : (t + 1) * LANES]
+        return 0
+
+    lax.fori_loop(0, sections, widen, 0)
     listed.wait()
     for c, slot in enumerate(slots):
         base = chunk_start(slot, size)
@@ -154,7 +154,7 @@
 def gather_rows(embeddings, index, slots, size):
     documents, width = embeddings.shape
     count = len(slots)
-    sections = 10
+    sections = 20
     group = 80
     return pl.pallas_call(
         functools.partial(gather_kernel, slots, size, group, sections),
@@ -411,7 +411,7 @@
     own[0], other[0] = late[2:]
     own[3], own[4] = go(3, late[0]), go(4, late[0])
     own[1], own[2] = tie(own[1], late[0]), tie(own[2], late[0])
-    own[5] = go(5, tie(late[1], own[4]))
+    own[5] = go(5, tie(late[1], own[1]))
     own[6] = go(6, tie(late[1], own[2]))
 
     named, table = tie(named, late[0]), tie(jnp.asarray(chunk_order()), late[0])

time: 129 us -> 142 us (1.10)
  blocking collectives: 16.6 us -> 31.5 us
  starting transfers between devices: 32.5 us -> 29.8 us
    all_to_all x1, blocking collectives: 16.6 us -> 31.5 us  [hosted(): lax.all_to_all(outbound, axes, split_axis=0, concat_axis=0, tiled=True)]
    ppermute x7, starting transfers between devices: 24.1 us -> 21.7 us  [go(): return lax.ppermute(chunk, axes, round_pairs(step - 1))]
  transfers between devices with their start and end apart: 12 -> 12, of which waited for: 1 -> 2; matrix products, arithmetic and copies ran while one was open for 2% -> 2% of each run, Pallas kernels for 50% -> 46%
where the time goes in v14:
time: 142 us; the launch traced here: 141 us
  Pallas kernels  70.4 us (50%)
  blocking collectives  31.5 us (22%)
  starting transfers between devices  29.8 us (21%)
  waiting for transfers between devices  5.08 us (4%)
  local copies, waits for them, and re-layouts  3.3 us (2%)
    pallas_call x4, Pallas kernels, gram_best(): pl.pallas_call(functools.partial(gram_kernel, passes, loads, size, limit)...  39.8 us
    all_to_all x1, blocking collectives, hosted(): lax.all_to_all(outbound, axes, split_axis=0, concat_axis=0, tiled=True)  31.5 us
    pallas_call x2, Pallas kernels, gather_rows(): pl.pallas_call(functools.partial(gather_kernel, slots, size, group, secti...  23.6 us
    ppermute x7, starting transfers between devices, go(): return lax.ppermute(chunk, axes, round_pairs(step - 1))  21.7 us
    ppermute x7, waiting for transfers between devices, go(): return lax.ppermute(chunk, axes, round_pairs(step - 1))  5.06 us
    ppermute x1, starting transfers between devices, hosted(): named = lax.ppermute(named, axes, metadata_pairs())  4.92 us
    ppermute x4, starting transfers between devices, swap(): return lax.ppermute(chunk, axes, SIBLINGS)  3.19 us
  transfers between devices with their start and end apart: 12, of which 2 were waited for; matrix products, arithmetic and copies ran while one was open for 2% of the time, Pallas kernels for 46%

profile of v14, /device:TPU:0, one launch (start us, length us, event | category | flops | bytes accessed | tf_op | source)
XLA Modules:
  0.0 141.2 jit_solution(7049244144930630744)
XLA Ops:
  0.0 1.5 %shard_map.55 = s32[50,128]{1,0:T(8,128)} custom-call(s32[50,128]{1,0:T(8,128)} %bitcast.9, s32[52,128]{1,0:T(8,128)} %bitcast.10), custom_call_target="tpu_custom_call" | custom-call | tf_op jit(solution)/shard_map/pallas_call | solution.py:87
  1.5 4.9 %collective-permute-start = (s32[50,128]{1,0:T(8,128)}, s32[50,128]{1,0:T(8,128)S(1)}, u32[]{:S(2)}, u32[]{:S(2)}) collective-permute-start(s32[50,128]{1,0:T(8,128)} %shard_map.55), channel_id=1, source_target_pairs={{0,8},{1,9},{4,12},{5,13},{10,10},{11,11},{14,14},{15,15},{16,16},... | collective-permute-start | bytes 76808 | tf_op jit(solution)/shard_map/ppermute | solution.py:398
  6.4 0.0 copy-start
  6.4 0.7 copy-done
  7.1 10.1 %shard_map.56 = bf16[400,1024]{1,0:T(8,128)(2,1)} custom-call(s32[6400]{0:T(1024)S(1)} %copy-done, bf16[6400,1024]{1,0:T(8,128)(2,1)} %refs_1_.1), custom_call_target="tpu_custom_call" | custom-call | flops 40000000000 | tf_op jit(solution)/shard_map/pallas_call | solution.py:159
  17.3 0.0 copy-done.1
  17.3 0.1 reshape.46.refs_5_.index_ref
  17.4 0.0 collective-permute-done
  17.4 0.7 collective-permute-start.4
  18.1 4.2 %collective-permute-start.3 = (bf16[400,1024]{1,0:T(8,128)(2,1)}, bf16[400,1024]{1,0:T(8,128)(2,1)S(1)}, u32[]{:S(2)}, u32[]{:S(2)}) collective-permute-start(bf16[400,1024]{1,0:T(8,128)(2,1)} %shard_map.56), channel_id=1, source_target_pairs={{0,8},{4,12},{24,16},{28,20},{5,9},{1,13},{29,17},{25,21},{2,10},{... | collective-permute-start | bytes 2457608 | tf_op jit(solution)/shard_map/ppermute | solution.py:403
  22.4 13.4 %shard_map.57 = (bf16[400,1024]{1,0:T(8,128)(2,1)}, bf16[400,1024]{1,0:T(8,128)(2,1)S(1)}, bf16[400,1024]{1,0:T(8,128)(2,1)S(1)}, bf16[400,1024]{1,0:T(8,128)(2,1)S(1)}) custom-call(s32[6400]{0:T(1024)S(1)} %copy-done.1, bf16[6400,1024]{1,0:T(8,128)(2,1)} %refs_1_.1), custom_call_target="tpu_custom_call" | custom-call | flops 40000000000 | tf_op jit(solution)/shard_map/pallas_call | solution.py:159
  35.8 0.0 copy-start.2
  35.8 0.9 copy-done.2
  36.7 1.6 %collective-permute-start.5 = (bf16[400,1024]{1,0:T(8,128)(2,1)}, bf16[400,1024]{1,0:T(8,128)(2,1)}, u32[]{:S(2)}, u32[]{:S(2)}) collective-permute-start(bf16[400,1024]{1,0:T(8,128)(2,1)} %get-tuple-element.28), channel_id=1, source_target_pairs={{20,8},{16,12},{12,16},{8,20},{17,9},{21,13},{9,17},{13,21},{22,10... | collective-permute-start | bytes 2457608 | tf_op jit(solution)/shard_map/ppermute | solution.py:403
  38.3 3.7 %collective-permute-start.1 = (bf16[400,1024]{1,0:T(8,128)(2,1)}, bf16[400,1024]{1,0:T(8,128)(2,1)}, u32[]{:S(2)}, u32[]{:S(2)}) collective-permute-start(bf16[400,1024]{1,0:T(8,128)(2,1)} %get-tuple-element.28), channel_id=1, source_target_pairs={{4,8},{0,12},{28,16},{24,20},{1,9},{5,13},{25,17},{29,21},{6,10},{... | collective-permute-start | bytes 2457608 | tf_op jit(solution)/shard_map/ppermute | solution.py:403
  42.0 0.1 reshape.49
  42.1 0.7 fusion
  42.8 0.6 gather_fusion
  43.4 0.1 reshape.50.refs_6_.refs_8_.refs_10_.clusters_ref
  43.5 0.0 copy-start.3
  43.5 0.8 fusion.1.refs_4_.order_ref
  44.2 0.0 collective-permute-done.4.refs_3_.refs_0_
  44.2 0.0 collective-permute-done.3.refs_2_
  44.3 5.9 %shard_map.58.refs_7_ = f32[1,6400]{1,0:T(1,128)S(1)} custom-call(bf16[400,1024]{1,0:T(8,128)(2,1)S(1)} %get-tuple-element.32.refs_0_, bf16[400,1024]{1,0:T(8,128)(2,1)S(1)} %get-tuple-element.31.refs_1_, bf16[400,1024]{1,0:T(8,128)(2,1)S(1)} %collective-permute-done.3.refs_2_, bf16[400,1024]{1,0:T(8,128)(2,1)S(1)} %collective-permute-done.4.refs_3_.refs_0_, ...), custom_call_target="tpu_custom_call" | custom-call | tf_op jit(solution)/shard_map/pallas_call | solution.py:264
  50.2 0.7 collective-permute-start.6
  50.9 0.7 collective-permute-start.9
  51.6 4.5 %collective-permute-start.8 = (bf16[400,1024]{1,0:T(8,128)(2,1)S(1)}, bf16[400,1024]{1,0:T(8,128)(2,1)S(1)}, u32[]{:S(2)}, u32[]{:S(2)}) collective-permute-start(bf16[400,1024]{1,0:T(8,128)(2,1)S(1)} %copy-done.3), channel_id=1, source_target_pairs={{24,8},{28,12},{0,16},{4,20},{25,9},{29,13},{1,17},{5,21},{26,10},... | collective-permute-start | bytes 2457608 | tf_op jit(solution)/shard_map/ppermute | solution.py:403
  56.2 0.0 collective-permute-done.5.refs_2_
  56.2 3.9 %collective-permute-done.1.refs_1_ = bf16[400,1024]{1,0:T(8,128)(2,1)} collective-permute-done((bf16[400,1024]{1,0:T(8,128)(2,1)}, bf16[400,1024]{1,0:T(8,128)(2,1)}, u32[]{:S(2)}, u32[]{:S(2)}) %collective-permute-start.1) | collective-permute-done | bytes 819232 | tf_op jit(solution)/shard_map/ppermute | solution.py:403
  60.1 6.3 %collective-permute-start.2 = (bf16[400,1024]{1,0:T(8,128)(2,1)S(1)}, bf16[400,1024]{1,0:T(8,128)(2,1)S(1)}, u32[]{:S(2)}, u32[]{:S(2)}) collective-permute-start(bf16[400,1024]{1,0:T(8,128)(2,1)S(1)} %get-tuple-element.31.refs_1_), channel_id=1, source_target_pairs={{28,8},{24,12},{4,16},{0,20},{29,9},{25,13},{5,17},{1,21},{30,10},... | collective-permute-start | bytes 2457608 | tf_op jit(solution)/shard_map/ppermute | solution.py:403
  66.4 1.5 %shard_map.59.refs_4_ = bf16[1200,1024]{1,0:T(8,128)(2,1)S(1)} custom-call(bf16[400,1024]{1,0:T(8,128)(2,1)S(1)} %collective-permute-done.4.refs_3_.refs_0_, bf16[400,1024]{1,0:T(8,128)(2,1)} %collective-permute-done.1.refs_1_, bf16[400,1024]{1,0:T(8,128)(2,1)} %collective-permute-done.5.refs_2_), custom_call_target="tpu_custom_call" | custom-call | flops 2000000000 | tf_op jit(solution)/shard_map/pallas_call | solution.py:294
  67.9 0.8 collective-permute-start.7
  68.7 0.0 collective-permute-done.6.refs_5_
  68.7 7.7 %shard_map.60.refs_9_ = f32[1,6400]{1,0:T(1,128)S(1)} custom-call(bf16[400,1024]{1,0:T(8,128)(2,1)S(1)} %get-tuple-element.32.refs_0_, bf16[400,1024]{1,0:T(8,128)(2,1)S(1)} %get-tuple-element.31.refs_1_, bf16[400,1024]{1,0:T(8,128)(2,1)S(1)} %collective-permute-done.3.refs_2_, bf16[400,1024]{1,0:T(8,128)(2,1)S(1)} %collective-permute-done.4.refs_3_.refs_0_, ...), custom_call_target="tpu_custom_call" | custom-call | tf_op jit(solution)/shard_map/pallas_call | solution.py:264
  76.4 0.0 collective-permute-done.9.refs_1_
  76.4 1.1 collective-permute-done.8.refs_0_
  77.5 0.2 shard_map.61.refs_7_
  77.8 0.9 collective-permute-start.11
  78.7 0.0 collective-permute-done.7.refs_6_
  78.7 15.6 %shard_map.62.refs_11_ = f32[1,6400]{1,0:T(1,128)S(1)} custom-call(bf16[400,1024]{1,0:T(8,128)(2,1)S(1)} %get-tuple-element.32.refs_0_, bf16[400,1024]{1,0:T(8,128)(2,1)S(1)} %get-tuple-element.31.refs_1_, bf16[400,1024]{1,0:T(8,128)(2,1)S(1)} %collective-permute-done.3.refs_2_, bf16[400,1024]{1,0:T(8,128)(2,1)S(1)} %collective-permute-done.4.refs_3_.refs_0_, ...), custom_call_target="tpu_custom_call" | custom-call | tf_op jit(solution)/shard_map/pallas_call | solution.py:264
  94.3 0.0 collective-permute-done.2.refs_9_.own_ref
  94.3 0.7 collective-permute-start.10
  95.0 0.0 collective-permute-done.11.refs_8_
  95.0 10.7 %shard_map.63.best_ref = f32[1,6400]{1,0:T(1,128)S(1)} custom-call(bf16[400,1024]{1,0:T(8,128)(2,1)S(1)} %get-tuple-element.32.refs_0_, bf16[400,1024]{1,0:T(8,128)(2,1)S(1)} %get-tuple-element.31.refs_1_, bf16[400,1024]{1,0:T(8,128)(2,1)S(1)} %collective-permute-done.3.refs_2_, bf16[400,1024]{1,0:T(8,128)(2,1)S(1)} %collective-permute-done.4.refs_3_.refs_0_, ...), custom_call_target="tpu_custom_call" | custom-call | tf_op jit(solution)/shard_map/pallas_call | solution.py:264
  105.8 0.0 collective-permute-done.10.other_ref
  105.8 1.5 %shard_map.64 = f32[32,2,400]{2,1,0:T(2,128)S(1)} custom-call(s32[16]{0:T(128)S(1)} %fusion.1.refs_4_.order_ref, bf16[400,1024]{1,0:T(8,128)(2,1)S(1)} %collective-permute-done.2.refs_9_.own_ref, bf16[400,1024]{1,0:T(8,128)(2,1)S(1)} %collective-permute-done.10.other_ref, s32[1,6400]{1,0:T(1,128)S(1)} %reshape.50.refs_6_.refs_8_.refs_10_.clusters_ref, ...), custom_call_target="tpu_custom_call" | custom-call | tf_op jit(solution)/shard_map/pallas_call | solution.py:339
  107.3 31.5 %all_to_all.5.values_ref = f32[32,2,400]{2,1,0:T(2,128)S(1)} all-to-all(f32[32,2,400]{2,1,0:T(2,128)S(1)} %shard_map.64), channel_id=1, replica_groups=mesh['shard'=8,'rep'=4] {'shard','rep'}, dimensions={0} | all-to-all | bytes 204800 | tf_op jit(solution)/shard_map/all_to_all | solution.py:449
  138.8 2.4 %shard_map.65 = f32[50,128]{1,0:T(8,128)} custom-call(s32[8,2,400]{2,1,0:T(2,128)S(1)} %reshape.46.refs_5_.index_ref, f32[32,2,400]{2,1,0:T(2,128)S(1)} %all_to_all.5.values_ref), custom_call_target="tpu_custom_call" | custom-call | tf_op jit(solution)/shard_map/pallas_call | solution.py:379
  (4 shorter events, 0.0 us)
Async XLA Ops:
  1.5 15.9 %collective-permute-start = (s32[50,128]{1,0:T(8,128)}, s32[50,128]{1,0:T(8,128)S(1)}, u32[]{:S(2)}, u32[]{:S(2)}) collective-permute-start(s32[50,128]{1,0:T(8,128)} %shard_map.55), channel_id=1, source_target_pairs={{0,8},{1,9},{4,12},{5,13},{10,10},{11,11},{14,14},{15,15},{16,16},... | collective-permute-start | bytes 76808 | tf_op jit(solution)/shard_map/ppermute | solution.py:398
  6.4 0.8 copy-start
  7.1 10.1 %copy-start.1 = (s32[6400]{0:T(1024)S(1)}, s32[6400]{0:T(1024)}, u32[]{:S(2)}) copy-start(s32[6400]{0:T(1024)} %refs_0_.3) | copy-start | bytes 76804
  17.4 26.8 %collective-permute-start.4 = (bf16[400,1024]{1,0:T(8,128)(2,1)}, bf16[400,1024]{1,0:T(8,128)(2,1)S(1)}, u32[]{:S(2)}, u32[]{:S(2)}) collective-permute-start(bf16[400,1024]{1,0:T(8,128)(2,1)} %shard_map.56), channel_id=1, source_target_pairs={{16,8},{20,12},{8,16},{12,20},{21,9},{17,13},{13,17},{9,21},{18,10... | collective-permute-start | bytes 2457608 | tf_op jit(solution)/shard_map/ppermute | solution.py:403
  18.1 26.1 %collective-permute-start.3 = (bf16[400,1024]{1,0:T(8,128)(2,1)}, bf16[400,1024]{1,0:T(8,128)(2,1)S(1)}, u32[]{:S(2)}, u32[]{:S(2)}) collective-permute-start(bf16[400,1024]{1,0:T(8,128)(2,1)} %shard_map.56), channel_id=1, source_target_pairs={{0,8},{4,12},{24,16},{28,20},{5,9},{1,13},{29,17},{25,21},{2,10},{... | collective-permute-start | bytes 2457608 | tf_op jit(solution)/shard_map/ppermute | solution.py:403
  35.8 0.9 copy-start.2
  36.7 19.5 %collective-permute-start.5 = (bf16[400,1024]{1,0:T(8,128)(2,1)}, bf16[400,1024]{1,0:T(8,128)(2,1)}, u32[]{:S(2)}, u32[]{:S(2)}) collective-permute-start(bf16[400,1024]{1,0:T(8,128)(2,1)} %get-tuple-element.28), channel_id=1, source_target_pairs={{20,8},{16,12},{12,16},{8,20},{17,9},{21,13},{9,17},{13,21},{22,10... | collective-permute-start | bytes 2457608 | tf_op jit(solution)/shard_map/ppermute | solution.py:403
  38.3 21.8 %collective-permute-start.1 = (bf16[400,1024]{1,0:T(8,128)(2,1)}, bf16[400,1024]{1,0:T(8,128)(2,1)}, u32[]{:S(2)}, u32[]{:S(2)}) collective-permute-start(bf16[400,1024]{1,0:T(8,128)(2,1)} %get-tuple-element.28), channel_id=1, source_target_pairs={{4,8},{0,12},{28,16},{24,20},{1,9},{5,13},{25,17},{29,21},{6,10},{... | collective-permute-start | bytes 2457608 | tf_op jit(solution)/shard_map/ppermute | solution.py:403
  43.5 7.4 %copy-start.3 = (bf16[400,1024]{1,0:T(8,128)(2,1)S(1)}, bf16[400,1024]{1,0:T(8,128)(2,1)}, u32[]{:S(2)}) copy-start(bf16[400,1024]{1,0:T(8,128)(2,1)} %copy-done.2) | copy-start | bytes 2457604
  50.2 18.5 %collective-permute-start.6 = (bf16[400,1024]{1,0:T(8,128)(2,1)S(1)}, bf16[400,1024]{1,0:T(8,128)(2,1)S(1)}, u32[]{:S(2)}, u32[]{:S(2)}) collective-permute-start(bf16[400,1024]{1,0:T(8,128)(2,1)S(1)} %collective-permute-done.3.refs_2_), channel_id=1, source_target_pairs={{8,9},{9,8},{10,11},{11,10},{12,13},{13,12},{14,15},{15,14},{16,17... | collective-permute-start | bytes 2457608 | tf_op jit(solution)/shard_map/ppermute | solution.py:406
  50.9 25.5 %collective-permute-start.9 = (bf16[400,1024]{1,0:T(8,128)(2,1)S(1)}, bf16[400,1024]{1,0:T(8,128)(2,1)S(1)}, u32[]{:S(2)}, u32[]{:S(2)}) collective-permute-start(bf16[400,1024]{1,0:T(8,128)(2,1)S(1)} %copy-done.3), channel_id=1, source_target_pairs={{12,8},{8,12},{20,16},{16,20},{13,9},{9,13},{21,17},{17,21},{14,10... | collective-permute-start | bytes 2457608 | tf_op jit(solution)/shard_map/ppermute | solution.py:403
  51.6 25.9 %collective-permute-start.8 = (bf16[400,1024]{1,0:T(8,128)(2,1)S(1)}, bf16[400,1024]{1,0:T(8,128)(2,1)S(1)}, u32[]{:S(2)}, u32[]{:S(2)}) collective-permute-start(bf16[400,1024]{1,0:T(8,128)(2,1)S(1)} %copy-done.3), channel_id=1, source_target_pairs={{24,8},{28,12},{0,16},{4,20},{25,9},{29,13},{1,17},{5,21},{26,10},... | collective-permute-start | bytes 2457608 | tf_op jit(solution)/shard_map/ppermute | solution.py:403
  60.1 34.2 %collective-permute-start.2 = (bf16[400,1024]{1,0:T(8,128)(2,1)S(1)}, bf16[400,1024]{1,0:T(8,128)(2,1)S(1)}, u32[]{:S(2)}, u32[]{:S(2)}) collective-permute-start(bf16[400,1024]{1,0:T(8,128)(2,1)S(1)} %get-tuple-element.31.refs_1_), channel_id=1, source_target_pairs={{28,8},{24,12},{4,16},{0,20},{29,9},{25,13},{5,17},{1,21},{30,10},... | collective-permute-start | bytes 2457608 | tf_op jit(solution)/shard_map/ppermute | solution.py:403
  67.9 10.8 %collective-permute-start.7 = (bf16[1200,1024]{1,0:T(8,128)(2,1)S(1)}, bf16[1200,1024]{1,0:T(8,128)(2,1)S(1)}, u32[]{:S(2)}, u32[]{:S(2)}) collective-permute-start(bf16[1200,1024]{1,0:T(8,128)(2,1)S(1)} %shard_map.59.refs_4_), channel_id=1, source_target_pairs={{8,9},{9,8},{10,11},{11,10},{12,13},{13,12},{14,15},{15,14},{16,17... | collective-permute-start | bytes 7372808 | tf_op jit(solution)/shard_map/ppermute | solution.py:406
  77.8 17.3 %collective-permute-start.11 = (bf16[800,1024]{1,0:T(8,128)(2,1)S(1)}, bf16[800,1024]{1,0:T(8,128)(2,1)S(1)}, u32[]{:S(2)}, u32[]{:S(2)}) collective-permute-start(bf16[800,1024]{1,0:T(8,128)(2,1)S(1)} %shard_map.61.refs_7_), channel_id=1, source_target_pairs={{8,9},{9,8},{10,11},{11,10},{12,13},{13,12},{14,15},{15,14},{16,17... | collective-permute-start | bytes 4915208 | tf_op jit(solution)/shard_map/ppermute | solution.py:406
  94.3 11.5 %collective-permute-start.10 = (bf16[400,1024]{1,0:T(8,128)(2,1)S(1)}, bf16[400,1024]{1,0:T(8,128)(2,1)S(1)}, u32[]{:S(2)}, u32[]{:S(2)}) collective-permute-start(bf16[400,1024]{1,0:T(8,128)(2,1)S(1)} %collective-permute-done.2.refs_9_.own_ref), channel_id=1, source_target_pairs={{8,9},{9,8},{10,11},{11,10},{12,13},{13,12},{14,15},{15,14},{16,17... | collective-permute-start | bytes 2457608 | tf_op jit(solution)/shard_map/ppermute | solution.py:406

commit v15 on v13

--- a/solution.py
+++ b/solution.py
@@ -186,7 +186,6 @@
 def gram_kernel(passes, loads, size, limit, *refs):
     cluster_row, before_ref, best_ref, held, acc, sems = refs[-6:]
     count = len(loads)
-    first = range(passes[0][0], passes[0][0] + passes[0][1])
 
     def source(i):
         array, place = loads[i]
@@ -199,13 +198,11 @@
         rows = held.at[pl.ds(0, size)]
         pltpu.make_async_copy(rows, rows, sems.at[i]).wait()
 
-    for i in first:
+    low = passes[0][5][0] * BLK // size
+    for i in (*range(low, count), *range(low)):
         copy(i).start()
-    for i in range(count):
-        if i not in first:
-            copy(i).start()
     best_ref[...] = before_ref[...]
-    for i in first:
+    for i in range(low, count):
         copy(i).wait()
     for n, (chunk, news, groups, group, meets, last) in enumerate(passes):
         height = news * size
@@ -230,27 +227,24 @@
                 acc[0:height, :], jnp.maximum(values[:, :LANES], values[:, LANES:])
             )
 
-        def visit(u, _, n=n, group=group, meets=meets, tile=tile):
-            if n == 0:
-                for i in (2 * u, 2 * u + 1):
-
-                    @pl.when(i < first[0])
-                    def _(i=i):
-                        arrive(i)
+        for t in last:
+            start, stop = t * BLK, (t + 1) * BLK
+            own = start < chunk * size + height and stop > chunk * size
+            tile(start, own or stop > limit)
+        step = -(-group * BLK // size)
+
+        def visit(u, _, n=n, group=group, meets=meets, tile=tile, step=step):
+            for i in range(step) if n == 0 else ():
+
+                @pl.when(u * step + i < low)
+                def _(i=i):
+                    arrive(u * step + i)
 
             for t in range(group):
                 tile(pl.multiple_of((u * group + t) * BLK, BLK), meets)
             return 0
 
         lax.fori_loop(0, groups, visit, 0)
-        if n == 0:
-            for i in range(count):
-                if i not in first and not i < min(2 * groups, first[0]):
-                    arrive(i)
-        for t in last:
-            start, stop = t * BLK, (t + 1) * BLK
-            meets = start < chunk * size + height and stop > chunk * size
-            tile(start, meets or stop > limit)
         span = slice(chunk * size, chunk * size + height)
         best_ref[:, span] = jnp.maximum(best_ref[:, span], best_of_rows(acc[...], height))
 
@@ -303,8 +297,9 @@
 
 
 def new_pass(chunk, news, count, size):
-    group = 3
-    groups = chunk * size // (group * BLK)
+    plain = chunk * size // BLK
+    group = max(n for n in range(1, 8) if plain % n == 0)
+    groups = plain // group
     tiles = -(-count * size // BLK)
     return (chunk, news, groups, group, False, tuple(range(groups * group, tiles)))
 

time: 129 us -> 127 us (0.984)
  Pallas kernels: 70 us -> 67 us
    pallas_call x4, Pallas kernels: 39.8 us -> 36.8 us  [gram_best(): pl.pallas_call(functools.partial(gram_kernel, passes, loads, size, limit)...]
  transfers between devices with their start and end apart: 12 -> 12, of which waited for: 1 -> 1; matrix products, arithmetic and copies ran while one was open for 2% -> 2% of each run, Pallas kernels for 50% -> 49%
where the time goes in v15:
time: 127 us
  Pallas kernels  67 us (53%)
  starting transfers between devices  33 us (26%)
  blocking collectives  16.6 us (13%)
  waiting for transfers between devices  5.65 us (4%)
  local copies, waits for them, and re-layouts  3.3 us (3%)
    pallas_call x4, Pallas kernels, gram_best(): pl.pallas_call(functools.partial(gram_kernel, passes, loads, size, limit)...  36.8 us
    ppermute x7, starting transfers between devices, go(): return lax.ppermute(chunk, axes, round_pairs(step - 1))  24.6 us
    pallas_call x2, Pallas kernels, gather_rows(): pl.pallas_call(functools.partial(gather_kernel, slots, size, group, secti...  23.2 us
    all_to_all x1, blocking collectives, hosted(): lax.all_to_all(outbound, axes, split_axis=0, concat_axis=0, tiled=True)  16.6 us
    ppermute x7, waiting for transfers between devices, go(): return lax.ppermute(chunk, axes, round_pairs(step - 1))  5.64 us
    ppermute x1, starting transfers between devices, hosted(): named = lax.ppermute(named, axes, metadata_pairs())  4.92 us
    ppermute x4, starting transfers between devices, swap(): return lax.ppermute(chunk, axes, SIBLINGS)  3.41 us
  transfers between devices with their start and end apart: 12, of which 1 were waited for; matrix products, arithmetic and copies ran while one was open for 2% of the time, Pallas kernels for 49%

profile of v15, /device:TPU:0, one launch (start us, length us, event | category | flops | bytes accessed | tf_op | source)
XLA Modules:
  0.0 126.5 jit_solution(14053808099796875583)
XLA Ops:
  0.0 1.5 %shard_map.55 = s32[50,128]{1,0:T(8,128)} custom-call(s32[50,128]{1,0:T(8,128)} %bitcast.9, s32[52,128]{1,0:T(8,128)} %bitcast.10), custom_call_target="tpu_custom_call" | custom-call | tf_op jit(solution)/shard_map/pallas_call | solution.py:87
  1.5 4.9 %collective-permute-start = (s32[50,128]{1,0:T(8,128)}, s32[50,128]{1,0:T(8,128)S(1)}, u32[]{:S(2)}, u32[]{:S(2)}) collective-permute-start(s32[50,128]{1,0:T(8,128)} %shard_map.55), channel_id=1, source_target_pairs={{0,8},{1,9},{4,12},{5,13},{10,10},{11,11},{14,14},{15,15},{16,16},... | collective-permute-start | bytes 76808 | tf_op jit(solution)/shard_map/ppermute | solution.py:393
  6.4 0.0 copy-start
  6.4 0.7 copy-done
  7.1 9.9 %shard_map.56 = bf16[400,1024]{1,0:T(8,128)(2,1)} custom-call(s32[6400]{0:T(1024)S(1)} %copy-done, bf16[6400,1024]{1,0:T(8,128)(2,1)} %refs_1_.1), custom_call_target="tpu_custom_call" | custom-call | flops 40000000000 | tf_op jit(solution)/shard_map/pallas_call | solution.py:159
  17.1 0.0 copy-start.1
  17.1 0.0 collective-permute-done
  17.1 0.7 collective-permute-start.4
  17.8 4.2 %collective-permute-start.3 = (bf16[400,1024]{1,0:T(8,128)(2,1)}, bf16[400,1024]{1,0:T(8,128)(2,1)S(1)}, u32[]{:S(2)}, u32[]{:S(2)}) collective-permute-start(bf16[400,1024]{1,0:T(8,128)(2,1)} %shard_map.56), channel_id=1, source_target_pairs={{0,8},{4,12},{24,16},{28,20},{5,9},{1,13},{29,17},{25,21},{2,10},{... | collective-permute-start | bytes 2457608 | tf_op jit(solution)/shard_map/ppermute | solution.py:398
  22.0 13.2 %shard_map.57 = (bf16[400,1024]{1,0:T(8,128)(2,1)}, bf16[400,1024]{1,0:T(8,128)(2,1)S(1)}, bf16[400,1024]{1,0:T(8,128)(2,1)S(1)}, bf16[400,1024]{1,0:T(8,128)(2,1)S(1)}) custom-call(s32[6400]{0:T(1024)S(1)} %copy-done, bf16[6400,1024]{1,0:T(8,128)(2,1)} %refs_1_.1), custom_call_target="tpu_custom_call" | custom-call | flops 40000000000 | tf_op jit(solution)/shard_map/pallas_call | solution.py:159
  35.3 0.0 copy-start.2
  35.3 0.9 copy-done.2
  36.2 1.6 %collective-permute-start.5 = (bf16[400,1024]{1,0:T(8,128)(2,1)}, bf16[400,1024]{1,0:T(8,128)(2,1)}, u32[]{:S(2)}, u32[]{:S(2)}) collective-permute-start(bf16[400,1024]{1,0:T(8,128)(2,1)} %get-tuple-element.28), channel_id=1, source_target_pairs={{20,8},{16,12},{12,16},{8,20},{17,9},{21,13},{9,17},{13,21},{22,10... | collective-permute-start | bytes 2457608 | tf_op jit(solution)/shard_map/ppermute | solution.py:398
  37.8 0.0 copy-done.1
  37.8 0.1 reshape.46.refs_5_.index_ref
  37.9 3.7 %collective-permute-start.1 = (bf16[400,1024]{1,0:T(8,128)(2,1)}, bf16[400,1024]{1,0:T(8,128)(2,1)}, u32[]{:S(2)}, u32[]{:S(2)}) collective-permute-start(bf16[400,1024]{1,0:T(8,128)(2,1)} %get-tuple-element.28), channel_id=1, source_target_pairs={{4,8},{0,12},{28,16},{24,20},{1,9},{5,13},{25,17},{29,21},{6,10},{... | collective-permute-start | bytes 2457608 | tf_op jit(solution)/shard_map/ppermute | solution.py:398
  41.6 0.1 reshape.49
  41.7 0.7 fusion
  42.4 0.6 gather_fusion
  43.0 0.1 reshape.50.refs_6_.refs_8_.refs_10_.clusters_ref
  43.1 0.8 fusion.1.refs_4_.order_ref
  43.9 0.0 collective-permute-done.4.refs_3_.refs_0_
  43.9 0.0 collective-permute-done.3.refs_2_
  43.9 5.4 %shard_map.58.refs_7_ = f32[1,6400]{1,0:T(1,128)S(1)} custom-call(bf16[400,1024]{1,0:T(8,128)(2,1)S(1)} %get-tuple-element.32.refs_0_, bf16[400,1024]{1,0:T(8,128)(2,1)S(1)} %get-tuple-element.31.refs_1_, bf16[400,1024]{1,0:T(8,128)(2,1)S(1)} %collective-permute-done.3.refs_2_, bf16[400,1024]{1,0:T(8,128)(2,1)S(1)} %collective-permute-done.4.refs_3_.refs_0_, ...), custom_call_target="tpu_custom_call" | custom-call | tf_op jit(solution)/shard_map/pallas_call | solution.py:258
  49.3 0.7 collective-permute-start.6
  50.0 0.7 collective-permute-start.9
  50.8 0.0 collective-permute-done.5.refs_2_
  50.8 10.3 %collective-permute-start.8 = (bf16[400,1024]{1,0:T(8,128)(2,1)S(1)}, bf16[400,1024]{1,0:T(8,128)(2,1)S(1)}, u32[]{:S(2)}, u32[]{:S(2)}) collective-permute-start(bf16[400,1024]{1,0:T(8,128)(2,1)S(1)} %copy-done.3), channel_id=1, source_target_pairs={{24,8},{28,12},{0,16},{4,20},{25,9},{29,13},{1,17},{5,21},{26,10},... | collective-permute-start | bytes 2457608 | tf_op jit(solution)/shard_map/ppermute | solution.py:398
  61.1 0.0 collective-permute-done.1.refs_1_
  61.1 3.4 %collective-permute-start.2 = (bf16[400,1024]{1,0:T(8,128)(2,1)S(1)}, bf16[400,1024]{1,0:T(8,128)(2,1)S(1)}, u32[]{:S(2)}, u32[]{:S(2)}) collective-permute-start(bf16[400,1024]{1,0:T(8,128)(2,1)S(1)} %get-tuple-element.31.refs_1_), channel_id=1, source_target_pairs={{28,8},{24,12},{4,16},{0,20},{29,9},{25,13},{5,17},{1,21},{30,10},... | collective-permute-start | bytes 2457608 | tf_op jit(solution)/shard_map/ppermute | solution.py:398
  64.5 1.5 %shard_map.59.refs_4_ = bf16[1200,1024]{1,0:T(8,128)(2,1)S(1)} custom-call(bf16[400,1024]{1,0:T(8,128)(2,1)S(1)} %collective-permute-done.4.refs_3_.refs_0_, bf16[400,1024]{1,0:T(8,128)(2,1)} %collective-permute-done.1.refs_1_, bf16[400,1024]{1,0:T(8,128)(2,1)} %collective-permute-done.5.refs_2_), custom_call_target="tpu_custom_call" | custom-call | flops 2000000000 | tf_op jit(solution)/shard_map/pallas_call | solution.py:288
  66.0 1.0 collective-permute-start.7
  67.0 0.0 collective-permute-done.6.refs_5_
  67.0 7.0 %shard_map.60.refs_9_ = f32[1,6400]{1,0:T(1,128)S(1)} custom-call(bf16[400,1024]{1,0:T(8,128)(2,1)S(1)} %get-tuple-element.32.refs_0_, bf16[400,1024]{1,0:T(8,128)(2,1)S(1)} %get-tuple-element.31.refs_1_, bf16[400,1024]{1,0:T(8,128)(2,1)S(1)} %collective-permute-done.3.refs_2_, bf16[400,1024]{1,0:T(8,128)(2,1)S(1)} %collective-permute-done.4.refs_3_.refs_0_, ...), custom_call_target="tpu_custom_call" | custom-call | tf_op jit(solution)/shard_map/pallas_call | solution.py:258
  74.1 0.0 collective-permute-done.9.refs_1_
  74.1 5.6 %collective-permute-done.8.refs_0_ = bf16[400,1024]{1,0:T(8,128)(2,1)S(1)} collective-permute-done((bf16[400,1024]{1,0:T(8,128)(2,1)S(1)}, bf16[400,1024]{1,0:T(8,128)(2,1)S(1)}, u32[]{:S(2)}, u32[]{:S(2)}) %collective-permute-start.8) | collective-permute-done | bytes 819232 | tf_op jit(solution)/shard_map/ppermute | solution.py:398
  79.7 0.2 shard_map.61.refs_7_
  79.9 0.8 collective-permute-start.11
  80.7 0.0 collective-permute-done.7.refs_6_
  80.7 14.6 %shard_map.62.refs_11_ = f32[1,6400]{1,0:T(1,128)S(1)} custom-call(bf16[400,1024]{1,0:T(8,128)(2,1)S(1)} %get-tuple-element.32.refs_0_, bf16[400,1024]{1,0:T(8,128)(2,1)S(1)} %get-tuple-element.31.refs_1_, bf16[400,1024]{1,0:T(8,128)(2,1)S(1)} %collective-permute-done.3.refs_2_, bf16[400,1024]{1,0:T(8,128)(2,1)S(1)} %collective-permute-done.4.refs_3_.refs_0_, ...), custom_call_target="tpu_custom_call" | custom-call | tf_op jit(solution)/shard_map/pallas_call | solution.py:258
  95.3 0.0 collective-permute-done.2.refs_9_.own_ref
  95.3 0.9 collective-permute-start.10
  96.3 0.0 collective-permute-done.11.refs_8_
  96.3 9.7 %shard_map.63.best_ref = f32[1,6400]{1,0:T(1,128)S(1)} custom-call(bf16[400,1024]{1,0:T(8,128)(2,1)S(1)} %get-tuple-element.32.refs_0_, bf16[400,1024]{1,0:T(8,128)(2,1)S(1)} %get-tuple-element.31.refs_1_, bf16[400,1024]{1,0:T(8,128)(2,1)S(1)} %collective-permute-done.3.refs_2_, bf16[400,1024]{1,0:T(8,128)(2,1)S(1)} %collective-permute-done.4.refs_3_.refs_0_, ...), custom_call_target="tpu_custom_call" | custom-call | tf_op jit(solution)/shard_map/pallas_call | solution.py:258
  106.0 0.0 collective-permute-done.10.other_ref
  106.0 1.5 %shard_map.64 = f32[32,2,400]{2,1,0:T(2,128)S(1)} custom-call(s32[16]{0:T(128)S(1)} %fusion.1.refs_4_.order_ref, bf16[400,1024]{1,0:T(8,128)(2,1)S(1)} %collective-permute-done.2.refs_9_.own_ref, bf16[400,1024]{1,0:T(8,128)(2,1)S(1)} %collective-permute-done.10.other_ref, s32[1,6400]{1,0:T(1,128)S(1)} %reshape.50.refs_6_.refs_8_.refs_10_.clusters_ref, ...), custom_call_target="tpu_custom_call" | custom-call | tf_op jit(solution)/shard_map/pallas_call | solution.py:334
  107.5 16.6 %all_to_all.5.values_ref = f32[32,2,400]{2,1,0:T(2,128)S(1)} all-to-all(f32[32,2,400]{2,1,0:T(2,128)S(1)} %shard_map.64), channel_id=1, replica_groups=mesh['shard'=8,'rep'=4] {'shard','rep'}, dimensions={0} | all-to-all | bytes 204800 | tf_op jit(solution)/shard_map/all_to_all | solution.py:444
  124.1 2.4 %shard_map.65 = f32[50,128]{1,0:T(8,128)} custom-call(s32[8,2,400]{2,1,0:T(2,128)S(1)} %reshape.46.refs_5_.index_ref, f32[32,2,400]{2,1,0:T(2,128)S(1)} %all_to_all.5.values_ref), custom_call_target="tpu_custom_call" | custom-call | tf_op jit(solution)/shard_map/pallas_call | solution.py:374
  (4 shorter events, 0.0 us)
Async XLA Ops:
  1.5 15.6 %collective-permute-start = (s32[50,128]{1,0:T(8,128)}, s32[50,128]{1,0:T(8,128)S(1)}, u32[]{:S(2)}, u32[]{:S(2)}) collective-permute-start(s32[50,128]{1,0:T(8,128)} %shard_map.55), channel_id=1, source_target_pairs={{0,8},{1,9},{4,12},{5,13},{10,10},{11,11},{14,14},{15,15},{16,16},... | collective-permute-start | bytes 76808 | tf_op jit(solution)/shard_map/ppermute | solution.py:393
  6.4 0.8 copy-start
  17.1 20.7 %copy-start.1 = (s32[6400]{0:T(1024)S(1)}, s32[6400]{0:T(1024)}, u32[]{:S(2)}) copy-start(s32[6400]{0:T(1024)} %refs_0_.3) | copy-start | bytes 76804
  17.1 26.8 %collective-permute-start.4 = (bf16[400,1024]{1,0:T(8,128)(2,1)}, bf16[400,1024]{1,0:T(8,128)(2,1)S(1)}, u32[]{:S(2)}, u32[]{:S(2)}) collective-permute-start(bf16[400,1024]{1,0:T(8,128)(2,1)} %shard_map.56), channel_id=1, source_target_pairs={{16,8},{20,12},{8,16},{12,20},{21,9},{17,13},{13,17},{9,21},{18,10... | collective-permute-start | bytes 2457608 | tf_op jit(solution)/shard_map/ppermute | solution.py:398
  17.8 26.0 %collective-permute-start.3 = (bf16[400,1024]{1,0:T(8,128)(2,1)}, bf16[400,1024]{1,0:T(8,128)(2,1)S(1)}, u32[]{:S(2)}, u32[]{:S(2)}) collective-permute-start(bf16[400,1024]{1,0:T(8,128)(2,1)} %shard_map.56), channel_id=1, source_target_pairs={{0,8},{4,12},{24,16},{28,20},{5,9},{1,13},{29,17},{25,21},{2,10},{... | collective-permute-start | bytes 2457608 | tf_op jit(solution)/shard_map/ppermute | solution.py:398
  35.3 0.9 copy-start.2
  36.2 14.6 %collective-permute-start.5 = (bf16[400,1024]{1,0:T(8,128)(2,1)}, bf16[400,1024]{1,0:T(8,128)(2,1)}, u32[]{:S(2)}, u32[]{:S(2)}) collective-permute-start(bf16[400,1024]{1,0:T(8,128)(2,1)} %get-tuple-element.28), channel_id=1, source_target_pairs={{20,8},{16,12},{12,16},{8,20},{17,9},{21,13},{9,17},{13,21},{22,10... | collective-permute-start | bytes 2457608 | tf_op jit(solution)/shard_map/ppermute | solution.py:398
  37.9 23.2 %collective-permute-start.1 = (bf16[400,1024]{1,0:T(8,128)(2,1)}, bf16[400,1024]{1,0:T(8,128)(2,1)}, u32[]{:S(2)}, u32[]{:S(2)}) collective-permute-start(bf16[400,1024]{1,0:T(8,128)(2,1)} %get-tuple-element.28), channel_id=1, source_target_pairs={{4,8},{0,12},{28,16},{24,20},{1,9},{5,13},{25,17},{29,21},{6,10},{... | collective-permute-start | bytes 2457608 | tf_op jit(solution)/shard_map/ppermute | solution.py:398
  43.1 6.9 %copy-start.3 = (bf16[400,1024]{1,0:T(8,128)(2,1)S(1)}, bf16[400,1024]{1,0:T(8,128)(2,1)}, u32[]{:S(2)}) copy-start(bf16[400,1024]{1,0:T(8,128)(2,1)} %copy-done.2) | copy-start | bytes 2457604
  49.3 17.7 %collective-permute-start.6 = (bf16[400,1024]{1,0:T(8,128)(2,1)S(1)}, bf16[400,1024]{1,0:T(8,128)(2,1)S(1)}, u32[]{:S(2)}, u32[]{:S(2)}) collective-permute-start(bf16[400,1024]{1,0:T(8,128)(2,1)S(1)} %collective-permute-done.3.refs_2_), channel_id=1, source_target_pairs={{8,9},{9,8},{10,11},{11,10},{12,13},{13,12},{14,15},{15,14},{16,17... | collective-permute-start | bytes 2457608 | tf_op jit(solution)/shard_map/ppermute | solution.py:401
  50.0 24.0 %collective-permute-start.9 = (bf16[400,1024]{1,0:T(8,128)(2,1)S(1)}, bf16[400,1024]{1,0:T(8,128)(2,1)S(1)}, u32[]{:S(2)}, u32[]{:S(2)}) collective-permute-start(bf16[400,1024]{1,0:T(8,128)(2,1)S(1)} %copy-done.3), channel_id=1, source_target_pairs={{12,8},{8,12},{20,16},{16,20},{13,9},{9,13},{21,17},{17,21},{14,10... | collective-permute-start | bytes 2457608 | tf_op jit(solution)/shard_map/ppermute | solution.py:398
  50.8 28.9 %collective-permute-start.8 = (bf16[400,1024]{1,0:T(8,128)(2,1)S(1)}, bf16[400,1024]{1,0:T(8,128)(2,1)S(1)}, u32[]{:S(2)}, u32[]{:S(2)}) collective-permute-start(bf16[400,1024]{1,0:T(8,128)(2,1)S(1)} %copy-done.3), channel_id=1, source_target_pairs={{24,8},{28,12},{0,16},{4,20},{25,9},{29,13},{1,17},{5,21},{26,10},... | collective-permute-start | bytes 2457608 | tf_op jit(solution)/shard_map/ppermute | solution.py:398
  61.1 34.2 %collective-permute-start.2 = (bf16[400,1024]{1,0:T(8,128)(2,1)S(1)}, bf16[400,1024]{1,0:T(8,128)(2,1)S(1)}, u32[]{:S(2)}, u32[]{:S(2)}) collective-permute-start(bf16[400,1024]{1,0:T(8,128)(2,1)S(1)} %get-tuple-element.31.refs_1_), channel_id=1, source_target_pairs={{28,8},{24,12},{4,16},{0,20},{29,9},{25,13},{5,17},{1,21},{30,10},... | collective-permute-start | bytes 2457608 | tf_op jit(solution)/shard_map/ppermute | solution.py:398
  66.0 14.7 %collective-permute-start.7 = (bf16[1200,1024]{1,0:T(8,128)(2,1)S(1)}, bf16[1200,1024]{1,0:T(8,128)(2,1)S(1)}, u32[]{:S(2)}, u32[]{:S(2)}) collective-permute-start(bf16[1200,1024]{1,0:T(8,128)(2,1)S(1)} %shard_map.59.refs_4_), channel_id=1, source_target_pairs={{8,9},{9,8},{10,11},{11,10},{12,13},{13,12},{14,15},{15,14},{16,17... | collective-permute-start | bytes 7372808 | tf_op jit(solution)/shard_map/ppermute | solution.py:401
  79.9 16.3 %collective-permute-start.11 = (bf16[800,1024]{1,0:T(8,128)(2,1)S(1)}, bf16[800,1024]{1,0:T(8,128)(2,1)S(1)}, u32[]{:S(2)}, u32[]{:S(2)}) collective-permute-start(bf16[800,1024]{1,0:T(8,128)(2,1)S(1)} %shard_map.61.refs_7_), channel_id=1, source_target_pairs={{8,9},{9,8},{10,11},{11,10},{12,13},{13,12},{14,15},{15,14},{16,17... | collective-permute-start | bytes 4915208 | tf_op jit(solution)/shard_map/ppermute | solution.py:401
  95.3 10.7 %collective-permute-start.10 = (bf16[400,1024]{1,0:T(8,128)(2,1)S(1)}, bf16[400,1024]{1,0:T(8,128)(2,1)S(1)}, u32[]{:S(2)}, u32[]{:S(2)}) collective-permute-start(bf16[400,1024]{1,0:T(8,128)(2,1)S(1)} %collective-permute-done.2.refs_9_.own_ref), channel_id=1, source_target_pairs={{8,9},{9,8},{10,11},{11,10},{12,13},{13,12},{14,15},{15,14},{16,17... | collective-permute-start | bytes 2457608 | tf_op jit(solution)/shard_map/ppermute | solution.py:401

commit v16 on v15

--- a/solution.py
+++ b/solution.py
@@ -204,21 +204,21 @@
     best_ref[...] = before_ref[...]
     for i in range(low, count):
         copy(i).wait()
-    for n, (chunk, news, groups, group, meets, last) in enumerate(passes):
-        height = news * size
+
+    def sweep(first, height, work):
         acc[...] = jnp.full_like(acc, -1.0)
-        rows = held[chunk * size : chunk * size + height, :]
-        left = as_column(cluster_row, chunk * size, height)
+        rows = held[first : first + height, :]
+        left = as_column(cluster_row, first, height)
         left = jnp.concatenate([left, left], axis=1)
 
-        def tile(start, special, chunk=chunk, height=height, rows=rows, left=left):
+        def tile(start, special):
             gram = lax.dot_general(
                 rows, held[pl.ds(start, BLK), :], NT, preferred_element_type=jnp.float32
             )
             counts = left == cluster_row[:, pl.ds(start, BLK)]
             if special:
                 column = start + lax.broadcasted_iota(jnp.int32, (height, BLK), 1)
-                row = chunk * size + lax.broadcasted_iota(jnp.int32, (height, BLK), 0)
+                row = first + lax.broadcasted_iota(jnp.int32, (height, BLK), 0)
                 counts = counts & (column != row) & (column < limit)
             values = jnp.where(counts, gram, jnp.float32(-1.0))
             top = jnp.max(values, axis=0, keepdims=True)
@@ -227,26 +227,51 @@
                 acc[0:height, :], jnp.maximum(values[:, :LANES], values[:, LANES:])
             )
 
-        for t in last:
-            start, stop = t * BLK, (t + 1) * BLK
-            own = start < chunk * size + height and stop > chunk * size
-            tile(start, own or stop > limit)
+        work(tile)
+        span = slice(first, first + height)
+        best_ref[:, span] = jnp.maximum(best_ref[:, span], best_of_rows(acc[...], height))
+
+    for n, (chunk, news, groups, group, meets, last, halved) in enumerate(passes):
+        first, height = chunk * size, news * size
+
+        def masked(t, first=first, height=height):
+            return (t * BLK < first + height and (t + 1) * BLK > first) or (t + 1) * BLK > limit
+
+        if halved:
+            count_of_tiles = len(last) // 2
+            cut = last[count_of_tiles] * BLK - halved * size
+            core = lax.axis_index("rep") % 2
+            for h, (top, bottom) in enumerate(((0, cut), (cut, height))):
+
+                def work(tile, h=h, masked=masked, last=last, count_of_tiles=count_of_tiles, core=core):
+                    side = h + core - 2 * h * core
+                    for t in range(count_of_tiles):
+                        start = (last[t] + count_of_tiles * side) * BLK
+                        special = masked(last[t]) or masked(last[t + count_of_tiles])
+                        tile(pl.multiple_of(start, BLK), special)
+
+                sweep(first + top, bottom - top, work)
+            continue
         step = -(-group * BLK // size)
 
-        def visit(u, _, n=n, group=group, meets=meets, tile=tile, step=step):
-            for i in range(step) if n == 0 else ():
-
-                @pl.when(u * step + i < low)
-                def _(i=i):
-                    arrive(u * step + i)
-
-            for t in range(group):
-                tile(pl.multiple_of((u * group + t) * BLK, BLK), meets)
-            return 0
-
-        lax.fori_loop(0, groups, visit, 0)
-        span = slice(chunk * size, chunk * size + height)
-        best_ref[:, span] = jnp.maximum(best_ref[:, span], best_of_rows(acc[...], height))
+        def work(tile, n=n, groups=groups, group=group, meets=meets, last=last, masked=masked, step=step):
+            for t in last:
+                tile(t * BLK, masked(t))
+
+            def visit(u, _):
+                for i in range(step) if n == 0 else ():
+
+                    @pl.when(u * step + i < low)
+                    def _(i=i):
+                        arrive(u * step + i)
+
+                for t in range(group):
+                    tile(pl.multiple_of((u * group + t) * BLK, BLK), meets)
+                return 0
+
+            lax.fori_loop(0, groups, visit, 0)
+
+        sweep(first, height, work)
 
 
 def gram_best(arrays, loads, size, cluster_row, before, passes, after=()):
@@ -301,11 +326,12 @@
     group = max(n for n in range(1, 8) if plain % n == 0)
     groups = plain // group
     tiles = -(-count * size // BLK)
-    return (chunk, news, groups, group, False, tuple(range(groups * group, tiles)))
-
-
-def late_pass(chunk, news, low, high, size):
-    return (chunk, news, 0, 1, True, tuple(range(low * size // BLK, -(-high * size // BLK))))
+    return (chunk, news, groups, group, False, tuple(range(groups * group, tiles)), 0)
+
+
+def late_pass(chunk, news, low, high, size, halved=False):
+    tiles = tuple(range(low * size // BLK, -(-high * size // BLK)))
+    return (chunk, news, 0, 1, True, tiles, low if halved else 0)
 
 
 def finish_kernel(size, order_ref, own_ref, other_ref, clusters_ref, best_ref, out_ref, acc):
@@ -435,11 +461,11 @@
     joined = join([tie(own[5], best), tie(own[6], best)], LONG)
     swapped = swap(joined)
     own[5], own[6] = (joined, 0), (joined, 1)
-    best = score(best, 12, (new_pass(10, 2, 12, size), late_pass(3, 3, 7, 10, size)))
+    best = score(best, 12, (new_pass(10, 2, 12, size), late_pass(3, 3, 7, 10, size, True)))
     other[5], other[6] = (swapped, 0), (swapped, 1)
     own[7] = tie(own[7], best)
     other[7] = swap(own[7])
-    best = score(best, 15, (new_pass(14, 1, 15, size), late_pass(10, 2, 12, 14, size)))
+    best = score(best, 15, (new_pass(14, 1, 15, size), late_pass(10, 2, 12, 14, size, True)))
     outbound = finish(order, own[7], other[7], flat, best)
     returned = lax.all_to_all(outbound, axes, split_axis=0, concat_axis=0, tiled=True)
     sources = []
@@ -468,7 +494,7 @@
     clusters = jnp.roll(clusters, -turn, axis=0)
     best = jnp.full((1, documents), -1.0, jnp.float32)
     tiles = tuple(range(documents // BLK))
-    passes = ((0, news, 0, 1, True, tiles),)
+    passes = ((0, news, 0, 1, True, tiles, 0),)
     chunks = [arrived[i] for i in range(parts)]
     loads = tuple((i, 0) for i in range(parts))
     best = gram_best(chunks, loads, size, clusters.reshape(1, -1), best, passes)

time: 127 us -> 124 us (0.976)
  Pallas kernels: 67 us -> 64.3 us
    pallas_call x4, Pallas kernels: 36.8 us -> 34.1 us  [gram_best(): pl.pallas_call(functools.partial(gram_kernel, passes, loads, size, limit)...]
  transfers between devices with their start and end apart: 12 -> 12, of which waited for: 1 -> 2; matrix products, arithmetic and copies ran while one was open for 2% -> 2% of each run, Pallas kernels for 49% -> 48%
where the time goes in v16:
time: 124 us
  Pallas kernels  64.3 us (52%)
  starting transfers between devices  32.9 us (27%)
  blocking collectives  15.8 us (13%)
  waiting for transfers between devices  6.46 us (5%)
  local copies, waits for them, and re-layouts  3.3 us (3%)
    pallas_call x4, Pallas kernels, gram_best(): pl.pallas_call(functools.partial(gram_kernel, passes, loads, size, limit)...  34.1 us
    ppermute x7, starting transfers between devices, go(): return lax.ppermute(chunk, axes, round_pairs(step - 1))  24.6 us
    pallas_call x2, Pallas kernels, gather_rows(): pl.pallas_call(functools.partial(gather_kernel, slots, size, group, secti...  23.2 us
    all_to_all x1, blocking collectives, hosted(): lax.all_to_all(outbound, axes, split_axis=0, concat_axis=0, tiled=True)  15.8 us
    ppermute x7, waiting for transfers between devices, go(): return lax.ppermute(chunk, axes, round_pairs(step - 1))  6.45 us
    ppermute x1, starting transfers between devices, hosted(): named = lax.ppermute(named, axes, metadata_pairs())  4.92 us
    ppermute x4, starting transfers between devices, swap(): return lax.ppermute(chunk, axes, SIBLINGS)  3.4 us
  transfers between devices with their start and end apart: 12, of which 2 were waited for; matrix products, arithmetic and copies ran while one was open for 2% of the time, Pallas kernels for 48%

profile of v16, /device:TPU:0, one launch (start us, length us, event | category | flops | bytes accessed | tf_op | source)
XLA Modules:
  0.0 123.7 jit_solution(8856105214769700164)
XLA Ops:
  0.0 1.5 %shard_map.55 = s32[50,128]{1,0:T(8,128)} custom-call(s32[50,128]{1,0:T(8,128)} %bitcast.9, s32[52,128]{1,0:T(8,128)} %bitcast.10), custom_call_target="tpu_custom_call" | custom-call | tf_op jit(solution)/shard_map/pallas_call | solution.py:87
  1.5 4.9 %collective-permute-start = (s32[50,128]{1,0:T(8,128)}, s32[50,128]{1,0:T(8,128)S(1)}, u32[]{:S(2)}, u32[]{:S(2)}) collective-permute-start(s32[50,128]{1,0:T(8,128)} %shard_map.55), channel_id=1, source_target_pairs={{0,8},{1,9},{4,12},{5,13},{10,10},{11,11},{14,14},{15,15},{16,16},... | collective-permute-start | bytes 76808 | tf_op jit(solution)/shard_map/ppermute | solution.py:419
  6.4 0.0 copy-start
  6.4 0.7 copy-done
  7.1 9.9 %shard_map.56 = bf16[400,1024]{1,0:T(8,128)(2,1)} custom-call(s32[6400]{0:T(1024)S(1)} %copy-done, bf16[6400,1024]{1,0:T(8,128)(2,1)} %refs_1_.1), custom_call_target="tpu_custom_call" | custom-call | flops 40000000000 | tf_op jit(solution)/shard_map/pallas_call | solution.py:159
  17.1 0.0 copy-start.1
  17.1 0.0 collective-permute-done
  17.1 0.7 collective-permute-start.4
  17.8 4.2 %collective-permute-start.3 = (bf16[400,1024]{1,0:T(8,128)(2,1)}, bf16[400,1024]{1,0:T(8,128)(2,1)S(1)}, u32[]{:S(2)}, u32[]{:S(2)}) collective-permute-start(bf16[400,1024]{1,0:T(8,128)(2,1)} %shard_map.56), channel_id=1, source_target_pairs={{0,8},{4,12},{24,16},{28,20},{5,9},{1,13},{29,17},{25,21},{2,10},{... | collective-permute-start | bytes 2457608 | tf_op jit(solution)/shard_map/ppermute | solution.py:424
  22.0 13.2 %shard_map.57 = (bf16[400,1024]{1,0:T(8,128)(2,1)}, bf16[400,1024]{1,0:T(8,128)(2,1)S(1)}, bf16[400,1024]{1,0:T(8,128)(2,1)S(1)}, bf16[400,1024]{1,0:T(8,128)(2,1)S(1)}) custom-call(s32[6400]{0:T(1024)S(1)} %copy-done, bf16[6400,1024]{1,0:T(8,128)(2,1)} %refs_1_.1), custom_call_target="tpu_custom_call" | custom-call | flops 40000000000 | tf_op jit(solution)/shard_map/pallas_call | solution.py:159
  35.3 0.0 copy-start.2
  35.3 0.9 copy-done.2
  36.2 1.6 %collective-permute-start.5 = (bf16[400,1024]{1,0:T(8,128)(2,1)}, bf16[400,1024]{1,0:T(8,128)(2,1)}, u32[]{:S(2)}, u32[]{:S(2)}) collective-permute-start(bf16[400,1024]{1,0:T(8,128)(2,1)} %get-tuple-element.28), channel_id=1, source_target_pairs={{20,8},{16,12},{12,16},{8,20},{17,9},{21,13},{9,17},{13,21},{22,10... | collective-permute-start | bytes 2457608 | tf_op jit(solution)/shard_map/ppermute | solution.py:424
  37.8 0.0 copy-done.1
  37.8 0.1 reshape.46.refs_5_.index_ref
  37.9 3.7 %collective-permute-start.1 = (bf16[400,1024]{1,0:T(8,128)(2,1)}, bf16[400,1024]{1,0:T(8,128)(2,1)}, u32[]{:S(2)}, u32[]{:S(2)}) collective-permute-start(bf16[400,1024]{1,0:T(8,128)(2,1)} %get-tuple-element.28), channel_id=1, source_target_pairs={{4,8},{0,12},{28,16},{24,20},{1,9},{5,13},{25,17},{29,21},{6,10},{... | collective-permute-start | bytes 2457608 | tf_op jit(solution)/shard_map/ppermute | solution.py:424
  41.6 0.1 reshape.49
  41.7 0.7 fusion
  42.4 0.6 gather_fusion
  43.0 0.1 reshape.50.refs_6_.refs_8_.refs_10_.clusters_ref
  43.1 0.8 fusion.1.refs_4_.order_ref
  43.9 0.0 collective-permute-done.4.refs_3_.refs_0_
  43.9 0.0 collective-permute-done.3.refs_2_
  43.9 5.4 %shard_map.58.refs_7_ = f32[1,6400]{1,0:T(1,128)S(1)} custom-call(bf16[400,1024]{1,0:T(8,128)(2,1)S(1)} %get-tuple-element.32.refs_0_, bf16[400,1024]{1,0:T(8,128)(2,1)S(1)} %get-tuple-element.31.refs_1_, bf16[400,1024]{1,0:T(8,128)(2,1)S(1)} %collective-permute-done.3.refs_2_, bf16[400,1024]{1,0:T(8,128)(2,1)S(1)} %collective-permute-done.4.refs_3_.refs_0_, ...), custom_call_target="tpu_custom_call" | custom-call | tf_op jit(solution)/shard_map/pallas_call | solution.py:283
  49.3 0.7 collective-permute-start.6
  50.0 0.7 collective-permute-start.9
  50.8 0.0 collective-permute-done.5.refs_2_
  50.8 10.3 %collective-permute-start.8 = (bf16[400,1024]{1,0:T(8,128)(2,1)S(1)}, bf16[400,1024]{1,0:T(8,128)(2,1)S(1)}, u32[]{:S(2)}, u32[]{:S(2)}) collective-permute-start(bf16[400,1024]{1,0:T(8,128)(2,1)S(1)} %copy-done.3), channel_id=1, source_target_pairs={{24,8},{28,12},{0,16},{4,20},{25,9},{29,13},{1,17},{5,21},{26,10},... | collective-permute-start | bytes 2457608 | tf_op jit(solution)/shard_map/ppermute | solution.py:424
  61.1 0.0 collective-permute-done.1.refs_1_
  61.1 3.4 %collective-permute-start.2 = (bf16[400,1024]{1,0:T(8,128)(2,1)S(1)}, bf16[400,1024]{1,0:T(8,128)(2,1)S(1)}, u32[]{:S(2)}, u32[]{:S(2)}) collective-permute-start(bf16[400,1024]{1,0:T(8,128)(2,1)S(1)} %get-tuple-element.31.refs_1_), channel_id=1, source_target_pairs={{28,8},{24,12},{4,16},{0,20},{29,9},{25,13},{5,17},{1,21},{30,10},... | collective-permute-start | bytes 2457608 | tf_op jit(solution)/shard_map/ppermute | solution.py:424
  64.5 1.5 %shard_map.59.refs_4_ = bf16[1200,1024]{1,0:T(8,128)(2,1)S(1)} custom-call(bf16[400,1024]{1,0:T(8,128)(2,1)S(1)} %collective-permute-done.4.refs_3_.refs_0_, bf16[400,1024]{1,0:T(8,128)(2,1)} %collective-permute-done.1.refs_1_, bf16[400,1024]{1,0:T(8,128)(2,1)} %collective-permute-done.5.refs_2_), custom_call_target="tpu_custom_call" | custom-call | flops 2000000000 | tf_op jit(solution)/shard_map/pallas_call | solution.py:313
  66.0 1.0 collective-permute-start.7
  67.0 0.0 collective-permute-done.6.refs_5_
  67.0 7.1 %shard_map.60.refs_9_ = f32[1,6400]{1,0:T(1,128)S(1)} custom-call(bf16[400,1024]{1,0:T(8,128)(2,1)S(1)} %get-tuple-element.32.refs_0_, bf16[400,1024]{1,0:T(8,128)(2,1)S(1)} %get-tuple-element.31.refs_1_, bf16[400,1024]{1,0:T(8,128)(2,1)S(1)} %collective-permute-done.3.refs_2_, bf16[400,1024]{1,0:T(8,128)(2,1)S(1)} %collective-permute-done.4.refs_3_.refs_0_, ...), custom_call_target="tpu_custom_call" | custom-call | tf_op jit(solution)/shard_map/pallas_call | solution.py:283
  74.1 0.0 collective-permute-done.9.refs_1_
  74.1 5.6 %collective-permute-done.8.refs_0_ = bf16[400,1024]{1,0:T(8,128)(2,1)S(1)} collective-permute-done((bf16[400,1024]{1,0:T(8,128)(2,1)S(1)}, bf16[400,1024]{1,0:T(8,128)(2,1)S(1)}, u32[]{:S(2)}, u32[]{:S(2)}) %collective-permute-start.8) | collective-permute-done | bytes 819232 | tf_op jit(solution)/shard_map/ppermute | solution.py:424
  79.7 0.2 shard_map.61.refs_7_
  79.9 0.8 collective-permute-start.11
  80.7 0.0 collective-permute-done.7.refs_6_
  80.7 12.6 %shard_map.62.refs_11_ = f32[1,6400]{1,0:T(1,128)S(1)} custom-call(bf16[400,1024]{1,0:T(8,128)(2,1)S(1)} %get-tuple-element.32.refs_0_, bf16[400,1024]{1,0:T(8,128)(2,1)S(1)} %get-tuple-element.31.refs_1_, bf16[400,1024]{1,0:T(8,128)(2,1)S(1)} %collective-permute-done.3.refs_2_, bf16[400,1024]{1,0:T(8,128)(2,1)S(1)} %collective-permute-done.4.refs_3_.refs_0_, ...), custom_call_target="tpu_custom_call" | custom-call | tf_op jit(solution)/shard_map/pallas_call | solution.py:283
  93.4 0.8 collective-permute-done.2.refs_9_.own_ref
  94.2 0.9 collective-permute-start.10
  95.1 0.0 collective-permute-done.11.refs_8_
  95.1 9.0 %shard_map.63.best_ref = f32[1,6400]{1,0:T(1,128)S(1)} custom-call(bf16[400,1024]{1,0:T(8,128)(2,1)S(1)} %get-tuple-element.32.refs_0_, bf16[400,1024]{1,0:T(8,128)(2,1)S(1)} %get-tuple-element.31.refs_1_, bf16[400,1024]{1,0:T(8,128)(2,1)S(1)} %collective-permute-done.3.refs_2_, bf16[400,1024]{1,0:T(8,128)(2,1)S(1)} %collective-permute-done.4.refs_3_.refs_0_, ...), custom_call_target="tpu_custom_call" | custom-call | tf_op jit(solution)/shard_map/pallas_call | solution.py:283
  104.1 0.0 collective-permute-done.10.other_ref
  104.1 1.5 %shard_map.64 = f32[32,2,400]{2,1,0:T(2,128)S(1)} custom-call(s32[16]{0:T(128)S(1)} %fusion.1.refs_4_.order_ref, bf16[400,1024]{1,0:T(8,128)(2,1)S(1)} %collective-permute-done.2.refs_9_.own_ref, bf16[400,1024]{1,0:T(8,128)(2,1)S(1)} %collective-permute-done.10.other_ref, s32[1,6400]{1,0:T(1,128)S(1)} %reshape.50.refs_6_.refs_8_.refs_10_.clusters_ref, ...), custom_call_target="tpu_custom_call" | custom-call | tf_op jit(solution)/shard_map/pallas_call | solution.py:360
  105.6 15.8 %all_to_all.5.values_ref = f32[32,2,400]{2,1,0:T(2,128)S(1)} all-to-all(f32[32,2,400]{2,1,0:T(2,128)S(1)} %shard_map.64), channel_id=1, replica_groups=mesh['shard'=8,'rep'=4] {'shard','rep'}, dimensions={0} | all-to-all | bytes 204800 | tf_op jit(solution)/shard_map/all_to_all | solution.py:470
  121.3 2.4 %shard_map.65 = f32[50,128]{1,0:T(8,128)} custom-call(s32[8,2,400]{2,1,0:T(2,128)S(1)} %reshape.46.refs_5_.index_ref, f32[32,2,400]{2,1,0:T(2,128)S(1)} %all_to_all.5.values_ref), custom_call_target="tpu_custom_call" | custom-call | tf_op jit(solution)/shard_map/pallas_call | solution.py:400
  (4 shorter events, 0.0 us)
Async XLA Ops:
  1.5 15.6 %collective-permute-start = (s32[50,128]{1,0:T(8,128)}, s32[50,128]{1,0:T(8,128)S(1)}, u32[]{:S(2)}, u32[]{:S(2)}) collective-permute-start(s32[50,128]{1,0:T(8,128)} %shard_map.55), channel_id=1, source_target_pairs={{0,8},{1,9},{4,12},{5,13},{10,10},{11,11},{14,14},{15,15},{16,16},... | collective-permute-start | bytes 76808 | tf_op jit(solution)/shard_map/ppermute | solution.py:419
  6.4 0.8 copy-start
  17.1 20.7 %copy-start.1 = (s32[6400]{0:T(1024)S(1)}, s32[6400]{0:T(1024)}, u32[]{:S(2)}) copy-start(s32[6400]{0:T(1024)} %refs_0_.3) | copy-start | bytes 76804
  17.1 26.8 %collective-permute-start.4 = (bf16[400,1024]{1,0:T(8,128)(2,1)}, bf16[400,1024]{1,0:T(8,128)(2,1)S(1)}, u32[]{:S(2)}, u32[]{:S(2)}) collective-permute-start(bf16[400,1024]{1,0:T(8,128)(2,1)} %shard_map.56), channel_id=1, source_target_pairs={{16,8},{20,12},{8,16},{12,20},{21,9},{17,13},{13,17},{9,21},{18,10... | collective-permute-start | bytes 2457608 | tf_op jit(solution)/shard_map/ppermute | solution.py:424
  17.8 26.1 %collective-permute-start.3 = (bf16[400,1024]{1,0:T(8,128)(2,1)}, bf16[400,1024]{1,0:T(8,128)(2,1)S(1)}, u32[]{:S(2)}, u32[]{:S(2)}) collective-permute-start(bf16[400,1024]{1,0:T(8,128)(2,1)} %shard_map.56), channel_id=1, source_target_pairs={{0,8},{4,12},{24,16},{28,20},{5,9},{1,13},{29,17},{25,21},{2,10},{... | collective-permute-start | bytes 2457608 | tf_op jit(solution)/shard_map/ppermute | solution.py:424
  35.3 0.9 copy-start.2
  36.2 14.6 %collective-permute-start.5 = (bf16[400,1024]{1,0:T(8,128)(2,1)}, bf16[400,1024]{1,0:T(8,128)(2,1)}, u32[]{:S(2)}, u32[]{:S(2)}) collective-permute-start(bf16[400,1024]{1,0:T(8,128)(2,1)} %get-tuple-element.28), channel_id=1, source_target_pairs={{20,8},{16,12},{12,16},{8,20},{17,9},{21,13},{9,17},{13,21},{22,10... | collective-permute-start | bytes 2457608 | tf_op jit(solution)/shard_map/ppermute | solution.py:424
  37.9 23.2 %collective-permute-start.1 = (bf16[400,1024]{1,0:T(8,128)(2,1)}, bf16[400,1024]{1,0:T(8,128)(2,1)}, u32[]{:S(2)}, u32[]{:S(2)}) collective-permute-start(bf16[400,1024]{1,0:T(8,128)(2,1)} %get-tuple-element.28), channel_id=1, source_target_pairs={{4,8},{0,12},{28,16},{24,20},{1,9},{5,13},{25,17},{29,21},{6,10},{... | collective-permute-start | bytes 2457608 | tf_op jit(solution)/shard_map/ppermute | solution.py:424
  43.1 7.0 %copy-start.3 = (bf16[400,1024]{1,0:T(8,128)(2,1)S(1)}, bf16[400,1024]{1,0:T(8,128)(2,1)}, u32[]{:S(2)}) copy-start(bf16[400,1024]{1,0:T(8,128)(2,1)} %copy-done.2) | copy-start | bytes 2457604
  49.3 17.7 %collective-permute-start.6 = (bf16[400,1024]{1,0:T(8,128)(2,1)S(1)}, bf16[400,1024]{1,0:T(8,128)(2,1)S(1)}, u32[]{:S(2)}, u32[]{:S(2)}) collective-permute-start(bf16[400,1024]{1,0:T(8,128)(2,1)S(1)} %collective-permute-done.3.refs_2_), channel_id=1, source_target_pairs={{8,9},{9,8},{10,11},{11,10},{12,13},{13,12},{14,15},{15,14},{16,17... | collective-permute-start | bytes 2457608 | tf_op jit(solution)/shard_map/ppermute | solution.py:427
  50.0 24.0 %collective-permute-start.9 = (bf16[400,1024]{1,0:T(8,128)(2,1)S(1)}, bf16[400,1024]{1,0:T(8,128)(2,1)S(1)}, u32[]{:S(2)}, u32[]{:S(2)}) collective-permute-start(bf16[400,1024]{1,0:T(8,128)(2,1)S(1)} %copy-done.3), channel_id=1, source_target_pairs={{12,8},{8,12},{20,16},{16,20},{13,9},{9,13},{21,17},{17,21},{14,10... | collective-permute-start | bytes 2457608 | tf_op jit(solution)/shard_map/ppermute | solution.py:424
  50.8 28.9 %collective-permute-start.8 = (bf16[400,1024]{1,0:T(8,128)(2,1)S(1)}, bf16[400,1024]{1,0:T(8,128)(2,1)S(1)}, u32[]{:S(2)}, u32[]{:S(2)}) collective-permute-start(bf16[400,1024]{1,0:T(8,128)(2,1)S(1)} %copy-done.3), channel_id=1, source_target_pairs={{24,8},{28,12},{0,16},{4,20},{25,9},{29,13},{1,17},{5,21},{26,10},... | collective-permute-start | bytes 2457608 | tf_op jit(solution)/shard_map/ppermute | solution.py:424
  61.1 33.1 %collective-permute-start.2 = (bf16[400,1024]{1,0:T(8,128)(2,1)S(1)}, bf16[400,1024]{1,0:T(8,128)(2,1)S(1)}, u32[]{:S(2)}, u32[]{:S(2)}) collective-permute-start(bf16[400,1024]{1,0:T(8,128)(2,1)S(1)} %get-tuple-element.31.refs_1_), channel_id=1, source_target_pairs={{28,8},{24,12},{4,16},{0,20},{29,9},{25,13},{5,17},{1,21},{30,10},... | collective-permute-start | bytes 2457608 | tf_op jit(solution)/shard_map/ppermute | solution.py:424
  66.0 14.7 %collective-permute-start.7 = (bf16[1200,1024]{1,0:T(8,128)(2,1)S(1)}, bf16[1200,1024]{1,0:T(8,128)(2,1)S(1)}, u32[]{:S(2)}, u32[]{:S(2)}) collective-permute-start(bf16[1200,1024]{1,0:T(8,128)(2,1)S(1)} %shard_map.59.refs_4_), channel_id=1, source_target_pairs={{8,9},{9,8},{10,11},{11,10},{12,13},{13,12},{14,15},{15,14},{16,17... | collective-permute-start | bytes 7372808 | tf_op jit(solution)/shard_map/ppermute | solution.py:427
  79.9 15.2 %collective-permute-start.11 = (bf16[800,1024]{1,0:T(8,128)(2,1)S(1)}, bf16[800,1024]{1,0:T(8,128)(2,1)S(1)}, u32[]{:S(2)}, u32[]{:S(2)}) collective-permute-start(bf16[800,1024]{1,0:T(8,128)(2,1)S(1)} %shard_map.61.refs_7_), channel_id=1, source_target_pairs={{8,9},{9,8},{10,11},{11,10},{12,13},{13,12},{14,15},{15,14},{16,17... | collective-permute-start | bytes 4915208 | tf_op jit(solution)/shard_map/ppermute | solution.py:427
  94.2 9.9 %collective-permute-start.10 = (bf16[400,1024]{1,0:T(8,128)(2,1)S(1)}, bf16[400,1024]{1,0:T(8,128)(2,1)S(1)}, u32[]{:S(2)}, u32[]{:S(2)}) collective-permute-start(bf16[400,1024]{1,0:T(8,128)(2,1)S(1)} %collective-permute-done.2.refs_9_.own_ref), channel_id=1, source_target_pairs={{8,9},{9,8},{10,11},{11,10},{12,13},{13,12},{14,15},{15,14},{16,17... | collective-permute-start | bytes 2457608 | tf_op jit(solution)/shard_map/ppermute | solution.py:427

commit v17 on v16

--- a/solution.py
+++ b/solution.py
@@ -73,7 +73,7 @@
     )
 
 
-def names_kernel(place_ref, slots_ref, out_ref):
+def write_names(place_ref, slots_ref, out_ref):
     block = place_ref[...] // BLK
     found = jnp.zeros_like(block)
     for i in range(slots_ref.shape[0] * LANES // BLK):
@@ -85,7 +85,7 @@
 def arrival_names(place_index, slot_cluster):
     places = place_index.reshape(-1, LANES)
     return pl.pallas_call(
-        names_kernel, out_shape=jax.ShapeDtypeStruct(places.shape, jnp.int32)
+        write_names, out_shape=jax.ShapeDtypeStruct(places.shape, jnp.int32)
     )(places, slot_cluster.reshape(-1, LANES))
 
 
@@ -103,7 +103,7 @@
     return owner * (2 * size) + half * size
 
 
-def gather_kernel(slots, size, group, sections, *refs):
+def gather_kernel(slots, size, group, sections, named, *refs):
     index_hbm, rows_ref = refs[:2]
     index_ref, raw, wide, picked, sems = refs[-5:]
     outs = refs[-5 - len(slots) : -5]
@@ -117,6 +117,8 @@
         rows = pl.ds(i * part, part)
         copies.append(pltpu.make_async_copy(rows_ref.at[rows], raw.at[rows], sems.at[i]))
         copies[-1].start()
+    if named:
+        write_names(*refs[2:5])
     step = 160
     for i in range(sections):
         copies[i].wait()
@@ -151,16 +153,20 @@
         lax.fori_loop(0, size // group, pick, 0)
 
 
-def gather_rows(embeddings, index, slots, size):
+def gather_rows(embeddings, index, slots, size, names=()):
     documents, width = embeddings.shape
     count = len(slots)
     sections = 10
     group = 80
+    names = [array.reshape(-1, LANES) for array in names]
+    outs = [jax.ShapeDtypeStruct(array.shape, jnp.int32) for array in names[:1]]
+    outs += [jax.ShapeDtypeStruct((size, width), jnp.bfloat16)] * count
     return pl.pallas_call(
-        functools.partial(gather_kernel, slots, size, group, sections),
-        out_shape=[jax.ShapeDtypeStruct((size, width), jnp.bfloat16)] * count,
-        in_specs=[pl.BlockSpec(memory_space=pltpu.HBM)] * 2,
-        out_specs=[pl.BlockSpec(memory_space=pltpu.VMEM)] * count,
+        functools.partial(gather_kernel, slots, size, group, sections, bool(names)),
+        out_shape=outs,
+        in_specs=[pl.BlockSpec(memory_space=pltpu.HBM)] * 2
+        + [pl.BlockSpec(memory_space=pltpu.VMEM)] * len(names),
+        out_specs=[pl.BlockSpec(memory_space=pltpu.VMEM)] * len(outs),
         scratch_shapes=[
             pltpu.SMEM(index.shape, jnp.int32),
             pltpu.VMEM((documents, width), jnp.bfloat16),
@@ -170,7 +176,7 @@
         ],
         compiler_params=pltpu.CompilerParams(vmem_limit_bytes=45 * MIB),
         cost_estimate=pl.CostEstimate(flops=LONG, bytes_accessed=0, transcendentals=0),
-    )(index, embeddings)
+    )(index, embeddings, *names)
 
 
 def best_of_rows(acc, size):
@@ -413,9 +419,7 @@
     documents = embeddings.shape[0]
     size = send_index.shape[0] // 16
     axes = ("shard", "rep")
-    named = arrival_names(place_index, slot_cluster)
-    embeddings = tie(embeddings, named)
-    (early,) = gather_rows(embeddings, send_index, (0,), size)
+    named, early = gather_rows(embeddings, send_index, (0,), size, (place_index, slot_cluster))
     named = lax.ppermute(named, axes, metadata_pairs())
     early = tie(early, named)
     index = send_index.reshape(8, 2, size)

time: 124 us -> 129 us (1.040)
  starting transfers between devices: 32.9 us -> 35.8 us
  Pallas kernels: 64.3 us -> 62.8 us
  local copies, waits for them, and re-layouts: 3.3 us -> 4.79 us
    ppermute x7, starting transfers between devices: 24.6 us -> 27.5 us  [go(): return lax.ppermute(chunk, axes, round_pairs(step - 1))]
    ppermute x1, waiting for transfers between devices: 0.01 us -> 1.54 us  [hosted(): named = lax.ppermute(named, axes, metadata_pairs())]
    unnamed x8 -> x12, local copies, waits for them, and re-layouts: 1.65 us -> 3.15 us
    pallas_call x1 -> x0, Pallas kernels: 1.46 us -> none  [arrival_names(): pl.pallas_call(names_kernel, out_shape=jax.ShapeDtypeStruct(places.shape,...]
  transfers between devices with their start and end apart: 12 -> 12, of which waited for: 2 -> 2; matrix products, arithmetic and copies ran while one was open for 2% -> 2% of each run, Pallas kernels for 48% -> 38%
where the time goes in v17:
time: 129 us; the launch traced here: 128 us
  Pallas kernels  62.8 us (49%)
  starting transfers between devices  35.8 us (28%)
  blocking collectives  16.7 us (13%)
  waiting for transfers between devices  7.24 us (6%)
  local copies, waits for them, and re-layouts  4.79 us (4%)
    pallas_call x4, Pallas kernels, gram_best(): pl.pallas_call(functools.partial(gram_kernel, passes, loads, size, limit)...  34 us
    ppermute x7, starting transfers between devices, go(): return lax.ppermute(chunk, axes, round_pairs(step - 1))  27.5 us
    pallas_call x2, Pallas kernels, gather_rows(): pl.pallas_call(functools.partial(gather_kernel, slots, size, group, secti...  23.2 us
    all_to_all x1, blocking collectives, hosted(): lax.all_to_all(outbound, axes, split_axis=0, concat_axis=0, tiled=True)  16.7 us
    ppermute x7, waiting for transfers between devices, go(): return lax.ppermute(chunk, axes, round_pairs(step - 1))  5.69 us
    ppermute x1, starting transfers between devices, hosted(): named = lax.ppermute(named, axes, metadata_pairs())  4.93 us
    ppermute x4, starting transfers between devices, swap(): return lax.ppermute(chunk, axes, SIBLINGS)  3.41 us
    unnamed x12, local copies, waits for them, and re-layouts  3.15 us
  transfers between devices with their start and end apart: 12, of which 2 were waited for; matrix products, arithmetic and copies ran while one was open for 2% of the time, Pallas kernels for 38%

profile of v17, /device:TPU:0, one launch (start us, length us, event | category | flops | bytes accessed | tf_op | source)
XLA Modules:
  0.0 128.3 jit_solution(3850900238291105491)
XLA Ops:
  0.0 0.7 copy-done
  0.8 0.7 copy-done.4
  1.5 0.7 copy-done.5
  2.2 9.9 %shard_map.55 = (s32[50,128]{1,0:T(8,128)S(1)}, bf16[400,1024]{1,0:T(8,128)(2,1)}) custom-call(s32[6400]{0:T(1024)S(1)} %copy-done, bf16[6400,1024]{1,0:T(8,128)(2,1)} %refs_1_.2, s32[50,128]{1,0:T(8,128)S(1)} %bitcast.9, s32[52,128]{1,0:T(8,128)S(1)} %bitcast.10), custom_call_target="tpu_custom_call" | custom-call | flops 40000000000 | tf_op jit(solution)/shard_map/pallas_call | solution.py:164
  12.2 4.9 %collective-permute-start = (s32[50,128]{1,0:T(8,128)S(1)}, s32[50,128]{1,0:T(8,128)S(1)}, u32[]{:S(2)}, u32[]{:S(2)}) collective-permute-start(s32[50,128]{1,0:T(8,128)S(1)} %get-tuple-element.27), channel_id=1, source_target_pairs={{0,8},{1,9},{4,12},{5,13},{10,10},{11,11},{14,14},{15,15},{16,16},... | collective-permute-start | bytes 76808 | tf_op jit(solution)/shard_map/ppermute | solution.py:423
  17.1 1.5 %collective-permute-done = s32[50,128]{1,0:T(8,128)S(1)} collective-permute-done((s32[50,128]{1,0:T(8,128)S(1)}, s32[50,128]{1,0:T(8,128)S(1)}, u32[]{:S(2)}, u32[]{:S(2)}) %collective-permute-start) | collective-permute-done | bytes 25632 | tf_op jit(solution)/shard_map/ppermute | solution.py:423
  18.7 0.8 collective-permute-start.4
  19.5 5.5 %collective-permute-start.3 = (bf16[400,1024]{1,0:T(8,128)(2,1)}, bf16[400,1024]{1,0:T(8,128)(2,1)S(1)}, u32[]{:S(2)}, u32[]{:S(2)}) collective-permute-start(bf16[400,1024]{1,0:T(8,128)(2,1)} %get-tuple-element.28), channel_id=1, source_target_pairs={{0,8},{4,12},{24,16},{28,20},{5,9},{1,13},{29,17},{25,21},{2,10},{... | collective-permute-start | bytes 2457608 | tf_op jit(solution)/shard_map/ppermute | solution.py:428
  25.0 13.2 %shard_map.56 = (bf16[400,1024]{1,0:T(8,128)(2,1)}, bf16[400,1024]{1,0:T(8,128)(2,1)S(1)}, bf16[400,1024]{1,0:T(8,128)(2,1)S(1)}, bf16[400,1024]{1,0:T(8,128)(2,1)S(1)}) custom-call(s32[6400]{0:T(1024)S(1)} %copy-done, bf16[6400,1024]{1,0:T(8,128)(2,1)} %refs_1_.2), custom_call_target="tpu_custom_call" | custom-call | flops 40000000000 | tf_op jit(solution)/shard_map/pallas_call | solution.py:164
  38.2 0.0 copy-start.2
  38.2 0.9 copy-done.2
  39.1 1.6 %collective-permute-start.5 = (bf16[400,1024]{1,0:T(8,128)(2,1)}, bf16[400,1024]{1,0:T(8,128)(2,1)}, u32[]{:S(2)}, u32[]{:S(2)}) collective-permute-start(bf16[400,1024]{1,0:T(8,128)(2,1)} %get-tuple-element.30), channel_id=1, source_target_pairs={{20,8},{16,12},{12,16},{8,20},{17,9},{21,13},{9,17},{13,21},{22,10... | collective-permute-start | bytes 2457608 | tf_op jit(solution)/shard_map/ppermute | solution.py:428
  40.7 0.0 copy-done.1
  40.7 0.1 reshape.46.refs_5_.index_ref
  40.8 5.4 %collective-permute-start.1 = (bf16[400,1024]{1,0:T(8,128)(2,1)}, bf16[400,1024]{1,0:T(8,128)(2,1)}, u32[]{:S(2)}, u32[]{:S(2)}) collective-permute-start(bf16[400,1024]{1,0:T(8,128)(2,1)} %get-tuple-element.30), channel_id=1, source_target_pairs={{4,8},{0,12},{28,16},{24,20},{1,9},{5,13},{25,17},{29,21},{6,10},{... | collective-permute-start | bytes 2457608 | tf_op jit(solution)/shard_map/ppermute | solution.py:428
  46.2 0.1 reshape.49
  46.3 0.7 fusion
  47.0 0.6 gather_fusion
  47.6 0.1 reshape.50.refs_6_.refs_8_.refs_10_.clusters_ref
  47.7 0.8 fusion.1.refs_4_.order_ref
  48.5 0.0 collective-permute-done.4.refs_3_.refs_0_
  48.5 0.0 collective-permute-done.3.refs_2_
  48.5 5.4 %shard_map.57.refs_7_ = f32[1,6400]{1,0:T(1,128)S(1)} custom-call(bf16[400,1024]{1,0:T(8,128)(2,1)S(1)} %get-tuple-element.34.refs_0_, bf16[400,1024]{1,0:T(8,128)(2,1)S(1)} %get-tuple-element.33.refs_1_, bf16[400,1024]{1,0:T(8,128)(2,1)S(1)} %collective-permute-done.3.refs_2_, bf16[400,1024]{1,0:T(8,128)(2,1)S(1)} %collective-permute-done.4.refs_3_.refs_0_, ...), custom_call_target="tpu_custom_call" | custom-call | tf_op jit(solution)/shard_map/pallas_call | solution.py:289
  53.9 0.7 collective-permute-start.6
  54.6 0.0 copy-done.3
  54.6 0.7 collective-permute-start.9
  55.4 0.0 collective-permute-done.5.refs_2_
  55.4 10.1 %collective-permute-start.8 = (bf16[400,1024]{1,0:T(8,128)(2,1)S(1)}, bf16[400,1024]{1,0:T(8,128)(2,1)S(1)}, u32[]{:S(2)}, u32[]{:S(2)}) collective-permute-start(bf16[400,1024]{1,0:T(8,128)(2,1)S(1)} %copy-done.3), channel_id=1, source_target_pairs={{24,8},{28,12},{0,16},{4,20},{25,9},{29,13},{1,17},{5,21},{26,10},... | collective-permute-start | bytes 2457608 | tf_op jit(solution)/shard_map/ppermute | solution.py:428
  65.5 0.0 collective-permute-done.1.refs_1_
  65.5 3.3 %collective-permute-start.2 = (bf16[400,1024]{1,0:T(8,128)(2,1)S(1)}, bf16[400,1024]{1,0:T(8,128)(2,1)S(1)}, u32[]{:S(2)}, u32[]{:S(2)}) collective-permute-start(bf16[400,1024]{1,0:T(8,128)(2,1)S(1)} %get-tuple-element.33.refs_1_), channel_id=1, source_target_pairs={{28,8},{24,12},{4,16},{0,20},{29,9},{25,13},{5,17},{1,21},{30,10},... | collective-permute-start | bytes 2457608 | tf_op jit(solution)/shard_map/ppermute | solution.py:428
  68.9 1.5 %shard_map.58.refs_4_ = bf16[1200,1024]{1,0:T(8,128)(2,1)S(1)} custom-call(bf16[400,1024]{1,0:T(8,128)(2,1)S(1)} %collective-permute-done.4.refs_3_.refs_0_, bf16[400,1024]{1,0:T(8,128)(2,1)} %collective-permute-done.1.refs_1_, bf16[400,1024]{1,0:T(8,128)(2,1)} %collective-permute-done.5.refs_2_), custom_call_target="tpu_custom_call" | custom-call | flops 2000000000 | tf_op jit(solution)/shard_map/pallas_call | solution.py:319
  70.4 1.0 collective-permute-start.7
  71.4 0.0 collective-permute-done.6.refs_5_
  71.4 7.0 %shard_map.59.refs_9_ = f32[1,6400]{1,0:T(1,128)S(1)} custom-call(bf16[400,1024]{1,0:T(8,128)(2,1)S(1)} %get-tuple-element.34.refs_0_, bf16[400,1024]{1,0:T(8,128)(2,1)S(1)} %get-tuple-element.33.refs_1_, bf16[400,1024]{1,0:T(8,128)(2,1)S(1)} %collective-permute-done.3.refs_2_, bf16[400,1024]{1,0:T(8,128)(2,1)S(1)} %collective-permute-done.4.refs_3_.refs_0_, ...), custom_call_target="tpu_custom_call" | custom-call | tf_op jit(solution)/shard_map/pallas_call | solution.py:289
  78.5 0.0 collective-permute-done.9.refs_1_
  78.5 5.7 %collective-permute-done.8.refs_0_ = bf16[400,1024]{1,0:T(8,128)(2,1)S(1)} collective-permute-done((bf16[400,1024]{1,0:T(8,128)(2,1)S(1)}, bf16[400,1024]{1,0:T(8,128)(2,1)S(1)}, u32[]{:S(2)}, u32[]{:S(2)}) %collective-permute-start.8) | collective-permute-done | bytes 819232 | tf_op jit(solution)/shard_map/ppermute | solution.py:428
  84.1 0.2 shard_map.60.refs_7_
  84.4 0.8 collective-permute-start.11
  85.1 0.0 collective-permute-done.7.refs_6_
  85.1 12.6 %shard_map.61.refs_11_ = f32[1,6400]{1,0:T(1,128)S(1)} custom-call(bf16[400,1024]{1,0:T(8,128)(2,1)S(1)} %get-tuple-element.34.refs_0_, bf16[400,1024]{1,0:T(8,128)(2,1)S(1)} %get-tuple-element.33.refs_1_, bf16[400,1024]{1,0:T(8,128)(2,1)S(1)} %collective-permute-done.3.refs_2_, bf16[400,1024]{1,0:T(8,128)(2,1)S(1)} %collective-permute-done.4.refs_3_.refs_0_, ...), custom_call_target="tpu_custom_call" | custom-call | tf_op jit(solution)/shard_map/pallas_call | solution.py:289
  97.8 0.0 collective-permute-done.2.refs_9_.own_ref
  97.8 0.9 collective-permute-start.10
  98.7 0.0 collective-permute-done.11.refs_8_
  98.7 8.9 %shard_map.62.best_ref = f32[1,6400]{1,0:T(1,128)S(1)} custom-call(bf16[400,1024]{1,0:T(8,128)(2,1)S(1)} %get-tuple-element.34.refs_0_, bf16[400,1024]{1,0:T(8,128)(2,1)S(1)} %get-tuple-element.33.refs_1_, bf16[400,1024]{1,0:T(8,128)(2,1)S(1)} %collective-permute-done.3.refs_2_, bf16[400,1024]{1,0:T(8,128)(2,1)S(1)} %collective-permute-done.4.refs_3_.refs_0_, ...), custom_call_target="tpu_custom_call" | custom-call | tf_op jit(solution)/shard_map/pallas_call | solution.py:289
  107.7 0.0 collective-permute-done.10.other_ref
  107.7 1.5 %shard_map.63 = f32[32,2,400]{2,1,0:T(2,128)S(1)} custom-call(s32[16]{0:T(128)S(1)} %fusion.1.refs_4_.order_ref, bf16[400,1024]{1,0:T(8,128)(2,1)S(1)} %collective-permute-done.2.refs_9_.own_ref, bf16[400,1024]{1,0:T(8,128)(2,1)S(1)} %collective-permute-done.10.other_ref, s32[1,6400]{1,0:T(1,128)S(1)} %reshape.50.refs_6_.refs_8_.refs_10_.clusters_ref, ...), custom_call_target="tpu_custom_call" | custom-call | tf_op jit(solution)/shard_map/pallas_call | solution.py:366
  109.2 16.7 %all_to_all.5.values_ref = f32[32,2,400]{2,1,0:T(2,128)S(1)} all-to-all(f32[32,2,400]{2,1,0:T(2,128)S(1)} %shard_map.63), channel_id=1, replica_groups=mesh['shard'=8,'rep'=4] {'shard','rep'}, dimensions={0} | all-to-all | bytes 204800 | tf_op jit(solution)/shard_map/all_to_all | solution.py:474
  125.9 2.4 %shard_map.64 = f32[50,128]{1,0:T(8,128)} custom-call(s32[8,2,400]{2,1,0:T(2,128)S(1)} %reshape.46.refs_5_.index_ref, f32[32,2,400]{2,1,0:T(2,128)S(1)} %all_to_all.5.values_ref), custom_call_target="tpu_custom_call" | custom-call | tf_op jit(solution)/shard_map/pallas_call | solution.py:406
  (7 shorter events, 0.0 us)
Async XLA Ops:
  0.0 0.7 copy-start
  0.7 0.7 copy-start.4
  1.5 0.7 copy-start.5
  12.2 6.5 %collective-permute-start = (s32[50,128]{1,0:T(8,128)S(1)}, s32[50,128]{1,0:T(8,128)S(1)}, u32[]{:S(2)}, u32[]{:S(2)}) collective-permute-start(s32[50,128]{1,0:T(8,128)S(1)} %get-tuple-element.27), channel_id=1, source_target_pairs={{0,8},{1,9},{4,12},{5,13},{10,10},{11,11},{14,14},{15,15},{16,16},... | collective-permute-start | bytes 76808 | tf_op jit(solution)/shard_map/ppermute | solution.py:423
  18.7 22.0 %copy-start.1 = (s32[6400]{0:T(1024)S(1)}, s32[6400]{0:T(1024)}, u32[]{:S(2)}) copy-start(s32[6400]{0:T(1024)} %refs_0_.3) | copy-start | bytes 76804
  18.7 29.8 %collective-permute-start.4 = (bf16[400,1024]{1,0:T(8,128)(2,1)}, bf16[400,1024]{1,0:T(8,128)(2,1)S(1)}, u32[]{:S(2)}, u32[]{:S(2)}) collective-permute-start(bf16[400,1024]{1,0:T(8,128)(2,1)} %get-tuple-element.28), channel_id=1, source_target_pairs={{16,8},{20,12},{8,16},{12,20},{21,9},{17,13},{13,17},{9,21},{18,10... | collective-permute-start | bytes 2457608 | tf_op jit(solution)/shard_map/ppermute | solution.py:428
  19.5 29.0 %collective-permute-start.3 = (bf16[400,1024]{1,0:T(8,128)(2,1)}, bf16[400,1024]{1,0:T(8,128)(2,1)S(1)}, u32[]{:S(2)}, u32[]{:S(2)}) collective-permute-start(bf16[400,1024]{1,0:T(8,128)(2,1)} %get-tuple-element.28), channel_id=1, source_target_pairs={{0,8},{4,12},{24,16},{28,20},{5,9},{1,13},{29,17},{25,21},{2,10},{... | collective-permute-start | bytes 2457608 | tf_op jit(solution)/shard_map/ppermute | solution.py:428
  38.2 0.9 copy-start.2
  39.1 16.2 %collective-permute-start.5 = (bf16[400,1024]{1,0:T(8,128)(2,1)}, bf16[400,1024]{1,0:T(8,128)(2,1)}, u32[]{:S(2)}, u32[]{:S(2)}) collective-permute-start(bf16[400,1024]{1,0:T(8,128)(2,1)} %get-tuple-element.30), channel_id=1, source_target_pairs={{20,8},{16,12},{12,16},{8,20},{17,9},{21,13},{9,17},{13,21},{22,10... | collective-permute-start | bytes 2457608 | tf_op jit(solution)/shard_map/ppermute | solution.py:428
  40.8 24.7 %collective-permute-start.1 = (bf16[400,1024]{1,0:T(8,128)(2,1)}, bf16[400,1024]{1,0:T(8,128)(2,1)}, u32[]{:S(2)}, u32[]{:S(2)}) collective-permute-start(bf16[400,1024]{1,0:T(8,128)(2,1)} %get-tuple-element.30), channel_id=1, source_target_pairs={{4,8},{0,12},{28,16},{24,20},{1,9},{5,13},{25,17},{29,21},{6,10},{... | collective-permute-start | bytes 2457608 | tf_op jit(solution)/shard_map/ppermute | solution.py:428
  47.7 6.9 %copy-start.3 = (bf16[400,1024]{1,0:T(8,128)(2,1)S(1)}, bf16[400,1024]{1,0:T(8,128)(2,1)}, u32[]{:S(2)}) copy-start(bf16[400,1024]{1,0:T(8,128)(2,1)} %copy-done.2) | copy-start | bytes 2457604
  53.9 17.5 %collective-permute-start.6 = (bf16[400,1024]{1,0:T(8,128)(2,1)S(1)}, bf16[400,1024]{1,0:T(8,128)(2,1)S(1)}, u32[]{:S(2)}, u32[]{:S(2)}) collective-permute-start(bf16[400,1024]{1,0:T(8,128)(2,1)S(1)} %collective-permute-done.3.refs_2_), channel_id=1, source_target_pairs={{8,9},{9,8},{10,11},{11,10},{12,13},{13,12},{14,15},{15,14},{16,17... | collective-permute-start | bytes 2457608 | tf_op jit(solution)/shard_map/ppermute | solution.py:431
  54.6 23.8 %collective-permute-start.9 = (bf16[400,1024]{1,0:T(8,128)(2,1)S(1)}, bf16[400,1024]{1,0:T(8,128)(2,1)S(1)}, u32[]{:S(2)}, u32[]{:S(2)}) collective-permute-start(bf16[400,1024]{1,0:T(8,128)(2,1)S(1)} %copy-done.3), channel_id=1, source_target_pairs={{12,8},{8,12},{20,16},{16,20},{13,9},{9,13},{21,17},{17,21},{14,10... | collective-permute-start | bytes 2457608 | tf_op jit(solution)/shard_map/ppermute | solution.py:428
  55.4 28.8 %collective-permute-start.8 = (bf16[400,1024]{1,0:T(8,128)(2,1)S(1)}, bf16[400,1024]{1,0:T(8,128)(2,1)S(1)}, u32[]{:S(2)}, u32[]{:S(2)}) collective-permute-start(bf16[400,1024]{1,0:T(8,128)(2,1)S(1)} %copy-done.3), channel_id=1, source_target_pairs={{24,8},{28,12},{0,16},{4,20},{25,9},{29,13},{1,17},{5,21},{26,10},... | collective-permute-start | bytes 2457608 | tf_op jit(solution)/shard_map/ppermute | solution.py:428
  65.5 32.2 %collective-permute-start.2 = (bf16[400,1024]{1,0:T(8,128)(2,1)S(1)}, bf16[400,1024]{1,0:T(8,128)(2,1)S(1)}, u32[]{:S(2)}, u32[]{:S(2)}) collective-permute-start(bf16[400,1024]{1,0:T(8,128)(2,1)S(1)} %get-tuple-element.33.refs_1_), channel_id=1, source_target_pairs={{28,8},{24,12},{4,16},{0,20},{29,9},{25,13},{5,17},{1,21},{30,10},... | collective-permute-start | bytes 2457608 | tf_op jit(solution)/shard_map/ppermute | solution.py:428
  70.4 14.8 %collective-permute-start.7 = (bf16[1200,1024]{1,0:T(8,128)(2,1)S(1)}, bf16[1200,1024]{1,0:T(8,128)(2,1)S(1)}, u32[]{:S(2)}, u32[]{:S(2)}) collective-permute-start(bf16[1200,1024]{1,0:T(8,128)(2,1)S(1)} %shard_map.58.refs_4_), channel_id=1, source_target_pairs={{8,9},{9,8},{10,11},{11,10},{12,13},{13,12},{14,15},{15,14},{16,17... | collective-permute-start | bytes 7372808 | tf_op jit(solution)/shard_map/ppermute | solution.py:431
  84.4 14.4 %collective-permute-start.11 = (bf16[800,1024]{1,0:T(8,128)(2,1)S(1)}, bf16[800,1024]{1,0:T(8,128)(2,1)S(1)}, u32[]{:S(2)}, u32[]{:S(2)}) collective-permute-start(bf16[800,1024]{1,0:T(8,128)(2,1)S(1)} %shard_map.60.refs_7_), channel_id=1, source_target_pairs={{8,9},{9,8},{10,11},{11,10},{12,13},{13,12},{14,15},{15,14},{16,17... | collective-permute-start | bytes 4915208 | tf_op jit(solution)/shard_map/ppermute | solution.py:431
  97.8 9.9 %collective-permute-start.10 = (bf16[400,1024]{1,0:T(8,128)(2,1)S(1)}, bf16[400,1024]{1,0:T(8,128)(2,1)S(1)}, u32[]{:S(2)}, u32[]{:S(2)}) collective-permute-start(bf16[400,1024]{1,0:T(8,128)(2,1)S(1)} %collective-permute-done.2.refs_9_.own_ref), channel_id=1, source_target_pairs={{8,9},{9,8},{10,11},{11,10},{12,13},{13,12},{14,15},{15,14},{16,17... | collective-permute-start | bytes 2457608 | tf_op jit(solution)/shard_map/ppermute | solution.py:431

commit v18 on v16

--- a/solution.py
+++ b/solution.py
@@ -370,8 +370,6 @@
 
 def settle_kernel(sources, size, high, index_ref, values_ref, out_ref, left_ref, right_ref):
     wide = left_ref.shape[1] // len(sources)
-    left_ref[...] = jnp.zeros_like(left_ref)
-    right_ref[...] = jnp.zeros_like(right_ref)
     rows = lax.broadcasted_iota(jnp.int32, (high, size), 0)
     lanes = lax.broadcasted_iota(jnp.int32, (LANES, size), 0)
     for g, places in enumerate(sources):
@@ -380,6 +378,10 @@
         for a, b in places[1:]:
             value = jnp.maximum(value, values_ref[a, b : b + 1, :])
         span = slice(g * wide, g * wide + size)
+        if size % LANES:
+            tail = slice((g + 1) * wide - LANES, (g + 1) * wide)
+            left_ref[:, tail] = jnp.zeros((3 * high, LANES), jnp.bfloat16)
+            right_ref[:, tail] = jnp.zeros((LANES, LANES), jnp.bfloat16)
         here = rows == index // LANES
         for piece in range(3):
             head = value.astype(jnp.bfloat16).astype(jnp.float32)

time: 124 us -> 125 us (level)
  no operation moved by 1% of the time
where the time goes in v18:
time: 125 us; the launch traced here: 124 us
  Pallas kernels  64.4 us (52%)
  starting transfers between devices  33 us (26%)
  blocking collectives  15.8 us (13%)
  waiting for transfers between devices  6.47 us (5%)
  local copies, waits for them, and re-layouts  3.3 us (3%)
    pallas_call x4, Pallas kernels, gram_best(): pl.pallas_call(functools.partial(gram_kernel, passes, loads, size, limit)...  34 us
    ppermute x7, starting transfers between devices, go(): return lax.ppermute(chunk, axes, round_pairs(step - 1))  24.6 us
    pallas_call x2, Pallas kernels, gather_rows(): pl.pallas_call(functools.partial(gather_kernel, slots, size, group, secti...  23.2 us
    all_to_all x1, blocking collectives, hosted(): lax.all_to_all(outbound, axes, split_axis=0, concat_axis=0, tiled=True)  15.8 us
    ppermute x7, waiting for transfers between devices, go(): return lax.ppermute(chunk, axes, round_pairs(step - 1))  6.46 us
    ppermute x1, starting transfers between devices, hosted(): named = lax.ppermute(named, axes, metadata_pairs())  4.92 us
    ppermute x4, starting transfers between devices, swap(): return lax.ppermute(chunk, axes, SIBLINGS)  3.4 us
    pallas_call x1, Pallas kernels, settle(): pl.pallas_call(functools.partial(settle_kernel, sources, size, high), out...  2.55 us
  transfers between devices with their start and end apart: 12, of which 2 were waited for; matrix products, arithmetic and copies ran while one was open for 2% of the time, Pallas kernels for 48%

profile of v18, /device:TPU:0, one launch (start us, length us, event | category | flops | bytes accessed | tf_op | source)
XLA Modules:
  0.0 123.9 jit_solution(3680522732360919177)
XLA Ops:
  0.0 1.5 %shard_map.55 = s32[50,128]{1,0:T(8,128)} custom-call(s32[50,128]{1,0:T(8,128)} %bitcast.9, s32[52,128]{1,0:T(8,128)} %bitcast.10), custom_call_target="tpu_custom_call" | custom-call | tf_op jit(solution)/shard_map/pallas_call | solution.py:87
  1.5 4.9 %collective-permute-start = (s32[50,128]{1,0:T(8,128)}, s32[50,128]{1,0:T(8,128)S(1)}, u32[]{:S(2)}, u32[]{:S(2)}) collective-permute-start(s32[50,128]{1,0:T(8,128)} %shard_map.55), channel_id=1, source_target_pairs={{0,8},{1,9},{4,12},{5,13},{10,10},{11,11},{14,14},{15,15},{16,16},... | collective-permute-start | bytes 76808 | tf_op jit(solution)/shard_map/ppermute | solution.py:421
  6.4 0.0 copy-start
  6.4 0.7 copy-done
  7.1 9.9 %shard_map.56 = bf16[400,1024]{1,0:T(8,128)(2,1)} custom-call(s32[6400]{0:T(1024)S(1)} %copy-done, bf16[6400,1024]{1,0:T(8,128)(2,1)} %refs_1_.1), custom_call_target="tpu_custom_call" | custom-call | flops 40000000000 | tf_op jit(solution)/shard_map/pallas_call | solution.py:159
  17.1 0.0 copy-start.1
  17.1 0.0 collective-permute-done
  17.1 0.7 collective-permute-start.4
  17.8 4.2 %collective-permute-start.3 = (bf16[400,1024]{1,0:T(8,128)(2,1)}, bf16[400,1024]{1,0:T(8,128)(2,1)S(1)}, u32[]{:S(2)}, u32[]{:S(2)}) collective-permute-start(bf16[400,1024]{1,0:T(8,128)(2,1)} %shard_map.56), channel_id=1, source_target_pairs={{0,8},{4,12},{24,16},{28,20},{5,9},{1,13},{29,17},{25,21},{2,10},{... | collective-permute-start | bytes 2457608 | tf_op jit(solution)/shard_map/ppermute | solution.py:426
  22.0 13.2 %shard_map.57 = (bf16[400,1024]{1,0:T(8,128)(2,1)}, bf16[400,1024]{1,0:T(8,128)(2,1)S(1)}, bf16[400,1024]{1,0:T(8,128)(2,1)S(1)}, bf16[400,1024]{1,0:T(8,128)(2,1)S(1)}) custom-call(s32[6400]{0:T(1024)S(1)} %copy-done, bf16[6400,1024]{1,0:T(8,128)(2,1)} %refs_1_.1), custom_call_target="tpu_custom_call" | custom-call | flops 40000000000 | tf_op jit(solution)/shard_map/pallas_call | solution.py:159
  35.3 0.0 copy-start.2
  35.3 0.9 copy-done.2
  36.2 1.6 %collective-permute-start.5 = (bf16[400,1024]{1,0:T(8,128)(2,1)}, bf16[400,1024]{1,0:T(8,128)(2,1)}, u32[]{:S(2)}, u32[]{:S(2)}) collective-permute-start(bf16[400,1024]{1,0:T(8,128)(2,1)} %get-tuple-element.28), channel_id=1, source_target_pairs={{20,8},{16,12},{12,16},{8,20},{17,9},{21,13},{9,17},{13,21},{22,10... | collective-permute-start | bytes 2457608 | tf_op jit(solution)/shard_map/ppermute | solution.py:426
  37.8 0.0 copy-done.1
  37.8 0.1 reshape.46.refs_5_.index_ref
  37.9 3.7 %collective-permute-start.1 = (bf16[400,1024]{1,0:T(8,128)(2,1)}, bf16[400,1024]{1,0:T(8,128)(2,1)}, u32[]{:S(2)}, u32[]{:S(2)}) collective-permute-start(bf16[400,1024]{1,0:T(8,128)(2,1)} %get-tuple-element.28), channel_id=1, source_target_pairs={{4,8},{0,12},{28,16},{24,20},{1,9},{5,13},{25,17},{29,21},{6,10},{... | collective-permute-start | bytes 2457608 | tf_op jit(solution)/shard_map/ppermute | solution.py:426
  41.6 0.1 reshape.49
  41.7 0.7 fusion
  42.4 0.6 gather_fusion
  43.0 0.1 reshape.50.refs_6_.refs_8_.refs_10_.clusters_ref
  43.1 0.8 fusion.1.refs_4_.order_ref
  43.9 0.0 collective-permute-done.4.refs_3_.refs_0_
  43.9 0.0 collective-permute-done.3.refs_2_
  43.9 5.4 %shard_map.58.refs_7_ = f32[1,6400]{1,0:T(1,128)S(1)} custom-call(bf16[400,1024]{1,0:T(8,128)(2,1)S(1)} %get-tuple-element.32.refs_0_, bf16[400,1024]{1,0:T(8,128)(2,1)S(1)} %get-tuple-element.31.refs_1_, bf16[400,1024]{1,0:T(8,128)(2,1)S(1)} %collective-permute-done.3.refs_2_, bf16[400,1024]{1,0:T(8,128)(2,1)S(1)} %collective-permute-done.4.refs_3_.refs_0_, ...), custom_call_target="tpu_custom_call" | custom-call | tf_op jit(solution)/shard_map/pallas_call | solution.py:283
  49.3 0.7 collective-permute-start.6
  50.0 0.7 collective-permute-start.9
  50.8 0.0 collective-permute-done.5.refs_2_
  50.8 10.3 %collective-permute-start.8 = (bf16[400,1024]{1,0:T(8,128)(2,1)S(1)}, bf16[400,1024]{1,0:T(8,128)(2,1)S(1)}, u32[]{:S(2)}, u32[]{:S(2)}) collective-permute-start(bf16[400,1024]{1,0:T(8,128)(2,1)S(1)} %copy-done.3), channel_id=1, source_target_pairs={{24,8},{28,12},{0,16},{4,20},{25,9},{29,13},{1,17},{5,21},{26,10},... | collective-permute-start | bytes 2457608 | tf_op jit(solution)/shard_map/ppermute | solution.py:426
  61.1 0.0 collective-permute-done.1.refs_1_
  61.1 3.4 %collective-permute-start.2 = (bf16[400,1024]{1,0:T(8,128)(2,1)S(1)}, bf16[400,1024]{1,0:T(8,128)(2,1)S(1)}, u32[]{:S(2)}, u32[]{:S(2)}) collective-permute-start(bf16[400,1024]{1,0:T(8,128)(2,1)S(1)} %get-tuple-element.31.refs_1_), channel_id=1, source_target_pairs={{28,8},{24,12},{4,16},{0,20},{29,9},{25,13},{5,17},{1,21},{30,10},... | collective-permute-start | bytes 2457608 | tf_op jit(solution)/shard_map/ppermute | solution.py:426
  64.5 1.5 %shard_map.59.refs_4_ = bf16[1200,1024]{1,0:T(8,128)(2,1)S(1)} custom-call(bf16[400,1024]{1,0:T(8,128)(2,1)S(1)} %collective-permute-done.4.refs_3_.refs_0_, bf16[400,1024]{1,0:T(8,128)(2,1)} %collective-permute-done.1.refs_1_, bf16[400,1024]{1,0:T(8,128)(2,1)} %collective-permute-done.5.refs_2_), custom_call_target="tpu_custom_call" | custom-call | flops 2000000000 | tf_op jit(solution)/shard_map/pallas_call | solution.py:313
  66.0 1.0 collective-permute-start.7
  67.0 0.0 collective-permute-done.6.refs_5_
  67.0 7.0 %shard_map.60.refs_9_ = f32[1,6400]{1,0:T(1,128)S(1)} custom-call(bf16[400,1024]{1,0:T(8,128)(2,1)S(1)} %get-tuple-element.32.refs_0_, bf16[400,1024]{1,0:T(8,128)(2,1)S(1)} %get-tuple-element.31.refs_1_, bf16[400,1024]{1,0:T(8,128)(2,1)S(1)} %collective-permute-done.3.refs_2_, bf16[400,1024]{1,0:T(8,128)(2,1)S(1)} %collective-permute-done.4.refs_3_.refs_0_, ...), custom_call_target="tpu_custom_call" | custom-call | tf_op jit(solution)/shard_map/pallas_call | solution.py:283
  74.1 0.0 collective-permute-done.9.refs_1_
  74.1 5.6 %collective-permute-done.8.refs_0_ = bf16[400,1024]{1,0:T(8,128)(2,1)S(1)} collective-permute-done((bf16[400,1024]{1,0:T(8,128)(2,1)S(1)}, bf16[400,1024]{1,0:T(8,128)(2,1)S(1)}, u32[]{:S(2)}, u32[]{:S(2)}) %collective-permute-start.8) | collective-permute-done | bytes 819232 | tf_op jit(solution)/shard_map/ppermute | solution.py:426
  79.7 0.2 shard_map.61.refs_7_
  79.9 0.8 collective-permute-start.11
  80.7 0.0 collective-permute-done.7.refs_6_
  80.7 12.6 %shard_map.62.refs_11_ = f32[1,6400]{1,0:T(1,128)S(1)} custom-call(bf16[400,1024]{1,0:T(8,128)(2,1)S(1)} %get-tuple-element.32.refs_0_, bf16[400,1024]{1,0:T(8,128)(2,1)S(1)} %get-tuple-element.31.refs_1_, bf16[400,1024]{1,0:T(8,128)(2,1)S(1)} %collective-permute-done.3.refs_2_, bf16[400,1024]{1,0:T(8,128)(2,1)S(1)} %collective-permute-done.4.refs_3_.refs_0_, ...), custom_call_target="tpu_custom_call" | custom-call | tf_op jit(solution)/shard_map/pallas_call | solution.py:283
  93.3 0.8 collective-permute-done.2.refs_9_.own_ref
  94.2 0.9 collective-permute-start.10
  95.1 0.0 collective-permute-done.11.refs_8_
  95.1 9.0 %shard_map.63.best_ref = f32[1,6400]{1,0:T(1,128)S(1)} custom-call(bf16[400,1024]{1,0:T(8,128)(2,1)S(1)} %get-tuple-element.32.refs_0_, bf16[400,1024]{1,0:T(8,128)(2,1)S(1)} %get-tuple-element.31.refs_1_, bf16[400,1024]{1,0:T(8,128)(2,1)S(1)} %collective-permute-done.3.refs_2_, bf16[400,1024]{1,0:T(8,128)(2,1)S(1)} %collective-permute-done.4.refs_3_.refs_0_, ...), custom_call_target="tpu_custom_call" | custom-call | tf_op jit(solution)/shard_map/pallas_call | solution.py:283
  104.1 0.0 collective-permute-done.10.other_ref
  104.1 1.5 %shard_map.64 = f32[32,2,400]{2,1,0:T(2,128)S(1)} custom-call(s32[16]{0:T(128)S(1)} %fusion.1.refs_4_.order_ref, bf16[400,1024]{1,0:T(8,128)(2,1)S(1)} %collective-permute-done.2.refs_9_.own_ref, bf16[400,1024]{1,0:T(8,128)(2,1)S(1)} %collective-permute-done.10.other_ref, s32[1,6400]{1,0:T(1,128)S(1)} %reshape.50.refs_6_.refs_8_.refs_10_.clusters_ref, ...), custom_call_target="tpu_custom_call" | custom-call | tf_op jit(solution)/shard_map/pallas_call | solution.py:360
  105.6 15.8 %all_to_all.5.values_ref = f32[32,2,400]{2,1,0:T(2,128)S(1)} all-to-all(f32[32,2,400]{2,1,0:T(2,128)S(1)} %shard_map.64), channel_id=1, replica_groups=mesh['shard'=8,'rep'=4] {'shard','rep'}, dimensions={0} | all-to-all | bytes 204800 | tf_op jit(solution)/shard_map/all_to_all | solution.py:472
  121.4 2.6 %shard_map.65 = f32[50,128]{1,0:T(8,128)} custom-call(s32[8,2,400]{2,1,0:T(2,128)S(1)} %reshape.46.refs_5_.index_ref, f32[32,2,400]{2,1,0:T(2,128)S(1)} %all_to_all.5.values_ref), custom_call_target="tpu_custom_call" | custom-call | tf_op jit(solution)/shard_map/pallas_call | solution.py:402
  (4 shorter events, 0.0 us)
Async XLA Ops:
  1.5 15.6 %collective-permute-start = (s32[50,128]{1,0:T(8,128)}, s32[50,128]{1,0:T(8,128)S(1)}, u32[]{:S(2)}, u32[]{:S(2)}) collective-permute-start(s32[50,128]{1,0:T(8,128)} %shard_map.55), channel_id=1, source_target_pairs={{0,8},{1,9},{4,12},{5,13},{10,10},{11,11},{14,14},{15,15},{16,16},... | collective-permute-start | bytes 76808 | tf_op jit(solution)/shard_map/ppermute | solution.py:421
  6.4 0.8 copy-start
  17.1 20.7 %copy-start.1 = (s32[6400]{0:T(1024)S(1)}, s32[6400]{0:T(1024)}, u32[]{:S(2)}) copy-start(s32[6400]{0:T(1024)} %refs_0_.3) | copy-start | bytes 76804
  17.1 26.8 %collective-permute-start.4 = (bf16[400,1024]{1,0:T(8,128)(2,1)}, bf16[400,1024]{1,0:T(8,128)(2,1)S(1)}, u32[]{:S(2)}, u32[]{:S(2)}) collective-permute-start(bf16[400,1024]{1,0:T(8,128)(2,1)} %shard_map.56), channel_id=1, source_target_pairs={{16,8},{20,12},{8,16},{12,20},{21,9},{17,13},{13,17},{9,21},{18,10... | collective-permute-start | bytes 2457608 | tf_op jit(solution)/shard_map/ppermute | solution.py:426
  17.8 26.0 %collective-permute-start.3 = (bf16[400,1024]{1,0:T(8,128)(2,1)}, bf16[400,1024]{1,0:T(8,128)(2,1)S(1)}, u32[]{:S(2)}, u32[]{:S(2)}) collective-permute-start(bf16[400,1024]{1,0:T(8,128)(2,1)} %shard_map.56), channel_id=1, source_target_pairs={{0,8},{4,12},{24,16},{28,20},{5,9},{1,13},{29,17},{25,21},{2,10},{... | collective-permute-start | bytes 2457608 | tf_op jit(solution)/shard_map/ppermute | solution.py:426
  35.3 0.9 copy-start.2
  36.2 14.6 %collective-permute-start.5 = (bf16[400,1024]{1,0:T(8,128)(2,1)}, bf16[400,1024]{1,0:T(8,128)(2,1)}, u32[]{:S(2)}, u32[]{:S(2)}) collective-permute-start(bf16[400,1024]{1,0:T(8,128)(2,1)} %get-tuple-element.28), channel_id=1, source_target_pairs={{20,8},{16,12},{12,16},{8,20},{17,9},{21,13},{9,17},{13,21},{22,10... | collective-permute-start | bytes 2457608 | tf_op jit(solution)/shard_map/ppermute | solution.py:426
  37.9 23.2 %collective-permute-start.1 = (bf16[400,1024]{1,0:T(8,128)(2,1)}, bf16[400,1024]{1,0:T(8,128)(2,1)}, u32[]{:S(2)}, u32[]{:S(2)}) collective-permute-start(bf16[400,1024]{1,0:T(8,128)(2,1)} %get-tuple-element.28), channel_id=1, source_target_pairs={{4,8},{0,12},{28,16},{24,20},{1,9},{5,13},{25,17},{29,21},{6,10},{... | collective-permute-start | bytes 2457608 | tf_op jit(solution)/shard_map/ppermute | solution.py:426
  43.1 7.0 %copy-start.3 = (bf16[400,1024]{1,0:T(8,128)(2,1)S(1)}, bf16[400,1024]{1,0:T(8,128)(2,1)}, u32[]{:S(2)}) copy-start(bf16[400,1024]{1,0:T(8,128)(2,1)} %copy-done.2) | copy-start | bytes 2457604
  49.3 17.7 %collective-permute-start.6 = (bf16[400,1024]{1,0:T(8,128)(2,1)S(1)}, bf16[400,1024]{1,0:T(8,128)(2,1)S(1)}, u32[]{:S(2)}, u32[]{:S(2)}) collective-permute-start(bf16[400,1024]{1,0:T(8,128)(2,1)S(1)} %collective-permute-done.3.refs_2_), channel_id=1, source_target_pairs={{8,9},{9,8},{10,11},{11,10},{12,13},{13,12},{14,15},{15,14},{16,17... | collective-permute-start | bytes 2457608 | tf_op jit(solution)/shard_map/ppermute | solution.py:429
  50.0 24.0 %collective-permute-start.9 = (bf16[400,1024]{1,0:T(8,128)(2,1)S(1)}, bf16[400,1024]{1,0:T(8,128)(2,1)S(1)}, u32[]{:S(2)}, u32[]{:S(2)}) collective-permute-start(bf16[400,1024]{1,0:T(8,128)(2,1)S(1)} %copy-done.3), channel_id=1, source_target_pairs={{12,8},{8,12},{20,16},{16,20},{13,9},{9,13},{21,17},{17,21},{14,10... | collective-permute-start | bytes 2457608 | tf_op jit(solution)/shard_map/ppermute | solution.py:426
  50.8 28.9 %collective-permute-start.8 = (bf16[400,1024]{1,0:T(8,128)(2,1)S(1)}, bf16[400,1024]{1,0:T(8,128)(2,1)S(1)}, u32[]{:S(2)}, u32[]{:S(2)}) collective-permute-start(bf16[400,1024]{1,0:T(8,128)(2,1)S(1)} %copy-done.3), channel_id=1, source_target_pairs={{24,8},{28,12},{0,16},{4,20},{25,9},{29,13},{1,17},{5,21},{26,10},... | collective-permute-start | bytes 2457608 | tf_op jit(solution)/shard_map/ppermute | solution.py:426
  61.1 33.1 %collective-permute-start.2 = (bf16[400,1024]{1,0:T(8,128)(2,1)S(1)}, bf16[400,1024]{1,0:T(8,128)(2,1)S(1)}, u32[]{:S(2)}, u32[]{:S(2)}) collective-permute-start(bf16[400,1024]{1,0:T(8,128)(2,1)S(1)} %get-tuple-element.31.refs_1_), channel_id=1, source_target_pairs={{28,8},{24,12},{4,16},{0,20},{29,9},{25,13},{5,17},{1,21},{30,10},... | collective-permute-start | bytes 2457608 | tf_op jit(solution)/shard_map/ppermute | solution.py:426
  66.0 14.7 %collective-permute-start.7 = (bf16[1200,1024]{1,0:T(8,128)(2,1)S(1)}, bf16[1200,1024]{1,0:T(8,128)(2,1)S(1)}, u32[]{:S(2)}, u32[]{:S(2)}) collective-permute-start(bf16[1200,1024]{1,0:T(8,128)(2,1)S(1)} %shard_map.59.refs_4_), channel_id=1, source_target_pairs={{8,9},{9,8},{10,11},{11,10},{12,13},{13,12},{14,15},{15,14},{16,17... | collective-permute-start | bytes 7372808 | tf_op jit(solution)/shard_map/ppermute | solution.py:429
  79.9 15.2 %collective-permute-start.11 = (bf16[800,1024]{1,0:T(8,128)(2,1)S(1)}, bf16[800,1024]{1,0:T(8,128)(2,1)S(1)}, u32[]{:S(2)}, u32[]{:S(2)}) collective-permute-start(bf16[800,1024]{1,0:T(8,128)(2,1)S(1)} %shard_map.61.refs_7_), channel_id=1, source_target_pairs={{8,9},{9,8},{10,11},{11,10},{12,13},{13,12},{14,15},{15,14},{16,17... | collective-permute-start | bytes 4915208 | tf_op jit(solution)/shard_map/ppermute | solution.py:429
  94.2 9.9 %collective-permute-start.10 = (bf16[400,1024]{1,0:T(8,128)(2,1)S(1)}, bf16[400,1024]{1,0:T(8,128)(2,1)S(1)}, u32[]{:S(2)}, u32[]{:S(2)}) collective-permute-start(bf16[400,1024]{1,0:T(8,128)(2,1)S(1)} %collective-permute-done.2.refs_9_.own_ref), channel_id=1, source_target_pairs={{8,9},{9,8},{10,11},{11,10},{12,13},{13,12},{14,15},{15,14},{16,17... | collective-permute-start | bytes 2457608 | tf_op jit(solution)/shard_map/ppermute | solution.py:429
